TPU v7x, 32 devices: a whole 2x2x4 slice. The times are simulated.
32 devices in a mesh: rows: 4 (over x, core), seq: 8 (over z, y).
Axes of the slice: x: 2, y: 2, z: 4, core: 2. Of those that a mesh axis runs over, the one named last changes fastest.
Arguments:
- tokens: bfloat16 [4, 3, 384, 2048], P('rows', None, 'seq'), may hold values from -6 to 6
- summary: bfloat16 [4, 2, 50, 2048], P('rows'), may hold values from -6 to 6
- doc_ids: int32 [4, 3, 384], P('rows'), may hold values from 0 to 3, as said below
- gain_attn: float32 [2048], replicated, may hold values from 0.25 to 1.75
- gain_ffn: float32 [2048], replicated, may hold values from 0.25 to 1.75
- w_query: bfloat16 [2048, 2048], P(('rows', 'seq')), may hold values from -0.125 to 0.125
- w_key: bfloat16 [2048, 2048], P(('rows', 'seq')), may hold values from -0.125 to 0.125
- w_value: bfloat16 [2048, 2048], P(('rows', 'seq')), may hold values from -0.125 to 0.125
- w_out: bfloat16 [2048, 2048], P(('rows', 'seq')), may hold values from -1.25 to 1.25
- w_up: bfloat16 [2048, 8192], P(('rows', 'seq')), may hold values from -0.125 to 0.125
- w_down: bfloat16 [2048, 8192], P(('rows', 'seq')), may hold values from -0.0625 to 0.0625
- cotangent: bfloat16 [4, 3, 384, 2048], P('rows', None, 'seq'), may hold values from -6 to 6
Outputs:
- activations: bfloat16 [4, 3, 384, 2048], P('rows', None, 'seq')
- d_tokens: float32 [4, 3, 384, 2048], P('rows', None, 'seq')
- d_summary: float32 [4, 2, 50, 2048], P('rows')
- d_gain_attn: float32 [2048], P(('rows', 'seq'))
- d_gain_ffn: float32 [2048], P(('rows', 'seq'))
- d_w_query: float32 [2048, 2048], P(('rows', 'seq'))
- d_w_key: float32 [2048, 2048], P(('rows', 'seq'))
- d_w_value: float32 [2048, 2048], P(('rows', 'seq'))
- d_w_out: float32 [2048, 2048], P(('rows', 'seq'))
- d_w_up: float32 [2048, 8192], P(('rows', 'seq'))
- d_w_down: float32 [2048, 8192], P(('rows', 'seq'))
Inputs may be any that keep to these rules, and one draw needn't show every extreme that they name: `doc_ids`: along each sequence the ids never fall; they start at 0 and rise by one at each document start. In each sequence one of the 3 segments lies within a single document.
All inputs are finite; a program needn't handle non-finite values.
Results may differ from a plain program's by a relative error of at most 0.025.
Values may be sent and summed in bfloat16 or wider, within the bound.
No kernel may reach another device: no remote copies, remote signals or barrier semaphores. Data moves between devices by JAX's collectives and lax.ppermute only.
A program may use at most 768 MiB of HBM per device.

v0:
```python
import jax
import jax.numpy as jnp
from jax import lax
from jax.sharding import PartitionSpec as P

H = 32


EPSILON = 1e-05
MASKED = -1e30
SQRT_HALF = 0.7071067811865476
NORMAL_PEAK = 0.3989422804014327


def normalize(inputs):
    average = jnp.mean(inputs, axis=-1, keepdims=True)
    centred = inputs - average
    inverse = lax.rsqrt(jnp.mean(centred * centred, axis=-1, keepdims=True) + EPSILON)
    return (centred * inverse, inverse)


def normalize_back(upstream, scaling, standard, inverse):
    scaled = upstream * scaling
    return inverse * (
        scaled
        - jnp.mean(scaled, axis=-1, keepdims=True)
        - standard * jnp.mean(scaled * standard, axis=-1, keepdims=True)
    )


def gelu_slope(inputs):
    return (
        0.5 * (1.0 + lax.erf(inputs * SQRT_HALF))
        + inputs * jnp.exp(-0.5 * inputs * inputs) * NORMAL_PEAK
    )


def block_size(total_rows, unit_rows):
    unit_rows = min(unit_rows, total_rows)
    shards = total_rows // unit_rows
    best_factor = 1
    for factor in range(1, shards + 1):
        if shards % factor == 0 and factor * unit_rows <= 256:
            best_factor = factor
    return best_factor * unit_rows


def over_blocks(carried, pieces, unit_rows, step_fn):
    total_rows = pieces[0].shape[2]
    span_rows = block_size(total_rows, unit_rows)

    def advance(running, number):
        first_row = number * span_rows
        block_parts = tuple(
            (lax.dynamic_slice_in_dim(member, first_row, span_rows, 2) for member in pieces)
        )
        return (step_fn(running, block_parts, first_row), None)

    carried, leftover = lax.scan(
        advance, carried, jnp.arange(total_rows // span_rows, dtype=jnp.int32)
    )
    return carried


def token_mask(doc_ids, query_first, query_rows, key_first, key_rows):
    query_pos = query_first + jnp.arange(query_rows, dtype=jnp.int32)
    key_pos = key_first + jnp.arange(key_rows, dtype=jnp.int32)
    query_docs = lax.dynamic_slice_in_dim(doc_ids, query_first, query_rows, 2)
    key_docs = lax.dynamic_slice_in_dim(doc_ids, key_first, key_rows, 2)
    causal = key_pos[None, :] <= query_pos[:, None]
    return causal[None, None] & (query_docs[:, :, :, None] == key_docs[:, :, None, :])


def attend_update(running, scores, allowed, values, pattern):
    row_top, row_total, accumulated = running
    allowed = allowed[:, :, None]
    new_top = jnp.maximum(row_top, jnp.max(jnp.where(allowed, scores, MASKED), axis=-1))
    weights = jnp.where(allowed, jnp.exp(scores - new_top[..., None]), 0.0)
    factor = jnp.exp(row_top - new_top)
    row_total = row_total * factor + jnp.sum(weights, axis=-1)
    accumulated = accumulated * factor[..., None] + jnp.einsum(
        pattern, weights.astype(jnp.bfloat16), values, preferred_element_type=jnp.float32
    )
    return (new_top, row_total, accumulated)


def row_folder(left_side, pieces):
    return jnp.dot(left_side, pieces, preferred_element_type=jnp.float32)


def transposed_map(left_side, pieces):
    return lax.dot_general(
        left_side, pieces, (((1,), (1,)), ((), ())), preferred_element_type=jnp.float32
    )


def weight_sums(pair_list):
    blocks = [
        lax.dot_general(
            left_side, right_side, (((0,), (0,)), ((), ())), preferred_element_type=jnp.float32
        )
        for left_side, right_side in pair_list
    ]
    return lax.psum_scatter(
        jnp.concatenate(blocks, axis=1), ("rows", "seq"), scatter_dimension=0, tiled=True
    )


def per_device(
    tokens,
    summary,
    doc_ids,
    gain_attn,
    gain_ffn,
    w_query,
    w_key,
    w_value,
    w_out,
    w_up,
    w_down,
    cotangent,
):
    row_dev, seg_count, seg_dev, model_width = tokens.shape
    head_count = H
    head_dim = model_width // head_count
    sum_per_seg = summary.shape[2]
    sum_rows = summary.shape[1] * sum_per_seg
    seg_len = doc_ids.shape[2]
    ff_width = w_up.shape[1]
    local_rows = w_query.shape[0]
    position = lax.axis_index("seq")
    query_first = position * seg_dev
    first_flag = position == 0
    shard_number = lax.axis_index("rows") * lax.axis_size("seq") + position
    tok_rows = row_dev * seg_count * seg_dev
    head_shape = (row_dev, seg_count, seg_dev, head_count, head_dim)
    flat_tokens = tokens.reshape(tok_rows, model_width).astype(jnp.float32)
    summary_flat = summary.reshape(row_dev * sum_rows, model_width).astype(jnp.float32)
    standard_tok, inverse_tok = normalize(flat_tokens)
    standard_sum, inverse_sum = normalize(summary_flat)
    hidden_tok = (standard_tok * gain_attn).astype(jnp.bfloat16)
    hidden_sum = (standard_sum * gain_attn).astype(jnp.bfloat16)
    pieces = (
        lax.all_gather(w_query, ("rows", "seq"), axis=0, tiled=True),
        lax.all_gather(w_key, ("rows", "seq"), axis=0, tiled=True),
        lax.all_gather(w_value, ("rows", "seq"), axis=0, tiled=True),
    )
    rows_here = pieces[0].shape[0]
    stacked = jnp.concatenate(pieces, axis=1)
    tok_proj = jnp.dot(hidden_tok, stacked, preferred_element_type=jnp.float32)
    sum_proj = jnp.dot(hidden_sum, stacked[:, model_width:], preferred_element_type=jnp.float32)
    queries = (tok_proj[:, :model_width] * 0.125).astype(jnp.bfloat16).reshape(head_shape)
    keys_send = (
        tok_proj[:, model_width : 2 * model_width]
        .astype(jnp.bfloat16)
        .reshape(row_dev, seg_count, seg_dev, model_width)
    )
    values_send = (
        tok_proj[:, 2 * model_width :]
        .astype(jnp.bfloat16)
        .reshape(row_dev, seg_count, seg_dev, model_width)
    )
    keys_heads = keys_send.reshape(head_shape)
    values_heads = values_send.reshape(head_shape)
    sum_keys = (
        sum_proj[:, :model_width]
        .astype(jnp.bfloat16)
        .reshape(row_dev, sum_rows, head_count, head_dim)
    )
    sum_values = (
        sum_proj[:, model_width:]
        .astype(jnp.bfloat16)
        .reshape(row_dev, sum_rows, head_count, head_dim)
    )
    query_docs = lax.dynamic_slice_in_dim(doc_ids, query_first, seg_dev, 2)
    last_docs = doc_ids[:, : seg_count - 1, seg_len - 1]
    sum_docs = jnp.repeat(last_docs, sum_per_seg, axis=1)
    sum_segment = jnp.arange(sum_rows, dtype=jnp.int32) // sum_per_seg
    segment_ids = jnp.arange(seg_count, dtype=jnp.int32)
    sum_allowed = (sum_segment[None, None, None, :] < segment_ids[None, :, None, None]) & (
        query_docs[..., None] == sum_docs[:, None, None, :]
    )
    start_attend = (
        jnp.full((row_dev, seg_count, head_count, seg_dev), MASKED, jnp.float32),
        jnp.zeros((row_dev, seg_count, head_count, seg_dev), jnp.float32),
        jnp.zeros((row_dev, seg_count, head_count, seg_dev, head_dim), jnp.float32),
    )
    sum_scores = jnp.einsum(
        "rsqhd,rkhd->rshqk", queries, sum_keys, preferred_element_type=jnp.float32
    )
    running = attend_update(start_attend, sum_scores, sum_allowed, sum_values, "rshqk,rkhd->rshqd")

    def forward_step(current, block_parts, key_first):
        key_rows = block_parts[0].shape[2]
        key_block = block_parts[0].reshape(row_dev, seg_count, key_rows, head_count, head_dim)
        value_block = block_parts[1].reshape(row_dev, seg_count, key_rows, head_count, head_dim)
        allowed = token_mask(doc_ids, query_first, seg_dev, key_first, key_rows)
        scores = jnp.einsum(
            "rsqhd,rskhd->rshqk", queries, key_block, preferred_element_type=jnp.float32
        )
        return attend_update(current, scores, allowed, value_block, "rshqk,rskhd->rshqd")

    row_top, row_total, accumulated = over_blocks(
        running,
        (
            lax.all_gather(keys_send, "seq", axis=2, tiled=True),
            lax.all_gather(values_send, "seq", axis=2, tiled=True),
        ),
        seg_dev,
        forward_step,
    )
    attention_out = accumulated / row_total[..., None]
    log_total = row_top + jnp.log(row_total)
    attended = (
        jnp.transpose(attention_out, (0, 1, 3, 2, 4))
        .reshape(tok_rows, model_width)
        .astype(jnp.bfloat16)
    )
    whole_out = lax.all_gather(w_out, ("rows", "seq"), axis=0, tiled=True)
    branch_attn = jnp.dot(attended, whole_out, preferred_element_type=jnp.float32)
    mixed_rows = flat_tokens + branch_attn
    standard_ffn, inverse_ffn = normalize(mixed_rows)
    normed = (standard_ffn * gain_ffn).astype(jnp.bfloat16)
    pre_active = row_folder(normed, lax.all_gather(w_up, ("rows", "seq"), axis=0, tiled=True))
    active = jax.nn.gelu(pre_active, approximate=False).astype(jnp.bfloat16)
    branch_ffn = transposed_map(active, lax.all_gather(w_down, ("rows", "seq"), axis=0, tiled=True))
    activations = (mixed_rows + branch_ffn).astype(jnp.bfloat16).reshape(tokens.shape)
    grad_out = cotangent.reshape(tok_rows, model_width)
    grad_active = row_folder(grad_out, lax.all_gather(w_down, ("rows", "seq"), axis=0, tiled=True))
    grad_upper = (gelu_slope(pre_active) * grad_active).astype(jnp.bfloat16)
    ffn_pairs = [(normed, grad_upper), (grad_out, active)]
    grad_normed = transposed_map(
        grad_upper, lax.all_gather(w_up, ("rows", "seq"), axis=0, tiled=True)
    )
    grad_mixed = grad_out.astype(jnp.float32) + normalize_back(
        grad_normed, gain_ffn, standard_ffn, inverse_ffn
    )
    ffn_gain_term = jnp.sum(grad_normed * standard_ffn, axis=0)
    grad_branch = grad_mixed.astype(jnp.bfloat16)
    grad_attended = lax.dot_general(
        grad_branch, whole_out, (((1,), (1,)), ((), ())), preferred_element_type=jnp.float32
    )
    grad_heads = grad_attended.astype(jnp.bfloat16).reshape(head_shape)
    row_delta = jnp.einsum("rsqhd,rshqd->rshq", grad_heads.astype(jnp.float32), attention_out)
    sum_probs = jnp.where(sum_allowed[:, :, None], jnp.exp(sum_scores - log_total[..., None]), 0.0)
    sum_dprob = jnp.einsum(
        "rsqhd,rkhd->rshqk", grad_heads, sum_values, preferred_element_type=jnp.float32
    )
    sum_dscore = (sum_probs * (sum_dprob - row_delta[..., None])).astype(jnp.bfloat16)
    grad_query_start = jnp.einsum(
        "rshqk,rkhd->rsqhd", sum_dscore, sum_keys, preferred_element_type=jnp.float32
    )
    sum_key_part = jnp.einsum(
        "rshqk,rsqhd->rkhd", sum_dscore, queries, preferred_element_type=jnp.float32
    )
    sum_value_part = jnp.einsum(
        "rshqk,rsqhd->rkhd",
        sum_probs.astype(jnp.bfloat16),
        grad_heads,
        preferred_element_type=jnp.float32,
    )

    def query_step(current, block_parts, key_first):
        key_rows = block_parts[0].shape[2]
        key_block = block_parts[0].reshape(row_dev, seg_count, key_rows, head_count, head_dim)
        value_block = block_parts[1].reshape(row_dev, seg_count, key_rows, head_count, head_dim)
        allowed = token_mask(doc_ids, query_first, seg_dev, key_first, key_rows)
        scores = jnp.einsum(
            "rsqhd,rskhd->rshqk", queries, key_block, preferred_element_type=jnp.float32
        )
        probabilities = jnp.where(allowed[:, :, None], jnp.exp(scores - log_total[..., None]), 0.0)
        grad_probs = jnp.einsum(
            "rsqhd,rskhd->rshqk", grad_heads, value_block, preferred_element_type=jnp.float32
        )
        dscore = (probabilities * (grad_probs - row_delta[..., None])).astype(jnp.bfloat16)
        return current + jnp.einsum(
            "rshqk,rskhd->rsqhd", dscore, key_block, preferred_element_type=jnp.float32
        )

    grad_queries = over_blocks(
        grad_query_start,
        (
            lax.all_gather(keys_send, "seq", axis=2, tiled=True),
            lax.all_gather(values_send, "seq", axis=2, tiled=True),
        ),
        seg_dev,
        query_step,
    )
    stats_all = (
        lax.all_gather(log_total.astype(jnp.bfloat16), "seq", axis=3, tiled=True).astype(
            log_total.dtype
        ),
        lax.all_gather(row_delta.astype(jnp.bfloat16), "seq", axis=3, tiled=True).astype(
            row_delta.dtype
        ),
    )
    queries_send = queries.reshape(row_dev, seg_count, seg_dev, model_width)
    grad_send = grad_attended.astype(jnp.bfloat16).reshape(row_dev, seg_count, seg_dev, model_width)

    def key_step(current, block_parts, remote_first):
        rows_here = block_parts[0].shape[2]
        query_block = block_parts[0].reshape(row_dev, seg_count, rows_here, head_count, head_dim)
        grad_block = block_parts[1].reshape(row_dev, seg_count, rows_here, head_count, head_dim)
        total_block = lax.dynamic_slice_in_dim(stats_all[0], remote_first, rows_here, 3)
        delta_block = lax.dynamic_slice_in_dim(stats_all[1], remote_first, rows_here, 3)
        allowed = token_mask(doc_ids, remote_first, rows_here, query_first, seg_dev)
        grad_keys, grad_values = current
        scores = jnp.einsum(
            "rsqhd,rskhd->rshqk", query_block, keys_heads, preferred_element_type=jnp.float32
        )
        probabilities = jnp.where(
            allowed[:, :, None], jnp.exp(scores - total_block[..., None]), 0.0
        )
        grad_probs = jnp.einsum(
            "rsqhd,rskhd->rshqk", grad_block, values_heads, preferred_element_type=jnp.float32
        )
        dscore = (probabilities * (grad_probs - delta_block[..., None])).astype(jnp.bfloat16)
        grad_values = grad_values + jnp.einsum(
            "rshqk,rsqhd->rskhd",
            probabilities.astype(jnp.bfloat16),
            grad_block,
            preferred_element_type=jnp.float32,
        )
        grad_keys = grad_keys + jnp.einsum(
            "rshqk,rsqhd->rskhd", dscore, query_block, preferred_element_type=jnp.float32
        )
        return (grad_keys, grad_values)

    start_keys = (jnp.zeros(head_shape, jnp.float32), jnp.zeros(head_shape, jnp.float32))
    grad_keys, grad_values = over_blocks(
        start_keys,
        (
            lax.all_gather(queries_send, "seq", axis=2, tiled=True),
            lax.all_gather(grad_send, "seq", axis=2, tiled=True),
        ),
        seg_dev,
        key_step,
    )
    sum_key_total, sum_value_total = (
        lax.psum(sum_key_part.astype(jnp.bfloat16), "seq").astype(jnp.float32),
        lax.psum(sum_value_part.astype(jnp.bfloat16), "seq").astype(jnp.float32),
    )
    grad_q_rows = grad_queries.reshape(tok_rows, model_width).astype(jnp.bfloat16) * 0.125
    grad_k_rows = grad_keys.reshape(tok_rows, model_width).astype(jnp.bfloat16)
    grad_v_rows = grad_values.reshape(tok_rows, model_width).astype(jnp.bfloat16)
    grad_sk_rows = sum_key_total.reshape(row_dev * sum_rows, model_width).astype(jnp.bfloat16)
    grad_sv_rows = sum_value_total.reshape(row_dev * sum_rows, model_width).astype(jnp.bfloat16)
    tok_grads = jnp.concatenate([grad_q_rows, grad_k_rows, grad_v_rows], axis=1)
    sum_grads = jnp.concatenate([grad_sk_rows, grad_sv_rows], axis=1)
    stacked = jnp.concatenate(
        lax.all_gather((w_query, w_key, w_value), ("rows", "seq"), axis=0, tiled=True), axis=1
    )
    grad_hidden_tok = lax.dot_general(
        tok_grads, stacked, (((1,), (1,)), ((), ())), preferred_element_type=jnp.float32
    )
    grad_hidden_sum = lax.dot_general(
        sum_grads,
        stacked[:, model_width:],
        (((1,), (1,)), ((), ())),
        preferred_element_type=jnp.float32,
    )
    d_tokens = grad_mixed + normalize_back(grad_hidden_tok, gain_attn, standard_tok, inverse_tok)
    d_summary = normalize_back(grad_hidden_sum, gain_attn, standard_sum, inverse_sum)
    sum_gain_part = jnp.sum(grad_hidden_sum * standard_sum, axis=0)
    attn_gain_term = jnp.sum(grad_hidden_tok * standard_tok, axis=0) + jnp.where(
        first_flag, sum_gain_part, jnp.zeros_like(sum_gain_part)
    )
    masked_sum = jnp.where(first_flag, hidden_sum, jnp.zeros_like(hidden_sum))
    left_kv = jnp.concatenate([hidden_tok, masked_sum], axis=0)
    right_kv = jnp.concatenate(
        [jnp.concatenate([grad_k_rows, grad_v_rows], axis=1), sum_grads], axis=0
    )
    attn_pairs = [(hidden_tok, grad_q_rows), (left_kv, right_kv), (attended, grad_branch)]
    ffn_total = weight_sums(ffn_pairs)
    attn_total = weight_sums(attn_pairs)
    gain_attn_all, gain_ffn_all = lax.psum((attn_gain_term, ffn_gain_term), ("rows", "seq"))
    gain_first = shard_number * local_rows
    d_gain_attn = lax.dynamic_slice_in_dim(gain_attn_all, gain_first, local_rows, 0)
    d_gain_ffn = lax.dynamic_slice_in_dim(gain_ffn_all, gain_first, local_rows, 0)
    d_w_query = attn_total[:, :model_width]
    d_w_key = attn_total[:, model_width : 2 * model_width]
    d_w_value = attn_total[:, 2 * model_width : 3 * model_width]
    d_w_out = attn_total[:, 3 * model_width : 4 * model_width]
    d_w_up = ffn_total[:, :ff_width]
    d_w_down = ffn_total[:, ff_width:]
    return (
        activations,
        d_tokens.reshape(tokens.shape),
        d_summary.reshape(summary.shape),
        d_gain_attn,
        d_gain_ffn,
        d_w_query,
        d_w_key,
        d_w_value,
        d_w_out,
        d_w_up,
        d_w_down,
    )


def solution(mesh):
    placed = (
        P("rows", None, "seq", None),
        P("rows", None, None, None),
        P("rows", None, None),
        P(),
        P(),
        P(("rows", "seq"), None),
        P(("rows", "seq"), None),
        P(("rows", "seq"), None),
        P(("rows", "seq"), None),
        P(("rows", "seq"), None),
        P(("rows", "seq"), None),
        P("rows", None, "seq", None),
    )
    return jax.shard_map(
        per_device,
        mesh=mesh,
        in_specs=placed,
        out_specs=(
            P("rows", None, "seq", None),
            P("rows", None, "seq", None),
            P("rows", None, None, None),
            P(("rows", "seq")),
            P(("rows", "seq")),
            P(("rows", "seq"), None),
            P(("rows", "seq"), None),
            P(("rows", "seq"), None),
            P(("rows", "seq"), None),
            P(("rows", "seq"), None),
            P(("rows", "seq"), None),
        ),
        check_vma=False,
    )
```

profile of v0, /device:TPU:0, one launch (start us, length us, event | category | flops | bytes accessed | tf_op | source)
XLA Modules:
  0.0 4508.3 jit_solution(7080330635612888340)
XLA Ops:
  14.4 76.8 %all-gather.16.cloned.1.call-done = bf16[2048,2048]{1,0:T(8,128)(2,1)} async-done(((bf16[64,2048]{1,0:T(8,128)(2,1)}), bf16[2048,2048]{1,0:T(8,128)(2,1)}) %all-gather.16.cloned.1.call-update) | async-done | bytes 8388624 | tf_op jit(solution)/shard_map/all_gather | solution.py:144
  99.5 70.7 %all-gather.12.cloned.1.call-done = bf16[2048,2048]{1,0:T(8,128)(2,1)} async-done(((bf16[64,2048]{1,0:T(8,128)(2,1)}), bf16[2048,2048]{1,0:T(8,128)(2,1)}) %all-gather.12.cloned.1.call-update) | async-done | bytes 8388624 | tf_op jit(solution)/shard_map/all_gather | solution.py:145
  170.1 10.1 constant_dynamic-update-slice_fusion.3
  180.2 68.9 %all-gather.14.cloned.1.call-done = bf16[2048,2048]{1,0:T(8,128)(2,1)} async-done(((bf16[64,2048]{1,0:T(8,128)(2,1)}), bf16[2048,2048]{1,0:T(8,128)(2,1)}) %all-gather.14.cloned.1.call-update) | async-done | bytes 8388624 | tf_op jit(solution)/shard_map/all_gather | solution.py:146
  249.2 10.1 constant_dynamic-update-slice_fusion.2
  259.2 13.7 fusion.121
  284.3 8.6 convolution_convert_fusion
  304.1 48.6 %all-gather.18.cloned.1.call-done = bf16[1,3,384,2048]{3,2,1,0:T(8,128)(2,1)} async-done(((bf16[1,3,48,2048]{3,2,1,0:T(8,128)(2,1)}), bf16[1,3,384,2048]{3,2,1,0:T(8,128)(2,1)}) %all-gather.18.cloned.1.call-update) | async-done | bytes 4718608 | tf_op jit(solution)/shard_map/all_gather | solution.py:206
  359.4 74.1 %all-gather.20.cloned.1.call-done = bf16[1,3,384,2048]{3,2,1,0:T(8,128)(2,1)} async-done(((bf16[1,3,48,2048]{3,2,1,0:T(8,128)(2,1)}), bf16[1,3,384,2048]{3,2,1,0:T(8,128)(2,1)}) %all-gather.20.cloned.1.call-update) | async-done | bytes 4718608 | tf_op jit(solution)/shard_map/all_gather | solution.py:207
  440.1 28.8 while.43
  479.4 32.3 all-gather.22.cloned.1.call-done
  517.2 190.9 %all-gather.24.cloned.1.call-done = bf16[2048,8192]{1,0:T(8,128)(2,1)} async-done(((bf16[64,8192]{1,0:T(8,128)(2,1)}), bf16[2048,8192]{1,0:T(8,128)(2,1)}) %all-gather.24.cloned.1.call-update) | async-done | bytes 33554448 | tf_op jit(solution)/shard_map/all_gather | solution.py:224
  708.1 16.2 fusion.113
  724.4 179.8 %all-gather.26.cloned.1.call-done = bf16[2048,8192]{1,0:T(8,128)(2,1)} async-done(((bf16[64,8192]{1,0:T(8,128)(2,1)}), bf16[2048,8192]{1,0:T(8,128)(2,1)}) %all-gather.26.cloned.1.call-update) | async-done | bytes 33554448 | tf_op jit(solution)/shard_map/all_gather | solution.py:226
  904.1 16.9 fusion.53
  921.1 20.0 multiply_reduce_fusion
  969.4 28.2 convolution_bitcast_fusion
  997.6 23.9 fusion.112
  1021.5 87.8 %pad_maximum_fusion = f32[2048,16384]{1,0:T(8,128)} fusion(f32[2048,8192]{1,0:T(8,128)} %convolution_bitcast_fusion, f32[2048,8192]{1,0:T(8,128)} %fusion.112), kind=kLoop, calls=%fused_computation.76 | loop fusion | flops 33554432 | bytes 268435456 | tf_op jit(solution)/shard_map/concatenate | solution.py:105
  1118.2 32.3 all_gather.52
  1155.0 32.4 all-gather
  1194.4 38.9 while.44
  1195.8 8.8 constant_dynamic-slice_fusion.12
  1256.7 65.1 %while.45 = (s32[]{:T(128)}, f32[1,3,48,32,64]{4,2,3,1,0:T(8,128)}, f32[1,3,48,32,64]{4,2,3,1,0:T(8,128)}, s32[2]{0:T(128)S(1)}, bf16[1,3,384,2048]{3,2,1,0:T(8,...) while((s32[]{:T(128)}, f32[1,3,48,32,64]{4,2,3,1,0:T(8,128)}, ...), condition=%wide.region_17.18_spmd.clone, body=%wide.region_16.17_spmd.clone.sunk | while | flops 461307136 | bytes 54890968 | solution.py:59
  1327.6 15.2 fusion.70
  1342.8 45.9 %pad_maximum_fusion.1 = f32[2048,8192]{1,0:T(8,128)} fusion(f32[2048,2048]{1,0:T(8,128)} %fusion.102, f32[2048,4096]{1,0:T(8,128)} %fusion.70, f32[2048,2048]{1,0:T(8,128)} %fusion.125), kind=kLoop, calls=%fused_computation.77 | loop fusion | flops 33554432 | bytes 134217728 | tf_op jit(solution)/shard_map/concatenate | solution.py:105
  1390.0 25.6 fusion.68
  1415.7 13.6 multiply_reduce_fusion.8
  1432.7 15.2 multiply_reduce_fusion.6
  1447.9 38.4 all-reduce.1
  1490.3 1604.3 %all-reduce.6.cloned.1.call-done = f32[2048,16384]{1,0:T(8,128)} async-done(((f32[2048,16384]{1,0:T(8,128)}), f32[2048,16384]{1,0:T(8,128)}) %all-reduce.6.cloned.1.call-update) | async-done | bytes 134217744
  3099.4 1399.3 %reduce-scatter.2.cloned.1.call-done = f32[64,8192]{1,0:T(8,128)} async-done(((f32[2048,8192]{1,0:T(8,128)}), f32[64,8192]{1,0:T(8,128)}) %reduce-scatter.2.cloned.1.call-update) | async-done | bytes 2097168 | tf_op jit(solution)/shard_map/reduce_scatter | solution.py:104
  (382 shorter events, 279.9 us)
Async XLA Ops:
  7.2 84.0 %all-gather.16.cloned.1.call-start = ((), (), s32[]{:S(2)}) async-start(), calls=%async_computation.3 | async-start | bytes 8650752 | tf_op jit(solution)/shard_map/all_gather | solution.py:144
  7.9 162.2 %all-gather.12.cloned.1.call-start = ((), (), s32[]{:S(2)}) async-start(), calls=%async_computation.1 | async-start | bytes 8650752 | tf_op jit(solution)/shard_map/all_gather | solution.py:145
  8.7 240.5 %all-gather.14.cloned.1.call-start = ((), (), s32[]{:S(2)}) async-start(), calls=%async_computation.2 | async-start | bytes 8650752 | tf_op jit(solution)/shard_map/all_gather | solution.py:146
  9.4 343.4 %all-gather.18.cloned.1.call-start = ((), (), s32[]{:S(2)}) async-start(), calls=%async_computation.4 | async-start | bytes 5308416 | tf_op jit(solution)/shard_map/all_gather | solution.py:206
  10.8 88.7 %copy-start.72 = (f32[144]{0:T(256)}, f32[144]{0:T(256)S(1)}, u32[]{:S(2)}) copy-start(f32[144]{0:T(256)S(1)} %div.65) | copy-start | bytes 1732
  12.8 86.6 %copy-start.74 = (f32[144]{0:T(256)}, f32[144]{0:T(256)S(1)}, u32[]{:S(2)}) copy-start(f32[144]{0:T(256)S(1)} %rsqrt.34) | copy-start | bytes 1732
  14.3 244.9 %copy-start.26 = (bf16[144,2048]{1,0:T(8,128)(2,1)}, bf16[144,2048]{1,0:T(8,128)(2,1)S(1)}, u32[]{:S(2)}) copy-start(bf16[144,2048]{1,0:T(8,128)(2,1)S(1)} %multiply_convert_fusion.7) | copy-start | bytes 1769476
  274.1 159.4 %all-gather.20.cloned.1.call-start = ((), (), s32[]{:S(2)}) async-start(), calls=%async_computation.5 | async-start | bytes 5308416 | tf_op jit(solution)/shard_map/all_gather | solution.py:207
  274.7 237.1 %all-gather.22.cloned.1.call-start = ((), (), s32[]{:S(2)}) async-start(), calls=%async_computation.6 | async-start | bytes 8650752 | tf_op jit(solution)/shard_map/all_gather | solution.py:219
  275.3 432.9 %all-gather.24.cloned.1.call-start = ((), (), s32[]{:S(2)}) async-start(), calls=%async_computation.7 | async-start | bytes 34603008 | tf_op jit(solution)/shard_map/all_gather | solution.py:224
  276.0 628.1 %all-gather.26.cloned.1.call-start = ((), (), s32[]{:S(2)}) async-start(), calls=%async_computation.8 | async-start | bytes 34603008 | tf_op jit(solution)/shard_map/all_gather | solution.py:226
  276.8 976.3 %all-reduce.8.cloned.1.call-start = ((), (), s32[]{:S(2)}) async-start(), calls=%async_computation.13 | async-start | bytes 1703936 | tf_op jit(solution)/shard_map/psum | solution.py:340
  278.7 14.3 copy-start.66
  279.4 19.4 copy-start.57
  478.7 33.0 copy-start.46
  511.7 196.4 %copy-start.51 = (f32[2048]{0:T(1024)S(1)}, f32[2048]{0:T(1024)}, u32[]{:S(2)}) copy-start(f32[2048]{0:T(1024)} %param.22) | copy-start | bytes 24580
  516.9 480.7 %copy-start.6 = (f32[144,2048]{1,0:T(8,128)}, f32[144,2048]{1,0:T(8,128)S(1)}, u32[]{:S(2)}) copy-start(f32[144,2048]{1,0:T(8,128)S(1)} %get-tuple-element.774) | copy-start | bytes 3538948
  968.7 288.0 %all-gather.28.cloned.1.call-start = ((), (), s32[]{:S(2)}) async-start(), calls=%async_computation.9 | async-start | bytes 5308416 | tf_op jit(solution)/shard_map/all_gather | solution.py:333
  969.3 28.3 copy-start.16
  969.3 287.4 %all-gather.30.cloned.1.call-start = ((), (), s32[]{:S(2)}) async-start(), calls=%async_computation.10 | async-start | bytes 5308416 | tf_op jit(solution)/shard_map/all_gather | solution.py:334
  997.5 2097.0 %all-reduce.6.cloned.1.call-start = ((), (), s32[]{:S(2)}) async-start(), calls=%async_computation.12 | async-start | bytes 268435456
  1109.4 3389.3 %reduce-scatter.2.cloned.1.call-start = ((), (), s32[]{:S(2)}) async-start(), calls=%async_computation.11 | async-start | bytes 69206016 | tf_op jit(solution)/shard_map/reduce_scatter | solution.py:104
  1115.1 37.8 copy-start.22
  1118.1 72.3 %copy-start.21 = (bf16[3,32,48,100]{3,2,0,1:T(8,128)(2,1)S(1)}, bf16[3,32,48,100]{3,2,0,1:T(8,128)(2,1)}, u32[]{:S(2)}) copy-start(bf16[3,32,48,100]{3,2,0,1:T(8,128)(2,1)} %copy-done.20) | copy-start | bytes 2764804
  1118.1 72.3 %copy-start.34 = (bf16[100,2048]{0,1:T(8,128)(2,1)S(1)}, bf16[100,2048]{0,1:T(8,128)(2,1)}, u32[]{:S(2)}) copy-start(bf16[100,2048]{0,1:T(8,128)(2,1)} %copy-done.33) | copy-start | bytes 1228804
  1327.6 15.2 copy-start.44
  1390.0 25.7 copy-start.10
  1390.0 25.7 copy-start.54
  1390.0 25.7 copy-start.68
  1390.0 25.7 copy-start.71
  1432.6 15.2 copy-start.61
  1432.6 54.8 %copy-start.15 = (f32[144,2048]{1,0:T(8,128)S(1)}, f32[144,2048]{1,0:T(8,128)}, u32[]{:S(2)}) copy-start(f32[144,2048]{1,0:T(8,128)} %copy-done.13) | copy-start | bytes 3538948
  (63 other events, 249.0 us)
Sparse Core Ops, SparseCore 0:
  11.0 80.0 all-gather.15
  94.1 75.9 all-gather.11
  173.1 75.9 all-gather.13
  274.2 78.5 all-gather.17
  355.4 78.0 all-gather.19
  436.3 75.4 all-gather.21
  514.7 193.3 all-gather.23
  711.1 192.9 all-gather.25
  968.8 73.7 all-reduce.7
  1044.7 79.6 all-gather.27
  1126.6 83.2 all-gather.29
  1216.3 1878.2 all-reduce.5
  3096.9 1401.8 reduce-scatter.1
where the time goes:
time: 4520 us; the launch traced here: 4510 us
  waiting for transfers between devices  3750 us (83%)
  matrix products  297 us (7%)
  other arithmetic  173 us (4%)
  local copies, waits for them, and re-layouts  164 us (4%)
  blocking collectives  103 us (2%)
    unnamed x14, waiting for transfers between devices  1610 us
    reduce_scatter x1, waiting for transfers between devices, weight_sums(): lax.psum_scatter(jnp.concatenate(blocks, axis=1), ('rows', 'seq'), scatte...  1400 us
    all_gather x1, waiting for transfers between devices, per_device(): lax.all_gather(w_up, ('rows', 'seq'), axis=0, tiled=True)  191 us
    all_gather x1, waiting for transfers between devices, per_device(): lax.all_gather(w_down, ('rows', 'seq'), axis=0, tiled=True)  180 us
    concatenate x2, other arithmetic, weight_sums(): jnp.concatenate(blocks, axis=1)  134 us
  transfers between devices with their start and end apart: 13, of which 10 were waited for; matrix products, arithmetic and copies ran while one was open for 12% of the time, Pallas kernels for 0%

commit v1 on v0

v1 whole, which is shorter than its diff:
```python
import functools

import jax
import jax.numpy as jnp
from jax import lax
from jax.experimental import pallas as pl
from jax.experimental.pallas import tpu as pltpu
from jax.sharding import Mesh, PartitionSpec as P

HEAD = 64
EPSILON = 1e-05
MASKED = -1e30
SQRT_HALF = 0.7071067811865476
NORMAL_PEAK = 0.3989422804014327

AXES = ("x", "c", "zh", "zl", "y")
ROWS = ("x", "c")
SEQ = ("zh", "zl", "y")
BF = jnp.bfloat16
F32 = jnp.float32


def dot(left, right, left_dim=1, right_dim=0):
    return lax.dot_general(
        left, right, (((left_dim,), (right_dim,)), ((), ())), preferred_element_type=F32
    )


def normalize(inputs):
    average = jnp.mean(inputs, axis=-1, keepdims=True)
    centred = inputs - average
    inverse = lax.rsqrt(jnp.mean(centred * centred, axis=-1, keepdims=True) + EPSILON)
    return centred * inverse, inverse


def normalize_back(upstream, scaling, standard, inverse):
    scaled = upstream * scaling
    return inverse * (
        scaled
        - jnp.mean(scaled, axis=-1, keepdims=True)
        - standard * jnp.mean(scaled * standard, axis=-1, keepdims=True)
    )


def swap(array, axis):
    return lax.ppermute(array, axis, [(0, 1), (1, 0)])


def pair(mine, theirs, axis, dim):
    first = lax.axis_index(axis) == 0
    return jnp.concatenate(
        [jnp.where(first, mine, theirs), jnp.where(first, theirs, mine)], axis=dim
    )


def halves(array, axis, dim):
    half = array.shape[dim] // 2
    place = lax.axis_index(axis)
    return (
        lax.dynamic_slice_in_dim(array, place * half, half, dim),
        lax.dynamic_slice_in_dim(array, (1 - place) * half, half, dim),
    )


def gather_dim(array, axis, dim):
    if lax.axis_size(axis) != 2:
        return lax.all_gather(array, axis, axis=dim, tiled=True)
    return pair(array, swap(array, axis), axis, dim)


def scatter_dim(array, axis, dim):
    if lax.axis_size(axis) != 2:
        return lax.psum_scatter(array, axis, scatter_dimension=dim, tiled=True)
    mine, theirs = halves(array, axis, dim)
    return mine + swap(theirs, axis)


def exchange(array, axis, cut, joined):
    if lax.axis_size(axis) != 2:
        return lax.all_to_all(array, axis, cut, joined, tiled=True)
    mine, theirs = halves(array, axis, cut)
    return pair(mine, swap(theirs, axis), axis, joined)


def gather_near(array, axes):
    for axis in axes:
        if lax.axis_size(axis) != 2:
            array = lax.all_gather(array, axis, axis=0, tiled=True)
        else:
            array = jnp.concatenate([array, swap(array, axis)], axis=0)
    return array


def scatter_near(array, axes):
    for axis in reversed(axes):
        if lax.axis_size(axis) != 2:
            array = lax.psum_scatter(array, axis, scatter_dimension=0, tiled=True)
        else:
            half = array.shape[0] // 2
            array = array[:half] + swap(array[half:], axis)
    return array


def columns_in(weight, group, rest):
    rows, cols = weight.shape
    array = weight.reshape((1,) * len(AXES) + (rows, cols))
    for axis in group:
        array = exchange(array, axis, len(AXES) + 1, AXES.index(axis))
    for axis in rest:
        array = gather_dim(array, axis, AXES.index(axis))
    return array.reshape(-1, array.shape[-1])


def columns_out(sums, group, rest):
    sizes = tuple(lax.axis_size(axis) for axis in AXES)
    array = sums.astype(BF).reshape(sizes + (-1, sums.shape[1]))
    for axis in reversed(rest):
        array = scatter_dim(array, axis, AXES.index(axis))
    for axis in reversed(group):
        array = exchange(array, axis, AXES.index(axis), len(AXES) + 1)
    return array.reshape(array.shape[-2:]).astype(F32)


def block_mask(col_ref, row_ref, sum_ref, first, rows, keys, segment, per_seg):
    query_docs = col_ref[0, first : first + rows, :]
    query_pos = first + lax.broadcasted_iota(jnp.int32, (rows, keys), 0)
    key_pos = lax.broadcasted_iota(jnp.int32, (rows, keys), 1)
    allowed = (key_pos <= query_pos) & (query_docs == row_ref[0, :, :keys])
    padded = sum_ref.shape[-1]
    place = lax.broadcasted_iota(jnp.int32, (rows, padded), 1)
    sum_allowed = (place < segment * per_seg) & (query_docs == sum_ref[...])
    return allowed, sum_allowed


def block_probs(query, key, sum_key, allowed, sum_allowed):
    scores = jnp.where(allowed, dot(query, key, 1, 1), MASKED)
    sum_scores = jnp.where(sum_allowed, dot(query, sum_key, 1, 1), MASKED)
    top = jnp.maximum(
        jnp.max(scores, axis=1, keepdims=True), jnp.max(sum_scores, axis=1, keepdims=True)
    )
    weights = jnp.exp(scores - top)
    sum_weights = jnp.exp(sum_scores - top)
    total = jnp.sum(weights, axis=1, keepdims=True) + jnp.sum(sum_weights, axis=1, keepdims=True)
    share = 1.0 / total
    return weights * share, sum_weights * share


def forward_kernel(
    per_seg, rows, col_ref, row_ref, sum_ref, q_ref, k_ref, v_ref, sk_ref, sv_ref, out_ref
):
    segment = pl.program_id(1)
    length, width = q_ref.shape
    for first in range(0, length, rows):
        keys = first + rows
        allowed, sum_allowed = block_mask(
            col_ref, row_ref, sum_ref, first, rows, keys, segment, per_seg
        )
        for low in range(0, width, HEAD):
            cols = slice(low, low + HEAD)
            probs, sum_probs = block_probs(
                q_ref[first:keys, cols], k_ref[:keys, cols], sk_ref[:, cols], allowed, sum_allowed
            )
            out = dot(probs.astype(BF), v_ref[:keys, cols])
            out += dot(sum_probs.astype(BF), sv_ref[:, cols])
            out_ref[first:keys, cols] = out.astype(BF)


def backward_kernel(
    per_seg, rows, col_ref, row_ref, sum_ref, q_ref, k_ref, v_ref, sk_ref, sv_ref, g_ref,
    dq_ref, dk_ref, dv_ref, dsk_ref, dsv_ref, dk_sum, dv_sum,
):
    segment = pl.program_id(1)
    length, width = q_ref.shape

    @pl.when(segment == 0)
    def _():
        dsk_ref[...] = jnp.zeros_like(dsk_ref)
        dsv_ref[...] = jnp.zeros_like(dsv_ref)

    dk_sum[...] = jnp.zeros_like(dk_sum)
    dv_sum[...] = jnp.zeros_like(dv_sum)
    for first in range(0, length, rows):
        keys = first + rows
        allowed, sum_allowed = block_mask(
            col_ref, row_ref, sum_ref, first, rows, keys, segment, per_seg
        )
        for low in range(0, width, HEAD):
            cols = slice(low, low + HEAD)
            query, grad = q_ref[first:keys, cols], g_ref[first:keys, cols]
            key, sum_key = k_ref[:keys, cols], sk_ref[:, cols]
            probs, sum_probs = block_probs(query, key, sum_key, allowed, sum_allowed)
            d_probs = dot(grad, v_ref[:keys, cols], 1, 1)
            d_sum_probs = dot(grad, sv_ref[:, cols], 1, 1)
            delta = jnp.sum(probs * d_probs, axis=1, keepdims=True)
            delta += jnp.sum(sum_probs * d_sum_probs, axis=1, keepdims=True)
            d_scores = (probs * (d_probs - delta)).astype(BF)
            d_sum_scores = (sum_probs * (d_sum_probs - delta)).astype(BF)
            d_query = (dot(d_scores, key) + dot(d_sum_scores, sum_key)).astype(BF)
            dq_ref[first:keys, cols] = (d_query.astype(F32) * 0.125).astype(BF)
            dk_sum[:keys, cols] += dot(d_scores, query, 0, 0)
            dv_sum[:keys, cols] += dot(probs.astype(BF), grad, 0, 0)
            dsk_ref[:, cols] += dot(d_sum_scores, query, 0, 0)
            dsv_ref[:, cols] += dot(sum_probs.astype(BF), grad, 0, 0)
    dk_ref[...] = dk_sum[...].astype(BF)
    dv_ref[...] = dv_sum[...].astype(BF)


def attention_calls(segs, length, width, padded, per_seg):
    lanes = min(2 * HEAD, width)
    rows = 128 if length <= 512 else 256
    grid = (width // lanes, segs)
    tok = pl.BlockSpec((length, lanes), lambda h, s: (s, h))
    summed = pl.BlockSpec((padded, lanes), lambda h, s: (0, h))
    docs = [
        pl.BlockSpec((1, length, 1), lambda h, s: (s, 0, 0)),
        pl.BlockSpec((1, 1, length), lambda h, s: (s, 0, 0)),
        pl.BlockSpec((1, padded), lambda h, s: (0, 0)),
    ]
    params = pltpu.CompilerParams(
        dimension_semantics=("arbitrary", "arbitrary"), vmem_limit_bytes=48 * 2**20
    )
    tokens = jax.ShapeDtypeStruct((segs * length, width), BF)
    sums = jax.ShapeDtypeStruct((padded, width), F32)
    work = 2 * segs * length * (length // 2 + padded) * width
    forward = pl.pallas_call(
        functools.partial(forward_kernel, per_seg, rows),
        grid=grid,
        in_specs=docs + [tok] * 3 + [summed] * 2,
        out_specs=tok,
        out_shape=tokens,
        compiler_params=params,
        cost_estimate=pl.CostEstimate(
            flops=8 * work, bytes_accessed=8 * segs * length * width, transcendentals=0
        ),
    )
    backward = pl.pallas_call(
        functools.partial(backward_kernel, per_seg, rows),
        grid=grid,
        in_specs=docs + [tok] * 3 + [summed] * 2 + [tok],
        out_specs=[tok] * 3 + [summed] * 2,
        out_shape=[tokens] * 3 + [sums] * 2,
        scratch_shapes=[pltpu.VMEM((length, lanes), F32)] * 2,
        compiler_params=params,
        cost_estimate=pl.CostEstimate(
            flops=20 * work, bytes_accessed=14 * segs * length * width, transcendentals=0
        ),
    )
    return forward, backward


def gelu_both(inputs):
    share = 0.5 * (1.0 + lax.erf(inputs * SQRT_HALF))
    slope = share + inputs * jnp.exp(-0.5 * inputs * inputs) * NORMAL_PEAK
    return inputs * share, slope


ATT_GROUP, ATT_REST = ("zh", "zl", "y"), ("x", "c")
FFN_GROUP, FFN_REST = ("y", "c", "zl"), ("zh", "x")
FFN_NEAR = ("zl", "c", "y")


def per_device(
    tokens, summary, doc_ids, gain_attn, gain_ffn, w_query, w_key, w_value, w_out, w_up, w_down,
    cotangent,
):
    _, segs, here, model = tokens.shape
    per_seg = summary.shape[2]
    sum_rows = summary.shape[1] * per_seg
    padded = -(-sum_rows // 128) * 128
    length = doc_ids.shape[2]
    shards = length // here
    rows = segs * here
    shard_rows = w_query.shape[0]
    heads = model // HEAD
    row_count = lax.axis_size("x") * lax.axis_size("c")
    width = model // shards
    heads_here = width // HEAD

    flat = tokens.reshape(rows, model).astype(F32)
    standard, inverse = normalize(flat)
    hidden = (standard * gain_attn).astype(BF)
    hidden_all = lax.all_gather(hidden, SEQ, axis=0, tiled=True)

    def by_place(weight):
        return weight.reshape(shard_rows, heads_here, shards, HEAD).swapaxes(1, 2)

    qkv_here = jnp.stack([by_place(w) for w in (w_query, w_key, w_value)], axis=2)
    w_qkv = columns_in(qkv_here.reshape(shard_rows, 3 * model), ATT_GROUP, ATT_REST)
    aligned = shard_rows == HEAD
    place = lax.axis_index(SEQ)
    if aligned:
        w_out_here = w_out
        for axis in reversed(ROWS):
            w_out_here = gather_dim(w_out_here, axis, 0)
    else:
        w_out_all = lax.all_gather(w_out, AXES, axis=0, tiled=True)
        w_out_heads = w_out_all.reshape(heads_here, shards, HEAD, model)
        w_out_here = lax.dynamic_index_in_dim(w_out_heads, place, 1, False).reshape(width, model)
    w_up_here = columns_in(w_up, FFN_GROUP, FFN_REST)
    w_down_here = columns_in(w_down, FFN_GROUP, FFN_REST)
    cot = cotangent.reshape(rows, model)
    cot_all = gather_near(cot, FFN_NEAR)

    summary_flat = summary.reshape(sum_rows, model).astype(F32)
    summary_pad = jnp.pad(summary_flat, ((0, padded - sum_rows), (0, 0)))
    standard_sum, inverse_sum = normalize(summary_pad)
    hidden_sum = (standard_sum * gain_attn).astype(BF)

    def in_order(array):
        array = array.reshape(shards, segs, here, -1)
        return array.swapaxes(0, 1).reshape(segs * length, -1)

    def in_shards(array):
        array = array.reshape(segs, shards, here, -1)
        return array.swapaxes(0, 1).reshape(shards * rows, -1)

    projected = dot(hidden_all, w_qkv)
    queries = in_order((projected[:, :width] * 0.125).astype(BF))
    keys = in_order(projected[:, width : 2 * width].astype(BF))
    values = in_order(projected[:, 2 * width :].astype(BF))
    sum_proj = dot(hidden_sum, w_qkv[:, width:]).astype(BF)
    sum_keys, sum_values = sum_proj[:, :width], sum_proj[:, width:]

    docs = doc_ids.reshape(segs, length)
    last_docs = jnp.repeat(docs[: segs - 1, length - 1], per_seg)
    sum_docs = jnp.pad(last_docs, (0, padded - sum_rows), constant_values=-1)[None]
    doc_args = (docs[:, :, None], docs[:, None, :], sum_docs)
    attend, attend_back = attention_calls(segs, length, width, padded, per_seg)
    attended = in_shards(attend(*doc_args, queries, keys, values, sum_keys, sum_values))

    branch = dot(attended, w_out_here).astype(BF)
    mixed = flat + lax.psum_scatter(branch, SEQ, scatter_dimension=0, tiled=True).astype(F32)
    standard_ffn, inverse_ffn = normalize(mixed)
    normed = (standard_ffn * gain_ffn).astype(BF)
    normed_all = gather_near(normed, FFN_NEAR)

    grad_active = dot(cot_all, w_down_here)
    active, slope = gelu_both(dot(normed_all, w_up_here))
    active = active.astype(BF)
    grad_upper = (slope * grad_active).astype(BF)
    grad_normed_part = dot(grad_upper, w_up_here, 1, 1).astype(BF)
    grad_normed = scatter_near(grad_normed_part, FFN_NEAR).astype(F32)
    d_w_up = columns_out(dot(normed_all, grad_upper, 0, 0), FFN_GROUP, FFN_REST)
    d_w_down = columns_out(dot(cot_all, active, 0, 0), FFN_GROUP, FFN_REST)
    ffn_part = dot(active, w_down_here, 1, 1).astype(BF)
    activations = (mixed + scatter_near(ffn_part, FFN_NEAR).astype(F32)).astype(BF)

    grad_mixed = cot.astype(F32) + normalize_back(grad_normed, gain_ffn, standard_ffn, inverse_ffn)
    ffn_gain = jnp.sum(grad_normed * standard_ffn, axis=0)
    grad_branch = grad_mixed.astype(BF)
    grad_branch_all = lax.all_gather(grad_branch, SEQ, axis=0, tiled=True)
    grad_attended = in_order(dot(grad_branch_all, w_out_here, 1, 1).astype(BF))
    d_queries, d_keys, d_values, d_sum_keys, d_sum_values = attend_back(
        *doc_args, queries, keys, values, sum_keys, sum_values, grad_attended
    )
    d_out_part = dot(attended, grad_branch_all, 0, 0).astype(BF)
    if aligned:
        for axis in ROWS:
            d_out_part = scatter_dim(d_out_part, axis, 0)
        d_w_out = d_out_part.astype(F32)
    else:
        spread = jnp.zeros((heads_here, shards, HEAD, model), BF)
        spread = lax.dynamic_update_slice_in_dim(
            spread, d_out_part.reshape(heads_here, 1, HEAD, model), place, 1
        )
        d_w_out = lax.psum_scatter(
            spread.reshape(model, model), AXES, scatter_dimension=0, tiled=True
        ).astype(F32)

    d_projected = in_shards(jnp.concatenate([d_queries, d_keys, d_values], axis=1))
    d_sum_proj = jnp.concatenate([d_sum_keys, d_sum_values], axis=1).astype(BF)

    grad_sum_part = dot(d_sum_proj, w_qkv[:, width:], 1, 1).astype(BF)
    share_rows = padded // shards
    for axis in SEQ:
        grad_sum_part = scatter_dim(grad_sum_part, axis, 0)
    grad_sum = grad_sum_part.astype(F32)
    first_row = place * share_rows
    standard_part = lax.dynamic_slice_in_dim(standard_sum, first_row, share_rows, 0)
    inverse_part = lax.dynamic_slice_in_dim(inverse_sum, first_row, share_rows, 0)
    d_sum_part = normalize_back(grad_sum, gain_attn, standard_part, inverse_part).astype(BF)
    for axis in reversed(SEQ):
        d_sum_part = gather_dim(d_sum_part, axis, 0)
    d_summary = d_sum_part[:sum_rows].astype(F32)

    grad_hidden_part = dot(d_projected, w_qkv, 1, 1).astype(BF)
    grad_hidden = lax.psum_scatter(
        grad_hidden_part, SEQ, scatter_dimension=0, tiled=True
    ).astype(F32)
    left = jnp.concatenate([hidden_all, hidden_sum], axis=0)
    right = jnp.concatenate(
        [d_projected, jnp.pad(d_sum_proj, ((0, 0), (width, 0)))], axis=0
    )
    d_w_qkv = columns_out(dot(left, right, 0, 0), ATT_GROUP, ATT_REST)
    d_w_qkv = d_w_qkv.reshape(shard_rows, shards, 3, heads_here, HEAD)
    d_w_qkv = d_w_qkv.transpose(2, 0, 3, 1, 4).reshape(3, shard_rows, model)

    d_tokens = grad_mixed + normalize_back(grad_hidden, gain_attn, standard, inverse)
    attn_gain = jnp.sum(grad_hidden * standard, axis=0)
    attn_gain += jnp.sum(grad_sum * standard_part, axis=0)
    gains = jnp.stack([attn_gain, ffn_gain])
    for axis in AXES:
        gains = scatter_dim(gains, axis, 1)

    return (
        activations.reshape(tokens.shape),
        d_tokens.reshape(tokens.shape),
        d_summary.reshape(summary.shape),
        gains[0],
        gains[1],
        d_w_qkv[0],
        d_w_qkv[1],
        d_w_qkv[2],
        d_w_out,
        d_w_up,
        d_w_down,
    )


def solution(mesh):
    rows, seq = mesh.shape["rows"], mesh.shape["seq"]
    fine = Mesh(mesh.devices.reshape(rows // 2, 2, seq // 4, 2, 2), AXES)
    by_token = P(ROWS, None, SEQ, None)
    by_row = P(ROWS, None, None, None)
    weight = P(AXES, None)
    return jax.shard_map(
        per_device,
        mesh=fine,
        in_specs=(by_token, by_row, P(ROWS, None, None), P(), P())
        + (weight,) * 6
        + (by_token,),
        out_specs=(by_token, by_token, by_row, P(AXES), P(AXES)) + (weight,) * 6,
        check_vma=False,
    )
```

time: 4520 us -> 993 us (0.22)
  waiting for transfers between devices: 3750 us -> 675 us
  matrix products: 297 us -> 74.9 us
  local copies, waits for them, and re-layouts: 164 us -> 51.1 us
  blocking collectives: 103 us -> 0 us
  other arithmetic: 173 us -> 75.1 us
  starting transfers between devices: 0.8 us -> 50 us
    unnamed x14 -> x4, waiting for transfers between devices: 1610 us -> 0.07 us
    reduce_scatter x1 -> x2, waiting for transfers between devices: 1400 us -> 60.7 us  [the longest x1 60.7 us: per_device(): lax.psum_scatter(branch, SEQ, scatter_dimension=0, tiled=True).astype(F32)]
    all_gather x10 -> x2, waiting for transfers between devices: 742 us -> 0.02 us  [the longest x1 0.02 us: per_device(): hidden_all = lax.all_gather(hidden, SEQ, axis=0, tiled=True)]
    ppermute x0 -> x57, waiting for transfers between devices: none -> 614 us  [swap(): return lax.ppermute(array, axis, [(0, 1), (1, 0)])]
    dot_general x33 -> x14, matrix products: 296 us -> 74.9 us  [dot(): lax.dot_general(left, right, (((left_dim,), (right_dim,)), ((), ())), pre...]
    concatenate x2 -> x30, other arithmetic: 134 us -> 15.6 us  [the longest x24 10.7 us: pair(): jnp.concatenate([jnp.where(first, mine, theirs), jnp.where(first, theirs,...]
    all_gather x2 -> x0, blocking collectives: 64.7 us -> none  [the longest x1 32.4 us: per_device(): lax.all_gather(row_delta.astype(jnp.bfloat16), 'seq', axis=3, tiled=True)]
    ppermute x0 -> x57, starting transfers between devices: none -> 49.4 us  [swap(): return lax.ppermute(array, axis, [(0, 1), (1, 0)])]
  transfers between devices with their start and end apart: 13 -> 61, of which waited for: 10 -> 37; matrix products, arithmetic and copies ran while one was open for 12% -> 14% of each run, Pallas kernels for 0% -> 0%
where the time goes in v1:
time: 993 us; the launch traced here: 983 us
  waiting for transfers between devices  675 us (68%)
  other arithmetic  75.1 us (8%)
  matrix products  74.9 us (8%)
  local copies, waits for them, and re-layouts  51.1 us (5%)
  starting transfers between devices  50 us (5%)
  Pallas kernels  40.4 us (4%)
  between operations  16.2 us (2%)
    ppermute x57, waiting for transfers between devices, swap(): return lax.ppermute(array, axis, [(0, 1), (1, 0)])  614 us
    dot_general x14, matrix products, dot(): lax.dot_general(left, right, (((left_dim,), (right_dim,)), ((), ())), pre...  74.9 us
    reduce_scatter x1, waiting for transfers between devices, per_device(): lax.psum_scatter(branch, SEQ, scatter_dimension=0, tiled=True).astype(F32)  60.7 us
    ppermute x57, starting transfers between devices, swap(): return lax.ppermute(array, axis, [(0, 1), (1, 0)])  49.4 us
    pallas_call x1, Pallas kernels, per_device(): attend_back(*doc_args, queries, keys, values, sum_keys, sum_values, grad_...  24.3 us
  transfers between devices with their start and end apart: 61, of which 37 were waited for; matrix products, arithmetic and copies ran while one was open for 14% of the time, Pallas kernels for 0%

profile of v1, /device:TPU:0, one launch (start us, length us, event | category | flops | bytes accessed | tf_op | source)
XLA Modules:
  0.0 982.8 jit_solution(16155509491574612324)
XLA Ops:
  22.9 35.2 %collective-permute-done = bf16[1,1,1,1,1,64,3072]{6,5,4,3,2,1,0:T(8,128)(2,1)S(1)} collective-permute-done((bf16[1,1,1,1,1,64,3072]{6,5,4,3,2,1,0:T(8,128)(2,1)S(1)}, bf16[1,1,1,1,1,64,3072]{6,5,4,3,2,1,0:T(8,128)(2,1)S(1)}, u32[]{:S(2)}, u32[]{:S(2)}) %collective-permute-start) | collective-permute-done | bytes 393248 | tf_op jit(solution)/shard_map/ppermute | solution.py:46
  59.3 10.9 %collective-permute-done.1 = bf16[1,1,2,1,1,64,1536]{6,5,4,3,2,1,0:T(8,128)(2,1)S(1)} collective-permute-done((bf16[1,1,2,1,1,64,1536]{6,5,4,3,2,1,0:T(8,128)(2,1)S(1)}, bf16[1,1,2,1,1,64,1536]{6,5,4,3,2,1,0:T(8,128)(2,1)S(1)}, u32[]{:S(2)}, u32[]{:S(2)}) %collective-permute-start.1) | collective-permute-done | bytes 393248 | tf_op jit(solution)/shard_map/ppermute | solution.py:46
  71.8 17.5 %collective-permute-done.2 = bf16[1,1,2,2,1,64,768]{6,5,4,3,2,1,0:T(8,128)(2,1)S(1)} collective-permute-done((bf16[1,1,2,2,1,64,768]{6,5,4,3,2,1,0:T(8,128)(2,1)S(1)}, bf16[1,1,2,2,1,64,768]{6,5,4,3,2,1,0:T(8,128)(2,1)S(1)}, u32[]{:S(2)}, u32[]{:S(2)}) %collective-permute-start.2) | collective-permute-done | bytes 393248 | tf_op jit(solution)/shard_map/ppermute | solution.py:46
  91.4 13.2 %collective-permute-done.3 = bf16[1,1,2,2,2,64,768]{6,5,4,3,2,1,0:T(8,128)(2,1)} collective-permute-done((bf16[1,1,2,2,2,64,768]{6,5,4,3,2,1,0:T(8,128)(2,1)S(1)}, bf16[1,1,2,2,2,64,768]{6,5,4,3,2,1,0:T(8,128)(2,1)}, u32[]{:S(2)}, u32[]{:S(2)}) %collective-permute-start.3) | collective-permute-done | bytes 786464 | tf_op jit(solution)/shard_map/ppermute | solution.py:46
  111.6 12.2 %collective-permute-done.6 = bf16[128,2048]{1,0:T(8,128)(2,1)} collective-permute-done((bf16[128,2048]{1,0:T(8,128)(2,1)}, bf16[128,2048]{1,0:T(8,128)(2,1)}, u32[]{:S(2)}, u32[]{:S(2)}) %collective-permute-start.6) | collective-permute-done | bytes 524320 | tf_op jit(solution)/shard_map/ppermute | solution.py:46
  137.0 16.1 %shard_map.203 = bf16[1152,256]{1,0:T(8,128)(2,1)S(1)} custom-call(s32[3,384,1]{2,1,0:T(8,128)S(1)} %copy.36.col_ref, s32[3,1,384]{2,1,0:T(1,128)S(1)} %bitcast.118, s32[1,128]{1,0:T(1,128)S(1)} %pad_bitcast_fusion.sum_ref, bf16[1152,256]{1,0:T(8,128)(2,1)S(1)} %bitcast.109, bf16[1152,256]{1,0:T(8,128)(2,1)S(1)} %bitcast.111, ...), custom_call_target="tpu_custom_call" | custom-call | flops 1509949440 | bytes 2359296 | tf_op jit(solution)/shard_map/pallas_call | solution.py:329
  163.5 12.9 %collective-permute-done.15 = bf16[1,1,1,1,1,64,4096]{6,5,4,3,2,1,0:T(8,128)(2,1)} collective-permute-done((bf16[1,1,1,1,1,64,4096]{6,5,4,3,2,1,0:T(8,128)(2,1)}, bf16[1,1,1,1,1,64,4096]{6,5,4,3,2,1,0:T(8,128)(2,1)}, u32[]{:S(2)}, u32[]{:S(2)}) %collective-permute-start.15) | collective-permute-done | bytes 524320 | tf_op jit(solution)/shard_map/ppermute | solution.py:46
  177.8 13.3 %collective-permute-done.10 = bf16[1,1,1,1,1,64,4096]{6,5,4,3,2,1,0:T(8,128)(2,1)} collective-permute-done((bf16[1,1,1,1,1,64,4096]{6,5,4,3,2,1,0:T(8,128)(2,1)}, bf16[1,1,1,1,1,64,4096]{6,5,4,3,2,1,0:T(8,128)(2,1)}, u32[]{:S(2)}, u32[]{:S(2)}) %collective-permute-start.10) | collective-permute-done | bytes 524320 | tf_op jit(solution)/shard_map/ppermute | solution.py:46
  198.6 29.3 %collective-permute-done.17 = bf16[1,2,1,1,2,64,1024]{6,5,4,3,2,1,0:T(8,128)(2,1)S(1)} collective-permute-done((bf16[1,2,1,1,2,64,1024]{6,5,4,3,2,1,0:T(8,128)(2,1)S(1)}, bf16[1,2,1,1,2,64,1024]{6,5,4,3,2,1,0:T(8,128)(2,1)S(1)}, u32[]{:S(2)}, u32[]{:S(2)}) %collective-permute-start.17) | collective-permute-done | bytes 524320 | tf_op jit(solution)/shard_map/ppermute | solution.py:46
  232.2 60.7 %reduce-scatter.3.cloned.1.call-done = bf16[144,2048]{1,0:T(8,128)(2,1)} async-done(((bf16[1152,2048]{1,0:T(8,128)(2,1)}), bf16[144,2048]{1,0:T(8,128)(2,1)}) %reduce-scatter.3.cloned.1.call-update) | async-done | bytes 589840 | tf_op jit(solution)/shard_map/reduce_scatter | solution.py:332
  299.6 20.6 %collective-permute-done.7 = bf16[144,2048]{1,0:T(8,128)(2,1)S(1)} collective-permute-done((bf16[144,2048]{1,0:T(8,128)(2,1)S(1)}, bf16[144,2048]{1,0:T(8,128)(2,1)S(1)}, u32[]{:S(2)}, u32[]{:S(2)}) %collective-permute-start.7) | collective-permute-done | bytes 589856 | tf_op jit(solution)/shard_map/ppermute | solution.py:46
  324.9 22.2 %collective-permute-done.13 = bf16[1,2,1,2,2,64,1024]{6,5,4,3,2,1,0:T(8,128)(2,1)S(1)} collective-permute-done((bf16[1,2,1,2,2,64,1024]{6,5,4,3,2,1,0:T(8,128)(2,1)S(1)}, bf16[1,2,1,2,2,64,1024]{6,5,4,3,2,1,0:T(8,128)(2,1)S(1)}, u32[]{:S(2)}, u32[]{:S(2)}) %collective-permute-start.13) | collective-permute-done | bytes 1048608 | tf_op jit(solution)/shard_map/ppermute | solution.py:46
  357.7 14.5 %collective-permute-done.19 = bf16[1,2,2,2,2,64,1024]{6,5,4,3,2,1,0:T(8,128)(2,1)} collective-permute-done((bf16[1,2,2,2,2,64,1024]{6,5,4,3,2,1,0:T(8,128)(2,1)}, bf16[1,2,2,2,2,64,1024]{6,5,4,3,2,1,0:T(8,128)(2,1)}, u32[]{:S(2)}, u32[]{:S(2)}) %collective-permute-start.19) | collective-permute-done | bytes 2097184 | tf_op jit(solution)/shard_map/ppermute | solution.py:46
  374.6 42.1 %collective-permute-done.14 = bf16[1,2,2,2,2,64,1024]{6,5,4,3,2,1,0:T(8,128)(2,1)} collective-permute-done((bf16[1,2,2,2,2,64,1024]{6,5,4,3,2,1,0:T(8,128)(2,1)}, bf16[1,2,2,2,2,64,1024]{6,5,4,3,2,1,0:T(8,128)(2,1)}, u32[]{:S(2)}, u32[]{:S(2)}) %collective-permute-start.14) | collective-permute-done | bytes 2097184 | tf_op jit(solution)/shard_map/ppermute | solution.py:46
  428.4 29.8 %collective-permute-done.25 = bf16[576,2048]{1,0:T(8,128)(2,1)S(1)} collective-permute-done((bf16[576,2048]{1,0:T(8,128)(2,1)S(1)}, bf16[576,2048]{1,0:T(8,128)(2,1)S(1)}, u32[]{:S(2)}, u32[]{:S(2)}) %collective-permute-start.25) | collective-permute-done | bytes 2359328 | tf_op jit(solution)/shard_map/ppermute | solution.py:46
  458.2 9.8 %fusion.9 = bf16[1152,1024]{1,0:T(8,128)(2,1)S(1)} fusion(bf16[2048,1024]{1,0:T(8,128)(2,1)S(1)} %bitcast.132, f32[1152,1024]{1,0:T(8,128)S(1)} %get-tuple-element.132, bf16[576,2048]{1,0:T(8,128)(2,1)S(1)} %collective-permute-done.25, bf16[288,2048]{1,0:T(8,128)(2,1)} %collective-permute-done.24, bf16[144,2048]{1,0:T(8,128)(2,1)S(1)} %copy-done.47, ...), kind=kOutput, calls=%fused_computation.22 | convolution fusion | flops 4862509056 | bytes 15990784 | tf_op jit(solution)/shard_map/dot_general | solution.py:24
  508.3 22.5 %collective-permute-done.26 = bf16[576,2048]{1,0:T(8,128)(2,1)} collective-permute-done((bf16[576,2048]{1,0:T(8,128)(2,1)}, bf16[576,2048]{1,0:T(8,128)(2,1)}, u32[]{:S(2)}, u32[]{:S(2)}) %collective-permute-start.26) | collective-permute-done | bytes 2359328 | tf_op jit(solution)/shard_map/ppermute | solution.py:46
  533.6 46.5 %collective-permute-done.20 = bf16[576,2048]{1,0:T(8,128)(2,1)} collective-permute-done((bf16[576,2048]{1,0:T(8,128)(2,1)}, bf16[576,2048]{1,0:T(8,128)(2,1)}, u32[]{:S(2)}, u32[]{:S(2)}) %collective-permute-start.20) | collective-permute-done | bytes 2359328 | tf_op jit(solution)/shard_map/ppermute | solution.py:46
  595.5 27.9 %collective-permute-done.28 = bf16[144,2048]{1,0:T(8,128)(2,1)S(1)} collective-permute-done((bf16[144,2048]{1,0:T(8,128)(2,1)S(1)}, bf16[144,2048]{1,0:T(8,128)(2,1)S(1)}, u32[]{:S(2)}, u32[]{:S(2)}) %collective-permute-start.28) | collective-permute-done | bytes 589856 | tf_op jit(solution)/shard_map/ppermute | solution.py:46
  624.5 18.2 %collective-permute-done.22 = bf16[144,2048]{1,0:T(8,128)(2,1)S(1)} collective-permute-done((bf16[144,2048]{1,0:T(8,128)(2,1)S(1)}, bf16[144,2048]{1,0:T(8,128)(2,1)S(1)}, u32[]{:S(2)}, u32[]{:S(2)}) %collective-permute-start.22) | collective-permute-done | bytes 589856 | tf_op jit(solution)/shard_map/ppermute | solution.py:46
  648.0 49.6 %collective-permute-done.53 = bf16[1,2,1,2,2,64,1024]{6,5,4,3,2,1,0:T(8,128)(2,1)} collective-permute-done((bf16[1,2,1,2,2,64,1024]{6,5,4,3,2,1,0:T(8,128)(2,1)}, bf16[1,2,1,2,2,64,1024]{6,5,4,3,2,1,0:T(8,128)(2,1)}, u32[]{:S(2)}, u32[]{:S(2)}) %collective-permute-start.53) | collective-permute-done | bytes 1048608 | tf_op jit(solution)/shard_map/ppermute | solution.py:46
  704.3 37.3 %collective-permute-done.54 = bf16[1,2,1,1,2,64,1024]{6,5,4,3,2,1,0:T(8,128)(2,1)} collective-permute-done((bf16[1,2,1,1,2,64,1024]{6,5,4,3,2,1,0:T(8,128)(2,1)}, bf16[1,2,1,1,2,64,1024]{6,5,4,3,2,1,0:T(8,128)(2,1)}, u32[]{:S(2)}, u32[]{:S(2)}) %collective-permute-start.54) | collective-permute-done | bytes 524320 | tf_op jit(solution)/shard_map/ppermute | solution.py:46
  746.9 12.3 %collective-permute-done.51 = bf16[1,1,1,1,1,64,4096]{6,5,4,3,2,1,0:T(8,128)(2,1)S(1)} collective-permute-done((bf16[1,1,1,1,1,64,4096]{6,5,4,3,2,1,0:T(8,128)(2,1)S(1)}, bf16[1,1,1,1,1,64,4096]{6,5,4,3,2,1,0:T(8,128)(2,1)S(1)}, u32[]{:S(2)}, u32[]{:S(2)}) %collective-permute-start.51) | collective-permute-done | bytes 524320 | tf_op jit(solution)/shard_map/ppermute | solution.py:46
  759.4 10.6 %collective-permute-done.56 = bf16[1,1,1,1,1,64,4096]{6,5,4,3,2,1,0:T(8,128)(2,1)S(1)} collective-permute-done((bf16[1,1,1,1,1,64,4096]{6,5,4,3,2,1,0:T(8,128)(2,1)S(1)}, bf16[1,1,1,1,1,64,4096]{6,5,4,3,2,1,0:T(8,128)(2,1)S(1)}, u32[]{:S(2)}, u32[]{:S(2)}) %collective-permute-start.56) | collective-permute-done | bytes 524320 | tf_op jit(solution)/shard_map/ppermute | solution.py:46
  777.1 24.3 %shard_map.204 = (bf16[1152,256]{1,0:T(8,128)(2,1)S(1)}, bf16[1152,256]{1,0:T(8,128)(2,1)S(1)}, bf16[1152,256]{1,0:T(8,128)(2,1)S(1)}, f32[128,256]{1,0:T(8,128)S(1)}, f32[128,256]{1,0:T(8,128)S(1)}) custom-call(s32[3,384,1]{2,1,0:T(8,128)S(1)} %copy.36.col_ref, s32[3,1,384]{2,1,0:T(1,128)S(1)} %bitcast.119, s32[1,128]{1,0:T(1,128)S(1)} %pad_bitcast_fusion.sum_ref, ...), custom_call_target="tpu_custom_call" | custom-call | flops 3774873600 | bytes 4128768 | tf_op jit(solution)/shard_map/pallas_call | solution.py:353
  818.4 17.9 %collective-permute-done.29 = bf16[64,2048]{1,0:T(8,128)(2,1)S(1)} collective-permute-done((bf16[64,2048]{1,0:T(8,128)(2,1)S(1)}, bf16[64,2048]{1,0:T(8,128)(2,1)S(1)}, u32[]{:S(2)}, u32[]{:S(2)}) %collective-permute-start.29) | collective-permute-done | bytes 262176 | tf_op jit(solution)/shard_map/ppermute | solution.py:46
  837.1 12.5 %collective-permute-done.30 = bf16[32,2048]{1,0:T(8,128)(2,1)S(1)} collective-permute-done((bf16[32,2048]{1,0:T(8,128)(2,1)S(1)}, bf16[32,2048]{1,0:T(8,128)(2,1)S(1)}, u32[]{:S(2)}, u32[]{:S(2)}) %collective-permute-start.30) | collective-permute-done | bytes 131104 | tf_op jit(solution)/shard_map/ppermute | solution.py:46
  861.0 11.9 %collective-permute-done.45 = bf16[128,2048]{1,0:T(8,128)(2,1)S(1)} collective-permute-done((bf16[128,2048]{1,0:T(8,128)(2,1)S(1)}, bf16[128,2048]{1,0:T(8,128)(2,1)S(1)}, u32[]{:S(2)}, u32[]{:S(2)}) %collective-permute-start.45) | collective-permute-done | bytes 524320 | tf_op jit(solution)/shard_map/ppermute | solution.py:46
  873.1 13.7 %collective-permute-done.41 = bf16[1,1,2,2,2,64,768]{6,5,4,3,2,1,0:T(8,128)(2,1)S(1)} collective-permute-done((bf16[1,1,2,2,2,64,768]{6,5,4,3,2,1,0:T(8,128)(2,1)S(1)}, bf16[1,1,2,2,2,64,768]{6,5,4,3,2,1,0:T(8,128)(2,1)S(1)}, u32[]{:S(2)}, u32[]{:S(2)}) %collective-permute-start.41) | collective-permute-done | bytes 786464 | tf_op jit(solution)/shard_map/ppermute | solution.py:46
  890.9 9.7 collective-permute-done.42
  901.6 21.0 %collective-permute-done.43 = bf16[1,1,2,1,1,64,1536]{6,5,4,3,2,1,0:T(8,128)(2,1)S(1)} collective-permute-done((bf16[1,1,2,1,1,64,1536]{6,5,4,3,2,1,0:T(8,128)(2,1)S(1)}, bf16[1,1,2,1,1,64,1536]{6,5,4,3,2,1,0:T(8,128)(2,1)S(1)}, u32[]{:S(2)}, u32[]{:S(2)}) %collective-permute-start.43) | collective-permute-done | bytes 393248 | tf_op jit(solution)/shard_map/ppermute | solution.py:46
  930.3 16.0 %collective-permute-done.44 = bf16[1,1,1,1,1,64,3072]{6,5,4,3,2,1,0:T(8,128)(2,1)} collective-permute-done((bf16[1,1,1,1,1,64,3072]{6,5,4,3,2,1,0:T(8,128)(2,1)}, bf16[1,1,1,1,1,64,3072]{6,5,4,3,2,1,0:T(8,128)(2,1)}, u32[]{:S(2)}, u32[]{:S(2)}) %collective-permute-start.44) | collective-permute-done | bytes 393248 | tf_op jit(solution)/shard_map/ppermute | solution.py:46
  (448 shorter events, 254.4 us)
Async XLA Ops:
  7.2 122.8 %all-gather.3.cloned.1.call-start = ((), (), s32[]{:S(2)}) async-start(), calls=%async_computation.2 | async-start | bytes 5308416 | tf_op jit(solution)/shard_map/all_gather | solution.py:282
  12.5 280.4 %reduce-scatter.3.cloned.1.call-start = ((), (), s32[]{:S(2)}) async-start(), calls=%async_computation.3 | async-start | bytes 5308416 | tf_op jit(solution)/shard_map/reduce_scatter | solution.py:332
  18.8 39.3 %collective-permute-start = (bf16[1,1,1,1,1,64,3072]{6,5,4,3,2,1,0:T(8,128)(2,1)S(1)}, bf16[1,1,1,1,1,64,3072]{6,5,4,3,2,1,0:T(8,128)(2,1)S(1)}, u32[]{:S(2)}, u32[]{:S(2)}) collective-permute-start(bf16[1,1,1,1,1,64,3072]{6,5,4,3,2,1,0:T(8,128)(2,1)S(1)} %constant_dynamic-slice_fusion.26), channel_id=1, source_target_pairs={{0,4},{4,0},{1,5},{5,1},{2,6},{6,2},{3,7},{7,3},{8,12},{12,8},{9,1... | collective-permute-start | bytes 1179656 | tf_op jit(solution)/shard_map/ppermute | solution.py:46
  157.6 615.6 %all-gather.5.cloned.1.call-start = ((), (), s32[]{:S(2)}) async-start(), calls=%async_computation.4 | async-start | bytes 5308416 | tf_op jit(solution)/shard_map/all_gather | solution.py:351
  163.4 27.8 %collective-permute-start.10 = (bf16[1,1,1,1,1,64,4096]{6,5,4,3,2,1,0:T(8,128)(2,1)}, bf16[1,1,1,1,1,64,4096]{6,5,4,3,2,1,0:T(8,128)(2,1)}, u32[]{:S(2)}, u32[]{:S(2)}) collective-permute-start(bf16[1,1,1,1,1,64,4096]{6,5,4,3,2,1,0:T(8,128)(2,1)} %dynamic-slice_bitcast_fusion.1), channel_id=1, source_target_pairs={{0,1},{1,0},{2,3},{3,2},{4,5},{5,4},{6,7},{7,6},{8,9},{9,8},{10,11... | collective-permute-start | bytes 1572872 | tf_op jit(solution)/shard_map/ppermute | solution.py:46
  192.9 35.0 %collective-permute-start.17 = (bf16[1,2,1,1,2,64,1024]{6,5,4,3,2,1,0:T(8,128)(2,1)S(1)}, bf16[1,2,1,1,2,64,1024]{6,5,4,3,2,1,0:T(8,128)(2,1)S(1)}, u32[]{:S(2)}, u32[]{:S(2)}) collective-permute-start(bf16[1,2,1,1,2,64,1024]{6,5,4,3,2,1,0:T(8,128)(2,1)S(1)} %fusion.56), channel_id=1, source_target_pairs={{0,2},{2,0},{1,3},{3,1},{4,6},{6,4},{5,7},{7,5},{8,10},{10,8},{9,1... | collective-permute-start | bytes 1572872 | tf_op jit(solution)/shard_map/ppermute | solution.py:46
  197.1 98.7 %collective-permute-start.12 = (bf16[1,2,1,1,2,64,1024]{6,5,4,3,2,1,0:T(8,128)(2,1)}, bf16[1,2,1,1,2,64,1024]{6,5,4,3,2,1,0:T(8,128)(2,1)}, u32[]{:S(2)}, u32[]{:S(2)}) collective-permute-start(bf16[1,2,1,1,2,64,1024]{6,5,4,3,2,1,0:T(8,128)(2,1)} %fusion.60), channel_id=1, source_target_pairs={{0,2},{2,0},{1,3},{3,1},{4,6},{6,4},{5,7},{7,5},{8,10},{10,8},{9,1... | collective-permute-start | bytes 1572872 | tf_op jit(solution)/shard_map/ppermute | solution.py:46
  230.0 90.3 %collective-permute-start.18 = (bf16[1,2,1,2,2,64,1024]{6,5,4,3,2,1,0:T(8,128)(2,1)}, bf16[1,2,1,2,2,64,1024]{6,5,4,3,2,1,0:T(8,128)(2,1)}, u32[]{:S(2)}, u32[]{:S(2)}) collective-permute-start(bf16[1,2,1,2,2,64,1024]{6,5,4,3,2,1,0:T(8,128)(2,1)} %pad_maximum_fusion.16), channel_id=1, source_target_pairs={{0,4},{4,0},{1,5},{5,1},{2,6},{6,2},{3,7},{7,3},{8,12},{12,8},{9,1... | collective-permute-start | bytes 3145736 | tf_op jit(solution)/shard_map/ppermute | solution.py:46
  298.5 48.7 %collective-permute-start.13 = (bf16[1,2,1,2,2,64,1024]{6,5,4,3,2,1,0:T(8,128)(2,1)S(1)}, bf16[1,2,1,2,2,64,1024]{6,5,4,3,2,1,0:T(8,128)(2,1)S(1)}, u32[]{:S(2)}, u32[]{:S(2)}) collective-permute-start(bf16[1,2,1,2,2,64,1024]{6,5,4,3,2,1,0:T(8,128)(2,1)S(1)} %pad_maximum_fusion.15), channel_id=1, source_target_pairs={{0,4},{4,0},{1,5},{5,1},{2,6},{6,2},{3,7},{7,3},{8,12},{12,8},{9,1... | collective-permute-start | bytes 3145736 | tf_op jit(solution)/shard_map/ppermute | solution.py:46
  298.5 52.2 %collective-permute-start.23 = (bf16[144,2048]{1,0:T(8,128)(2,1)S(1)}, bf16[144,2048]{1,0:T(8,128)(2,1)S(1)}, u32[]{:S(2)}, u32[]{:S(2)}) collective-permute-start(bf16[144,2048]{1,0:T(8,128)(2,1)S(1)} %bitcast.124), channel_id=1, source_target_pairs={{0,2},{2,0},{1,3},{3,1},{4,6},{6,4},{5,7},{7,5},{8,10},{10,8},{9,1... | collective-permute-start | bytes 1769480 | tf_op jit(solution)/shard_map/ppermute | solution.py:46
  320.3 31.7 %collective-permute-start.8 = (bf16[288,2048]{1,0:T(8,128)(2,1)S(1)}, bf16[288,2048]{1,0:T(8,128)(2,1)S(1)}, u32[]{:S(2)}, u32[]{:S(2)}) collective-permute-start(bf16[288,2048]{1,0:T(8,128)(2,1)S(1)} %pad_maximum_fusion.12), channel_id=1, source_target_pairs={{0,8},{8,0},{1,9},{9,1},{2,10},{10,2},{3,11},{11,3},{4,12},{12,4},... | collective-permute-start | bytes 3538952 | tf_op jit(solution)/shard_map/ppermute | solution.py:46
  323.5 48.7 %collective-permute-start.19 = (bf16[1,2,2,2,2,64,1024]{6,5,4,3,2,1,0:T(8,128)(2,1)}, bf16[1,2,2,2,2,64,1024]{6,5,4,3,2,1,0:T(8,128)(2,1)}, u32[]{:S(2)}, u32[]{:S(2)}) collective-permute-start(bf16[1,2,2,2,2,64,1024]{6,5,4,3,2,1,0:T(8,128)(2,1)} %pad_maximum_fusion.8), channel_id=1, source_target_pairs={{0,16},{16,0},{1,17},{17,1},{2,18},{18,2},{3,19},{19,3},{4,20},{20... | collective-permute-start | bytes 6291464 | tf_op jit(solution)/shard_map/ppermute | solution.py:46
  349.2 67.5 %collective-permute-start.14 = (bf16[1,2,2,2,2,64,1024]{6,5,4,3,2,1,0:T(8,128)(2,1)}, bf16[1,2,2,2,2,64,1024]{6,5,4,3,2,1,0:T(8,128)(2,1)}, u32[]{:S(2)}, u32[]{:S(2)}) collective-permute-start(bf16[1,2,2,2,2,64,1024]{6,5,4,3,2,1,0:T(8,128)(2,1)} %pad_maximum_fusion.7), channel_id=1, source_target_pairs={{0,16},{16,0},{1,17},{17,1},{2,18},{18,2},{3,19},{19,3},{4,20},{20... | collective-permute-start | bytes 6291464 | tf_op jit(solution)/shard_map/ppermute | solution.py:46
  353.7 65.3 %collective-permute-start.9 = (bf16[576,2048]{1,0:T(8,128)(2,1)}, bf16[576,2048]{1,0:T(8,128)(2,1)}, u32[]{:S(2)}, u32[]{:S(2)}) collective-permute-start(bf16[576,2048]{1,0:T(8,128)(2,1)} %pad_maximum_fusion.5), channel_id=1, source_target_pairs={{0,1},{1,0},{2,3},{3,2},{4,5},{5,4},{6,7},{7,6},{8,9},{9,8},{10,11... | collective-permute-start | bytes 7077896 | tf_op jit(solution)/shard_map/ppermute | solution.py:46
  356.9 101.3 %collective-permute-start.25 = (bf16[576,2048]{1,0:T(8,128)(2,1)S(1)}, bf16[576,2048]{1,0:T(8,128)(2,1)S(1)}, u32[]{:S(2)}, u32[]{:S(2)}) collective-permute-start(bf16[576,2048]{1,0:T(8,128)(2,1)S(1)} %pad_maximum_fusion.6), channel_id=1, source_target_pairs={{0,1},{1,0},{2,3},{3,2},{4,5},{5,4},{6,7},{7,6},{8,9},{9,8},{10,11... | collective-permute-start | bytes 7077896 | tf_op jit(solution)/shard_map/ppermute | solution.py:46
  476.3 54.5 %collective-permute-start.26 = (bf16[576,2048]{1,0:T(8,128)(2,1)}, bf16[576,2048]{1,0:T(8,128)(2,1)}, u32[]{:S(2)}, u32[]{:S(2)}) collective-permute-start(bf16[576,2048]{1,0:T(8,128)(2,1)} %slice.120), channel_id=1, source_target_pairs={{0,1},{1,0},{2,3},{3,2},{4,5},{5,4},{6,7},{7,6},{8,9},{9,8},{10,11... | collective-permute-start | bytes 7077896 | tf_op jit(solution)/shard_map/ppermute | solution.py:46
  485.1 95.0 %collective-permute-start.20 = (bf16[576,2048]{1,0:T(8,128)(2,1)}, bf16[576,2048]{1,0:T(8,128)(2,1)}, u32[]{:S(2)}, u32[]{:S(2)}) collective-permute-start(bf16[576,2048]{1,0:T(8,128)(2,1)} %slice.114), channel_id=1, source_target_pairs={{0,1},{1,0},{2,3},{3,2},{4,5},{5,4},{6,7},{7,6},{8,9},{9,8},{10,11... | collective-permute-start | bytes 7077896 | tf_op jit(solution)/shard_map/ppermute | solution.py:46
  496.5 86.5 %collective-permute-start.47 = (bf16[1,2,2,2,2,64,1024]{6,5,4,3,2,1,0:T(8,128)(2,1)}, bf16[1,2,2,2,2,64,1024]{6,5,4,3,2,1,0:T(8,128)(2,1)}, u32[]{:S(2)}, u32[]{:S(2)}) collective-permute-start(bf16[1,2,2,2,2,64,1024]{6,5,4,3,2,1,0:T(8,128)(2,1)} %constant_dynamic-slice_fusion.5), channel_id=1, source_target_pairs={{0,16},{16,0},{1,17},{17,1},{2,18},{18,2},{3,19},{19,3},{4,20},{20... | collective-permute-start | bytes 6291464 | tf_op jit(solution)/shard_map/ppermute | solution.py:46
  506.8 81.7 %collective-permute-start.52 = (bf16[1,2,2,2,2,64,1024]{6,5,4,3,2,1,0:T(8,128)(2,1)}, bf16[1,2,2,2,2,64,1024]{6,5,4,3,2,1,0:T(8,128)(2,1)}, u32[]{:S(2)}, u32[]{:S(2)}) collective-permute-start(bf16[1,2,2,2,2,64,1024]{6,5,4,3,2,1,0:T(8,128)(2,1)} %constant_dynamic-slice_fusion.2), channel_id=1, source_target_pairs={{0,16},{16,0},{1,17},{17,1},{2,18},{18,2},{3,19},{19,3},{4,20},{20... | collective-permute-start | bytes 6291464 | tf_op jit(solution)/shard_map/ppermute | solution.py:46
  533.5 57.0 %collective-permute-start.27 = (bf16[288,2048]{1,0:T(8,128)(2,1)S(1)}, bf16[288,2048]{1,0:T(8,128)(2,1)S(1)}, u32[]{:S(2)}, u32[]{:S(2)}) collective-permute-start(bf16[288,2048]{1,0:T(8,128)(2,1)S(1)} %slice.122), channel_id=1, source_target_pairs={{0,8},{8,0},{1,9},{9,1},{2,10},{10,2},{3,11},{11,3},{4,12},{12,4},... | collective-permute-start | bytes 3538952 | tf_op jit(solution)/shard_map/ppermute | solution.py:46
  586.9 58.2 %collective-permute-start.48 = (bf16[1,2,1,2,2,64,1024]{6,5,4,3,2,1,0:T(8,128)(2,1)}, bf16[1,2,1,2,2,64,1024]{6,5,4,3,2,1,0:T(8,128)(2,1)}, u32[]{:S(2)}, u32[]{:S(2)}) collective-permute-start(bf16[1,2,1,2,2,64,1024]{6,5,4,3,2,1,0:T(8,128)(2,1)} %constant_dynamic-slice_fusion.4), channel_id=1, source_target_pairs={{0,4},{4,0},{1,5},{5,1},{2,6},{6,2},{3,7},{7,3},{8,12},{12,8},{9,1... | collective-permute-start | bytes 3145736 | tf_op jit(solution)/shard_map/ppermute | solution.py:46
  590.7 32.7 %collective-permute-start.28 = (bf16[144,2048]{1,0:T(8,128)(2,1)S(1)}, bf16[144,2048]{1,0:T(8,128)(2,1)S(1)}, u32[]{:S(2)}, u32[]{:S(2)}) collective-permute-start(bf16[144,2048]{1,0:T(8,128)(2,1)S(1)} %slice.124), channel_id=1, source_target_pairs={{0,2},{2,0},{1,3},{3,1},{4,6},{6,4},{5,7},{7,5},{8,10},{10,8},{9,1... | collective-permute-start | bytes 1769480 | tf_op jit(solution)/shard_map/ppermute | solution.py:46
  591.0 51.7 %collective-permute-start.22 = (bf16[144,2048]{1,0:T(8,128)(2,1)S(1)}, bf16[144,2048]{1,0:T(8,128)(2,1)S(1)}, u32[]{:S(2)}, u32[]{:S(2)}) collective-permute-start(bf16[144,2048]{1,0:T(8,128)(2,1)S(1)} %slice.118), channel_id=1, source_target_pairs={{0,2},{2,0},{1,3},{3,1},{4,6},{6,4},{5,7},{7,5},{8,10},{10,8},{9,1... | collective-permute-start | bytes 1769480 | tf_op jit(solution)/shard_map/ppermute | solution.py:46
  594.1 103.5 %collective-permute-start.53 = (bf16[1,2,1,2,2,64,1024]{6,5,4,3,2,1,0:T(8,128)(2,1)}, bf16[1,2,1,2,2,64,1024]{6,5,4,3,2,1,0:T(8,128)(2,1)}, u32[]{:S(2)}, u32[]{:S(2)}) collective-permute-start(bf16[1,2,1,2,2,64,1024]{6,5,4,3,2,1,0:T(8,128)(2,1)} %constant_dynamic-slice_fusion.1), channel_id=1, source_target_pairs={{0,4},{4,0},{1,5},{5,1},{2,6},{6,2},{3,7},{7,3},{8,12},{12,8},{9,1... | collective-permute-start | bytes 3145736 | tf_op jit(solution)/shard_map/ppermute | solution.py:46
  644.9 302.7 %reduce-scatter.5.cloned.1.call-start = ((), (), s32[]{:S(2)}) async-start(), calls=%async_computation.5 | async-start | bytes 5308416 | tf_op jit(solution)/shard_map/reduce_scatter | solution.py:387
  647.9 52.4 %collective-permute-start.49 = (bf16[1,2,1,1,2,64,1024]{6,5,4,3,2,1,0:T(8,128)(2,1)S(1)}, bf16[1,2,1,1,2,64,1024]{6,5,4,3,2,1,0:T(8,128)(2,1)}, u32[]{:S(2)}, u32[]{:S(2)}) collective-permute-start(bf16[1,2,1,1,2,64,1024]{6,5,4,3,2,1,0:T(8,128)(2,1)S(1)} %constant_dynamic-slice_fusion.3), channel_id=1, source_target_pairs={{0,2},{2,0},{1,3},{3,1},{4,6},{6,4},{5,7},{7,5},{8,10},{10,8},{9,1... | collective-permute-start | bytes 1572872 | tf_op jit(solution)/shard_map/ppermute | solution.py:46
  700.2 41.5 %collective-permute-start.54 = (bf16[1,2,1,1,2,64,1024]{6,5,4,3,2,1,0:T(8,128)(2,1)}, bf16[1,2,1,1,2,64,1024]{6,5,4,3,2,1,0:T(8,128)(2,1)}, u32[]{:S(2)}, u32[]{:S(2)}) collective-permute-start(bf16[1,2,1,1,2,64,1024]{6,5,4,3,2,1,0:T(8,128)(2,1)} %constant_dynamic-slice_fusion), channel_id=1, source_target_pairs={{0,2},{2,0},{1,3},{3,1},{4,6},{6,4},{5,7},{7,5},{8,10},{10,8},{9,1... | collective-permute-start | bytes 1572872 | tf_op jit(solution)/shard_map/ppermute | solution.py:46
  702.3 40.8 %collective-permute-start.50 = (bf16[1,1,1,1,2,64,2048]{6,5,4,3,2,1,0:T(8,128)(2,1)}, bf16[1,1,1,1,2,64,2048]{6,5,4,3,2,1,0:T(8,128)(2,1)}, u32[]{:S(2)}, u32[]{:S(2)}) collective-permute-start(bf16[1,1,1,1,2,64,2048]{6,5,4,3,2,1,0:T(8,128)(2,1)} %fusion.54), channel_id=1, source_target_pairs={{0,8},{8,0},{1,9},{9,1},{2,10},{10,2},{3,11},{11,3},{4,12},{12,4},... | collective-permute-start | bytes 1572872 | tf_op jit(solution)/shard_map/ppermute | solution.py:46
  809.7 26.6 %collective-permute-start.29 = (bf16[64,2048]{1,0:T(8,128)(2,1)S(1)}, bf16[64,2048]{1,0:T(8,128)(2,1)S(1)}, u32[]{:S(2)}, u32[]{:S(2)}) collective-permute-start(bf16[64,2048]{1,0:T(8,128)(2,1)S(1)} %constant_dynamic-slice_fusion.23), channel_id=1, source_target_pairs={{0,4},{4,0},{1,5},{5,1},{2,6},{6,2},{3,7},{7,3},{8,12},{12,8},{9,1... | collective-permute-start | bytes 786440 | tf_op jit(solution)/shard_map/ppermute | solution.py:46
  860.9 26.4 %collective-permute-start.33 = (bf16[32,2048]{1,0:T(8,128)(2,1)S(1)}, bf16[32,2048]{1,0:T(8,128)(2,1)S(1)}, u32[]{:S(2)}, u32[]{:S(2)}) collective-permute-start(bf16[32,2048]{1,0:T(8,128)(2,1)S(1)} %pad_maximum_fusion.28), channel_id=1, source_target_pairs={{0,2},{2,0},{1,3},{3,1},{4,6},{6,4},{5,7},{7,5},{8,10},{10,8},{9,1... | collective-permute-start | bytes 393224 | tf_op jit(solution)/shard_map/ppermute | solution.py:46
  873.0 27.7 %collective-permute-start.46 = (bf16[64,2048]{1,0:T(8,128)(2,1)S(1)}, bf16[64,2048]{1,0:T(8,128)(2,1)S(1)}, u32[]{:S(2)}, u32[]{:S(2)}) collective-permute-start(bf16[64,2048]{1,0:T(8,128)(2,1)S(1)} %constant_dynamic-slice_fusion.6), channel_id=1, source_target_pairs={{0,8},{8,0},{1,9},{9,1},{2,10},{10,2},{3,11},{11,3},{4,12},{12,4},... | collective-permute-start | bytes 786440 | tf_op jit(solution)/shard_map/ppermute | solution.py:46
  887.4 41.1 %collective-permute-start.34 = (bf16[64,2048]{1,0:T(8,128)(2,1)S(1)}, bf16[64,2048]{1,0:T(8,128)(2,1)S(1)}, u32[]{:S(2)}, u32[]{:S(2)}) collective-permute-start(bf16[64,2048]{1,0:T(8,128)(2,1)S(1)} %pad_maximum_fusion.26), channel_id=1, source_target_pairs={{0,4},{4,0},{1,5},{5,1},{2,6},{6,2},{3,7},{7,3},{8,12},{12,8},{9,1... | collective-permute-start | bytes 786440 | tf_op jit(solution)/shard_map/ppermute | solution.py:46
  (111 other events, 1496.2 us)
Sparse Core Ops, SparseCore 0:
  12.6 106.1 all-gather.2
  157.7 135.1 reduce-scatter.2
  645.0 107.5 all-gather.4
  809.8 112.6 reduce-scatter.4

commit v2 on v1

v2 whole, which is shorter than its diff:
```python
import functools

import jax
import jax.numpy as jnp
from jax import lax
from jax.experimental import pallas as pl
from jax.experimental.pallas import tpu as pltpu
from jax.sharding import Mesh, PartitionSpec as P

HEAD = 64
EPSILON = 1e-05
MASKED = -1e30
SQRT_HALF = 0.7071067811865476
NORMAL_PEAK = 0.3989422804014327

AXES = ("x", "c", "zh", "zl", "y")
ROWS = ("x", "c")
SEQ = ("zh", "zl", "y")
FFN_GROUP = ("y", "c", "zl")
FFN_DIMS = ("c", "zl", "y")
FFN_NEAR = ("y", "zl", "c")
BF = jnp.bfloat16
F32 = jnp.float32


def dot(left, right, left_dim=1, right_dim=0):
    return lax.dot_general(
        left, right, (((left_dim,), (right_dim,)), ((), ())), preferred_element_type=F32
    )


def normalize(inputs):
    average = jnp.mean(inputs, axis=-1, keepdims=True)
    centred = inputs - average
    inverse = lax.rsqrt(jnp.mean(centred * centred, axis=-1, keepdims=True) + EPSILON)
    return centred * inverse, inverse


def normalize_back(upstream, scaling, standard, inverse):
    scaled = upstream * scaling
    return inverse * (
        scaled
        - jnp.mean(scaled, axis=-1, keepdims=True)
        - standard * jnp.mean(scaled * standard, axis=-1, keepdims=True)
    )


def swap(array, axis):
    return lax.ppermute(array, axis, [(0, 1), (1, 0)])


def pair(mine, theirs, axis, dim):
    first = lax.axis_index(axis) == 0
    return jnp.concatenate(
        [jnp.where(first, mine, theirs), jnp.where(first, theirs, mine)], axis=dim
    )


def halves(array, axis, dim):
    half = array.shape[dim] // 2
    place = lax.axis_index(axis)
    return (
        lax.dynamic_slice_in_dim(array, place * half, half, dim),
        lax.dynamic_slice_in_dim(array, (1 - place) * half, half, dim),
    )


def together(*transfers):
    results = [None] * len(transfers)
    flying = {}

    def advance(place, sent):
        try:
            flying[place] = transfers[place].send(sent)
        except StopIteration as end:
            flying.pop(place, None)
            results[place] = end.value

    for place in range(len(transfers)):
        advance(place, None)
    while flying:
        for place, landed in lax.optimization_barrier(dict(flying)).items():
            advance(place, landed)
    return results


def tie(*arrays):
    return lax.optimization_barrier(arrays)


def pause(rounds, transfer):
    for _ in range(rounds):
        yield ()
    return (yield from transfer)


def gather_dim(array, axis, dim):
    if lax.axis_size(axis) != 2:
        return lax.all_gather(array, axis, axis=dim, tiled=True)
    theirs = yield swap(array, axis)
    return pair(array, theirs, axis, dim)


def scatter_dim(array, axis, dim):
    if lax.axis_size(axis) != 2:
        return lax.psum_scatter(array, axis, scatter_dimension=dim, tiled=True)
    mine, theirs = halves(array, axis, dim)
    theirs = yield swap(theirs, axis)
    return mine + theirs


def exchange(array, axis, cut, joined):
    if lax.axis_size(axis) != 2:
        return lax.all_to_all(array, axis, cut, joined, tiled=True)
    mine, theirs = halves(array, axis, cut)
    theirs = yield swap(theirs, axis)
    return pair(mine, theirs, axis, joined)


def gather_plane(array, first, second, last):
    cut = -(-array.shape[0] // 32) * 16
    by_first, by_second, near = yield (swap(array, first), swap(array, second), swap(array, last))
    low, high, near_first, near_second = yield (
        swap(by_second[:cut], first),
        swap(by_first[cut:], second),
        swap(by_first, last),
        swap(by_second, last),
    )
    both = jnp.concatenate([low, high], axis=0)
    near_both = yield swap(both, last)
    return jnp.concatenate(
        [array, by_first, by_second, both, near, near_first, near_second, near_both], axis=0
    )


def scatter_plane(array, first, second, last):
    half, rows = array.shape[0] // 2, array.shape[0] // 8
    cut = -(-rows // 32) * 16
    theirs = yield swap(array[half:], last)
    array = array[:half] + theirs
    here, by_first, by_second, both = (array[i * rows : (i + 1) * rows] for i in range(4))
    low, high = yield (swap(both[:cut], first), swap(both[cut:], second))
    by_second = jnp.concatenate([by_second[:cut] + low, by_second[cut:]], axis=0)
    by_first = jnp.concatenate([by_first[:cut], by_first[cut:] + high], axis=0)
    by_first, by_second = yield (swap(by_first, first), swap(by_second, second))
    return here + by_first + by_second


def ring_size():
    return 4 if lax.axis_size("zh") == 2 else 0


def ring_shift(array, step):
    return lax.ppermute(array, ("zh", "zl"), [(i, (i + step) % 4) for i in range(4)])


def gather_ring(array):
    if not ring_size():
        return [lax.all_gather(array, SEQ, axis=0, tiled=True)]
    along, across = [array], []
    for step in range(3):
        coming = ring_shift(along[-1], 1)
        across.append(swap(along[-1], "y"))
        if step == 0:
            coming = yield coming
        else:
            coming, across[step - 1] = yield (coming, across[step - 1])
        along.append(coming)
    across.append(swap(along[-1], "y"))
    across[2], across[3] = yield (across[2], across[3])
    return [jnp.concatenate(blocks, axis=0) for blocks in zip(along, across)]


def scatter_ring(blocks):
    if not ring_size():
        return lax.psum_scatter(blocks[0], SEQ, scatter_dimension=0, tiled=True)
    half = blocks[0].shape[0] // 2
    across = swap(blocks[3][half:], "y")
    later = swap(blocks[2][half:], "y")
    across = yield across
    running = blocks[3][:half] + across
    for step in (2, 1, 0):
        across = later
        coming = ring_shift(running, -1)
        if step:
            later = swap(blocks[step - 1][half:], "y")
        coming, across = yield (coming, across)
        running = blocks[step][:half] + across + coming
    return running


def ring_order(shards):
    places = jnp.arange(shards, dtype=jnp.int32)
    if not ring_size():
        return places
    along = lax.axis_index(("zh", "zl"))
    return (along - places // 2) % 4 * 2 + (places % 2 ^ lax.axis_index("y"))


def columns_of_qkv(weights):
    array = weights.reshape((1,) * 5 + weights.shape)
    for axis in SEQ:
        array = yield from exchange(array, axis, 6, AXES.index(axis))
    for axis in ROWS:
        array = yield from gather_dim(array, axis, AXES.index(axis))
    return array.reshape(-1, array.shape[-1])


def sums_of_qkv(sums):
    sizes = tuple(lax.axis_size(axis) for axis in AXES)
    array = sums.reshape(sizes + (-1, sums.shape[1]))
    for axis in reversed(ROWS):
        array = yield from scatter_dim(array, axis, AXES.index(axis))
    for axis in reversed(SEQ):
        array = yield from exchange(array, axis, AXES.index(axis), 6)
    return array.reshape(array.shape[-2:])


def columns_of_ffn(weights):
    array = weights.reshape((weights.shape[0], 1, 1, 1) + weights.shape[1:])
    for axis in FFN_GROUP:
        array = yield from exchange(array, axis, 5, FFN_DIMS.index(axis) + 1)
    return array.reshape(weights.shape[0], -1, array.shape[-1])


def sums_of_ffn(sums):
    sizes = tuple(lax.axis_size(axis) for axis in FFN_DIMS)
    array = sums.reshape((sums.shape[0],) + sizes + (-1, sums.shape[-1]))
    for axis in reversed(FFN_GROUP):
        array = yield from exchange(array, axis, FFN_DIMS.index(axis) + 1, 5)
    return array.reshape(array.shape[0], array.shape[-2], array.shape[-1])


def gather_bulk(array):
    return lax.all_gather(array, "zh", axis=0, tiled=True)


def scatter_bulk(array):
    return lax.psum_scatter(array, "zh", scatter_dimension=0, tiled=True)


def columns_over_x(array, rounds):
    cols = array.shape[-1]
    split = array.reshape(lax.axis_size("zh"), lax.axis_size("c"), -1, cols)
    theirs = swap(array, "x")
    for _ in range(rounds):
        yield ()
    theirs = (yield theirs).reshape(split.shape)
    whole = pair(split.swapaxes(0, 1)[None], theirs.swapaxes(0, 1)[None], "x", 0)
    return whole.reshape(-1, cols)


def sums_over_x(sums, rounds):
    cols = sums.shape[-1]
    split = sums.reshape(2, lax.axis_size("c"), lax.axis_size("zh"), -1, cols)
    mine, theirs = (half[0].swapaxes(0, 1).reshape(-1, cols) for half in halves(split, "x", 0))
    theirs = swap(theirs, "x")
    for _ in range(rounds):
        yield ()
    theirs = yield theirs
    return mine + theirs


def block_mask(col_ref, row_ref, sum_ref, first, rows, keys, segment, per_seg):
    query_docs = col_ref[0, first : first + rows, :]
    query_pos = first + lax.broadcasted_iota(jnp.int32, (rows, keys), 0)
    key_pos = lax.broadcasted_iota(jnp.int32, (rows, keys), 1)
    allowed = (key_pos <= query_pos) & (query_docs == row_ref[0, :, :keys])
    padded = sum_ref.shape[-1]
    place = lax.broadcasted_iota(jnp.int32, (rows, padded), 1)
    sum_allowed = (place < segment * per_seg) & (query_docs == sum_ref[...])
    return allowed, sum_allowed


def block_probs(query, key, sum_key, allowed, sum_allowed):
    scores = jnp.where(allowed, dot(query, key, 1, 1), MASKED)
    sum_scores = jnp.where(sum_allowed, dot(query, sum_key, 1, 1), MASKED)
    top = jnp.maximum(
        jnp.max(scores, axis=1, keepdims=True), jnp.max(sum_scores, axis=1, keepdims=True)
    )
    weights = jnp.exp(scores - top)
    sum_weights = jnp.exp(sum_scores - top)
    total = jnp.sum(weights, axis=1, keepdims=True) + jnp.sum(sum_weights, axis=1, keepdims=True)
    share = 1.0 / total
    return weights * share, sum_weights * share


def load_ordered(order_ref, refs, scratches):
    shards, _, here, _ = refs[0].shape
    for place in range(shards):
        block = order_ref[place]
        for ref, scratch in zip(refs, scratches):
            scratch[place * here : (place + 1) * here, :] = ref[block, 0]


def store_ordered(order_ref, refs, scratches):
    shards, _, here, _ = refs[0].shape
    for place in range(shards):
        block = order_ref[place]
        for ref, scratch in zip(refs, scratches):
            ref[block, 0] = scratch[place * here : (place + 1) * here, :].astype(ref.dtype)


def forward_kernel(
    per_seg, rows, order_ref, col_ref, row_ref, sum_ref, q_in, k_in, v_in, sk_ref, sv_ref, out_ref,
    q_ref, k_ref, v_ref, o_ref,
):
    segment = pl.program_id(1)
    load_ordered(order_ref, (q_in, k_in, v_in), (q_ref, k_ref, v_ref))
    length, width = q_ref.shape
    for first in range(0, length, rows):
        keys = first + rows
        allowed, sum_allowed = block_mask(
            col_ref, row_ref, sum_ref, first, rows, keys, segment, per_seg
        )
        for low in range(0, width, HEAD):
            cols = slice(low, low + HEAD)
            probs, sum_probs = block_probs(
                q_ref[first:keys, cols], k_ref[:keys, cols], sk_ref[:, cols], allowed, sum_allowed
            )
            out = dot(probs.astype(BF), v_ref[:keys, cols])
            out += dot(sum_probs.astype(BF), sv_ref[:, cols])
            o_ref[first:keys, cols] = out.astype(BF)
    store_ordered(order_ref, (out_ref,), (o_ref,))


def backward_kernel(
    per_seg, rows, order_ref, col_ref, row_ref, sum_ref, q_in, k_in, v_in, sk_ref, sv_ref, g_in,
    dq_out, dk_out, dv_out, dsk_ref, dsv_ref,
    q_ref, k_ref, v_ref, g_ref, dq_ref, dk_sum, dv_sum,
):
    segment = pl.program_id(1)
    load_ordered(order_ref, (q_in, k_in, v_in, g_in), (q_ref, k_ref, v_ref, g_ref))
    length, width = q_ref.shape

    @pl.when(segment == 0)
    def _():
        dsk_ref[...] = jnp.zeros_like(dsk_ref)
        dsv_ref[...] = jnp.zeros_like(dsv_ref)

    dk_sum[...] = jnp.zeros_like(dk_sum)
    dv_sum[...] = jnp.zeros_like(dv_sum)
    for first in range(0, length, rows):
        keys = first + rows
        allowed, sum_allowed = block_mask(
            col_ref, row_ref, sum_ref, first, rows, keys, segment, per_seg
        )
        for low in range(0, width, HEAD):
            cols = slice(low, low + HEAD)
            query, grad = q_ref[first:keys, cols], g_ref[first:keys, cols]
            key, sum_key = k_ref[:keys, cols], sk_ref[:, cols]
            probs, sum_probs = block_probs(query, key, sum_key, allowed, sum_allowed)
            d_probs = dot(grad, v_ref[:keys, cols], 1, 1)
            d_sum_probs = dot(grad, sv_ref[:, cols], 1, 1)
            delta = jnp.sum(probs * d_probs, axis=1, keepdims=True)
            delta += jnp.sum(sum_probs * d_sum_probs, axis=1, keepdims=True)
            d_scores = (probs * (d_probs - delta)).astype(BF)
            d_sum_scores = (sum_probs * (d_sum_probs - delta)).astype(BF)
            d_query = (dot(d_scores, key) + dot(d_sum_scores, sum_key)).astype(BF)
            dq_ref[first:keys, cols] = (d_query.astype(F32) * 0.125).astype(BF)
            dk_sum[:keys, cols] += dot(d_scores, query, 0, 0)
            dv_sum[:keys, cols] += dot(probs.astype(BF), grad, 0, 0)
            dsk_ref[:, cols] += dot(d_sum_scores, query, 0, 0)
            dsv_ref[:, cols] += dot(sum_probs.astype(BF), grad, 0, 0)
    store_ordered(order_ref, (dq_out, dk_out, dv_out), (dq_ref, dk_sum, dv_sum))


def attention_calls(segs, shards, here, width, padded, per_seg):
    lanes = min(2 * HEAD, width)
    length = shards * here
    rows = 128 if length <= 512 else 256
    grid = (width // lanes, segs)
    tok = pl.BlockSpec((shards, 1, here, lanes), lambda h, s: (0, s, 0, h))
    summed = pl.BlockSpec((padded, lanes), lambda h, s: (0, h))
    docs = [
        pl.BlockSpec(memory_space=pltpu.SMEM),
        pl.BlockSpec((1, length, 1), lambda h, s: (s, 0, 0)),
        pl.BlockSpec((1, 1, length), lambda h, s: (s, 0, 0)),
        pl.BlockSpec((1, padded), lambda h, s: (0, 0)),
    ]
    params = pltpu.CompilerParams(
        dimension_semantics=("arbitrary", "arbitrary"), vmem_limit_bytes=48 * 2**20
    )
    tokens = jax.ShapeDtypeStruct((shards, segs, here, width), BF)
    sums = jax.ShapeDtypeStruct((padded, width), F32)
    narrow, wide = pltpu.VMEM((length, lanes), BF), pltpu.VMEM((length, lanes), F32)
    work = 2 * segs * length * (length // 2 + padded) * width
    forward = pl.pallas_call(
        functools.partial(forward_kernel, per_seg, rows),
        grid=grid,
        in_specs=docs + [tok] * 3 + [summed] * 2,
        out_specs=tok,
        out_shape=tokens,
        scratch_shapes=[narrow] * 4,
        compiler_params=params,
        cost_estimate=pl.CostEstimate(
            flops=8 * work, bytes_accessed=8 * segs * length * width, transcendentals=0
        ),
    )
    backward = pl.pallas_call(
        functools.partial(backward_kernel, per_seg, rows),
        grid=grid,
        in_specs=docs + [tok] * 3 + [summed] * 2 + [tok],
        out_specs=[tok] * 3 + [summed] * 2,
        out_shape=[tokens] * 3 + [sums] * 2,
        scratch_shapes=[narrow] * 5 + [wide] * 2,
        compiler_params=params,
        cost_estimate=pl.CostEstimate(
            flops=20 * work, bytes_accessed=14 * segs * length * width, transcendentals=0
        ),
    )
    return forward, backward


def gelu_both(inputs):
    share = 0.5 * (1.0 + lax.erf(inputs * SQRT_HALF))
    slope = share + inputs * jnp.exp(-0.5 * inputs * inputs) * NORMAL_PEAK
    return inputs * share, slope


def per_device(
    tokens, summary, doc_ids, gain_attn, gain_ffn, w_query, w_key, w_value, w_out, w_up, w_down,
    cotangent,
):
    _, segs, here, model = tokens.shape
    per_seg = summary.shape[2]
    sum_rows = summary.shape[1] * per_seg
    padded = -(-sum_rows // 128) * 128
    length = doc_ids.shape[2]
    shards = length // here
    rows = segs * here
    shard_rows = w_query.shape[0]
    width = model // shards
    heads_here = width // HEAD

    place = lax.axis_index(SEQ)
    aligned = shard_rows == HEAD

    def by_place(weight):
        return weight.reshape(shard_rows, heads_here, shards, HEAD).swapaxes(1, 2)

    def out_rows():
        if aligned:
            array = w_out
            for axis in reversed(ROWS):
                array = yield from gather_dim(array, axis, 0)
            return array
        whole = lax.all_gather(w_out, AXES, axis=0, tiled=True)
        whole = whole.reshape(heads_here, shards, HEAD, model)
        return lax.dynamic_index_in_dim(whole, place, 1, False).reshape(width, model)

    def out_sums(array):
        if aligned:
            for axis in ROWS:
                array = yield from scatter_dim(array, axis, 0)
            return array
        spread = jnp.zeros((heads_here, shards, HEAD, model), BF)
        spread = lax.dynamic_update_slice_in_dim(
            spread, array.reshape(heads_here, 1, HEAD, model), place, 1
        )
        return lax.psum_scatter(
            spread.reshape(model, model), AXES, scatter_dimension=0, tiled=True
        )

    flat = tokens.reshape(rows, model).astype(F32)
    standard, inverse = normalize(flat)
    hidden = (standard * gain_attn).astype(BF)
    qkv_here = jnp.stack([by_place(w) for w in (w_query, w_key, w_value)], axis=2)
    qkv_here = qkv_here.reshape(shard_rows, 3 * model)
    hidden_blocks, w_qkv, ffn_part = together(
        gather_ring(hidden), columns_of_qkv(qkv_here), columns_of_ffn(jnp.stack([w_up, w_down]))
    )
    w_up_half = gather_bulk(ffn_part[0])
    w_down_half = gather_bulk(ffn_part[1])

    summary_flat = summary.reshape(sum_rows, model).astype(F32)
    summary_pad = jnp.pad(summary_flat, ((0, padded - sum_rows), (0, 0)))
    standard_sum, inverse_sum = normalize(summary_pad)
    hidden_sum = (standard_sum * gain_attn).astype(BF)

    cot = cotangent.reshape(rows, model)
    cot_tied, w_out, _ = tie(cot, w_out, hidden_blocks[-1])
    cot_all, w_out_here = together(gather_plane(cot_tied, *FFN_NEAR), out_rows())
    projected = jnp.concatenate([dot(block, w_qkv) for block in hidden_blocks], axis=0)
    split = (shards, segs, here, width)
    queries = (projected[:, :width] * 0.125).astype(BF).reshape(split)
    keys = projected[:, width : 2 * width].astype(BF).reshape(split)
    values = projected[:, 2 * width :].astype(BF).reshape(split)
    sum_proj = dot(hidden_sum, w_qkv[:, width:]).astype(BF)
    sum_keys, sum_values = sum_proj[:, :width], sum_proj[:, width:]

    docs = doc_ids.reshape(segs, length)
    last_docs = jnp.repeat(docs[: segs - 1, length - 1], per_seg)
    sum_docs = jnp.pad(last_docs, (0, padded - sum_rows), constant_values=-1)[None]
    doc_args = (ring_order(shards), docs[:, :, None], docs[:, None, :], sum_docs)
    attend, attend_back = attention_calls(segs, shards, here, width, padded, per_seg)
    attended = attend(*doc_args, queries, keys, values, sum_keys, sum_values)
    attended = attended.reshape(shards * rows, width)

    block_rows = hidden_blocks[0].shape[0]

    def by_block(array):
        return [array[i : i + block_rows] for i in range(0, shards * rows, block_rows)]

    attended, cot_all, w_out_here = tie(attended, cot_all, w_out_here)
    branch = [dot(block, w_out_here).astype(BF) for block in by_block(attended)]
    summed, w_up_here = together(scatter_ring(branch), columns_over_x(w_up_half, 3))
    mixed = flat + summed.astype(F32)
    standard_ffn, inverse_ffn = normalize(mixed)
    normed = (standard_ffn * gain_ffn).astype(BF)
    normed, w_down_half = tie(normed, w_down_half)
    normed_all, w_down_here = together(
        gather_plane(normed, *FFN_NEAR), columns_over_x(w_down_half, 2)
    )

    active, slope = gelu_both(dot(normed_all, w_up_here))
    active = active.astype(BF)
    grad_active = dot(cot_all, w_down_here)
    grad_upper = (slope * grad_active).astype(BF)
    grad_normed_part = dot(grad_upper, w_up_here, 1, 1).astype(BF)
    d_w_up = dot(normed_all, grad_upper, 0, 0).astype(BF)
    d_w_down = dot(cot_all, active, 0, 0).astype(BF)
    ffn_out_part = dot(active, w_down_here, 1, 1).astype(BF)
    grad_normed, d_w_up = together(
        scatter_plane(grad_normed_part, *FFN_NEAR), sums_over_x(d_w_up, 2)
    )
    d_w_up = scatter_bulk(d_w_up)
    grad_normed = grad_normed.astype(F32)
    grad_mixed = cot.astype(F32) + normalize_back(grad_normed, gain_ffn, standard_ffn, inverse_ffn)
    ffn_gain = jnp.sum(grad_normed * standard_ffn, axis=0)
    grad_branch = grad_mixed.astype(BF)

    grad_branch, d_w_down = tie(grad_branch, d_w_down)
    grad_blocks, d_w_down = together(gather_ring(grad_branch), sums_over_x(d_w_down, 3))
    d_w_down = scatter_bulk(d_w_down)
    ffn_out_part, _ = tie(ffn_out_part, grad_blocks[-1])
    grad_attended = jnp.concatenate(
        [dot(block, w_out_here, 1, 1).astype(BF) for block in grad_blocks], axis=0
    )
    d_queries, d_keys, d_values, d_sum_keys, d_sum_values = attend_back(
        *doc_args, queries, keys, values, sum_keys, sum_values, grad_attended.reshape(split)
    )
    d_out_part = dot(attended, jnp.concatenate(grad_blocks, axis=0), 0, 0).astype(BF)
    ffn_out, d_w_out = together(scatter_plane(ffn_out_part, *FFN_NEAR), out_sums(d_out_part))
    activations = (mixed + ffn_out.astype(F32)).astype(BF)

    d_projected = jnp.concatenate(
        [part.reshape(shards * rows, width) for part in (d_queries, d_keys, d_values)], axis=1
    )
    d_projected, ffn_out = tie(d_projected, ffn_out)
    d_sum_proj = jnp.concatenate([d_sum_keys, d_sum_values], axis=1).astype(BF)
    grad_hidden_blocks = [dot(block, w_qkv, 1, 1).astype(BF) for block in by_block(d_projected)]
    grad_sum_part = dot(d_sum_proj, w_qkv[:, width:], 1, 1).astype(BF)
    left = jnp.concatenate(hidden_blocks + [hidden_sum], axis=0)
    right = jnp.concatenate([d_projected, jnp.pad(d_sum_proj, ((0, 0), (width, 0)))], axis=0)
    d_w_qkv = dot(left, right, 0, 0).astype(BF)

    attn_gain = jnp.sum(grad_sum_part.astype(F32) * hidden_sum.astype(F32), axis=0)
    for grad_block, block in zip(grad_hidden_blocks, hidden_blocks):
        attn_gain += jnp.sum(grad_block.astype(F32) * block.astype(F32), axis=0)
    gains = jnp.stack([attn_gain / gain_attn, ffn_gain])

    per_place = -(-sum_rows // shards)
    held = -(-(per_place + 1) // 16) * 16

    def in_places(array):
        array = jnp.pad(array, ((0, shards * per_place - array.shape[0]), (0, 0)))
        return array.reshape(shards, per_place, model)

    def sum_and_gains():
        by_shard = gains.reshape(2, -1, shards, shard_rows).transpose(2, 0, 1, 3)
        gain_rows = by_shard.reshape(shards, 1, -1).astype(BF)
        gain_cols = gain_rows.shape[-1]
        gain_rows = jnp.pad(gain_rows, ((0, 0), (0, held - per_place - 1), (0, model - gain_cols)))
        array = jnp.concatenate([in_places(grad_sum_part[:sum_rows]), gain_rows], axis=1)
        array = array.reshape(shards * held, model)
        for axis in SEQ:
            array = yield from scatter_dim(array, axis, 0)
        grad_sum = array[:per_place].astype(F32)
        standard_part = lax.dynamic_index_in_dim(in_places(standard_sum[:sum_rows]), place, 0, False)
        inverse_part = jnp.pad(inverse_sum[:sum_rows], ((0, shards * per_place - sum_rows), (0, 0)))
        inverse_part = lax.dynamic_slice_in_dim(inverse_part, place * per_place, per_place, 0)
        part = normalize_back(grad_sum, gain_attn, standard_part, inverse_part).astype(BF)
        part = jnp.pad(part, ((0, held - per_place), (0, 0)))
        both = array[per_place, :gain_cols].astype(F32).reshape(2, -1)
        for axis in ROWS:
            both = yield from scatter_dim(both, axis, 1)
        for axis in reversed(SEQ):
            part = yield from gather_dim(part, axis, 0)
        part = part.reshape(shards, held, model)[:, :per_place].reshape(-1, model)
        return part[:sum_rows].astype(F32), both

    grad_hidden, d_w_qkv, (d_summary, gains), d_ffn = together(
        scatter_ring(grad_hidden_blocks),
        sums_of_qkv(d_w_qkv),
        sum_and_gains(),
        pause(3, sums_of_ffn(jnp.stack([d_w_up, d_w_down]))),
    )
    grad_hidden = grad_hidden.astype(F32)
    d_tokens = grad_mixed + normalize_back(grad_hidden, gain_attn, standard, inverse)
    d_w_qkv = d_w_qkv.reshape(shard_rows, shards, 3, heads_here, HEAD)
    d_w_qkv = d_w_qkv.transpose(2, 0, 3, 1, 4).reshape(3, shard_rows, model).astype(F32)

    return (
        activations.reshape(tokens.shape),
        d_tokens.reshape(tokens.shape),
        d_summary.reshape(summary.shape),
        gains[0],
        gains[1],
        d_w_qkv[0],
        d_w_qkv[1],
        d_w_qkv[2],
        d_w_out.astype(F32),
        d_ffn[0].astype(F32),
        d_ffn[1].astype(F32),
    )


def solution(mesh):
    rows, seq = mesh.shape["rows"], mesh.shape["seq"]
    fine = Mesh(mesh.devices.reshape(rows // 2, 2, seq // 4, 2, 2), AXES)
    by_token = P(ROWS, None, SEQ, None)
    by_row = P(ROWS, None, None, None)
    weight = P(AXES, None)
    return jax.shard_map(
        per_device,
        mesh=fine,
        in_specs=(by_token, by_row, P(ROWS, None, None), P(), P())
        + (weight,) * 6
        + (by_token,),
        out_specs=(by_token, by_token, by_row, P(AXES), P(AXES)) + (weight,) * 6,
        check_vma=False,
    )
```

time: 993 us -> 805 us (0.81)
  waiting for transfers between devices: 675 us -> 431 us
  starting transfers between devices: 50 us -> 82.2 us
  local copies, waits for them, and re-layouts: 51.1 us -> 82.5 us
    ppermute x57 -> x74, waiting for transfers between devices: 614 us -> 358 us  [swap(): return lax.ppermute(array, axis, [(0, 1), (1, 0)])]
    reduce_scatter x2, waiting for transfers between devices: 60.7 us -> 0.01 us  [scatter_bulk(): return lax.psum_scatter(array, 'zh', scatter_dimension=0, tiled=True)]
    ppermute x0 -> x12, waiting for transfers between devices: none -> 41.4 us  [ring_shift(): lax.ppermute(array, ('zh', 'zl'), [(i, (i + step) % 4) for i in range(4)])]
    all_gather x2, waiting for transfers between devices: 0.02 us -> 31.2 us  [gather_bulk(): return lax.all_gather(array, 'zh', axis=0, tiled=True)]
    unnamed x167 -> x245, local copies, waits for them, and re-layouts: 15.8 us -> 37.6 us
    ppermute x57 -> x74, starting transfers between devices: 49.4 us -> 68.7 us  [swap(): return lax.ppermute(array, axis, [(0, 1), (1, 0)])]
    ppermute x0 -> x12, starting transfers between devices: none -> 12.3 us  [ring_shift(): lax.ppermute(array, ('zh', 'zl'), [(i, (i + step) % 4) for i in range(4)])]
    select_n x17 -> x10, other arithmetic: 15.4 us -> 4.04 us  [pair(): jnp.where(first, mine, theirs)]
  transfers between devices with their start and end apart: 61 -> 90, of which waited for: 37 -> 46; matrix products, arithmetic and copies ran while one was open for 14% -> 22% of each run, Pallas kernels for 0% -> 5%
where the time goes in v2:
time: 805 us; the launch traced here: 796 us
  waiting for transfers between devices  431 us (54%)
  local copies, waits for them, and re-layouts  82.5 us (10%)
  starting transfers between devices  82.2 us (10%)
  other arithmetic  72.6 us (9%)
  matrix products  70.3 us (9%)
  Pallas kernels  41.9 us (5%)
  between operations  16.1 us (2%)
    ppermute x74, waiting for transfers between devices, swap(): return lax.ppermute(array, axis, [(0, 1), (1, 0)])  358 us
    dot_general x26, matrix products, dot(): lax.dot_general(left, right, (((left_dim,), (right_dim,)), ((), ())), pre...  70.3 us
    ppermute x74, starting transfers between devices, swap(): return lax.ppermute(array, axis, [(0, 1), (1, 0)])  68.7 us
    ppermute x12, waiting for transfers between devices, ring_shift(): lax.ppermute(array, ('zh', 'zl'), [(i, (i + step) % 4) for i in range(4)])  41.4 us
    unnamed x245, local copies, waits for them, and re-layouts  37.6 us
    all_gather x2, waiting for transfers between devices, gather_bulk(): return lax.all_gather(array, 'zh', axis=0, tiled=True)  31.2 us
    pallas_call x1, Pallas kernels, per_device(): attend_back(*doc_args, queries, keys, values, sum_keys, sum_values, grad_...  25.1 us
    pallas_call x1, Pallas kernels, per_device(): attended = attend(*doc_args, queries, keys, values, sum_keys, sum_values)  16.9 us
  transfers between devices with their start and end apart: 90, of which 46 were waited for; matrix products, arithmetic and copies ran while one was open for 22% of the time, Pallas kernels for 5%

profile of v2, /device:TPU:0, one launch (start us, length us, event | category | flops | bytes accessed | tf_op | source)
XLA Modules:
  0.0 796.4 jit_solution(6719818629719213269)
XLA Ops:
  24.0 24.4 %collective-permute-done.1 = bf16[1,1,1,1,1,64,3072]{6,5,4,3,2,1,0:T(8,128)(2,1)S(1)} collective-permute-done((bf16[1,1,1,1,1,64,3072]{6,5,4,3,2,1,0:T(8,128)(2,1)S(1)}, bf16[1,1,1,1,1,64,3072]{6,5,4,3,2,1,0:T(8,128)(2,1)S(1)}, u32[]{:S(2)}, u32[]{:S(2)}) %collective-permute-start.1) | collective-permute-done | bytes 393248 | tf_op jit(solution)/shard_map/ppermute | solution.py:49
  56.6 18.4 %collective-permute-done.5 = bf16[1,1,2,1,1,64,1536]{6,5,4,3,2,1,0:T(8,128)(2,1)} collective-permute-done((bf16[1,1,2,1,1,64,1536]{6,5,4,3,2,1,0:T(8,128)(2,1)}, bf16[1,1,2,1,1,64,1536]{6,5,4,3,2,1,0:T(8,128)(2,1)}, u32[]{:S(2)}, u32[]{:S(2)}) %collective-permute-start.5) | collective-permute-done | bytes 393248 | tf_op jit(solution)/shard_map/ppermute | solution.py:49
  85.3 13.6 %collective-permute-done.9 = bf16[1,1,2,2,1,64,768]{6,5,4,3,2,1,0:T(8,128)(2,1)S(1)} collective-permute-done((bf16[1,1,2,2,1,64,768]{6,5,4,3,2,1,0:T(8,128)(2,1)S(1)}, bf16[1,1,2,2,1,64,768]{6,5,4,3,2,1,0:T(8,128)(2,1)S(1)}, u32[]{:S(2)}, u32[]{:S(2)}) %collective-permute-start.9) | collective-permute-done | bytes 393248 | tf_op jit(solution)/shard_map/ppermute | solution.py:49
  98.9 17.0 %collective-permute-done.10 = bf16[2,2,1,2,64,1024]{5,4,3,2,1,0:T(8,128)(2,1)S(1)} collective-permute-done((bf16[2,2,1,2,64,1024]{5,4,3,2,1,0:T(8,128)(2,1)S(1)}, bf16[2,2,1,2,64,1024]{5,4,3,2,1,0:T(8,128)(2,1)S(1)}, u32[]{:S(2)}, u32[]{:S(2)}) %collective-permute-start.10) | collective-permute-done | bytes 1048608 | tf_op jit(solution)/shard_map/ppermute | solution.py:49
  122.8 8.2 %collective-permute-done.12 = bf16[144,2048]{1,0:T(8,128)(2,1)S(1)} collective-permute-done((bf16[144,2048]{1,0:T(8,128)(2,1)S(1)}, bf16[144,2048]{1,0:T(8,128)(2,1)S(1)}, u32[]{:S(2)}, u32[]{:S(2)}) %collective-permute-start.12) | collective-permute-done | bytes 589856 | tf_op jit(solution)/shard_map/ppermute | solution.py:49
  144.7 12.2 %collective-permute-done.16 = bf16[144,2048]{1,0:T(8,128)(2,1)S(1)} collective-permute-done((bf16[144,2048]{1,0:T(8,128)(2,1)S(1)}, bf16[144,2048]{1,0:T(8,128)(2,1)S(1)}, u32[]{:S(2)}, u32[]{:S(2)}) %collective-permute-start.16) | collective-permute-done | bytes 589856 | tf_op jit(solution)/shard_map/ppermute | solution.py:49
  163.0 10.3 %collective-permute-done.20 = bf16[64,2048]{1,0:T(8,128)(2,1)S(1)} collective-permute-done((bf16[64,2048]{1,0:T(8,128)(2,1)S(1)}, bf16[64,2048]{1,0:T(8,128)(2,1)S(1)}, u32[]{:S(2)}, u32[]{:S(2)}) %collective-permute-start.20) | collective-permute-done | bytes 262176 | tf_op jit(solution)/shard_map/ppermute | solution.py:49
  188.1 16.9 %shard_map.203 = bf16[8,3,48,256]{3,2,1,0:T(8,128)(2,1)S(1)} custom-call(s32[8]{0:T(128)S(1)} %fusion.109.order_ref, s32[3,384,1]{2,1,0:T(8,128)S(1)} %copy.36.col_ref, s32[3,1,384]{2,1,0:T(1,128)S(1)} %bitcast.188, s32[1,128]{1,0:T(1,128)S(1)} %pad_bitcast_fusion.sum_ref, bf16[8,3,48,256]{3,2,1,0:T(8,128)(2,1)S(1)} %bitcast.177, ...), custom_call_target="tpu_custom_call" | custom-call | flops 1509949440 | bytes 2359296 | tf_op jit(solution)/shard_map/pallas_call | solution.py:497
  211.0 12.7 %collective-permute-done.25 = bf16[144,2048]{1,0:T(8,128)(2,1)S(1)} collective-permute-done((bf16[144,2048]{1,0:T(8,128)(2,1)S(1)}, bf16[144,2048]{1,0:T(8,128)(2,1)S(1)}, u32[]{:S(2)}, u32[]{:S(2)}) %collective-permute-start.25) | collective-permute-done | bytes 589856 | tf_op jit(solution)/shard_map/ppermute | solution.py:49
  227.4 9.1 %collective-permute-done.27 = bf16[144,2048]{1,0:T(8,128)(2,1)} collective-permute-done((bf16[144,2048]{1,0:T(8,128)(2,1)}, bf16[144,2048]{1,0:T(8,128)(2,1)}, u32[]{:S(2)}, u32[]{:S(2)}) %collective-permute-start.27) | collective-permute-done | bytes 589856 | tf_op jit(solution)/shard_map/ppermute | solution.py:49
  260.8 10.1 %collective-permute-done.32 = bf16[1024,1024]{1,0:T(8,128)(2,1)} collective-permute-done((bf16[1024,1024]{1,0:T(8,128)(2,1)}, bf16[1024,1024]{1,0:T(8,128)(2,1)}, u32[]{:S(2)}, u32[]{:S(2)}) %collective-permute-start.32) | collective-permute-done | bytes 2097184 | tf_op jit(solution)/shard_map/ppermute | solution.py:49
  281.2 31.2 %all-gather.5.cloned.1.call-done = bf16[1024,1024]{1,0:T(8,128)(2,1)} async-done(((bf16[512,1024]{1,0:T(8,128)(2,1)}), bf16[1024,1024]{1,0:T(8,128)(2,1)}) %all-gather.5.cloned.1.call-update) | async-done | bytes 2097168 | tf_op jit(solution)/shard_map/all_gather | solution.py:235
  315.8 12.5 %collective-permute-done.34 = bf16[144,2048]{1,0:T(8,128)(2,1)S(1)} collective-permute-done((bf16[144,2048]{1,0:T(8,128)(2,1)}, bf16[144,2048]{1,0:T(8,128)(2,1)S(1)}, u32[]{:S(2)}, u32[]{:S(2)}) %collective-permute-start.34) | collective-permute-done | bytes 589856 | tf_op jit(solution)/shard_map/ppermute | solution.py:49
  343.2 19.5 %collective-permute-done.41 = bf16[1024,1024]{1,0:T(8,128)(2,1)S(1)} collective-permute-done((bf16[1024,1024]{1,0:T(8,128)(2,1)}, bf16[1024,1024]{1,0:T(8,128)(2,1)S(1)}, u32[]{:S(2)}, u32[]{:S(2)}) %collective-permute-start.41) | collective-permute-done | bytes 2097184 | tf_op jit(solution)/shard_map/ppermute | solution.py:49
  366.4 7.0 multiply_convert_fusion
  373.5 6.4 fusion.5
  414.0 37.3 %collective-permute-done.47 = bf16[1024,1024]{1,0:T(8,128)(2,1)S(1)} collective-permute-done((bf16[1024,1024]{1,0:T(8,128)(2,1)S(1)}, bf16[1024,1024]{1,0:T(8,128)(2,1)S(1)}, u32[]{:S(2)}, u32[]{:S(2)}) %collective-permute-start.47) | collective-permute-done | bytes 2097184 | tf_op jit(solution)/shard_map/ppermute | solution.py:49
  462.3 8.7 %collective-permute-done.48 = bf16[144,2048]{1,0:T(8,128)(2,1)S(1)} collective-permute-done((bf16[144,2048]{1,0:T(8,128)(2,1)}, bf16[144,2048]{1,0:T(8,128)(2,1)S(1)}, u32[]{:S(2)}, u32[]{:S(2)}) %collective-permute-start.48) | collective-permute-done | bytes 589856 | tf_op jit(solution)/shard_map/ppermute | solution.py:154
  470.9 6.8 convolution_convert_fusion.1
  497.2 6.8 collective-permute-done.51
  510.3 7.8 collective-permute-done.54
  530.7 25.1 %shard_map.204 = (bf16[8,3,48,256]{3,2,1,0:T(8,128)(2,1)S(1)}, bf16[8,3,48,256]{3,2,1,0:T(8,128)(2,1)S(1)}, bf16[8,3,48,256]{3,2,1,0:T(8,128)(2,1)S(1)}, f32[128,256]{1,0:T(8,128)S(1)}, f32[128,256]{1,0:T(8,128)S(1)}) custom-call(s32[8]{0:T(128)S(1)} %fusion.109.order_ref, s32[3,384,1]{2,1,0:T(8,128)S(1)} %copy.36.col_ref, s32[3,1,384]{2,1,0:T(1,128)S(1)} %bitcast.189, ...), custom_call_target="tpu_custom_call" | custom-call | flops 3774873600 | bytes 4128768 | tf_op jit(solution)/shard_map/pallas_call | solution.py:540
  563.5 7.6 collective-permute-done.59
  578.7 8.8 %collective-permute-done.61 = bf16[144,2048]{1,0:T(8,128)(2,1)} collective-permute-done((bf16[144,2048]{1,0:T(8,128)(2,1)}, bf16[144,2048]{1,0:T(8,128)(2,1)}, u32[]{:S(2)}, u32[]{:S(2)}) %collective-permute-start.61) | collective-permute-done | bytes 589856 | tf_op jit(solution)/shard_map/ppermute | solution.py:49
  619.3 15.1 %collective-permute-done.65 = bf16[64,2048]{1,0:T(8,128)(2,1)} collective-permute-done((bf16[64,2048]{1,0:T(8,128)(2,1)}, bf16[64,2048]{1,0:T(8,128)(2,1)}, u32[]{:S(2)}, u32[]{:S(2)}) %collective-permute-start.65) | collective-permute-done | bytes 262176 | tf_op jit(solution)/shard_map/ppermute | solution.py:49
  646.3 13.3 %collective-permute-done.69 = bf16[32,2048]{1,0:T(8,128)(2,1)S(1)} collective-permute-done((bf16[32,2048]{1,0:T(8,128)(2,1)S(1)}, bf16[32,2048]{1,0:T(8,128)(2,1)S(1)}, u32[]{:S(2)}, u32[]{:S(2)}) %collective-permute-start.69) | collective-permute-done | bytes 131104 | tf_op jit(solution)/shard_map/ppermute | solution.py:49
  688.7 13.2 %collective-permute-done.78 = bf16[2,2,1,2,64,1024]{5,4,3,2,1,0:T(8,128)(2,1)} collective-permute-done((bf16[2,2,1,2,64,1024]{5,4,3,2,1,0:T(8,128)(2,1)}, bf16[2,2,1,2,64,1024]{5,4,3,2,1,0:T(8,128)(2,1)}, u32[]{:S(2)}, u32[]{:S(2)}) %collective-permute-start.78) | collective-permute-done | bytes 1048608 | tf_op jit(solution)/shard_map/ppermute | solution.py:49
  701.9 8.3 %collective-permute-done.76 = bf16[1,1,2,1,1,64,1536]{6,5,4,3,2,1,0:T(8,128)(2,1)S(1)} collective-permute-done((bf16[1,1,2,1,1,64,1536]{6,5,4,3,2,1,0:T(8,128)(2,1)S(1)}, bf16[1,1,2,1,1,64,1536]{6,5,4,3,2,1,0:T(8,128)(2,1)S(1)}, u32[]{:S(2)}, u32[]{:S(2)}) %collective-permute-start.76) | collective-permute-done | bytes 393248 | tf_op jit(solution)/shard_map/ppermute | solution.py:49
  710.3 10.9 %collective-permute-done.74 = bf16[144,2048]{1,0:T(8,128)(2,1)S(1)} collective-permute-done((bf16[144,2048]{1,0:T(8,128)(2,1)S(1)}, bf16[144,2048]{1,0:T(8,128)(2,1)S(1)}, u32[]{:S(2)}, u32[]{:S(2)}) %collective-permute-start.74) | collective-permute-done | bytes 589856 | tf_op jit(solution)/shard_map/ppermute | solution.py:154
  727.5 16.2 %collective-permute-done.80 = bf16[1,1,1,1,1,64,3072]{6,5,4,3,2,1,0:T(8,128)(2,1)S(1)} collective-permute-done((bf16[1,1,1,1,1,64,3072]{6,5,4,3,2,1,0:T(8,128)(2,1)S(1)}, bf16[1,1,1,1,1,64,3072]{6,5,4,3,2,1,0:T(8,128)(2,1)S(1)}, u32[]{:S(2)}, u32[]{:S(2)}) %collective-permute-start.80) | collective-permute-done | bytes 393248 | tf_op jit(solution)/shard_map/ppermute | solution.py:49
  763.6 6.8 collective-permute-done.83
  778.3 9.4 %collective-permute-done.85 = bf16[64,2048]{1,0:T(8,128)(2,1)S(1)} collective-permute-done((bf16[64,2048]{1,0:T(8,128)(2,1)S(1)}, bf16[64,2048]{1,0:T(8,128)(2,1)S(1)}, u32[]{:S(2)}, u32[]{:S(2)}) %collective-permute-start.85) | collective-permute-done | bytes 262176 | tf_op jit(solution)/shard_map/ppermute | solution.py:49
  (622 shorter events, 348.9 us)
Async XLA Ops:
  7.2 217.5 %all-gather.3.cloned.1.call-start = ((), (), s32[]{:S(2)}) async-start(), calls=%async_computation.2 | async-start | bytes 3145728 | tf_op jit(solution)/shard_map/all_gather | solution.py:235
  9.6 38.9 %collective-permute-start.2 = (bf16[2,1,1,1,64,4096]{5,4,3,2,1,0:T(8,128)(2,1)}, bf16[2,1,1,1,64,4096]{5,4,3,2,1,0:T(8,128)(2,1)}, u32[]{:S(2)}, u32[]{:S(2)}) collective-permute-start(bf16[2,1,1,1,64,4096]{5,4,3,2,1,0:T(8,128)(2,1)} %fusion.68), channel_id=1, source_target_pairs={{0,1},{1,0},{2,3},{3,2},{4,5},{5,4},{6,7},{7,6},{8,9},{9,8},{10,11... | collective-permute-start | bytes 3145736 | tf_op jit(solution)/shard_map/ppermute | solution.py:49
  14.5 42.1 %collective-permute-start.4 = (bf16[144,2048]{1,0:T(8,128)(2,1)}, bf16[144,2048]{1,0:T(8,128)(2,1)}, u32[]{:S(2)}, u32[]{:S(2)}) collective-permute-start(bf16[144,2048]{1,0:T(8,128)(2,1)} %get-tuple-element.322), channel_id=1, source_target_pairs={{0,1},{1,0},{2,3},{3,2},{4,5},{5,4},{6,7},{7,6},{8,9},{9,8},{10,11... | collective-permute-start | bytes 1769480 | tf_op jit(solution)/shard_map/ppermute | solution.py:49
  14.5 34.0 %collective-permute-start = (bf16[144,2048]{1,0:T(8,128)(2,1)}, bf16[144,2048]{1,0:T(8,128)(2,1)}, u32[]{:S(2)}, u32[]{:S(2)}) collective-permute-start(bf16[144,2048]{1,0:T(8,128)(2,1)} %get-tuple-element.322), channel_id=1, source_target_pairs={{0,2},{2,4},{4,6},{6,0},{1,3},{3,5},{5,7},{7,1},{8,10},{10,12},{12... | collective-permute-start | bytes 1769480 | tf_op jit(solution)/shard_map/ppermute | solution.py:154
  20.6 27.9 %collective-permute-start.1 = (bf16[1,1,1,1,1,64,3072]{6,5,4,3,2,1,0:T(8,128)(2,1)S(1)}, bf16[1,1,1,1,1,64,3072]{6,5,4,3,2,1,0:T(8,128)(2,1)S(1)}, u32[]{:S(2)}, u32[]{:S(2)}) collective-permute-start(bf16[1,1,1,1,1,64,3072]{6,5,4,3,2,1,0:T(8,128)(2,1)S(1)} %constant_dynamic-slice_fusion.12), channel_id=1, source_target_pairs={{0,4},{4,0},{1,5},{5,1},{2,6},{6,2},{3,7},{7,3},{8,12},{12,8},{9,1... | collective-permute-start | bytes 1179656 | tf_op jit(solution)/shard_map/ppermute | solution.py:49
  49.2 25.8 %collective-permute-start.3 = (bf16[144,2048]{1,0:T(8,128)(2,1)}, bf16[144,2048]{1,0:T(8,128)(2,1)}, u32[]{:S(2)}, u32[]{:S(2)}) collective-permute-start(bf16[144,2048]{1,0:T(8,128)(2,1)} %collective-permute-done), channel_id=1, source_target_pairs={{0,2},{2,4},{4,6},{6,0},{1,3},{3,5},{5,7},{7,1},{8,10},{10,12},{12... | collective-permute-start | bytes 1769480 | tf_op jit(solution)/shard_map/ppermute | solution.py:154
  55.0 30.3 %collective-permute-start.8 = (bf16[144,2048]{1,0:T(8,128)(2,1)}, bf16[144,2048]{1,0:T(8,128)(2,1)S(1)}, u32[]{:S(2)}, u32[]{:S(2)}) collective-permute-start(bf16[144,2048]{1,0:T(8,128)(2,1)} %collective-permute-done), channel_id=1, source_target_pairs={{0,1},{1,0},{2,3},{3,2},{4,5},{5,4},{6,7},{7,6},{8,9},{9,8},{10,11... | collective-permute-start | bytes 1769480 | tf_op jit(solution)/shard_map/ppermute | solution.py:49
  75.0 47.8 %collective-permute-start.11 = (bf16[144,2048]{1,0:T(8,128)(2,1)}, bf16[144,2048]{1,0:T(8,128)(2,1)S(1)}, u32[]{:S(2)}, u32[]{:S(2)}) collective-permute-start(bf16[144,2048]{1,0:T(8,128)(2,1)} %collective-permute-done.3), channel_id=1, source_target_pairs={{0,1},{1,0},{2,3},{3,2},{4,5},{5,4},{6,7},{7,6},{8,9},{9,8},{10,11... | collective-permute-start | bytes 1769480 | tf_op jit(solution)/shard_map/ppermute | solution.py:49
  78.4 37.5 %collective-permute-start.10 = (bf16[2,2,1,2,64,1024]{5,4,3,2,1,0:T(8,128)(2,1)S(1)}, bf16[2,2,1,2,64,1024]{5,4,3,2,1,0:T(8,128)(2,1)S(1)}, u32[]{:S(2)}, u32[]{:S(2)}) collective-permute-start(bf16[2,2,1,2,64,1024]{5,4,3,2,1,0:T(8,128)(2,1)S(1)} %fusion.62), channel_id=1, source_target_pairs={{0,2},{2,0},{1,3},{3,1},{4,6},{6,4},{5,7},{7,5},{8,10},{10,8},{9,1... | collective-permute-start | bytes 3145736 | tf_op jit(solution)/shard_map/ppermute | solution.py:49
  142.9 169.5 %all-gather.5.cloned.1.call-start = ((), (), s32[]{:S(2)}) async-start(), calls=%async_computation.3 | async-start | bytes 3145728 | tf_op jit(solution)/shard_map/all_gather | solution.py:235
  174.2 30.8 %collective-permute-start.24 = (bf16[144,2048]{1,0:T(8,128)(2,1)}, bf16[144,2048]{1,0:T(8,128)(2,1)}, u32[]{:S(2)}, u32[]{:S(2)}) collective-permute-start(bf16[144,2048]{1,0:T(8,128)(2,1)} %pad_maximum_fusion.13), channel_id=1, source_target_pairs={{0,8},{8,0},{1,9},{9,1},{2,10},{10,2},{3,11},{11,3},{4,12},{12,4},... | collective-permute-start | bytes 1769480 | tf_op jit(solution)/shard_map/ppermute | solution.py:49
  210.6 26.0 %collective-permute-start.27 = (bf16[144,2048]{1,0:T(8,128)(2,1)}, bf16[144,2048]{1,0:T(8,128)(2,1)}, u32[]{:S(2)}, u32[]{:S(2)}) collective-permute-start(bf16[144,2048]{1,0:T(8,128)(2,1)} %slice.320), channel_id=1, source_target_pairs={{0,1},{1,0},{2,3},{3,2},{4,5},{5,4},{6,7},{7,6},{8,9},{9,8},{10,11... | collective-permute-start | bytes 1769480 | tf_op jit(solution)/shard_map/ppermute | solution.py:49
  224.7 46.1 %collective-permute-start.32 = (bf16[1024,1024]{1,0:T(8,128)(2,1)}, bf16[1024,1024]{1,0:T(8,128)(2,1)}, u32[]{:S(2)}, u32[]{:S(2)}) collective-permute-start(bf16[1024,1024]{1,0:T(8,128)(2,1)} %all-gather.3.cloned.1.call-done), channel_id=1, source_target_pairs={{0,16},{16,0},{1,17},{17,1},{2,18},{18,2},{3,19},{19,3},{4,20},{20... | collective-permute-start | bytes 6291464 | tf_op jit(solution)/shard_map/ppermute | solution.py:49
  257.4 407.7 %reduce-scatter.3.cloned.1.call-start = ((), (), s32[]{:S(2)}) async-start(), calls=%async_computation.4 | async-start | bytes 3145728 | tf_op jit(solution)/shard_map/reduce_scatter | solution.py:239
  315.2 47.6 %collective-permute-start.41 = (bf16[1024,1024]{1,0:T(8,128)(2,1)}, bf16[1024,1024]{1,0:T(8,128)(2,1)S(1)}, u32[]{:S(2)}, u32[]{:S(2)}) collective-permute-start(bf16[1024,1024]{1,0:T(8,128)(2,1)} %all-gather.5.cloned.1.call-done), channel_id=1, source_target_pairs={{0,16},{16,0},{1,17},{17,1},{2,18},{18,2},{3,19},{19,3},{4,20},{20... | collective-permute-start | bytes 6291464 | tf_op jit(solution)/shard_map/ppermute | solution.py:49
  404.1 47.2 %collective-permute-start.47 = (bf16[1024,1024]{1,0:T(8,128)(2,1)S(1)}, bf16[1024,1024]{1,0:T(8,128)(2,1)S(1)}, u32[]{:S(2)}, u32[]{:S(2)}) collective-permute-start(bf16[1024,1024]{1,0:T(8,128)(2,1)S(1)} %bitcast.230), channel_id=1, source_target_pairs={{0,16},{16,0},{1,17},{17,1},{2,18},{18,2},{3,19},{19,3},{4,20},{20... | collective-permute-start | bytes 6291464 | tf_op jit(solution)/shard_map/ppermute | solution.py:49
  405.8 45.4 %collective-permute-start.45 = (bf16[144,2048]{1,0:T(8,128)(2,1)S(1)}, bf16[144,2048]{1,0:T(8,128)(2,1)S(1)}, u32[]{:S(2)}, u32[]{:S(2)}) collective-permute-start(bf16[144,2048]{1,0:T(8,128)(2,1)S(1)} %pad_maximum_fusion.15), channel_id=1, source_target_pairs={{0,1},{1,0},{2,3},{3,2},{4,5},{5,4},{6,7},{7,6},{8,9},{9,8},{10,11... | collective-permute-start | bytes 1769480 | tf_op jit(solution)/shard_map/ppermute | solution.py:49
  406.5 44.8 %collective-permute-start.46 = (bf16[144,2048]{1,0:T(8,128)(2,1)S(1)}, bf16[144,2048]{1,0:T(8,128)(2,1)S(1)}, u32[]{:S(2)}, u32[]{:S(2)}) collective-permute-start(bf16[144,2048]{1,0:T(8,128)(2,1)S(1)} %pad_maximum_fusion.16), channel_id=1, source_target_pairs={{0,2},{2,0},{1,3},{3,1},{4,6},{6,4},{5,7},{7,5},{8,10},{10,8},{9,1... | collective-permute-start | bytes 1769480 | tf_op jit(solution)/shard_map/ppermute | solution.py:49
  456.8 24.3 %collective-permute-start.50 = (bf16[144,2048]{1,0:T(8,128)(2,1)}, bf16[144,2048]{1,0:T(8,128)(2,1)S(1)}, u32[]{:S(2)}, u32[]{:S(2)}) collective-permute-start(bf16[144,2048]{1,0:T(8,128)(2,1)} %get-tuple-element.156), channel_id=1, source_target_pairs={{0,1},{1,0},{2,3},{3,2},{4,5},{5,4},{6,7},{7,6},{8,9},{9,8},{10,11... | collective-permute-start | bytes 1769480 | tf_op jit(solution)/shard_map/ppermute | solution.py:49
  461.7 48.7 %collective-permute-start.55 = (bf16[1024,1024]{1,0:T(8,128)(2,1)}, bf16[1024,1024]{1,0:T(8,128)(2,1)}, u32[]{:S(2)}, u32[]{:S(2)}) collective-permute-start(bf16[1024,1024]{1,0:T(8,128)(2,1)} %bitcast.43), channel_id=1, source_target_pairs={{0,16},{16,0},{1,17},{17,1},{2,18},{18,2},{3,19},{19,3},{4,20},{20... | collective-permute-start | bytes 6291464 | tf_op jit(solution)/shard_map/ppermute | solution.py:49
  488.1 177.1 %reduce-scatter.5.cloned.1.call-start = ((), (), s32[]{:S(2)}) async-start(), calls=%async_computation.5 | async-start | bytes 3145728 | tf_op jit(solution)/shard_map/reduce_scatter | solution.py:239
  522.7 36.2 %collective-permute-start.56 = (bf16[576,2048]{1,0:T(8,128)(2,1)}, bf16[576,2048]{1,0:T(8,128)(2,1)}, u32[]{:S(2)}, u32[]{:S(2)}) collective-permute-start(bf16[576,2048]{1,0:T(8,128)(2,1)} %slice.274), channel_id=1, source_target_pairs={{0,8},{8,0},{1,9},{9,1},{2,10},{10,2},{3,11},{11,3},{4,12},{12,4},... | collective-permute-start | bytes 7077896 | tf_op jit(solution)/shard_map/ppermute | solution.py:49
  527.3 31.6 %collective-permute-start.57 = (bf16[128,2048]{1,0:T(8,128)(2,1)}, bf16[128,2048]{1,0:T(8,128)(2,1)S(1)}, u32[]{:S(2)}, u32[]{:S(2)}) collective-permute-start(bf16[128,2048]{1,0:T(8,128)(2,1)} %constant_dynamic-slice_fusion.11), channel_id=1, source_target_pairs={{0,16},{16,0},{1,17},{17,1},{2,18},{18,2},{3,19},{19,3},{4,20},{20... | collective-permute-start | bytes 1572872 | tf_op jit(solution)/shard_map/ppermute | solution.py:49
  607.0 27.4 %collective-permute-start.64 = (bf16[2,1,2,2,2,64,768]{6,5,4,3,2,1,0:T(8,128)(2,1)}, bf16[2,1,2,2,2,64,768]{6,5,4,3,2,1,0:T(8,128)(2,1)}, u32[]{:S(2)}, u32[]{:S(2)}) collective-permute-start(bf16[2,1,2,2,2,64,768]{6,5,4,3,2,1,0:T(8,128)(2,1)} %constant_dynamic-slice_fusion.9), channel_id=1, source_target_pairs={{0,8},{8,0},{1,9},{9,1},{2,10},{10,2},{3,11},{11,3},{4,12},{12,4},... | collective-permute-start | bytes 4718600 | tf_op jit(solution)/shard_map/ppermute | solution.py:49
  617.2 29.1 %collective-permute-start.67 = (bf16[144,2048]{1,0:T(8,128)(2,1)S(1)}, bf16[144,2048]{1,0:T(8,128)(2,1)S(1)}, u32[]{:S(2)}, u32[]{:S(2)}) collective-permute-start(bf16[144,2048]{1,0:T(8,128)(2,1)S(1)} %slice.347), channel_id=1, source_target_pairs={{0,1},{1,0},{2,3},{3,2},{4,5},{5,4},{6,7},{7,6},{8,9},{9,8},{10,11... | collective-permute-start | bytes 1769480 | tf_op jit(solution)/shard_map/ppermute | solution.py:49
  644.2 43.0 %collective-permute-start.75 = (bf16[144,2048]{1,0:T(8,128)(2,1)S(1)}, bf16[144,2048]{1,0:T(8,128)(2,1)}, u32[]{:S(2)}, u32[]{:S(2)}) collective-permute-start(bf16[144,2048]{1,0:T(8,128)(2,1)S(1)} %slice.349), channel_id=1, source_target_pairs={{0,1},{1,0},{2,3},{3,2},{4,5},{5,4},{6,7},{7,6},{8,9},{9,8},{10,11... | collective-permute-start | bytes 1769480 | tf_op jit(solution)/shard_map/ppermute | solution.py:49
  646.2 27.0 %collective-permute-start.71 = (bf16[144,2048]{1,0:T(8,128)(2,1)S(1)}, bf16[144,2048]{1,0:T(8,128)(2,1)}, u32[]{:S(2)}, u32[]{:S(2)}) collective-permute-start(bf16[144,2048]{1,0:T(8,128)(2,1)S(1)} %slice.348), channel_id=1, source_target_pairs={{0,1},{1,0},{2,3},{3,2},{4,5},{5,4},{6,7},{7,6},{8,9},{9,8},{10,11... | collective-permute-start | bytes 1769480 | tf_op jit(solution)/shard_map/ppermute | solution.py:49
  673.3 28.7 %collective-permute-start.78 = (bf16[2,2,1,2,64,1024]{5,4,3,2,1,0:T(8,128)(2,1)}, bf16[2,2,1,2,64,1024]{5,4,3,2,1,0:T(8,128)(2,1)}, u32[]{:S(2)}, u32[]{:S(2)}) collective-permute-start(bf16[2,2,1,2,64,1024]{5,4,3,2,1,0:T(8,128)(2,1)} %fusion.60), channel_id=1, source_target_pairs={{0,2},{2,0},{1,3},{3,1},{4,6},{6,4},{5,7},{7,5},{8,10},{10,8},{9,1... | collective-permute-start | bytes 3145736 | tf_op jit(solution)/shard_map/ppermute | solution.py:49
  683.0 27.3 %collective-permute-start.76 = (bf16[1,1,2,1,1,64,1536]{6,5,4,3,2,1,0:T(8,128)(2,1)S(1)}, bf16[1,1,2,1,1,64,1536]{6,5,4,3,2,1,0:T(8,128)(2,1)S(1)}, u32[]{:S(2)}, u32[]{:S(2)}) collective-permute-start(bf16[1,1,2,1,1,64,1536]{6,5,4,3,2,1,0:T(8,128)(2,1)S(1)} %fusion.90), channel_id=1, source_target_pairs={{0,2},{2,0},{1,3},{3,1},{4,6},{6,4},{5,7},{7,5},{8,10},{10,8},{9,1... | collective-permute-start | bytes 1179656 | tf_op jit(solution)/shard_map/ppermute | solution.py:49
  686.3 34.8 %collective-permute-start.74 = (bf16[144,2048]{1,0:T(8,128)(2,1)S(1)}, bf16[144,2048]{1,0:T(8,128)(2,1)S(1)}, u32[]{:S(2)}, u32[]{:S(2)}) collective-permute-start(bf16[144,2048]{1,0:T(8,128)(2,1)S(1)} %fusion.75), channel_id=1, source_target_pairs={{0,6},{2,0},{4,2},{6,4},{1,7},{3,1},{5,3},{7,5},{8,14},{10,8},{12,... | collective-permute-start | bytes 1769480 | tf_op jit(solution)/shard_map/ppermute | solution.py:154
  687.2 76.4 %collective-permute-start.79 = (bf16[16,2048]{1,0:T(8,128)(2,1)S(1)}, bf16[16,2048]{1,0:T(8,128)(2,1)S(1)}, u32[]{:S(2)}, u32[]{:S(2)}) collective-permute-start(bf16[16,2048]{1,0:T(8,128)(2,1)S(1)} %pad.43), channel_id=1, source_target_pairs={{0,1},{1,0},{2,3},{3,2},{4,5},{5,4},{6,7},{7,6},{8,9},{9,8},{10,11... | collective-permute-start | bytes 196616 | tf_op jit(solution)/shard_map/ppermute | solution.py:49
  745.3 25.1 %collective-permute-start.83 = (bf16[2,1,1,1,64,4096]{5,4,3,2,1,0:T(8,128)(2,1)}, bf16[2,1,1,1,64,4096]{5,4,3,2,1,0:T(8,128)(2,1)}, u32[]{:S(2)}, u32[]{:S(2)}) collective-permute-start(bf16[2,1,1,1,64,4096]{5,4,3,2,1,0:T(8,128)(2,1)} %fusion.56), channel_id=1, source_target_pairs={{0,1},{1,0},{2,3},{3,2},{4,5},{5,4},{6,7},{7,6},{8,9},{9,8},{10,11... | collective-permute-start | bytes 3145736 | tf_op jit(solution)/shard_map/ppermute | solution.py:49
  (164 other events, 2294.3 us)
Sparse Core Ops, SparseCore 0:
  143.0 55.2 all-gather.2
  257.6 54.7 all-gather.4
  488.2 58.5 reduce-scatter.2
  578.7 72.9 reduce-scatter.4

commit v3 on v2

v3 whole, which is shorter than its diff:
```python
import functools
import itertools
import math

import jax
import jax.numpy as jnp
from jax import lax
from jax.experimental import pallas as pl
from jax.experimental.pallas import tpu as pltpu
from jax.sharding import Mesh, PartitionSpec as P

HEAD = 64
EPSILON = 1e-05
MASKED = -1e30
SQRT_HALF = 0.7071067811865476
NORMAL_PEAK = 0.3989422804014327

AXES = ("x", "c", "zh", "zl", "y")
ROWS = ("x", "c")
SEQ = ("zh", "zl", "y")
FFN_GROUP = ("y", "c", "zl")
FFN_DIMS = ("c", "zl", "y")
FFN_NEAR = ("y", "zl", "c")
FFN_REST = ("x", "zh")
BF = jnp.bfloat16
F32 = jnp.float32


def dot(left, right, left_dim=1, right_dim=0):
    return lax.dot_general(
        left, right, (((left_dim,), (right_dim,)), ((), ())), preferred_element_type=F32
    )


def normalize(inputs):
    average = jnp.mean(inputs, axis=-1, keepdims=True)
    centred = inputs - average
    inverse = lax.rsqrt(jnp.mean(centred * centred, axis=-1, keepdims=True) + EPSILON)
    return centred * inverse, inverse


def normalize_back(upstream, scaling, standard, inverse):
    scaled = upstream * scaling
    return inverse * (
        scaled
        - jnp.mean(scaled, axis=-1, keepdims=True)
        - standard * jnp.mean(scaled * standard, axis=-1, keepdims=True)
    )


def swap(array, axis):
    return lax.ppermute(array, axis, [(0, 1), (1, 0)])


def pair(mine, theirs, axis, dim):
    first = lax.axis_index(axis) == 0
    return jnp.concatenate(
        [jnp.where(first, mine, theirs), jnp.where(first, theirs, mine)], axis=dim
    )


def halves(array, axis, dim):
    half = array.shape[dim] // 2
    place = lax.axis_index(axis)
    return (
        lax.dynamic_slice_in_dim(array, place * half, half, dim),
        lax.dynamic_slice_in_dim(array, (1 - place) * half, half, dim),
    )


def together(**transfers):
    flying = {}

    def advance(name, sent):
        try:
            with jax.named_scope(name):
                flying[name] = transfers[name].send(sent)
        except StopIteration:
            flying.pop(name, None)

    for name in transfers:
        advance(name, None)
    while flying:
        landed = lax.optimization_barrier(dict(flying))
        for name in transfers:
            if name in landed:
                advance(name, landed[name])


class Box(dict):
    def wait(self, key):
        while key not in self:
            yield ()
        return self[key]

    def put(self, key, transfer):
        self[key] = yield from transfer


def pause(rounds):
    for _ in range(rounds):
        yield ()


def late(rounds, *arrays):
    for _ in range(rounds):
        yield ()
    return (yield arrays)


def in_pieces(array, axis, pieces):
    step = array.shape[0] // pieces
    landed = []
    for piece in range(pieces):
        landed.append((yield swap(array[piece * step : (piece + 1) * step], axis)))
    return jnp.concatenate(landed, axis=0)


def gather_dim(array, axis, dim):
    if lax.axis_size(axis) != 2:
        return lax.all_gather(array, axis, axis=dim, tiled=True)
    theirs = yield swap(array, axis)
    return pair(array, theirs, axis, dim)


def scatter_dim(array, axis, dim):
    if lax.axis_size(axis) != 2:
        return lax.psum_scatter(array, axis, scatter_dimension=dim, tiled=True)
    mine, theirs = halves(array, axis, dim)
    theirs = yield swap(theirs, axis)
    return mine + theirs


def exchange(array, axis, cut, joined, rounds=0):
    if lax.axis_size(axis) != 2:
        return lax.all_to_all(array, axis, cut, joined, tiled=True)
    mine, theirs = halves(array, axis, cut)
    (theirs,) = yield from late(rounds, swap(theirs, axis))
    return pair(mine, theirs, axis, joined)


def gather_plane(array, first, second, last, rounds=0):
    cut = -(-array.shape[0] // 32) * 16
    by_first, by_second = yield from late(rounds, swap(array, first), swap(array, second))
    low, high = yield (swap(by_second[:cut], first), swap(by_first[cut:], second))
    near = jnp.concatenate([array, by_first, by_second, low, high], axis=0)
    far = yield swap(near, last)
    return jnp.concatenate([near, far], axis=0)


def scatter_last(array, last):
    half = array.shape[0] // 2
    theirs = yield swap(array[half:], last)
    return array[:half] + theirs


def scatter_near(array, first, second):
    rows = array.shape[0] // 4
    cut = -(-rows // 32) * 16
    here, by_first, by_second, both = (array[i * rows : (i + 1) * rows] for i in range(4))
    low, high = yield (swap(both[:cut], first), swap(both[cut:], second))
    by_second = jnp.concatenate([by_second[:cut] + low, by_second[cut:]], axis=0)
    by_first = jnp.concatenate([by_first[:cut], by_first[cut:] + high], axis=0)
    by_first, by_second = yield (swap(by_first, first), swap(by_second, second))
    return here + by_first + by_second


def ring_size():
    return 4 if lax.axis_size("zh") == 2 else 0


def ring_shift(array, step):
    return lax.ppermute(array, ("zh", "zl"), [(i, (i + step) % 4) for i in range(4)])


def gather_ring(array):
    if not ring_size():
        return [lax.all_gather(array, SEQ, axis=0, tiled=True)]
    along, across = [array], []
    for step in range(3):
        coming = ring_shift(along[-1], 1)
        across.append(swap(along[-1], "y"))
        if step == 0:
            coming = yield coming
        else:
            coming, across[step - 1] = yield (coming, across[step - 1])
        along.append(coming)
    across.append(swap(along[-1], "y"))
    across[2], across[3] = yield (across[2], across[3])
    return [jnp.concatenate(blocks, axis=0) for blocks in zip(along, across)]


def scatter_ring(blocks):
    if not ring_size():
        return lax.psum_scatter(blocks[0], SEQ, scatter_dimension=0, tiled=True)
    half = blocks[0].shape[0] // 2
    across = swap(blocks[3][half:], "y")
    later = swap(blocks[2][half:], "y")
    across = yield across
    running = blocks[3][:half] + across
    for step in (2, 1, 0):
        across = later
        coming = ring_shift(running, -1)
        if step:
            later = swap(blocks[step - 1][half:], "y")
        coming, across = yield (coming, across)
        running = blocks[step][:half] + across + coming
    return running


def ring_order(shards):
    places = jnp.arange(shards, dtype=jnp.int32)
    if not ring_size():
        return places
    along = lax.axis_index(("zh", "zl"))
    return (along - places // 2) % 4 * 2 + (places % 2 ^ lax.axis_index("y"))


def columns_of_qkv(weights):
    array = weights.reshape((3,) + (1,) * len(AXES) + weights.shape[1:])
    for axis in SEQ:
        array = yield from exchange(array, axis, 7, AXES.index(axis) + 1)
    for axis in ROWS:
        array = yield from gather_dim(array, axis, AXES.index(axis) + 1)
    return array.reshape(3, -1, array.shape[-1])


def sums_of_qkv(sums):
    sizes = tuple(lax.axis_size(axis) for axis in AXES)
    array = sums.reshape((3,) + sizes + (-1, sums.shape[-1]))
    for axis in reversed(ROWS):
        array = yield from scatter_dim(array, axis, AXES.index(axis) + 1)
    for axis in reversed(SEQ):
        array = yield from exchange(array, axis, AXES.index(axis) + 1, 7)
    return array.reshape((3,) + array.shape[-2:])


def columns_of_ffn(weight):
    array = weight.reshape((1, 1, 1) + weight.shape)
    for axis in FFN_GROUP:
        array = yield from exchange(array, axis, 4, FFN_DIMS.index(axis))
    return array.reshape(-1, array.shape[-1])


def sums_of_ffn(sums):
    sizes = tuple(lax.axis_size(axis) for axis in FFN_DIMS)
    array = sums.reshape(sizes + (-1, sums.shape[-1]))
    for axis in reversed(FFN_GROUP):
        array = yield from exchange(array, axis, FFN_DIMS.index(axis), 4)
    return array.reshape(array.shape[-2:])


def near_blocks(array, axes, kept=()):
    sizes = [lax.axis_size(axis) for axis in AXES]
    lead = list(axes) + list(kept)
    depth = max(AXES.index(axis) for axis in lead) + 1
    lanes = array.shape[1] // math.prod(sizes[:depth])
    blocks = []
    for places in itertools.product(*(range(lax.axis_size(axis)) for axis in lead)):
        at = {axis: place for axis, place in zip(lead, places)}
        for axis in axes:
            at[axis] = relative(at[axis], axis)
        first = 0
        for axis, size in zip(AXES[:depth], sizes):
            first = first * size + at[axis]
        blocks.append(lax.dynamic_slice_in_dim(array, first * lanes, lanes, 1))
    return jnp.concatenate(blocks, axis=1)


def relative(place, axis):
    return place if lax.axis_size(axis) != 2 else lax.axis_index(axis) ^ place


def near_blocks_back(array, axes, kept):
    sizes = [lax.axis_size(axis) for axis in AXES]
    lead = list(axes) + list(kept)
    depth = max(AXES.index(axis) for axis in lead) + 1
    lanes = array.shape[1] // math.prod(sizes[:depth])
    blocks = []
    for places in itertools.product(*(range(size) for size in sizes[:depth])):
        at = dict(zip(AXES, places))
        first = 0
        for axis in lead:
            place = relative(at[axis], axis) if axis in axes else at[axis]
            first = first * lax.axis_size(axis) + place
        blocks.append(lax.dynamic_slice_in_dim(array, first * lanes, lanes, 1))
    return jnp.concatenate(blocks, axis=1)


def all_rows(parts):
    if lax.axis_size("zh") != 2:
        parts = [lax.all_gather(part, "zh", axis=0, tiled=True) for part in parts]
    return jnp.concatenate(parts, axis=0)


def part_of(sums, x, zh):
    rows = sums.shape[0] // 4
    first = (2 * x + zh) * rows
    return sums[first : first + rows]


def sums_over_all_zh(sums):
    half = sums.shape[0] // 2
    theirs = yield swap(sums[half:], "x")
    return lax.psum_scatter(sums[:half] + theirs, "zh", scatter_dimension=0, tiled=True)


def block_mask(col_ref, row_ref, sum_ref, first, rows, keys, segment, per_seg):
    query_docs = col_ref[0, first : first + rows, :]
    query_pos = first + lax.broadcasted_iota(jnp.int32, (rows, keys), 0)
    key_pos = lax.broadcasted_iota(jnp.int32, (rows, keys), 1)
    allowed = (key_pos <= query_pos) & (query_docs == row_ref[0, :, :keys])
    padded = sum_ref.shape[-1]
    place = lax.broadcasted_iota(jnp.int32, (rows, padded), 1)
    sum_allowed = (place < segment * per_seg) & (query_docs == sum_ref[...])
    return allowed, sum_allowed


def block_probs(query, key, sum_key, allowed, sum_allowed):
    scores = jnp.where(allowed, dot(query, key, 1, 1), MASKED)
    sum_scores = jnp.where(sum_allowed, dot(query, sum_key, 1, 1), MASKED)
    top = jnp.maximum(
        jnp.max(scores, axis=1, keepdims=True), jnp.max(sum_scores, axis=1, keepdims=True)
    )
    weights = jnp.exp(scores - top)
    sum_weights = jnp.exp(sum_scores - top)
    total = jnp.sum(weights, axis=1, keepdims=True) + jnp.sum(sum_weights, axis=1, keepdims=True)
    share = 1.0 / total
    return weights * share, sum_weights * share


def load_ordered(order_ref, refs, scratches):
    shards, _, here, _ = refs[0].shape
    for place in range(shards):
        block = order_ref[place]
        for ref, scratch in zip(refs, scratches):
            scratch[place * here : (place + 1) * here, :] = ref[block, 0]


def store_ordered(order_ref, refs, scratches):
    shards, _, here, _ = refs[0].shape
    for place in range(shards):
        block = order_ref[place]
        for ref, scratch in zip(refs, scratches):
            ref[block, 0] = scratch[place * here : (place + 1) * here, :].astype(ref.dtype)


def forward_kernel(
    per_seg, rows, order_ref, col_ref, row_ref, sum_ref, q_in, k_in, v_in, sk_ref, sv_ref, out_ref,
    q_ref, k_ref, v_ref, o_ref,
):
    segment = pl.program_id(1)
    load_ordered(order_ref, (q_in, k_in, v_in), (q_ref, k_ref, v_ref))
    length, width = q_ref.shape
    for first in range(0, length, rows):
        keys = first + rows
        allowed, sum_allowed = block_mask(
            col_ref, row_ref, sum_ref, first, rows, keys, segment, per_seg
        )
        for low in range(0, width, HEAD):
            cols = slice(low, low + HEAD)
            probs, sum_probs = block_probs(
                q_ref[first:keys, cols], k_ref[:keys, cols], sk_ref[:, cols], allowed, sum_allowed
            )
            out = dot(probs.astype(BF), v_ref[:keys, cols])
            out += dot(sum_probs.astype(BF), sv_ref[:, cols])
            o_ref[first:keys, cols] = out.astype(BF)
    here = out_ref.shape[2]
    for place in range(out_ref.shape[0]):
        out_ref[place, 0] = o_ref[place * here : (place + 1) * here, :]


def backward_kernel(
    per_seg, rows, order_ref, col_ref, row_ref, sum_ref, q_in, k_in, v_in, sk_ref, sv_ref, g_in,
    dq_out, dk_out, dv_out, dsk_ref, dsv_ref,
    q_ref, k_ref, v_ref, g_ref, dq_ref, dk_sum, dv_sum,
):
    segment = pl.program_id(1)
    load_ordered(order_ref, (q_in, k_in, v_in), (q_ref, k_ref, v_ref))
    here = g_in.shape[2]
    for place in range(g_in.shape[0]):
        g_ref[place * here : (place + 1) * here, :] = g_in[place, 0]
    length, width = q_ref.shape

    @pl.when(segment == 0)
    def _():
        dsk_ref[...] = jnp.zeros_like(dsk_ref)
        dsv_ref[...] = jnp.zeros_like(dsv_ref)

    dk_sum[...] = jnp.zeros_like(dk_sum)
    dv_sum[...] = jnp.zeros_like(dv_sum)
    for first in range(0, length, rows):
        keys = first + rows
        allowed, sum_allowed = block_mask(
            col_ref, row_ref, sum_ref, first, rows, keys, segment, per_seg
        )
        for low in range(0, width, HEAD):
            cols = slice(low, low + HEAD)
            query, grad = q_ref[first:keys, cols], g_ref[first:keys, cols]
            key, sum_key = k_ref[:keys, cols], sk_ref[:, cols]
            probs, sum_probs = block_probs(query, key, sum_key, allowed, sum_allowed)
            d_probs = dot(grad, v_ref[:keys, cols], 1, 1)
            d_sum_probs = dot(grad, sv_ref[:, cols], 1, 1)
            delta = jnp.sum(probs * d_probs, axis=1, keepdims=True)
            delta += jnp.sum(sum_probs * d_sum_probs, axis=1, keepdims=True)
            d_scores = (probs * (d_probs - delta)).astype(BF)
            d_sum_scores = (sum_probs * (d_sum_probs - delta)).astype(BF)
            d_query = (dot(d_scores, key) + dot(d_sum_scores, sum_key)).astype(BF)
            dq_ref[first:keys, cols] = (d_query.astype(F32) * 0.125).astype(BF)
            dk_sum[:keys, cols] += dot(d_scores, query, 0, 0)
            dv_sum[:keys, cols] += dot(probs.astype(BF), grad, 0, 0)
            dsk_ref[:, cols] += dot(d_sum_scores, query, 0, 0)
            dsv_ref[:, cols] += dot(sum_probs.astype(BF), grad, 0, 0)
    store_ordered(order_ref, (dq_out, dk_out, dv_out), (dq_ref, dk_sum, dv_sum))


def attention_calls(segs, shards, here, width, padded, per_seg):
    lanes = min(2 * HEAD, width)
    length = shards * here
    rows = 128 if length <= 512 else 256
    grid = (width // lanes, segs)
    tok = pl.BlockSpec((shards, 1, here, lanes), lambda h, s: (0, s, 0, h))
    summed = pl.BlockSpec((padded, lanes), lambda h, s: (0, h))
    docs = [
        pl.BlockSpec(memory_space=pltpu.SMEM),
        pl.BlockSpec((1, length, 1), lambda h, s: (s, 0, 0)),
        pl.BlockSpec((1, 1, length), lambda h, s: (s, 0, 0)),
        pl.BlockSpec((1, padded), lambda h, s: (0, 0)),
    ]
    params = pltpu.CompilerParams(
        dimension_semantics=("arbitrary", "arbitrary"), vmem_limit_bytes=24 * 2**20
    )
    tokens = jax.ShapeDtypeStruct((shards, segs, here, width), BF)
    sums = jax.ShapeDtypeStruct((padded, width), F32)
    narrow, wide = pltpu.VMEM((length, lanes), BF), pltpu.VMEM((length, lanes), F32)
    work = 2 * segs * length * (length // 2 + padded) * width
    forward = pl.pallas_call(
        functools.partial(forward_kernel, per_seg, rows),
        grid=grid,
        in_specs=docs + [tok] * 3 + [summed] * 2,
        out_specs=tok,
        out_shape=tokens,
        scratch_shapes=[narrow] * 4,
        compiler_params=params,
        cost_estimate=pl.CostEstimate(
            flops=120 * work, bytes_accessed=8 * segs * length * width, transcendentals=0
        ),
    )
    backward = pl.pallas_call(
        functools.partial(backward_kernel, per_seg, rows),
        grid=grid,
        in_specs=docs + [tok] * 3 + [summed] * 2 + [tok],
        out_specs=[tok] * 3 + [summed] * 2,
        out_shape=[tokens] * 3 + [sums] * 2,
        scratch_shapes=[narrow] * 5 + [wide] * 2,
        compiler_params=params,
        cost_estimate=pl.CostEstimate(
            flops=160 * work, bytes_accessed=14 * segs * length * width, transcendentals=0
        ),
    )
    return forward, backward


def gelu_both(inputs):
    share = 0.5 * (1.0 + lax.erf(inputs * SQRT_HALF))
    slope = share + inputs * jnp.exp(-0.5 * inputs * inputs) * NORMAL_PEAK
    return inputs * share, slope


def per_device(
    tokens, summary, doc_ids, gain_attn, gain_ffn, w_query, w_key, w_value, w_out, w_up, w_down,
    cotangent,
):
    _, segs, here, model = tokens.shape
    per_seg = summary.shape[2]
    sum_rows = summary.shape[1] * per_seg
    padded = -(-sum_rows // 128) * 128
    length = doc_ids.shape[2]
    shards = length // here
    rows = segs * here
    shard_rows = w_query.shape[0]
    width = model // shards

    place = lax.axis_index(SEQ)

    flat = tokens.reshape(rows, model).astype(F32)
    standard, inverse = normalize(flat)
    hidden = (standard * gain_attn).astype(BF)
    cot = cotangent.reshape(rows, model)
    summary_flat = summary.reshape(sum_rows, model).astype(F32)
    summary_pad = jnp.pad(summary_flat, ((0, padded - sum_rows), (0, 0)))
    standard_sum, inverse_sum = normalize(summary_pad)
    hidden_sum = (standard_sum * gain_attn).astype(BF)

    docs = doc_ids.reshape(segs, length)
    last_docs = jnp.repeat(docs[: segs - 1, length - 1], per_seg)
    sum_docs = jnp.pad(last_docs, (0, padded - sum_rows), constant_values=-1)[None]
    doc_args = (ring_order(shards), docs[:, :, None], docs[:, None, :], sum_docs)
    attend, attend_back = attention_calls(segs, shards, here, width, padded, per_seg)
    split = (shards, segs, here, width)
    block_rows = shards * rows // max(ring_size(), 1)

    box = Box()
    out = {}

    half_sums = -(-sum_rows // 2)

    def in_halves(array):
        array = jnp.pad(array[:sum_rows], ((0, 2 * half_sums - sum_rows), (0, 0)))
        return array.reshape(2, half_sums, -1)

    def ready_early():
        yield ()
        place_y = lax.axis_index("y")
        sum_parts = [
            lax.dynamic_index_in_dim(in_halves(array), place_y, 0, False)
            for array in (standard_sum, inverse_sum)
        ]
        ready = yield (doc_args, hidden_sum, sum_parts)
        box["doc_args"], box["hidden_sum"], box["sum_parts"] = ready

    def critical():
        hidden_blocks = yield from gather_ring(hidden)
        box["A"] = True
        w_qkv = yield from box.wait("w_qkv")
        doc_args, hidden_sum = box["doc_args"], box["hidden_sum"]
        def project(weight, scale=1.0):
            blocks = [(dot(block, weight) * scale).astype(BF) for block in hidden_blocks]
            return jnp.concatenate(blocks, axis=0).reshape(split)

        operands = [project(w_qkv[0], 0.125), project(w_qkv[1]), project(w_qkv[2])]
        operands += [dot(hidden_sum, w_qkv[1]).astype(BF), dot(hidden_sum, w_qkv[2]).astype(BF)]
        operands = yield operands
        attended = yield attend(*doc_args, *operands)

        box["C"] = True
        attended = attended.reshape(shards, rows, width)
        attended = yield lax.all_to_all(attended, SEQ, 0, 0, tiled=True)
        attended = near_blocks(attended.swapaxes(0, 1).reshape(rows, model), ROWS)
        w_out_all = yield from box.wait("w_out")
        summed = dot(attended, w_out_all)
        mixed = flat + summed
        standard_ffn, inverse_ffn = normalize(mixed)
        normed = near_blocks((standard_ffn * gain_ffn).astype(BF), FFN_REST, ("c",))
        box["D"] = True

        normed_all = yield from gather_plane(normed, *FFN_NEAR)
        cot_all = yield from box.wait("cot_all")
        w_up_here = yield from box.wait("w_up")
        active, slope = gelu_both(dot(normed_all, w_up_here))
        active = active.astype(BF)
        d_w_down = dot(cot_all, active, 0, 0).astype(BF)
        active, slope, d_w_down = yield (active, slope, d_w_down)
        box["d_w_down"] = d_w_down
        w_down_here = yield from box.wait("w_down")
        grad_upper = (slope * dot(cot_all, w_down_here)).astype(BF)
        grad_normed_part = dot(grad_upper, w_up_here, 1, 1).astype(BF)
        scatter = scatter_last(grad_normed_part, FFN_NEAR[2])
        in_flight = next(scatter)
        d_w_up = dot(normed_all, grad_upper, 0, 0).astype(BF)
        in_flight, d_w_up = yield (in_flight, d_w_up)
        box["d_w_up"] = d_w_up
        try:
            scatter.send(in_flight)
        except StopIteration as end:
            near = scatter_near(end.value, *FFN_NEAR[:2])
        in_flight = next(near)
        ffn_out_part = dot(active, w_down_here, 1, 1).astype(BF)
        in_flight, ffn_out_part = yield (in_flight, ffn_out_part)
        box["ffn_out_part"] = ffn_out_part
        in_flight = yield near.send(in_flight)
        try:
            near.send(in_flight)
        except StopIteration as end:
            grad_normed = near_blocks_back(end.value, FFN_REST, ("c",)).astype(F32)
        grad_mixed = cot.astype(F32) + normalize_back(
            grad_normed, gain_ffn, standard_ffn, inverse_ffn
        )

        grad_branch = grad_mixed.astype(BF)
        grad_attended = near_blocks(dot(grad_branch, w_out_all, 1, 1).astype(BF), ROWS)
        grad_attended = grad_attended.reshape(rows, shards, width).swapaxes(0, 1)
        box["d_w_out"] = dot(attended, grad_branch, 0, 0).astype(BF)
        grad_attended = yield lax.all_to_all(grad_attended, SEQ, 0, 0, tiled=True)
        grads = yield attend_back(*doc_args, *operands, grad_attended.reshape(split))

        box["F"] = True
        d_qkv = [part.reshape(shards * rows, width) for part in grads[:3]]
        d_sums = [part.astype(BF) for part in grads[3:]]

        def grad_block(first):
            parts = [dot(d[first : first + block_rows], w, 1, 1) for d, w in zip(d_qkv, w_qkv)]
            return sum(parts).astype(BF)

        grad_hidden_blocks = [grad_block(i) for i in range(0, shards * rows, block_rows)]
        grad_sum_part = sum(dot(d, w, 1, 1) for d, w in zip(d_sums, w_qkv[1:])).astype(BF)
        left = jnp.concatenate(hidden_blocks + [hidden_sum], axis=0)
        d_w_qkv = [dot(left[: shards * rows], d_qkv[0], 0, 0).astype(BF)]
        for d, d_sum in zip(d_qkv[1:], d_sums):
            d_w_qkv.append(dot(left, jnp.concatenate([d, d_sum], axis=0), 0, 0).astype(BF))
        d_w_qkv = jnp.stack(d_w_qkv)
        box["sums"] = grad_sum_part
        scatter = scatter_ring(grad_hidden_blocks)
        try:
            in_flight = next(scatter)
            in_flight, d_w_qkv = yield (in_flight, d_w_qkv)
            box["d_w_qkv"] = d_w_qkv
            while True:
                in_flight = yield scatter.send(in_flight)
        except StopIteration as end:
            grad_hidden = end.value.astype(F32)
        box["d_w_qkv"] = d_w_qkv
        out["d_tokens"] = grad_mixed + normalize_back(grad_hidden, gain_attn, standard, inverse)
        ffn_out = yield from box.wait("ffn_out")
        ffn_out = near_blocks_back(ffn_out, FFN_REST, ("c",))
        out["activations"] = (mixed + ffn_out.astype(F32)).astype(BF)

    def cotangent_rows():
        yield from box.wait("A")
        yield from pause(2)
        box["cot_all"] = yield from gather_plane(near_blocks(cot, FFN_REST, ("c",)), *FFN_NEAR)

    def weight_up():
        part = yield from columns_of_ffn(w_up)
        box["up"] = part
        far = []
        if lax.axis_size("zh") == 2:
            far = [(yield from in_pieces(part, "zh", 4))]
            far.append((yield swap(far[0], "x")))
        part_x = yield from box.wait("up_x")
        box["w_up"] = all_rows([part] + far[:1] + [part_x] + far[1:])

    def weight_up_x():
        part = yield from box.wait("up")
        yield from pause(3)
        box["up_x"] = yield swap(part, "x")

    def weight_down():
        yield from pause(1)
        part = yield from columns_of_ffn(w_down)
        box["down"] = part
        yield from box.wait("C")
        far = far_x = []
        if lax.axis_size("zh") == 2:
            half = part.shape[0] // 2
            step = half // 2
            low = yield swap(part[:half], "zh")
            third = yield swap(part[half : half + step], "zh")
            fourth, low_x = yield (swap(part[half + step :], "zh"), swap(low, "x"))
            high = jnp.concatenate([third, fourth], axis=0)
            yield ()
            high_x = yield swap(high, "x")
            far, far_x = [low, high], [low_x, high_x]
        part_x = yield from box.wait("down_x")
        box["w_down"] = all_rows([part, *far, part_x, *far_x])

    def weight_down_x():
        yield from box.wait("C")
        part = yield from box.wait("down")
        yield from box.put("down_x", in_pieces(part, "x", 2))

    def weight_out():
        yield from pause(2)
        array = w_out.reshape((1,) * len(AXES) + w_out.shape)
        for axis in ("zh", "zl"):
            array = yield from gather_dim(array, axis, AXES.index(axis))
        yield from box.wait("A")
        half = array.shape[-1] // 2
        by_x, by_y = yield (swap(array, "x"), swap(array, "y"))
        low, high = yield (swap(by_y[..., :half], "x"), swap(by_x[..., half:], "y"))
        both = jnp.concatenate([low, high], axis=-1)
        dim_y = AXES.index("y")
        near = pair(array, by_y, "y", dim_y).reshape(-1, model)
        far = pair(by_x, both, "y", dim_y).reshape(-1, model)
        near_c, far_c = yield (swap(near, "c"), swap(far, "c"))
        box["w_out"] = jnp.concatenate([near, near_c, far, far_c], axis=0)

    def out_back():
        array = yield from box.wait("d_w_out")
        rows_c = model // 4
        near, near_c, far, far_c = (array[i * rows_c : (i + 1) * rows_c] for i in range(4))
        near_c, far_c = yield (swap(near_c, "c"), swap(far_c, "c"))
        near, far = near + near_c, far + far_c
        half = rows_c // 2
        low = yield swap(far[:half], "x")
        high = yield swap(far[half:], "x")
        array = near + jnp.concatenate([low, high], axis=0)
        seq_sizes = tuple(lax.axis_size(axis) for axis in SEQ)
        array = array.reshape((1, 1) + seq_sizes + (shard_rows, model))
        yield from pause(3)
        for axis in ("y", "zl", "zh"):
            array = yield from scatter_dim(array, axis, AXES.index(axis))
        out["d_w_out"] = array.reshape(shard_rows, model).astype(F32)

    def down_back():
        sums = yield from box.wait("d_w_down")
        if lax.axis_size("zh") != 2:
            array = yield from sums_over_all_zh(sums)
        else:
            far, sent = part_of(sums, 0, 1), part_of(sums, 1, 1)
            near = part_of(sums, 1, 0)
            half = far.shape[0] // 2
            step = half // 2
            low = (yield swap(sent[:half], "x")) + far[:half]
            first, high = yield (swap(low[:step], "zh"), swap(sent[half:], "x"))
            high = high + far[half:]
            second = yield swap(low[step:], "zh")
            third, near = yield (swap(high, "zh"), swap(near, "x"))
            far = jnp.concatenate([first, second, third], axis=0)
            array = part_of(sums, 0, 0) + near + far
        yield from box.wait("F")
        array = yield from sums_of_ffn(array)
        out["d_w_down"] = array.astype(F32)

    def up_back():
        sums = yield from box.wait("d_w_up")
        if lax.axis_size("zh") != 2:
            array = yield from sums_over_all_zh(sums)
        else:
            far, sent = part_of(sums, 0, 1), part_of(sums, 1, 1)
            near = part_of(sums, 1, 0)
            yield ()
            far = far + (yield from in_pieces(sent, "x", 2))
            half = far.shape[0] // 2
            step = half // 2
            low = yield swap(far[:half], "zh")
            third = yield swap(far[half : half + step], "zh")
            fourth, near = yield (swap(far[half + step :], "zh"), swap(near, "x"))
            far = jnp.concatenate([low, third, fourth], axis=0)
            array = part_of(sums, 0, 0) + near + far
            yield ()
        array = yield from sums_of_ffn(array)
        out["d_w_up"] = array.astype(F32)

    def activations_back():
        part = yield from box.wait("ffn_out_part")
        part = yield from scatter_last(part, FFN_NEAR[2])
        box["ffn_out"] = yield from scatter_near(part, *FFN_NEAR[:2])

    def qkv_back():
        array = yield from box.wait("d_w_qkv")
        array = yield from sums_of_qkv(array)
        array = array.astype(F32)
        out["d_w_query"], out["d_w_key"], out["d_w_value"] = array

    def sums_back():
        grad_sum_part = yield from box.wait("sums")
        yield ()
        array = yield from scatter_dim(in_halves(grad_sum_part), "y", 0)
        for axis in ("zl", "zh"):
            if lax.axis_size(axis) == 2:
                theirs = yield swap(array, axis)
                array = array + theirs
            else:
                array = lax.psum(array, axis)
        grad_sum = array[0].astype(F32)
        standard_part, inverse_part = box["sum_parts"]
        part = normalize_back(grad_sum, gain_attn, standard_part, inverse_part).astype(BF)
        theirs = yield swap(part, "y")
        part = pair(part[None], theirs[None], "y", 0).reshape(2 * half_sums, model)
        out["d_summary"] = part[:sum_rows].astype(F32)

    together(
        critical=critical(),
        ready_early=ready_early(),
        weight_qkv=box.put("w_qkv", columns_of_qkv(jnp.stack([w_query, w_key, w_value]))),
        weight_up=weight_up(),
        weight_up_x=weight_up_x(),
        weight_down=weight_down(),
        weight_down_x=weight_down_x(),
        cotangent_rows=cotangent_rows(),
        weight_out=weight_out(),
        out_back=out_back(),
        down_back=down_back(),
        up_back=up_back(),
        activations_back=activations_back(),
        sums_back=sums_back(),
        qkv_back=qkv_back(),
    )

    def gain_sum(gain, *pairs):
        total = sum(jnp.sum(w.astype(F32) * d, axis=1) for w, d in pairs)
        shard = lax.axis_index(AXES)
        return total / lax.dynamic_slice_in_dim(gain, shard * shard_rows, shard_rows, 0)

    d_gain_attn = gain_sum(
        gain_attn,
        (w_query, out["d_w_query"]),
        (w_key, out["d_w_key"]),
        (w_value, out["d_w_value"]),
    )
    d_gain_ffn = gain_sum(gain_ffn, (w_up, out["d_w_up"]))
    return (
        out["activations"].reshape(tokens.shape),
        out["d_tokens"].reshape(tokens.shape),
        out["d_summary"].reshape(summary.shape),
        d_gain_attn,
        d_gain_ffn,
        out["d_w_query"],
        out["d_w_key"],
        out["d_w_value"],
        out["d_w_out"],
        out["d_w_up"],
        out["d_w_down"],
    )


def solution(mesh):
    rows, seq = mesh.shape["rows"], mesh.shape["seq"]
    fine = Mesh(mesh.devices.reshape(rows // 2, 2, seq // 4, 2, 2), AXES)
    by_token = P(ROWS, None, SEQ, None)
    by_row = P(ROWS, None, None, None)
    weight = P(AXES, None)
    return jax.shard_map(
        per_device,
        mesh=fine,
        in_specs=(by_token, by_row, P(ROWS, None, None), P(), P())
        + (weight,) * 6
        + (by_token,),
        out_specs=(by_token, by_token, by_row, P(AXES), P(AXES)) + (weight,) * 6,
        check_vma=False,
    )
```

time: 805 us -> 688 us (0.85)
  waiting for transfers between devices: 431 us -> 292 us
  starting transfers between devices: 82.2 us -> 120 us
  between operations: 16.1 us -> 3.97 us
    ppermute x74 -> x94, waiting for transfers between devices: 358 us -> 292 us  [swap(): return lax.ppermute(array, axis, [(0, 1), (1, 0)])]
    ppermute x12 -> x6, waiting for transfers between devices: 41.4 us -> 0.13 us  [ring_shift(): lax.ppermute(array, ('zh', 'zl'), [(i, (i + step) % 4) for i in range(4)])]
    ppermute x74 -> x94, starting transfers between devices: 68.7 us -> 102 us  [swap(): return lax.ppermute(array, axis, [(0, 1), (1, 0)])]
    all_gather x2 -> x0, waiting for transfers between devices: 31.2 us -> none  [gather_bulk(): return lax.all_gather(array, 'zh', axis=0, tiled=True)]
    unnamed x245 -> x336, local copies, waits for them, and re-layouts: 37.6 us -> 51.3 us
    add x10 -> x15, other arithmetic: 13 us -> 22.1 us  [the longest x1 3.81 us: out_back(): array = near + jnp.concatenate([low, high], axis=0)]
    dot_general x26 -> x40, matrix products: 70.3 us -> 76.1 us  [dot(): lax.dot_general(left, right, (((left_dim,), (right_dim,)), ((), ())), pre...]
  transfers between devices with their start and end apart: 90 -> 102, of which waited for: 46 -> 36; matrix products, arithmetic and copies ran while one was open for 22% -> 27% of each run, Pallas kernels for 5% -> 6%
where the time goes in v3:
time: 688 us; the launch traced here: 683 us
  waiting for transfers between devices  292 us (42%)
  starting transfers between devices  120 us (17%)
  local copies, waits for them, and re-layouts  79 us (11%)
  matrix products  76.1 us (11%)
  other arithmetic  69.4 us (10%)
  Pallas kernels  42.8 us (6%)
    ppermute x94, waiting for transfers between devices, swap(): return lax.ppermute(array, axis, [(0, 1), (1, 0)])  292 us
    ppermute x94, starting transfers between devices, swap(): return lax.ppermute(array, axis, [(0, 1), (1, 0)])  102 us
    dot_general x40, matrix products, dot(): lax.dot_general(left, right, (((left_dim,), (right_dim,)), ((), ())), pre...  76.1 us
    unnamed x336, local copies, waits for them, and re-layouts  51.3 us
    pallas_call x1, Pallas kernels, critical(): attend_back(*doc_args, *operands, grad_attended.reshape(split))  25.2 us
    pallas_call x1, Pallas kernels, critical(): attended = (yield attend(*doc_args, *operands))  17.6 us
  transfers between devices with their start and end apart: 102, of which 36 were waited for; matrix products, arithmetic and copies ran while one was open for 27% of the time, Pallas kernels for 6%

profile of v3, /device:TPU:0, one launch (start us, length us, event | category | flops | bytes accessed | tf_op | source)
XLA Modules:
  0.0 682.8 jit_solution(12501661034048114264)
XLA Ops:
  31.5 12.0 %collective-permute-done.3 = bf16[3,1,1,1,1,1,64,1024]{7,6,5,4,3,2,1,0:T(8,128)(2,1)S(1)} collective-permute-done((bf16[3,1,1,1,1,1,64,1024]{7,6,5,4,3,2,1,0:T(8,128)(2,1)S(1)}, bf16[3,1,1,1,1,1,64,1024]{7,6,5,4,3,2,1,0:T(8,128)(2,1)S(1)}, u32[]{:S(2)}, u32[]{:S(2)}) %collective-permute-start.3) | collective-permute-done | bytes 393248 | tf_op jit(solution)/shard_map/weight_qkv/ppermute | solution.py:52
  57.4 18.3 %collective-permute-done.8 = bf16[3,1,1,2,1,1,64,512]{7,6,5,4,3,2,1,0:T(8,128)(2,1)} collective-permute-done((bf16[3,1,1,2,1,1,64,512]{7,6,5,4,3,2,1,0:T(8,128)(2,1)}, bf16[3,1,1,2,1,1,64,512]{7,6,5,4,3,2,1,0:T(8,128)(2,1)}, u32[]{:S(2)}, u32[]{:S(2)}) %collective-permute-start.8) | collective-permute-done | bytes 393248 | tf_op jit(solution)/shard_map/weight_qkv/ppermute | solution.py:52
  91.5 5.3 collective-permute-done.14
  96.7 7.8 %collective-permute-done.15 = bf16[2,1,2,64,1024]{4,3,2,1,0:T(8,128)(2,1)S(1)} collective-permute-done((bf16[2,1,2,64,1024]{4,3,2,1,0:T(8,128)(2,1)}, bf16[2,1,2,64,1024]{4,3,2,1,0:T(8,128)(2,1)S(1)}, u32[]{:S(2)}, u32[]{:S(2)}) %collective-permute-start.15) | collective-permute-done | bytes 524320 | tf_op jit(solution)/shard_map/weight_up/ppermute | solution.py:52
  114.9 20.9 %collective-permute-done.21 = bf16[128,1024]{1,0:T(8,128)(2,1)S(1)} collective-permute-done((bf16[128,1024]{1,0:T(8,128)(2,1)S(1)}, bf16[128,1024]{1,0:T(8,128)(2,1)S(1)}, u32[]{:S(2)}, u32[]{:S(2)}) %collective-permute-start.21) | collective-permute-done | bytes 262176 | tf_op jit(solution)/shard_map/weight_up/ppermute | solution.py:52
  153.7 14.5 %collective-permute-done.23 = bf16[1,1,2,2,1,64,2048]{6,5,4,3,2,1,0:T(8,128)(2,1)S(1)} collective-permute-done((bf16[1,1,2,2,1,64,2048]{6,5,4,3,2,1,0:T(8,128)(2,1)S(1)}, bf16[1,1,2,2,1,64,2048]{6,5,4,3,2,1,0:T(8,128)(2,1)S(1)}, u32[]{:S(2)}, u32[]{:S(2)}) %collective-permute-start.23) | collective-permute-done | bytes 1048608 | tf_op jit(solution)/shard_map/weight_out/ppermute | solution.py:52
  183.6 8.1 %collective-permute-done.28 = bf16[1,1,2,2,1,64,1024]{6,5,4,3,2,1,0:T(8,128)(2,1)S(1)} collective-permute-done((bf16[1,1,2,2,1,64,1024]{6,5,4,3,2,1,0:T(8,128)(2,1)S(1)}, bf16[1,1,2,2,1,64,1024]{6,5,4,3,2,1,0:T(8,128)(2,1)S(1)}, u32[]{:S(2)}, u32[]{:S(2)}) %collective-permute-start.28) | collective-permute-done | bytes 524320 | tf_op jit(solution)/shard_map/weight_out/ppermute | solution.py:52
  196.6 14.8 %collective-permute-done.31 = bf16[128,1024]{1,0:T(8,128)(2,1)S(1)} collective-permute-done((bf16[128,1024]{1,0:T(8,128)(2,1)S(1)}, bf16[128,1024]{1,0:T(8,128)(2,1)S(1)}, u32[]{:S(2)}, u32[]{:S(2)}) %collective-permute-start.31) | collective-permute-done | bytes 262176 | tf_op jit(solution)/shard_map/weight_up/ppermute | solution.py:52
  213.8 17.6 %critical.2 = bf16[8,3,48,256]{3,2,1,0:T(8,128)(2,1)} custom-call(s32[8]{0:T(128)S(1)} %fusion.73.order_ref, s32[3,384,1]{2,1,0:T(8,128)S(1)} %copy.33.col_ref, s32[3,1,384]{2,1,0:T(1,128)S(1)} %bitcast.203, s32[1,128]{1,0:T(1,128)S(1)} %pad_bitcast_fusion.sum_ref, bf16[8,3,48,256]{3,2,1,0:T(8,128)(2,1)S(1)} %bitcast.192, ...), custom_call_target="tpu_custom_call" | custom-call | flops 22649241600 | bytes 2359296 | tf_op jit(solution)/shard_map/critical/pallas_call | solution.py:534
  254.6 6.9 %collective-permute-done.38 = bf16[256,1024]{1,0:T(8,128)(2,1)} collective-permute-done((bf16[256,1024]{1,0:T(8,128)(2,1)}, bf16[256,1024]{1,0:T(8,128)(2,1)}, u32[]{:S(2)}, u32[]{:S(2)}) %collective-permute-start.38) | collective-permute-done | bytes 524320 | tf_op jit(solution)/shard_map/weight_down_x/ppermute | solution.py:52
  261.5 27.1 %collective-permute-done.37 = bf16[256,1024]{1,0:T(8,128)(2,1)} collective-permute-done((bf16[256,1024]{1,0:T(8,128)(2,1)}, bf16[256,1024]{1,0:T(8,128)(2,1)}, u32[]{:S(2)}, u32[]{:S(2)}) %collective-permute-start.37) | collective-permute-done | bytes 524320 | tf_op jit(solution)/shard_map/weight_down/ppermute | solution.py:52
  290.4 5.0 fusion.102
  301.4 15.3 %collective-permute-done.40 = bf16[144,2048]{1,0:T(8,128)(2,1)S(1)} collective-permute-done((bf16[144,2048]{1,0:T(8,128)(2,1)S(1)}, bf16[144,2048]{1,0:T(8,128)(2,1)S(1)}, u32[]{:S(2)}, u32[]{:S(2)}) %collective-permute-start.40) | collective-permute-done | bytes 589856 | tf_op jit(solution)/shard_map/critical/ppermute | solution.py:52
  334.9 6.5 fusion.3
  341.5 9.5 %convolution_convert_fusion.4 = bf16[2048,1024]{1,0:T(8,128)(2,1)S(1)} fusion(bf16[1152,2048]{1,0:T(8,128)(2,1)} %copy-done.115, bf16[1152,1024]{1,0:T(8,128)(2,1)S(1)} %get-tuple-element.202), kind=kOutput, calls=%fused_computation.13 | convolution fusion | flops 4833935360 | bytes 11272192 | tf_op jit(solution)/shard_map/critical/dot_general | solution.py:30
  351.0 5.1 fusion.103
  357.5 5.4 convolution_convert_fusion.1
  364.4 13.2 %collective-permute-done.50 = bf16[256,1024]{1,0:T(8,128)(2,1)S(1)} collective-permute-done((bf16[256,1024]{1,0:T(8,128)(2,1)S(1)}, bf16[256,1024]{1,0:T(8,128)(2,1)S(1)}, u32[]{:S(2)}, u32[]{:S(2)}) %collective-permute-start.50) | collective-permute-done | bytes 524320 | tf_op jit(solution)/shard_map/down_back/ppermute | solution.py:52
  381.8 8.5 %convolution_convert_fusion.3 = bf16[2048,1024]{1,0:T(8,128)(2,1)S(1)} fusion(bf16[1152,2048]{1,0:T(8,128)(2,1)} %copy-done.117, bf16[1152,1024]{1,0:T(8,128)(2,1)S(1)} %multiply_convert_fusion), kind=kOutput, calls=%fused_computation.12 | convolution fusion | flops 4833935360 | bytes 11272192 | tf_op jit(solution)/shard_map/critical/dot_general | solution.py:30
  398.8 5.8 convolution_convert_fusion
  417.2 9.6 %collective-permute-done.60 = bf16[512,1024]{1,0:T(8,128)(2,1)S(1)} collective-permute-done((bf16[512,1024]{1,0:T(8,128)(2,1)S(1)}, bf16[512,1024]{1,0:T(8,128)(2,1)S(1)}, u32[]{:S(2)}, u32[]{:S(2)}) %collective-permute-start.60) | collective-permute-done | bytes 1048608 | tf_op jit(solution)/shard_map/down_back/ppermute | solution.py:52
  430.4 6.4 collective-permute-done.59
  473.3 7.9 %collective-permute-done.63 = bf16[64,2048]{1,0:T(8,128)(2,1)S(1)} collective-permute-done((bf16[64,2048]{1,0:T(8,128)(2,1)S(1)}, bf16[64,2048]{1,0:T(8,128)(2,1)S(1)}, u32[]{:S(2)}, u32[]{:S(2)}) %collective-permute-start.63) | collective-permute-done | bytes 262176 | tf_op jit(solution)/shard_map/activations_back/ppermute | solution.py:52
  497.5 25.2 %critical.3 = (bf16[8,3,48,256]{3,2,1,0:T(8,128)(2,1)S(1)}, bf16[8,3,48,256]{3,2,1,0:T(8,128)(2,1)S(1)}, bf16[8,3,48,256]{3,2,1,0:T(8,128)(2,1)S(1)}, f32[128,256]{1,0:T(8,128)S(1)}, f32[128,256]{1,0:T(8,128)S(1)}) custom-call(s32[8]{0:T(128)S(1)} %fusion.73.order_ref, s32[3,384,1]{2,1,0:T(8,128)S(1)} %copy.33.col_ref, s32[3,1,384]{2,1,0:T(1,128)S(1)} %bitcast.204, ...), custom_call_target="tpu_custom_call" | custom-call | flops 30198988800 | bytes 4128768 | tf_op jit(solution)/shard_map/critical/pallas_call | solution.py:585
  563.1 9.2 %collective-permute-done.81 = bf16[512,1024]{1,0:T(8,128)(2,1)S(1)} collective-permute-done((bf16[512,1024]{1,0:T(8,128)(2,1)}, bf16[512,1024]{1,0:T(8,128)(2,1)S(1)}, u32[]{:S(2)}, u32[]{:S(2)}) %collective-permute-start.81) | collective-permute-done | bytes 1048608 | tf_op jit(solution)/shard_map/up_back/ppermute | solution.py:52
  574.2 6.7 collective-permute-done.79
  589.7 7.4 %collective-permute-done.83 = bf16[144,2048]{1,0:T(8,128)(2,1)S(1)} collective-permute-done((bf16[144,2048]{1,0:T(8,128)(2,1)S(1)}, bf16[144,2048]{1,0:T(8,128)(2,1)S(1)}, u32[]{:S(2)}, u32[]{:S(2)}) %collective-permute-start.83) | collective-permute-done | bytes 589856 | tf_op jit(solution)/shard_map/critical/ppermute | solution.py:52
  598.9 7.0 %collective-permute-done.86 = bf16[1,50,2048]{2,1,0:T(8,128)(2,1)S(1)} collective-permute-done((bf16[1,50,2048]{2,1,0:T(8,128)(2,1)S(1)}, bf16[1,50,2048]{2,1,0:T(8,128)(2,1)S(1)}, u32[]{:S(2)}, u32[]{:S(2)}) %collective-permute-start.86) | collective-permute-done | bytes 204832 | tf_op jit(solution)/shard_map/sums_back/ppermute | solution.py:52
  615.2 5.8 collective-permute-done.88
  622.7 6.7 collective-permute-done.89
  634.8 12.6 %collective-permute-done.92 = bf16[1,1,2,2,1,64,2048]{6,5,4,3,2,1,0:T(8,128)(2,1)S(1)} collective-permute-done((bf16[1,1,2,2,1,64,2048]{6,5,4,3,2,1,0:T(8,128)(2,1)S(1)}, bf16[1,1,2,2,1,64,2048]{6,5,4,3,2,1,0:T(8,128)(2,1)S(1)}, u32[]{:S(2)}, u32[]{:S(2)}) %collective-permute-start.92) | collective-permute-done | bytes 1048608 | tf_op jit(solution)/shard_map/out_back/ppermute | solution.py:52
  658.7 12.8 %collective-permute-done.97 = bf16[3,1,1,1,1,1,64,1024]{7,6,5,4,3,2,1,0:T(8,128)(2,1)S(1)} collective-permute-done((bf16[3,1,1,1,1,1,64,1024]{7,6,5,4,3,2,1,0:T(8,128)(2,1)S(1)}, bf16[3,1,1,1,1,1,64,1024]{7,6,5,4,3,2,1,0:T(8,128)(2,1)S(1)}, u32[]{:S(2)}, u32[]{:S(2)}) %collective-permute-start.97) | collective-permute-done | bytes 393248 | tf_op jit(solution)/shard_map/qkv_back/ppermute | solution.py:52
  (744 shorter events, 333.7 us)
Async XLA Ops:
  6.8 50.1 %collective-permute-start.6 = (bf16[144,2048]{1,0:T(8,128)(2,1)}, bf16[144,2048]{1,0:T(8,128)(2,1)}, u32[]{:S(2)}, u32[]{:S(2)}) collective-permute-start(bf16[144,2048]{1,0:T(8,128)(2,1)} %get-tuple-element.487), channel_id=1, source_target_pairs={{0,1},{1,0},{2,3},{3,2},{4,5},{5,4},{6,7},{7,6},{8,9},{9,8},{10,11... | collective-permute-start | bytes 1769480 | tf_op jit(solution)/shard_map/critical/ppermute | solution.py:52
  9.7 33.8 %collective-permute-start.2 = (bf16[144,2048]{1,0:T(8,128)(2,1)}, bf16[144,2048]{1,0:T(8,128)(2,1)}, u32[]{:S(2)}, u32[]{:S(2)}) collective-permute-start(bf16[144,2048]{1,0:T(8,128)(2,1)} %get-tuple-element.487), channel_id=1, source_target_pairs={{0,2},{2,4},{4,6},{6,0},{1,3},{3,5},{5,7},{7,1},{8,10},{10,12},{12... | collective-permute-start | bytes 1769480 | tf_op jit(solution)/shard_map/critical/ppermute | solution.py:173
  12.2 31.3 %collective-permute-start.4 = (bf16[1,1,1,64,4096]{4,3,2,1,0:T(8,128)(2,1)}, bf16[1,1,1,64,4096]{4,3,2,1,0:T(8,128)(2,1)}, u32[]{:S(2)}, u32[]{:S(2)}) collective-permute-start(bf16[1,1,1,64,4096]{4,3,2,1,0:T(8,128)(2,1)} %dynamic-slice_bitcast_fusion.1), channel_id=1, source_target_pairs={{0,1},{1,0},{2,3},{3,2},{4,5},{5,4},{6,7},{7,6},{8,9},{9,8},{10,11... | collective-permute-start | bytes 1572872 | tf_op jit(solution)/shard_map/weight_up/ppermute | solution.py:52
  13.5 39.1 %collective-permute-start.7 = (bf16[1,1,1,64,4096]{4,3,2,1,0:T(8,128)(2,1)}, bf16[1,1,1,64,4096]{4,3,2,1,0:T(8,128)(2,1)}, u32[]{:S(2)}, u32[]{:S(2)}) collective-permute-start(bf16[1,1,1,64,4096]{4,3,2,1,0:T(8,128)(2,1)} %dynamic-slice_bitcast_fusion), channel_id=1, source_target_pairs={{0,1},{1,0},{2,3},{3,2},{4,5},{5,4},{6,7},{7,6},{8,9},{9,8},{10,11... | collective-permute-start | bytes 1572872 | tf_op jit(solution)/shard_map/weight_down/ppermute | solution.py:52
  44.2 31.4 %collective-permute-start.5 = (bf16[144,2048]{1,0:T(8,128)(2,1)}, bf16[144,2048]{1,0:T(8,128)(2,1)}, u32[]{:S(2)}, u32[]{:S(2)}) collective-permute-start(bf16[144,2048]{1,0:T(8,128)(2,1)} %collective-permute-done.2), channel_id=1, source_target_pairs={{0,2},{2,4},{4,6},{6,0},{1,3},{3,5},{5,7},{7,1},{8,10},{10,12},{12... | collective-permute-start | bytes 1769480 | tf_op jit(solution)/shard_map/critical/ppermute | solution.py:173
  46.5 29.1 %collective-permute-start.9 = (bf16[1,1,2,64,2048]{4,3,2,1,0:T(8,128)(2,1)}, bf16[1,1,2,64,2048]{4,3,2,1,0:T(8,128)(2,1)}, u32[]{:S(2)}, u32[]{:S(2)}) collective-permute-start(bf16[1,1,2,64,2048]{4,3,2,1,0:T(8,128)(2,1)} %fusion.52), channel_id=1, source_target_pairs={{0,8},{8,0},{1,9},{9,1},{2,10},{10,2},{3,11},{11,3},{4,12},{12,4},... | collective-permute-start | bytes 1572872 | tf_op jit(solution)/shard_map/weight_up/ppermute | solution.py:52
  52.6 31.9 %collective-permute-start.13 = (bf16[1,1,1,1,1,64,2048]{6,5,4,3,2,1,0:T(8,128)(2,1)S(1)}, bf16[1,1,1,1,1,64,2048]{6,5,4,3,2,1,0:T(8,128)(2,1)S(1)}, u32[]{:S(2)}, u32[]{:S(2)}) collective-permute-start(bf16[1,1,1,1,1,64,2048]{6,5,4,3,2,1,0:T(8,128)(2,1)S(1)} %bitcast.289), channel_id=1, source_target_pairs={{0,4},{4,0},{1,5},{5,1},{2,6},{6,2},{3,7},{7,3},{8,12},{12,8},{9,1... | collective-permute-start | bytes 786440 | tf_op jit(solution)/shard_map/weight_out/ppermute | solution.py:52
  56.9 33.2 %collective-permute-start.11 = (bf16[144,2048]{1,0:T(8,128)(2,1)}, bf16[144,2048]{1,0:T(8,128)(2,1)}, u32[]{:S(2)}, u32[]{:S(2)}) collective-permute-start(bf16[144,2048]{1,0:T(8,128)(2,1)} %collective-permute-done.2), channel_id=1, source_target_pairs={{0,1},{1,0},{2,3},{3,2},{4,5},{5,4},{6,7},{7,6},{8,9},{9,8},{10,11... | collective-permute-start | bytes 1769480 | tf_op jit(solution)/shard_map/critical/ppermute | solution.py:52
  107.2 28.7 %collective-permute-start.19 = (bf16[1,1,2,1,1,64,2048]{6,5,4,3,2,1,0:T(8,128)(2,1)S(1)}, bf16[1,1,2,1,1,64,2048]{6,5,4,3,2,1,0:T(8,128)(2,1)S(1)}, u32[]{:S(2)}, u32[]{:S(2)}) collective-permute-start(bf16[1,1,2,1,1,64,2048]{6,5,4,3,2,1,0:T(8,128)(2,1)S(1)} %pad_maximum_fusion.24), channel_id=1, source_target_pairs={{0,2},{2,0},{1,3},{3,1},{4,6},{6,4},{5,7},{7,5},{8,10},{10,8},{9,1... | collective-permute-start | bytes 1572872 | tf_op jit(solution)/shard_map/weight_out/ppermute | solution.py:52
  107.3 33.6 %collective-permute-start.18 = (bf16[2,1,2,64,1024]{4,3,2,1,0:T(8,128)(2,1)S(1)}, bf16[2,1,2,64,1024]{4,3,2,1,0:T(8,128)(2,1)S(1)}, u32[]{:S(2)}, u32[]{:S(2)}) collective-permute-start(bf16[2,1,2,64,1024]{4,3,2,1,0:T(8,128)(2,1)S(1)} %fusion.46), channel_id=1, source_target_pairs={{0,2},{2,0},{1,3},{3,1},{4,6},{6,4},{5,7},{7,5},{8,10},{10,8},{9,1... | collective-permute-start | bytes 1572872 | tf_op jit(solution)/shard_map/weight_down/ppermute | solution.py:52
  109.4 31.5 %collective-permute-start.17 = (bf16[144,2048]{1,0:T(8,128)(2,1)}, bf16[144,2048]{1,0:T(8,128)(2,1)S(1)}, u32[]{:S(2)}, u32[]{:S(2)}) collective-permute-start(bf16[144,2048]{1,0:T(8,128)(2,1)} %collective-permute-done.10), channel_id=1, source_target_pairs={{0,1},{1,0},{2,3},{3,2},{4,5},{5,4},{6,7},{7,6},{8,9},{9,8},{10,11... | collective-permute-start | bytes 1769480 | tf_op jit(solution)/shard_map/critical/ppermute | solution.py:52
  110.2 31.5 %collective-permute-start.20 = (bf16[3,1,1,2,2,2,64,256]{7,6,5,4,3,2,1,0:T(8,128)(2,1)S(1)}, bf16[3,1,1,2,2,2,64,256]{7,6,5,4,3,2,1,0:T(8,128)(2,1)S(1)}, u32[]{:S(2)}, u32[]{:S(2)}) collective-permute-start(bf16[3,1,1,2,2,2,64,256]{7,6,5,4,3,2,1,0:T(8,128)(2,1)S(1)} %pad_maximum_fusion.14), channel_id=1, source_target_pairs={{0,16},{16,0},{1,17},{17,1},{2,18},{18,2},{3,19},{19,3},{4,20},{20... | collective-permute-start | bytes 2359304 | tf_op jit(solution)/shard_map/weight_qkv/ppermute | solution.py:52
  135.9 60.3 %collective-permute-start.1 = (bf16[144,2048]{1,0:T(8,128)(2,1)S(1)}, bf16[144,2048]{1,0:T(8,128)(2,1)S(1)}, u32[]{:S(2)}, u32[]{:S(2)}) collective-permute-start(bf16[144,2048]{1,0:T(8,128)(2,1)S(1)} %copy-done.114), channel_id=1, source_target_pairs={{0,2},{2,0},{1,3},{3,1},{4,6},{6,4},{5,7},{7,5},{8,10},{10,8},{9,1... | collective-permute-start | bytes 1769480 | tf_op jit(solution)/shard_map/cotangent_rows/ppermute | solution.py:52
  153.2 43.4 %collective-permute-start = (bf16[144,2048]{1,0:T(8,128)(2,1)S(1)}, bf16[144,2048]{1,0:T(8,128)(2,1)S(1)}, u32[]{:S(2)}, u32[]{:S(2)}) collective-permute-start(bf16[144,2048]{1,0:T(8,128)(2,1)S(1)} %copy-done.114), channel_id=1, source_target_pairs={{0,1},{1,0},{2,3},{3,2},{4,5},{5,4},{6,7},{7,6},{8,9},{9,8},{10,11... | collective-permute-start | bytes 1769480 | tf_op jit(solution)/shard_map/cotangent_rows/ppermute | solution.py:52
  182.1 29.3 %collective-permute-start.32 = (bf16[512,1024]{1,0:T(8,128)(2,1)S(1)}, bf16[512,1024]{1,0:T(8,128)(2,1)S(1)}, u32[]{:S(2)}, u32[]{:S(2)}) collective-permute-start(bf16[512,1024]{1,0:T(8,128)(2,1)S(1)} %bitcast.238), channel_id=1, source_target_pairs={{0,16},{16,0},{1,17},{17,1},{2,18},{18,2},{3,19},{19,3},{4,20},{20... | collective-permute-start | bytes 3145736 | tf_op jit(solution)/shard_map/weight_up_x/ppermute | solution.py:52
  239.1 49.6 %collective-permute-start.36 = (bf16[576,2048]{1,0:T(8,128)(2,1)}, bf16[576,2048]{1,0:T(8,128)(2,1)}, u32[]{:S(2)}, u32[]{:S(2)}) collective-permute-start(bf16[576,2048]{1,0:T(8,128)(2,1)} %get-tuple-element.484), channel_id=1, source_target_pairs={{0,8},{8,0},{1,9},{9,1},{2,10},{10,2},{3,11},{11,3},{4,12},{12,4},... | collective-permute-start | bytes 7077896 | tf_op jit(solution)/shard_map/cotangent_rows/ppermute | solution.py:52
  239.1 49.6 %all-to-all-start = ((bf16[8,144,256]{2,1,0:T(8,128)(2,1)}), bf16[8,144,256]{2,1,0:T(8,128)(2,1)}, u32[]{:S(2)}, u32[]{:S(2)}) async-start(bf16[8,144,256]{2,1,0:T(8,128)(2,1)} %bitcast.26), calls=%async_computation | async-start | bytes 1179648 | tf_op jit(solution)/shard_map/critical/all_to_all | solution.py:538
  248.0 40.7 %collective-permute-start.37 = (bf16[256,1024]{1,0:T(8,128)(2,1)}, bf16[256,1024]{1,0:T(8,128)(2,1)}, u32[]{:S(2)}, u32[]{:S(2)}) collective-permute-start(bf16[256,1024]{1,0:T(8,128)(2,1)} %bitcast.27), channel_id=1, source_target_pairs={{0,4},{4,0},{1,5},{5,1},{2,6},{6,2},{3,7},{7,3},{8,12},{12,8},{9,1... | collective-permute-start | bytes 1572872 | tf_op jit(solution)/shard_map/weight_down/ppermute | solution.py:52
  253.9 45.7 %collective-permute-start.41 = (bf16[128,1024]{1,0:T(8,128)(2,1)}, bf16[128,1024]{1,0:T(8,128)(2,1)S(1)}, u32[]{:S(2)}, u32[]{:S(2)}) collective-permute-start(bf16[128,1024]{1,0:T(8,128)(2,1)} %get-tuple-element.378), channel_id=1, source_target_pairs={{0,4},{4,0},{1,5},{5,1},{2,6},{6,2},{3,7},{7,3},{8,12},{12,8},{9,1... | collective-permute-start | bytes 786440 | tf_op jit(solution)/shard_map/weight_down/ppermute | solution.py:52
  254.0 47.4 %collective-permute-start.42 = (bf16[256,1024]{1,0:T(8,128)(2,1)}, bf16[256,1024]{1,0:T(8,128)(2,1)}, u32[]{:S(2)}, u32[]{:S(2)}) collective-permute-start(bf16[256,1024]{1,0:T(8,128)(2,1)} %bitcast.30), channel_id=1, source_target_pairs={{0,16},{16,0},{1,17},{17,1},{2,18},{18,2},{3,19},{19,3},{4,20},{20... | collective-permute-start | bytes 1572872 | tf_op jit(solution)/shard_map/weight_down_x/ppermute | solution.py:52
  363.2 30.5 %collective-permute-start.49 = (bf16[576,2048]{1,0:T(8,128)(2,1)S(1)}, bf16[576,2048]{1,0:T(8,128)(2,1)S(1)}, u32[]{:S(2)}, u32[]{:S(2)}) collective-permute-start(bf16[576,2048]{1,0:T(8,128)(2,1)S(1)} %slice.442), channel_id=1, source_target_pairs={{0,8},{8,0},{1,9},{9,1},{2,10},{10,2},{3,11},{11,3},{4,12},{12,4},... | collective-permute-start | bytes 7077896 | tf_op jit(solution)/shard_map/critical/ppermute | solution.py:52
  408.4 34.3 %collective-permute-start.56 = (bf16[576,2048]{1,0:T(8,128)(2,1)}, bf16[576,2048]{1,0:T(8,128)(2,1)}, u32[]{:S(2)}, u32[]{:S(2)}) collective-permute-start(bf16[576,2048]{1,0:T(8,128)(2,1)} %slice.362), channel_id=1, source_target_pairs={{0,8},{8,0},{1,9},{9,1},{2,10},{10,2},{3,11},{11,3},{4,12},{12,4},... | collective-permute-start | bytes 7077896 | tf_op jit(solution)/shard_map/activations_back/ppermute | solution.py:52
  436.9 35.9 %collective-permute-start.66 = (bf16[256,1024]{1,0:T(8,128)(2,1)}, bf16[256,1024]{1,0:T(8,128)(2,1)}, u32[]{:S(2)}, u32[]{:S(2)}) collective-permute-start(bf16[256,1024]{1,0:T(8,128)(2,1)} %get-tuple-element.310), channel_id=1, source_target_pairs={{0,16},{16,0},{1,17},{17,1},{2,18},{18,2},{3,19},{19,3},{4,20},{20... | collective-permute-start | bytes 1572872 | tf_op jit(solution)/shard_map/up_back/ppermute | solution.py:52
  472.8 79.0 %collective-permute-start.72 = (bf16[2,1,2,64,1024]{4,3,2,1,0:T(8,128)(2,1)}, bf16[2,1,2,64,1024]{4,3,2,1,0:T(8,128)(2,1)}, u32[]{:S(2)}, u32[]{:S(2)}) collective-permute-start(bf16[2,1,2,64,1024]{4,3,2,1,0:T(8,128)(2,1)} %constant_dynamic-slice_fusion.8), channel_id=1, source_target_pairs={{0,2},{2,0},{1,3},{3,1},{4,6},{6,4},{5,7},{7,5},{8,10},{10,8},{9,1... | collective-permute-start | bytes 1572872 | tf_op jit(solution)/shard_map/down_back/ppermute | solution.py:52
  484.7 40.0 %collective-permute-start.67 = (bf16[144,2048]{1,0:T(8,128)(2,1)S(1)}, bf16[144,2048]{1,0:T(8,128)(2,1)S(1)}, u32[]{:S(2)}, u32[]{:S(2)}) collective-permute-start(bf16[144,2048]{1,0:T(8,128)(2,1)S(1)} %pad_maximum_fusion.22), channel_id=1, source_target_pairs={{0,1},{1,0},{2,3},{3,2},{4,5},{5,4},{6,7},{7,6},{8,9},{9,8},{10,11... | collective-permute-start | bytes 1769480 | tf_op jit(solution)/shard_map/activations_back/ppermute | solution.py:52
  486.3 40.2 %collective-permute-start.68 = (bf16[144,2048]{1,0:T(8,128)(2,1)S(1)}, bf16[144,2048]{1,0:T(8,128)(2,1)S(1)}, u32[]{:S(2)}, u32[]{:S(2)}) collective-permute-start(bf16[144,2048]{1,0:T(8,128)(2,1)S(1)} %pad_maximum_fusion.23), channel_id=1, source_target_pairs={{0,2},{2,0},{1,3},{3,1},{4,6},{6,4},{5,7},{7,5},{8,10},{10,8},{9,1... | collective-permute-start | bytes 1769480 | tf_op jit(solution)/shard_map/activations_back/ppermute | solution.py:52
  490.6 33.0 %collective-permute-start.70 = (bf16[256,1024]{1,0:T(8,128)(2,1)S(1)}, bf16[256,1024]{1,0:T(8,128)(2,1)S(1)}, u32[]{:S(2)}, u32[]{:S(2)}) collective-permute-start(bf16[256,1024]{1,0:T(8,128)(2,1)S(1)} %slice.463), channel_id=1, source_target_pairs={{0,4},{4,0},{1,5},{5,1},{2,6},{6,2},{3,7},{7,3},{8,12},{12,8},{9,1... | collective-permute-start | bytes 1572872 | tf_op jit(solution)/shard_map/up_back/ppermute | solution.py:52
  496.3 31.0 %collective-permute-start.69 = (bf16[256,2048]{1,0:T(8,128)(2,1)S(1)}, bf16[256,2048]{1,0:T(8,128)(2,1)S(1)}, u32[]{:S(2)}, u32[]{:S(2)}) collective-permute-start(bf16[256,2048]{1,0:T(8,128)(2,1)S(1)} %get-tuple-element.328), channel_id=1, source_target_pairs={{0,16},{16,0},{1,17},{17,1},{2,18},{18,2},{3,19},{19,3},{4,20},{20... | collective-permute-start | bytes 3145736 | tf_op jit(solution)/shard_map/out_back/ppermute | solution.py:52
  523.6 34.2 %collective-permute-start.80 = (bf16[128,1024]{1,0:T(8,128)(2,1)}, bf16[128,1024]{1,0:T(8,128)(2,1)}, u32[]{:S(2)}, u32[]{:S(2)}) collective-permute-start(bf16[128,1024]{1,0:T(8,128)(2,1)} %get-tuple-element.375), channel_id=1, source_target_pairs={{0,4},{4,0},{1,5},{5,1},{2,6},{6,2},{3,7},{7,3},{8,12},{12,8},{9,1... | collective-permute-start | bytes 786440 | tf_op jit(solution)/shard_map/up_back/ppermute | solution.py:52
  524.7 28.4 %collective-permute-start.74 = (bf16[128,1024]{1,0:T(8,128)(2,1)}, bf16[128,1024]{1,0:T(8,128)(2,1)}, u32[]{:S(2)}, u32[]{:S(2)}) collective-permute-start(bf16[128,1024]{1,0:T(8,128)(2,1)} %get-tuple-element.376), channel_id=1, source_target_pairs={{0,4},{4,0},{1,5},{5,1},{2,6},{6,2},{3,7},{7,3},{8,12},{12,8},{9,1... | collective-permute-start | bytes 786440 | tf_op jit(solution)/shard_map/up_back/ppermute | solution.py:52
  526.5 28.1 %collective-permute-start.73 = (bf16[256,2048]{1,0:T(8,128)(2,1)}, bf16[256,2048]{1,0:T(8,128)(2,1)}, u32[]{:S(2)}, u32[]{:S(2)}) collective-permute-start(bf16[256,2048]{1,0:T(8,128)(2,1)} %get-tuple-element.327), channel_id=1, source_target_pairs={{0,16},{16,0},{1,17},{17,1},{2,18},{18,2},{3,19},{19,3},{4,20},{20... | collective-permute-start | bytes 3145736 | tf_op jit(solution)/shard_map/out_back/ppermute | solution.py:52
  553.1 29.5 %collective-permute-start.76 = (bf16[144,2048]{1,0:T(8,128)(2,1)S(1)}, bf16[144,2048]{1,0:T(8,128)(2,1)S(1)}, u32[]{:S(2)}, u32[]{:S(2)}) collective-permute-start(bf16[144,2048]{1,0:T(8,128)(2,1)S(1)} %slice.471), channel_id=1, source_target_pairs={{0,1},{1,0},{2,3},{3,2},{4,5},{5,4},{6,7},{7,6},{8,9},{9,8},{10,11... | collective-permute-start | bytes 1769480 | tf_op jit(solution)/shard_map/critical/ppermute | solution.py:52
  (201 other events, 2830.0 us)

commit v4 on v3

--- a/solution.py
+++ b/solution.py
@@ -18,7 +18,7 @@
 AXES = ("x", "c", "zh", "zl", "y")
 ROWS = ("x", "c")
 SEQ = ("zh", "zl", "y")
-FFN_GROUP = ("y", "c", "zl")
+FFN_GROUP = ("c", "y", "zl")
 FFN_DIMS = ("c", "zl", "y")
 FFN_NEAR = ("y", "zl", "c")
 FFN_REST = ("x", "zh")
@@ -102,24 +102,26 @@
         yield ()
 
 
-def late(rounds, *arrays):
-    for _ in range(rounds):
-        yield ()
-    return (yield arrays)
-
-
-def in_pieces(array, axis, pieces):
-    step = array.shape[0] // pieces
-    landed = []
-    for piece in range(pieces):
-        landed.append((yield swap(array[piece * step : (piece + 1) * step], axis)))
-    return jnp.concatenate(landed, axis=0)
+def in_pieces(array, axis, *pieces):
+    first, landed = 0, []
+    for piece in pieces:
+        count = array.shape[0] * piece // sum(pieces)
+        landed.append((yield swap(array[first : first + count], axis)))
+        first += count
+    return landed
+
+
+def one_round(array, axis):
+    theirs = swap(array, axis)
+    if axis != "c":
+        theirs = yield theirs
+    return theirs
 
 
 def gather_dim(array, axis, dim):
     if lax.axis_size(axis) != 2:
         return lax.all_gather(array, axis, axis=dim, tiled=True)
-    theirs = yield swap(array, axis)
+    theirs = yield from one_round(array, axis)
     return pair(array, theirs, axis, dim)
 
 
@@ -127,34 +129,29 @@
     if lax.axis_size(axis) != 2:
         return lax.psum_scatter(array, axis, scatter_dimension=dim, tiled=True)
     mine, theirs = halves(array, axis, dim)
-    theirs = yield swap(theirs, axis)
+    theirs = yield from one_round(theirs, axis)
     return mine + theirs
 
 
-def exchange(array, axis, cut, joined, rounds=0):
+def exchange(array, axis, cut, joined):
     if lax.axis_size(axis) != 2:
         return lax.all_to_all(array, axis, cut, joined, tiled=True)
     mine, theirs = halves(array, axis, cut)
-    (theirs,) = yield from late(rounds, swap(theirs, axis))
+    theirs = yield from one_round(theirs, axis)
     return pair(mine, theirs, axis, joined)
 
 
-def gather_plane(array, first, second, last, rounds=0):
+def gather_plane(array, first, second, last):
     cut = -(-array.shape[0] // 32) * 16
-    by_first, by_second = yield from late(rounds, swap(array, first), swap(array, second))
+    by_first, by_second = yield (swap(array, first), swap(array, second))
     low, high = yield (swap(by_second[:cut], first), swap(by_first[cut:], second))
     near = jnp.concatenate([array, by_first, by_second, low, high], axis=0)
-    far = yield swap(near, last)
-    return jnp.concatenate([near, far], axis=0)
-
-
-def scatter_last(array, last):
+    return jnp.concatenate([near, swap(near, last)], axis=0)
+
+
+def scatter_plane(array, first, second, last):
     half = array.shape[0] // 2
-    theirs = yield swap(array[half:], last)
-    return array[:half] + theirs
-
-
-def scatter_near(array, first, second):
+    array = array[:half] + swap(array[half:], last)
     rows = array.shape[0] // 4
     cut = -(-rows // 32) * 16
     here, by_first, by_second, both = (array[i * rows : (i + 1) * rows] for i in range(4))
@@ -163,6 +160,24 @@
     by_first = jnp.concatenate([by_first[:cut], by_first[cut:] + high], axis=0)
     by_first, by_second = yield (swap(by_first, first), swap(by_second, second))
     return here + by_first + by_second
+
+
+def scatter_line(array):
+    if not ring_size():
+        array = lax.psum_scatter(array, "zh", scatter_dimension=0, tiled=True)
+        return lax.psum_scatter(array, "zl", scatter_dimension=1, tiled=True)[0, 0]
+    blocks = array.reshape((4,) + array.shape[2:])
+    here = lax.axis_index(("zh", "zl"))
+    mine = lax.dynamic_index_in_dim(blocks, here, 0, False)
+    theirs = yield tuple(
+        lax.ppermute(
+            lax.dynamic_index_in_dim(blocks, here ^ step, 0, False),
+            ("zh", "zl"),
+            [(i, i ^ step) for i in range(4)],
+        )
+        for step in (1, 2, 3)
+    )
+    return mine + theirs[0] + theirs[1] + theirs[2]
 
 
 def ring_size():
@@ -235,18 +250,26 @@
     return array.reshape((3,) + array.shape[-2:])
 
 
-def columns_of_ffn(weight):
+def exchange_first(weight):
     array = weight.reshape((1, 1, 1) + weight.shape)
-    for axis in FFN_GROUP:
+    for axis in FFN_GROUP[:-1]:
         array = yield from exchange(array, axis, 4, FFN_DIMS.index(axis))
+    return array
+
+
+def exchange_last(array):
+    axis = FFN_GROUP[-1]
+    array = yield from exchange(array, axis, 4, FFN_DIMS.index(axis))
     return array.reshape(-1, array.shape[-1])
 
 
-def sums_of_ffn(sums):
+def sums_of_ffn(sums, wait=0):
     sizes = tuple(lax.axis_size(axis) for axis in FFN_DIMS)
     array = sums.reshape(sizes + (-1, sums.shape[-1]))
     for axis in reversed(FFN_GROUP):
         array = yield from exchange(array, axis, FFN_DIMS.index(axis), 4)
+        if axis == FFN_GROUP[-1]:
+            yield from pause(wait)
     return array.reshape(array.shape[-2:])
 
 
@@ -255,7 +278,7 @@
     lead = list(axes) + list(kept)
     depth = max(AXES.index(axis) for axis in lead) + 1
     lanes = array.shape[1] // math.prod(sizes[:depth])
-    blocks = []
+    firsts = []
     for places in itertools.product(*(range(lax.axis_size(axis)) for axis in lead)):
         at = {axis: place for axis, place in zip(lead, places)}
         for axis in axes:
@@ -263,8 +286,23 @@
         first = 0
         for axis, size in zip(AXES[:depth], sizes):
             first = first * size + at[axis]
-        blocks.append(lax.dynamic_slice_in_dim(array, first * lanes, lanes, 1))
-    return jnp.concatenate(blocks, axis=1)
+        firsts.append(first)
+    return reorder(array, firsts, lanes)
+
+
+def reorder(array, firsts, lanes):
+    def kernel(firsts_ref, array_ref, out_ref):
+        for place in range(len(firsts)):
+            first = pl.multiple_of(firsts_ref[place] * lanes, 128)
+            out_ref[:, place * lanes : (place + 1) * lanes] = array_ref[:, pl.ds(first, lanes)]
+
+    return pl.pallas_call(
+        kernel,
+        in_specs=[pl.BlockSpec(memory_space=pltpu.SMEM), pl.BlockSpec(memory_space=pltpu.VMEM)],
+        out_specs=pl.BlockSpec(memory_space=pltpu.VMEM),
+        out_shape=jax.ShapeDtypeStruct(array.shape, array.dtype),
+        compiler_params=pltpu.CompilerParams(vmem_limit_bytes=8 * 2**20),
+    )(jnp.stack([jnp.int32(first) for first in firsts]), array)
 
 
 def relative(place, axis):
@@ -276,15 +314,15 @@
     lead = list(axes) + list(kept)
     depth = max(AXES.index(axis) for axis in lead) + 1
     lanes = array.shape[1] // math.prod(sizes[:depth])
-    blocks = []
+    firsts = []
     for places in itertools.product(*(range(size) for size in sizes[:depth])):
         at = dict(zip(AXES, places))
         first = 0
         for axis in lead:
             place = relative(at[axis], axis) if axis in axes else at[axis]
             first = first * lax.axis_size(axis) + place
-        blocks.append(lax.dynamic_slice_in_dim(array, first * lanes, lanes, 1))
-    return jnp.concatenate(blocks, axis=1)
+        firsts.append(first)
+    return reorder(array, firsts, lanes)
 
 
 def all_rows(parts):
@@ -305,154 +343,158 @@
     return lax.psum_scatter(sums[:half] + theirs, "zh", scatter_dimension=0, tiled=True)
 
 
-def block_mask(col_ref, row_ref, sum_ref, first, rows, keys, segment, per_seg):
-    query_docs = col_ref[0, first : first + rows, :]
-    query_pos = first + lax.broadcasted_iota(jnp.int32, (rows, keys), 0)
-    key_pos = lax.broadcasted_iota(jnp.int32, (rows, keys), 1)
-    allowed = (key_pos <= query_pos) & (query_docs == row_ref[0, :, :keys])
-    padded = sum_ref.shape[-1]
-    place = lax.broadcasted_iota(jnp.int32, (rows, padded), 1)
-    sum_allowed = (place < segment * per_seg) & (query_docs == sum_ref[...])
-    return allowed, sum_allowed
-
-
-def block_probs(query, key, sum_key, allowed, sum_allowed):
-    scores = jnp.where(allowed, dot(query, key, 1, 1), MASKED)
-    sum_scores = jnp.where(sum_allowed, dot(query, sum_key, 1, 1), MASKED)
-    top = jnp.maximum(
-        jnp.max(scores, axis=1, keepdims=True), jnp.max(sum_scores, axis=1, keepdims=True)
-    )
-    weights = jnp.exp(scores - top)
-    sum_weights = jnp.exp(sum_scores - top)
-    total = jnp.sum(weights, axis=1, keepdims=True) + jnp.sum(sum_weights, axis=1, keepdims=True)
-    share = 1.0 / total
-    return weights * share, sum_weights * share
-
-
-def load_ordered(order_ref, refs, scratches):
+def load_ordered(order_ref, refs, scratches, first=0):
     shards, _, here, _ = refs[0].shape
     for place in range(shards):
         block = order_ref[place]
         for ref, scratch in zip(refs, scratches):
-            scratch[place * here : (place + 1) * here, :] = ref[block, 0]
-
-
-def store_ordered(order_ref, refs, scratches):
-    shards, _, here, _ = refs[0].shape
+            scratch[first + place * here : first + (place + 1) * here, :] = ref[block, 0]
+
+
+def block_mask(doc_col_ref, doc_row_ref, pos_row_ref, first, rows, keys):
+    query_pos = first + lax.broadcasted_iota(jnp.int32, (rows, 1), 0)
+    in_reach = pos_row_ref[0, :, :keys] <= query_pos
+    return in_reach & (doc_row_ref[0, :, :keys] == doc_col_ref[0, first : first + rows, :])
+
+
+def heads_of(width):
+    lane = lax.broadcasted_iota(jnp.int32, (1, width), 1) // HEAD
+    return [lane == head for head in range(width // HEAD)]
+
+
+def of_heads(parts, heads):
+    total = parts[0]
+    for part, head in zip(parts[1:], heads[1:]):
+        total = jnp.where(head, part, total)
+    return total
+
+
+def block_probs(query, key, allowed):
+    scores = jnp.where(allowed, dot(query, key, 1, 1), MASKED)
+    weights = jnp.exp(scores - jnp.max(scores, axis=1, keepdims=True))
+    return weights * (1.0 / jnp.sum(weights, axis=1, keepdims=True))
+
+
+def forward_kernel(
+    rows, order_ref, doc_col_ref, doc_row_ref, pos_row_ref, q_in, k_in, v_in, sk_ref, sv_ref, out_ref,
+    q_ref, k_ref, v_ref,
+):
+    shards, _, here, width = out_ref.shape
+    padded = sk_ref.shape[0]
+    k_ref[:padded, :], v_ref[:padded, :] = sk_ref[...], sv_ref[...]
+    load_ordered(order_ref, (q_in,), (q_ref,))
+    load_ordered(order_ref, (k_in, v_in), (k_ref, v_ref), padded)
+    heads = heads_of(width)
+    for first in range(0, shards * here, rows):
+        keys = padded + first + rows
+        allowed = block_mask(doc_col_ref, doc_row_ref, pos_row_ref, first, rows, keys)
+        query, key, value = q_ref[first : first + rows, :], k_ref[:keys, :], v_ref[:keys, :]
+        outs = []
+        for head in heads:
+            probs = block_probs(jnp.where(head, query, jnp.zeros_like(query)), key, allowed)
+            outs.append(dot(probs.astype(BF), value))
+        q_ref[first : first + rows, :] = of_heads(outs, heads).astype(BF)
     for place in range(shards):
-        block = order_ref[place]
-        for ref, scratch in zip(refs, scratches):
-            ref[block, 0] = scratch[place * here : (place + 1) * here, :].astype(ref.dtype)
-
-
-def forward_kernel(
-    per_seg, rows, order_ref, col_ref, row_ref, sum_ref, q_in, k_in, v_in, sk_ref, sv_ref, out_ref,
-    q_ref, k_ref, v_ref, o_ref,
+        out_ref[place, 0] = q_ref[place * here : (place + 1) * here, :]
+
+
+def backward_kernel(
+    rows, order_ref, doc_col_ref, doc_row_ref, pos_row_ref, q_in, k_in, v_in, sk_ref, sv_ref, g_in,
+    dq_out, dk_out, dv_out, dsk_ref, dsv_ref,
+    q_ref, k_ref, v_ref, g_ref, dk_sum, dv_sum,
 ):
-    segment = pl.program_id(1)
-    load_ordered(order_ref, (q_in, k_in, v_in), (q_ref, k_ref, v_ref))
-    length, width = q_ref.shape
-    for first in range(0, length, rows):
-        keys = first + rows
-        allowed, sum_allowed = block_mask(
-            col_ref, row_ref, sum_ref, first, rows, keys, segment, per_seg
-        )
-        for low in range(0, width, HEAD):
-            cols = slice(low, low + HEAD)
-            probs, sum_probs = block_probs(
-                q_ref[first:keys, cols], k_ref[:keys, cols], sk_ref[:, cols], allowed, sum_allowed
-            )
-            out = dot(probs.astype(BF), v_ref[:keys, cols])
-            out += dot(sum_probs.astype(BF), sv_ref[:, cols])
-            o_ref[first:keys, cols] = out.astype(BF)
-    here = out_ref.shape[2]
-    for place in range(out_ref.shape[0]):
-        out_ref[place, 0] = o_ref[place * here : (place + 1) * here, :]
-
-
-def backward_kernel(
-    per_seg, rows, order_ref, col_ref, row_ref, sum_ref, q_in, k_in, v_in, sk_ref, sv_ref, g_in,
-    dq_out, dk_out, dv_out, dsk_ref, dsv_ref,
-    q_ref, k_ref, v_ref, g_ref, dq_ref, dk_sum, dv_sum,
-):
-    segment = pl.program_id(1)
-    load_ordered(order_ref, (q_in, k_in, v_in), (q_ref, k_ref, v_ref))
-    here = g_in.shape[2]
-    for place in range(g_in.shape[0]):
+    shards, _, here, width = g_in.shape
+    padded = sk_ref.shape[0]
+    k_ref[:padded, :], v_ref[:padded, :] = sk_ref[...], sv_ref[...]
+    load_ordered(order_ref, (q_in,), (q_ref,))
+    load_ordered(order_ref, (k_in, v_in), (k_ref, v_ref), padded)
+    for place in range(shards):
         g_ref[place * here : (place + 1) * here, :] = g_in[place, 0]
-    length, width = q_ref.shape
-
-    @pl.when(segment == 0)
+
+    @pl.when(pl.program_id(1) == 0)
     def _():
         dsk_ref[...] = jnp.zeros_like(dsk_ref)
         dsv_ref[...] = jnp.zeros_like(dsv_ref)
 
-    dk_sum[...] = jnp.zeros_like(dk_sum)
-    dv_sum[...] = jnp.zeros_like(dv_sum)
-    for first in range(0, length, rows):
-        keys = first + rows
-        allowed, sum_allowed = block_mask(
-            col_ref, row_ref, sum_ref, first, rows, keys, segment, per_seg
-        )
-        for low in range(0, width, HEAD):
-            cols = slice(low, low + HEAD)
-            query, grad = q_ref[first:keys, cols], g_ref[first:keys, cols]
-            key, sum_key = k_ref[:keys, cols], sk_ref[:, cols]
-            probs, sum_probs = block_probs(query, key, sum_key, allowed, sum_allowed)
-            d_probs = dot(grad, v_ref[:keys, cols], 1, 1)
-            d_sum_probs = dot(grad, sv_ref[:, cols], 1, 1)
-            delta = jnp.sum(probs * d_probs, axis=1, keepdims=True)
-            delta += jnp.sum(sum_probs * d_sum_probs, axis=1, keepdims=True)
-            d_scores = (probs * (d_probs - delta)).astype(BF)
-            d_sum_scores = (sum_probs * (d_sum_probs - delta)).astype(BF)
-            d_query = (dot(d_scores, key) + dot(d_sum_scores, sum_key)).astype(BF)
-            dq_ref[first:keys, cols] = (d_query.astype(F32) * 0.125).astype(BF)
-            dk_sum[:keys, cols] += dot(d_scores, query, 0, 0)
-            dv_sum[:keys, cols] += dot(probs.astype(BF), grad, 0, 0)
-            dsk_ref[:, cols] += dot(d_sum_scores, query, 0, 0)
-            dsv_ref[:, cols] += dot(sum_probs.astype(BF), grad, 0, 0)
-    store_ordered(order_ref, (dq_out, dk_out, dv_out), (dq_ref, dk_sum, dv_sum))
-
-
-def attention_calls(segs, shards, here, width, padded, per_seg):
-    lanes = min(2 * HEAD, width)
+    heads = heads_of(width)
+    for first in reversed(range(0, shards * here, rows)):
+        keys = padded + first + rows
+        last = first + rows == shards * here
+        allowed = block_mask(doc_col_ref, doc_row_ref, pos_row_ref, first, rows, keys)
+        query, grad = q_ref[first : first + rows, :], g_ref[first : first + rows, :]
+        key, value = k_ref[:keys, :], v_ref[:keys, :]
+        query_t, grad_t = query.T, grad.T
+        d_queries = []
+        for place, head in enumerate(heads):
+            probs = block_probs(jnp.where(head, query, jnp.zeros_like(query)), key, allowed)
+            d_probs = dot(jnp.where(head, grad, jnp.zeros_like(grad)), value, 1, 1)
+            product = probs * d_probs
+            delta = jnp.sum(product, axis=1, keepdims=True)
+            d_scores = (product - probs * delta).astype(BF)
+            d_queries.append(dot(d_scores, key))
+            lanes = slice(place * HEAD, (place + 1) * HEAD)
+            d_key = dot(query_t[lanes], d_scores)
+            d_value = dot(grad_t[lanes], probs.astype(BF))
+            if last:
+                dk_sum[lanes, :], dv_sum[lanes, :] = d_key, d_value
+            else:
+                dk_sum[lanes, :keys] += d_key
+                dv_sum[lanes, :keys] += d_value
+        d_query = of_heads(d_queries, heads).astype(BF)
+        q_ref[first : first + rows, :] = (d_query.astype(F32) * 0.125).astype(BF)
+    d_key, d_value = dk_sum[...].T, dv_sum[...].T
+    dsk_ref[...] += d_key[:padded]
+    dsv_ref[...] += d_value[:padded]
+    k_ref[...], v_ref[...] = d_key.astype(BF), d_value.astype(BF)
+    for place in range(shards):
+        block = order_ref[place]
+        tokens = slice(place * here, (place + 1) * here)
+        dq_out[block, 0] = q_ref[tokens, :]
+        tokens = slice(padded + place * here, padded + (place + 1) * here)
+        dk_out[block, 0], dv_out[block, 0] = k_ref[tokens, :], v_ref[tokens, :]
+
+
+def attention_calls(segs, shards, here, width, padded):
+    lanes = min(4 * HEAD, width)
     length = shards * here
-    rows = 128 if length <= 512 else 256
+    rows = length if length <= 512 else 384
     grid = (width // lanes, segs)
     tok = pl.BlockSpec((shards, 1, here, lanes), lambda h, s: (0, s, 0, h))
     summed = pl.BlockSpec((padded, lanes), lambda h, s: (0, h))
+    row = pl.BlockSpec((1, 1, padded + length), lambda h, s: (s, 0, 0))
     docs = [
         pl.BlockSpec(memory_space=pltpu.SMEM),
         pl.BlockSpec((1, length, 1), lambda h, s: (s, 0, 0)),
-        pl.BlockSpec((1, 1, length), lambda h, s: (s, 0, 0)),
-        pl.BlockSpec((1, padded), lambda h, s: (0, 0)),
+        row,
+        row,
     ]
     params = pltpu.CompilerParams(
         dimension_semantics=("arbitrary", "arbitrary"), vmem_limit_bytes=24 * 2**20
     )
     tokens = jax.ShapeDtypeStruct((shards, segs, here, width), BF)
     sums = jax.ShapeDtypeStruct((padded, width), F32)
-    narrow, wide = pltpu.VMEM((length, lanes), BF), pltpu.VMEM((length, lanes), F32)
+    queries, keys = pltpu.VMEM((length, lanes), BF), pltpu.VMEM((padded + length, lanes), BF)
+    key_sums = pltpu.VMEM((lanes, padded + length), F32)
     work = 2 * segs * length * (length // 2 + padded) * width
     forward = pl.pallas_call(
-        functools.partial(forward_kernel, per_seg, rows),
+        functools.partial(forward_kernel, rows),
         grid=grid,
         in_specs=docs + [tok] * 3 + [summed] * 2,
         out_specs=tok,
         out_shape=tokens,
-        scratch_shapes=[narrow] * 4,
+        scratch_shapes=[queries, keys, keys],
         compiler_params=params,
         cost_estimate=pl.CostEstimate(
             flops=120 * work, bytes_accessed=8 * segs * length * width, transcendentals=0
         ),
     )
     backward = pl.pallas_call(
-        functools.partial(backward_kernel, per_seg, rows),
+        functools.partial(backward_kernel, rows),
         grid=grid,
         in_specs=docs + [tok] * 3 + [summed] * 2 + [tok],
         out_specs=[tok] * 3 + [summed] * 2,
         out_shape=[tokens] * 3 + [sums] * 2,
-        scratch_shapes=[narrow] * 5 + [wide] * 2,
+        scratch_shapes=[queries, keys, keys, queries, key_sums, key_sums],
         compiler_params=params,
         cost_estimate=pl.CostEstimate(
             flops=160 * work, bytes_accessed=14 * segs * length * width, transcendentals=0
@@ -495,8 +537,14 @@
     docs = doc_ids.reshape(segs, length)
     last_docs = jnp.repeat(docs[: segs - 1, length - 1], per_seg)
     sum_docs = jnp.pad(last_docs, (0, padded - sum_rows), constant_values=-1)[None]
-    doc_args = (ring_order(shards), docs[:, :, None], docs[:, None, :], sum_docs)
-    attend, attend_back = attention_calls(segs, shards, here, width, padded, per_seg)
+    doc_rows = jnp.concatenate([jnp.broadcast_to(sum_docs, (segs, padded)), docs], axis=1)
+    far = jnp.where(
+        jnp.arange(padded)[None] < jnp.arange(segs)[:, None] * per_seg, -1, length
+    ).astype(jnp.int32)
+    places = jnp.broadcast_to(jnp.arange(length, dtype=jnp.int32), (segs, length))
+    pos_rows = jnp.concatenate([far, places], axis=1)
+    doc_args = (ring_order(shards), docs[:, :, None], doc_rows[:, None], pos_rows[:, None])
+    attend, attend_back = attention_calls(segs, shards, here, width, padded)
     split = (shards, segs, here, width)
     block_rows = shards * rows // max(ring_size(), 1)
 
@@ -521,7 +569,6 @@
 
     def critical():
         hidden_blocks = yield from gather_ring(hidden)
-        box["A"] = True
         w_qkv = yield from box.wait("w_qkv")
         doc_args, hidden_sum = box["doc_args"], box["hidden_sum"]
         def project(weight, scale=1.0):
@@ -533,7 +580,6 @@
         operands = yield operands
         attended = yield attend(*doc_args, *operands)
 
-        box["C"] = True
         attended = attended.reshape(shards, rows, width)
         attended = yield lax.all_to_all(attended, SEQ, 0, 0, tiled=True)
         attended = near_blocks(attended.swapaxes(0, 1).reshape(rows, model), ROWS)
@@ -542,7 +588,6 @@
         mixed = flat + summed
         standard_ffn, inverse_ffn = normalize(mixed)
         normed = near_blocks((standard_ffn * gain_ffn).astype(BF), FFN_REST, ("c",))
-        box["D"] = True
 
         normed_all = yield from gather_plane(normed, *FFN_NEAR)
         cot_all = yield from box.wait("cot_all")
@@ -555,20 +600,16 @@
         w_down_here = yield from box.wait("w_down")
         grad_upper = (slope * dot(cot_all, w_down_here)).astype(BF)
         grad_normed_part = dot(grad_upper, w_up_here, 1, 1).astype(BF)
-        scatter = scatter_last(grad_normed_part, FFN_NEAR[2])
-        in_flight = next(scatter)
+        grad_upper, grad_normed_part = yield (grad_upper, grad_normed_part)
+        near = scatter_plane(grad_normed_part, *FFN_NEAR)
+        in_flight = next(near)
         d_w_up = dot(normed_all, grad_upper, 0, 0).astype(BF)
-        in_flight, d_w_up = yield (in_flight, d_w_up)
+        in_flight, d_w_up, late_active, blocks = yield (in_flight, d_w_up, active, hidden_blocks)
         box["d_w_up"] = d_w_up
-        try:
-            scatter.send(in_flight)
-        except StopIteration as end:
-            near = scatter_near(end.value, *FFN_NEAR[:2])
-        in_flight = next(near)
-        ffn_out_part = dot(active, w_down_here, 1, 1).astype(BF)
-        in_flight, ffn_out_part = yield (in_flight, ffn_out_part)
+        ffn_out_part = dot(late_active, w_down_here, 1, 1).astype(BF)
+        left = jnp.concatenate(blocks + [hidden_sum], axis=0)
+        in_flight, ffn_out_part, left = yield (near.send(in_flight), ffn_out_part, left)
         box["ffn_out_part"] = ffn_out_part
-        in_flight = yield near.send(in_flight)
         try:
             near.send(in_flight)
         except StopIteration as end:
@@ -580,7 +621,7 @@
         grad_branch = grad_mixed.astype(BF)
         grad_attended = near_blocks(dot(grad_branch, w_out_all, 1, 1).astype(BF), ROWS)
         grad_attended = grad_attended.reshape(rows, shards, width).swapaxes(0, 1)
-        box["d_w_out"] = dot(attended, grad_branch, 0, 0).astype(BF)
+        box["for_out"] = attended, grad_branch
         grad_attended = yield lax.all_to_all(grad_attended, SEQ, 0, 0, tiled=True)
         grads = yield attend_back(*doc_args, *operands, grad_attended.reshape(split))
 
@@ -594,7 +635,6 @@
 
         grad_hidden_blocks = [grad_block(i) for i in range(0, shards * rows, block_rows)]
         grad_sum_part = sum(dot(d, w, 1, 1) for d, w in zip(d_sums, w_qkv[1:])).astype(BF)
-        left = jnp.concatenate(hidden_blocks + [hidden_sum], axis=0)
         d_w_qkv = [dot(left[: shards * rows], d_qkv[0], 0, 0).astype(BF)]
         for d, d_sum in zip(d_qkv[1:], d_sums):
             d_w_qkv.append(dot(left, jnp.concatenate([d, d_sum], axis=0), 0, 0).astype(BF))
@@ -616,55 +656,63 @@
         out["activations"] = (mixed + ffn_out.astype(F32)).astype(BF)
 
     def cotangent_rows():
-        yield from box.wait("A")
-        yield from pause(2)
-        box["cot_all"] = yield from gather_plane(near_blocks(cot, FFN_REST, ("c",)), *FFN_NEAR)
+        yield from pause(5)
+        cot_all = yield from gather_plane(near_blocks(cot, FFN_REST, ("c",)), *FFN_NEAR)
+        box["cot_all"] = yield cot_all
 
     def weight_up():
-        part = yield from columns_of_ffn(w_up)
+        part = yield from exchange_first(w_up)
+        yield ()
+        part = yield from exchange_last(part)
         box["up"] = part
         far = []
         if lax.axis_size("zh") == 2:
-            far = [(yield from in_pieces(part, "zh", 4))]
+            far = [jnp.concatenate((yield from in_pieces(part, "zh", 1, 2, 1)), axis=0)]
             far.append((yield swap(far[0], "x")))
         part_x = yield from box.wait("up_x")
-        box["w_up"] = all_rows([part] + far[:1] + [part_x] + far[1:])
+        box["w_up"] = yield all_rows([part] + far[:1] + [part_x] + far[1:])
 
     def weight_up_x():
         part = yield from box.wait("up")
-        yield from pause(3)
-        box["up_x"] = yield swap(part, "x")
+        half = part.shape[0] // 2
+        low = yield swap(part[:half], "x")
+        yield ()
+        high = yield swap(part[half:], "x")
+        box["up_x"] = jnp.concatenate([low, high], axis=0)
 
     def weight_down():
-        yield from pause(1)
-        part = yield from columns_of_ffn(w_down)
+        yield ()
+        part = yield from exchange_first(w_down)
+        yield ()
+        part = yield from exchange_last(part)
         box["down"] = part
-        yield from box.wait("C")
+        yield from pause(2)
         far = far_x = []
         if lax.axis_size("zh") == 2:
-            half = part.shape[0] // 2
-            step = half // 2
-            low = yield swap(part[:half], "zh")
-            third = yield swap(part[half : half + step], "zh")
-            fourth, low_x = yield (swap(part[half + step :], "zh"), swap(low, "x"))
+            step = part.shape[0] // 4
+            low = yield swap(part[: 2 * step], "zh")
+            third, low_x = yield (swap(part[2 * step : 3 * step], "zh"), swap(low, "x"))
+            fourth = yield swap(part[3 * step :], "zh")
             high = jnp.concatenate([third, fourth], axis=0)
-            yield ()
             high_x = yield swap(high, "x")
             far, far_x = [low, high], [low_x, high_x]
         part_x = yield from box.wait("down_x")
         box["w_down"] = all_rows([part, *far, part_x, *far_x])
 
     def weight_down_x():
-        yield from box.wait("C")
         part = yield from box.wait("down")
-        yield from box.put("down_x", in_pieces(part, "x", 2))
+        yield from pause(2)
+        half = part.shape[0] // 2
+        low = yield swap(part[:half], "x")
+        yield ()
+        high = yield swap(part[half:], "x")
+        box["down_x"] = jnp.concatenate([low, high], axis=0)
 
     def weight_out():
         yield from pause(2)
         array = w_out.reshape((1,) * len(AXES) + w_out.shape)
         for axis in ("zh", "zl"):
             array = yield from gather_dim(array, axis, AXES.index(axis))
-        yield from box.wait("A")
         half = array.shape[-1] // 2
         by_x, by_y = yield (swap(array, "x"), swap(array, "y"))
         low, high = yield (swap(by_y[..., :half], "x"), swap(by_x[..., half:], "y"))
@@ -672,24 +720,25 @@
         dim_y = AXES.index("y")
         near = pair(array, by_y, "y", dim_y).reshape(-1, model)
         far = pair(by_x, both, "y", dim_y).reshape(-1, model)
-        near_c, far_c = yield (swap(near, "c"), swap(far, "c"))
-        box["w_out"] = jnp.concatenate([near, near_c, far, far_c], axis=0)
+        near_c, far_c = swap(near, "c"), swap(far, "c")
+        box["w_out"] = yield jnp.concatenate([near, near_c, far, far_c], axis=0)
 
     def out_back():
-        array = yield from box.wait("d_w_out")
-        rows_c = model // 4
-        near, near_c, far, far_c = (array[i * rows_c : (i + 1) * rows_c] for i in range(4))
-        near_c, far_c = yield (swap(near_c, "c"), swap(far_c, "c"))
-        near, far = near + near_c, far + far_c
-        half = rows_c // 2
-        low = yield swap(far[:half], "x")
-        high = yield swap(far[half:], "x")
+        attended, grad_branch = yield from box.wait("for_out")
+        half = model // 2
+        far = dot(attended[:, half:], grad_branch, 0, 0).astype(BF)
+        far = far[: half // 2] + swap(far[half // 2 :], "c")
+        low = yield swap(far[: half // 4], "x")
+        near = dot(attended[:, :half], grad_branch, 0, 0).astype(BF)
+        near = near[: half // 2] + swap(near[half // 2 :], "c")
+        near = yield near
+        high = yield swap(far[half // 4 :], "x")
         array = near + jnp.concatenate([low, high], axis=0)
         seq_sizes = tuple(lax.axis_size(axis) for axis in SEQ)
         array = array.reshape((1, 1) + seq_sizes + (shard_rows, model))
         yield from pause(3)
-        for axis in ("y", "zl", "zh"):
-            array = yield from scatter_dim(array, axis, AXES.index(axis))
+        array = yield from scatter_dim(array, "y", AXES.index("y"))
+        array = yield from scatter_line(array[0, 0])
         out["d_w_out"] = array.reshape(shard_rows, model).astype(F32)
 
     def down_back():
@@ -705,11 +754,11 @@
             first, high = yield (swap(low[:step], "zh"), swap(sent[half:], "x"))
             high = high + far[half:]
             second = yield swap(low[step:], "zh")
-            third, near = yield (swap(high, "zh"), swap(near, "x"))
+            third = yield swap(high, "zh")
+            near = yield swap(near, "x")
             far = jnp.concatenate([first, second, third], axis=0)
             array = part_of(sums, 0, 0) + near + far
-        yield from box.wait("F")
-        array = yield from sums_of_ffn(array)
+        array = yield from sums_of_ffn(array, 2)
         out["d_w_down"] = array.astype(F32)
 
     def up_back():
@@ -719,29 +768,24 @@
         else:
             far, sent = part_of(sums, 0, 1), part_of(sums, 1, 1)
             near = part_of(sums, 1, 0)
-            yield ()
-            far = far + (yield from in_pieces(sent, "x", 2))
-            half = far.shape[0] // 2
-            step = half // 2
-            low = yield swap(far[:half], "zh")
-            third = yield swap(far[half : half + step], "zh")
-            fourth, near = yield (swap(far[half + step :], "zh"), swap(near, "x"))
-            far = jnp.concatenate([low, third, fourth], axis=0)
-            array = part_of(sums, 0, 0) + near + far
+            far = far + jnp.concatenate((yield from in_pieces(sent, "x", 1, 1)), axis=0)
+            pieces = yield from in_pieces(far, "zh", 1, 2, 1)
+            near = yield swap(near, "x")
+            array = part_of(sums, 0, 0) + near + jnp.concatenate(pieces, axis=0)
             yield ()
         array = yield from sums_of_ffn(array)
         out["d_w_up"] = array.astype(F32)
 
     def activations_back():
         part = yield from box.wait("ffn_out_part")
-        part = yield from scatter_last(part, FFN_NEAR[2])
-        box["ffn_out"] = yield from scatter_near(part, *FFN_NEAR[:2])
+        part = yield from scatter_plane(part, *FFN_NEAR)
+        yield from pause(3)
+        box["ffn_out"] = yield part
 
     def qkv_back():
         array = yield from box.wait("d_w_qkv")
         array = yield from sums_of_qkv(array)
-        array = array.astype(F32)
-        out["d_w_query"], out["d_w_key"], out["d_w_value"] = array
+        out["d_w_query"], out["d_w_key"], out["d_w_value"] = array.astype(F32)
 
     def sums_back():
         grad_sum_part = yield from box.wait("sums")
@@ -761,15 +805,15 @@
         out["d_summary"] = part[:sum_rows].astype(F32)
 
     together(
-        critical=critical(),
         ready_early=ready_early(),
         weight_qkv=box.put("w_qkv", columns_of_qkv(jnp.stack([w_query, w_key, w_value]))),
         weight_up=weight_up(),
         weight_up_x=weight_up_x(),
         weight_down=weight_down(),
         weight_down_x=weight_down_x(),
+        weight_out=weight_out(),
         cotangent_rows=cotangent_rows(),
-        weight_out=weight_out(),
+        critical=critical(),
         out_back=out_back(),
         down_back=down_back(),
         up_back=up_back(),

time: 688 us -> 634 us (0.922)
  waiting for transfers between devices: 292 us -> 258 us
  Pallas kernels: 42.8 us -> 23 us
  starting transfers between devices: 120 us -> 103 us
  other arithmetic: 69.4 us -> 84.5 us
    ppermute x94 -> x92, waiting for transfers between devices: 292 us -> 222 us  [swap(): return lax.ppermute(array, axis, [(0, 1), (1, 0)])]
    ppermute x94 -> x92, starting transfers between devices: 102 us -> 79.1 us  [swap(): return lax.ppermute(array, axis, [(0, 1), (1, 0)])]
    unnamed x336 -> x330, local copies, waits for them, and re-layouts: 51.3 us -> 35.4 us
    pallas_call x1, Pallas kernels: 25.2 us -> 12 us  [critical(): attend_back(*doc_args, *operands, grad_attended.reshape(split))]
    ppermute x0 -> x3, waiting for transfers between devices: none -> 12.8 us  [scatter_line(): lax.ppermute(lax.dynamic_index_in_dim(blocks, here ^ step, 0, False), ('z...]
    ppermute x6, waiting for transfers between devices: 0.13 us -> 11.6 us  [ring_shift(): lax.ppermute(array, ('zh', 'zl'), [(i, (i + step) % 4) for i in range(4)])]
    pallas_call x1, Pallas kernels: 17.6 us -> 7.33 us  [critical(): attended = (yield attend(*doc_args, *operands))]
    all_to_all x1, waiting for transfers between devices: 0.01 us -> 7.94 us  [critical(): attended = (yield lax.all_to_all(attended, SEQ, 0, 0, tiled=True))]
  transfers between devices with their start and end apart: 102 -> 103, of which waited for: 36 -> 40; matrix products, arithmetic and copies ran while one was open for 27% -> 33% of each run, Pallas kernels for 6% -> 4%
where the time goes in v4:
time: 634 us; the launch traced here: 626 us
  waiting for transfers between devices  258 us (41%)
  starting transfers between devices  103 us (16%)
  other arithmetic  84.5 us (13%)
  matrix products  78 us (12%)
  local copies, waits for them, and re-layouts  75.1 us (12%)
  Pallas kernels  23 us (4%)
    ppermute x92, waiting for transfers between devices, swap(): return lax.ppermute(array, axis, [(0, 1), (1, 0)])  222 us
    ppermute x92, starting transfers between devices, swap(): return lax.ppermute(array, axis, [(0, 1), (1, 0)])  79.1 us
    dot_general x41, matrix products, dot(): lax.dot_general(left, right, (((left_dim,), (right_dim,)), ((), ())), pre...  78 us
    unnamed x330, local copies, waits for them, and re-layouts  35.4 us
    ppermute x3, waiting for transfers between devices, scatter_line(): lax.ppermute(lax.dynamic_index_in_dim(blocks, here ^ step, 0, False), ('z...  12.8 us
  transfers between devices with their start and end apart: 103, of which 40 were waited for; matrix products, arithmetic and copies ran while one was open for 33% of the time, Pallas kernels for 4%

profile of v4, /device:TPU:0, one launch (start us, length us, event | category | flops | bytes accessed | tf_op | source)
XLA Modules:
  0.0 626.0 jit_solution(478336122726426630)
XLA Ops:
  26.8 20.4 %collective-permute-done.3 = bf16[3,1,1,1,1,1,64,1024]{7,6,5,4,3,2,1,0:T(8,128)(2,1)} collective-permute-done((bf16[3,1,1,1,1,1,64,1024]{7,6,5,4,3,2,1,0:T(8,128)(2,1)}, bf16[3,1,1,1,1,1,64,1024]{7,6,5,4,3,2,1,0:T(8,128)(2,1)}, u32[]{:S(2)}, u32[]{:S(2)}) %collective-permute-start.3) | collective-permute-done | bytes 393248 | tf_op jit(solution)/shard_map/weight_qkv/ppermute | solution.py:52
  52.9 9.1 %collective-permute-done.9 = bf16[2,1,1,64,2048]{4,3,2,1,0:T(8,128)(2,1)S(1)} collective-permute-done((bf16[2,1,1,64,2048]{4,3,2,1,0:T(8,128)(2,1)S(1)}, bf16[2,1,1,64,2048]{4,3,2,1,0:T(8,128)(2,1)S(1)}, u32[]{:S(2)}, u32[]{:S(2)}) %collective-permute-start.9) | collective-permute-done | bytes 524320 | tf_op jit(solution)/shard_map/weight_down/ppermute | solution.py:52
  61.9 11.9 %collective-permute-done.10 = bf16[3,1,1,2,1,1,64,512]{7,6,5,4,3,2,1,0:T(8,128)(2,1)S(1)} collective-permute-done((bf16[3,1,1,2,1,1,64,512]{7,6,5,4,3,2,1,0:T(8,128)(2,1)S(1)}, bf16[3,1,1,2,1,1,64,512]{7,6,5,4,3,2,1,0:T(8,128)(2,1)S(1)}, u32[]{:S(2)}, u32[]{:S(2)}) %collective-permute-start.10) | collective-permute-done | bytes 393248 | tf_op jit(solution)/shard_map/weight_qkv/ppermute | solution.py:52
  78.6 17.3 %collective-permute-done.15 = bf16[2,1,2,64,1024]{4,3,2,1,0:T(8,128)(2,1)S(1)} collective-permute-done((bf16[2,1,2,64,1024]{4,3,2,1,0:T(8,128)(2,1)S(1)}, bf16[2,1,2,64,1024]{4,3,2,1,0:T(8,128)(2,1)S(1)}, u32[]{:S(2)}, u32[]{:S(2)}) %collective-permute-start.15) | collective-permute-done | bytes 524320 | tf_op jit(solution)/shard_map/weight_up/ppermute | solution.py:52
  105.0 5.7 collective-permute-done.18
  117.7 10.3 %collective-permute-done.21 = bf16[128,1024]{1,0:T(8,128)(2,1)S(1)} collective-permute-done((bf16[128,1024]{1,0:T(8,128)(2,1)}, bf16[128,1024]{1,0:T(8,128)(2,1)S(1)}, u32[]{:S(2)}, u32[]{:S(2)}) %collective-permute-start.21) | collective-permute-done | bytes 262176 | tf_op jit(solution)/shard_map/weight_up/ppermute | solution.py:52
  167.1 7.3 %critical.7 = bf16[8,3,48,256]{3,2,1,0:T(8,128)(2,1)} custom-call(s32[8]{0:T(128)S(1)} %copy-done.11, s32[3,384,1]{2,1,0:T(8,128)S(1)} %copy.42.doc_col_ref, s32[3,1,512]{2,1,0:T(1,128)S(1)} %broadcast_in_dim.20.doc_row_ref, s32[3,1,512]{2,1,0:T(1,128)S(1)} %broadcast_in_dim.24.pos_row_ref, bf16[8,3,48,256]{3,2,1,0:T(8,128)(2,1)S(1)} %bitcast.240, ...), custom_call_target="tpu_custom_call" | custom-call | flops 22649241600 | bytes 2359296 | tf_op jit(solution)/shard_map/critical/pallas_call | solution.py:581
  179.5 9.1 %collective-permute-done.29 = bf16[128,1024]{1,0:T(8,128)(2,1)S(1)} collective-permute-done((bf16[128,1024]{1,0:T(8,128)(2,1)S(1)}, bf16[128,1024]{1,0:T(8,128)(2,1)S(1)}, u32[]{:S(2)}, u32[]{:S(2)}) %collective-permute-start.29) | collective-permute-done | bytes 262176 | tf_op jit(solution)/shard_map/weight_up/ppermute | solution.py:52
  200.6 5.1 all-to-all-start
  215.7 7.0 %pad_maximum_fusion = bf16[2048,2048]{1,0:T(8,128)(2,1)} fusion(bf16[512,2048]{1,0:T(8,128)(2,1)} %collective-permute-done.36, bf16[512,2048]{1,0:T(8,128)(2,1)} %bitcast.39, bf16[512,2048]{1,0:T(8,128)(2,1)} %collective-permute-done.35, bf16[512,2048]{1,0:T(8,128)(2,1)} %bitcast.38), kind=kLoop, calls=%fused_computation | loop fusion | flops 33554432 | bytes 16777216 | tf_op jit(solution)/shard_map/weight_out/concatenate | solution.py:724
  222.7 5.2 collective-permute-done.33
  231.8 7.9 %all-to-all-done = bf16[8,144,256]{2,1,0:T(8,128)(2,1)S(1)} async-done(((bf16[8,144,256]{2,1,0:T(8,128)(2,1)}), bf16[8,144,256]{2,1,0:T(8,128)(2,1)S(1)}, u32[]{:S(2)}, u32[]{:S(2)}) %all-to-all-start) | async-done | bytes 589856 | tf_op jit(solution)/shard_map/critical/all_to_all | solution.py:584
  248.7 5.4 fusion.109
  262.8 9.0 %collective-permute-done.42 = bf16[256,1024]{1,0:T(8,128)(2,1)S(1)} collective-permute-done((bf16[256,1024]{1,0:T(8,128)(2,1)}, bf16[256,1024]{1,0:T(8,128)(2,1)S(1)}, u32[]{:S(2)}, u32[]{:S(2)}) %collective-permute-start.42) | collective-permute-done | bytes 524320 | tf_op jit(solution)/shard_map/weight_down/ppermute | solution.py:52
  271.8 6.1 collective-permute-done.40
  293.3 6.5 %fusion.3 = (f32[1152,1024]{1,0:T(8,128)S(1)}, bf16[1152,1024]{1,0:T(8,128)(2,1)S(1)}) fusion(bf16[1152,2048]{1,0:T(8,128)(2,1)S(1)} %constant_dynamic-update-slice_fusion.31, bf16[2048,1024]{1,0:T(8,128)(2,1)S(1)} %constant_dynamic-update-slice_fusion.19), kind=kOutput, calls=%fused_computation.7 | convolution fusion | flops 4843634688 | bytes 15990784 | tf_op jit(solution)/shard_map/critical/dot_general | solution.py:30
  299.8 6.4 %convolution_convert_fusion.5 = bf16[2048,1024]{1,0:T(8,128)(2,1)S(1)} fusion(bf16[1152,2048]{1,0:T(8,128)(2,1)S(1)} %constant_dynamic-update-slice_fusion.13, bf16[1152,1024]{1,0:T(8,128)(2,1)S(1)} %get-tuple-element.207), kind=kOutput, calls=%fused_computation.16 | convolution fusion | flops 4833935360 | bytes 11272192 | tf_op jit(solution)/shard_map/critical/dot_general | solution.py:30
  313.5 5.4 convolution_convert_fusion.1
  318.9 6.7 %collective-permute-done.49 = bf16[256,1024]{1,0:T(8,128)(2,1)S(1)} collective-permute-done((bf16[256,1024]{1,0:T(8,128)(2,1)S(1)}, bf16[256,1024]{1,0:T(8,128)(2,1)S(1)}, u32[]{:S(2)}, u32[]{:S(2)}) %collective-permute-start.49) | collective-permute-done | bytes 524320 | tf_op jit(solution)/shard_map/down_back/ppermute | solution.py:52
  336.7 8.6 %convolution_convert_fusion.4 = bf16[2048,1024]{1,0:T(8,128)(2,1)S(1)} fusion(bf16[1152,2048]{1,0:T(8,128)(2,1)} %copy-done.129, bf16[1152,1024]{1,0:T(8,128)(2,1)S(1)} %copy-done.75), kind=kOutput, calls=%fused_computation.15 | convolution fusion | flops 4833935360 | bytes 11272192 | tf_op jit(solution)/shard_map/critical/dot_general | solution.py:30
  348.7 5.3 convolution_convert_fusion
  360.0 9.9 %collective-permute-done.58 = bf16[256,1024]{1,0:T(8,128)(2,1)S(1)} collective-permute-done((bf16[256,1024]{1,0:T(8,128)(2,1)S(1)}, bf16[256,1024]{1,0:T(8,128)(2,1)S(1)}, u32[]{:S(2)}, u32[]{:S(2)}) %collective-permute-start.58) | collective-permute-done | bytes 524320 | tf_op jit(solution)/shard_map/up_back/ppermute | solution.py:52
  385.9 6.3 %convolution_convert_fusion.8.array_ref = bf16[144,2048]{1,0:T(8,128)(2,1)S(1)} fusion(bf16[2048,2048]{1,0:T(8,128)(2,1)} %pad_maximum_fusion, f32[144,2048]{1,0:T(8,128)S(1)} %copy-done.24), kind=kOutput, calls=%fused_computation.41 | convolution fusion | flops 1208549376 | bytes 10158080 | tf_op jit(solution)/shard_map/critical/dot_general | solution.py:30
  425.1 7.7 %collective-permute-done.64 = bf16[256,2048]{1,0:T(8,128)(2,1)} collective-permute-done((bf16[256,2048]{1,0:T(8,128)(2,1)}, bf16[256,2048]{1,0:T(8,128)(2,1)}, u32[]{:S(2)}, u32[]{:S(2)}) %collective-permute-start.64) | collective-permute-done | bytes 1048608 | tf_op jit(solution)/shard_map/out_back/ppermute | solution.py:52
  445.3 12.0 %critical.12 = (bf16[8,3,48,256]{3,2,1,0:T(8,128)(2,1)S(1)}, bf16[8,3,48,256]{3,2,1,0:T(8,128)(2,1)S(1)}, bf16[8,3,48,256]{3,2,1,0:T(8,128)(2,1)S(1)}, f32[128,256]{1,0:T(8,128)S(1)}, f32[128,256]{1,0:T(8,128)S(1)}) custom-call(s32[8]{0:T(128)S(1)} %copy-done.12, s32[3,384,1]{2,1,0:T(8,128)S(1)} %copy.42.doc_col_ref, ...), custom_call_target="tpu_custom_call" | custom-call | flops 30198988800 | bytes 4128768 | tf_op jit(solution)/shard_map/critical/pallas_call | solution.py:626
  507.0 6.6 %collective-permute-done.75 = bf16[144,2048]{1,0:T(8,128)(2,1)S(1)} collective-permute-done((bf16[144,2048]{1,0:T(8,128)(2,1)S(1)}, bf16[144,2048]{1,0:T(8,128)(2,1)S(1)}, u32[]{:S(2)}, u32[]{:S(2)}) %collective-permute-start.75) | collective-permute-done | bytes 589856 | tf_op jit(solution)/shard_map/critical/ppermute | solution.py:188
  513.5 7.5 %collective-permute-done.78 = bf16[3,1,1,2,2,2,64,256]{7,6,5,4,3,2,1,0:T(8,128)(2,1)S(1)} collective-permute-done((bf16[3,1,1,2,2,2,64,256]{7,6,5,4,3,2,1,0:T(8,128)(2,1)S(1)}, bf16[3,1,1,2,2,2,64,256]{7,6,5,4,3,2,1,0:T(8,128)(2,1)S(1)}, u32[]{:S(2)}, u32[]{:S(2)}) %collective-permute-start.78) | collective-permute-done | bytes 786464 | tf_op jit(solution)/shard_map/qkv_back/ppermute | solution.py:52
  523.9 18.8 %collective-permute-done.85 = bf16[512,1024]{1,0:T(8,128)(2,1)S(1)} collective-permute-done((bf16[512,1024]{1,0:T(8,128)(2,1)S(1)}, bf16[512,1024]{1,0:T(8,128)(2,1)S(1)}, u32[]{:S(2)}, u32[]{:S(2)}) %collective-permute-start.85) | collective-permute-done | bytes 1048608 | tf_op jit(solution)/shard_map/up_back/ppermute | solution.py:52
  549.5 9.5 %collective-permute-done.87 = bf16[144,2048]{1,0:T(8,128)(2,1)S(1)} collective-permute-done((bf16[144,2048]{1,0:T(8,128)(2,1)S(1)}, bf16[144,2048]{1,0:T(8,128)(2,1)S(1)}, u32[]{:S(2)}, u32[]{:S(2)}) %collective-permute-start.87) | collective-permute-done | bytes 589856 | tf_op jit(solution)/shard_map/critical/ppermute | solution.py:52
  559.4 10.8 %collective-permute-done.88 = bf16[2,1,1,64,2048]{4,3,2,1,0:T(8,128)(2,1)S(1)} collective-permute-done((bf16[2,1,1,64,2048]{4,3,2,1,0:T(8,128)(2,1)S(1)}, bf16[2,1,1,64,2048]{4,3,2,1,0:T(8,128)(2,1)S(1)}, u32[]{:S(2)}, u32[]{:S(2)}) %collective-permute-start.88) | collective-permute-done | bytes 524320 | tf_op jit(solution)/shard_map/down_back/ppermute | solution.py:52
  581.6 11.1 %collective-permute-done.91 = bf16[1,1,2,2,1,64,2048]{6,5,4,3,2,1,0:T(8,128)(2,1)S(1)} collective-permute-done((bf16[1,1,2,2,1,64,2048]{6,5,4,3,2,1,0:T(8,128)(2,1)S(1)}, bf16[1,1,2,2,1,64,2048]{6,5,4,3,2,1,0:T(8,128)(2,1)S(1)}, u32[]{:S(2)}, u32[]{:S(2)}) %collective-permute-start.91) | collective-permute-done | bytes 1048608 | tf_op jit(solution)/shard_map/out_back/ppermute | solution.py:52
  610.2 9.4 %collective-permute-done.96 = bf16[1,64,2048]{2,1,0:T(8,128)(2,1)S(1)} collective-permute-done((bf16[1,64,2048]{2,1,0:T(8,128)(2,1)S(1)}, bf16[1,64,2048]{2,1,0:T(8,128)(2,1)S(1)}, u32[]{:S(2)}, u32[]{:S(2)}) %collective-permute-start.96) | collective-permute-done | bytes 262176 | tf_op jit(solution)/shard_map/out_back/ppermute | solution.py:173
  (759 shorter events, 336.8 us)
Async XLA Ops:
  5.9 42.7 %collective-permute-start.2 = (bf16[144,2048]{1,0:T(8,128)(2,1)}, bf16[144,2048]{1,0:T(8,128)(2,1)}, u32[]{:S(2)}, u32[]{:S(2)}) collective-permute-start(bf16[144,2048]{1,0:T(8,128)(2,1)} %multiply_convert_fusion.3), channel_id=1, source_target_pairs={{0,2},{2,4},{4,6},{6,0},{1,3},{3,5},{5,7},{7,1},{8,10},{10,12},{12... | collective-permute-start | bytes 1769480 | tf_op jit(solution)/shard_map/critical/ppermute | solution.py:188
  8.9 43.3 %collective-permute-start.7 = (bf16[144,2048]{1,0:T(8,128)(2,1)}, bf16[144,2048]{1,0:T(8,128)(2,1)}, u32[]{:S(2)}, u32[]{:S(2)}) collective-permute-start(bf16[144,2048]{1,0:T(8,128)(2,1)} %multiply_convert_fusion.3), channel_id=1, source_target_pairs={{0,1},{1,0},{2,3},{3,2},{4,5},{5,4},{6,7},{7,6},{8,9},{9,8},{10,11... | collective-permute-start | bytes 1769480 | tf_op jit(solution)/shard_map/critical/ppermute | solution.py:52
  12.2 34.9 %collective-permute-start.3 = (bf16[3,1,1,1,1,1,64,1024]{7,6,5,4,3,2,1,0:T(8,128)(2,1)}, bf16[3,1,1,1,1,1,64,1024]{7,6,5,4,3,2,1,0:T(8,128)(2,1)}, u32[]{:S(2)}, u32[]{:S(2)}) collective-permute-start(bf16[3,1,1,1,1,1,64,1024]{7,6,5,4,3,2,1,0:T(8,128)(2,1)} %dynamic-slice_bitcast_fusion.3), channel_id=1, source_target_pairs={{0,4},{4,0},{1,5},{5,1},{2,6},{6,2},{3,7},{7,3},{8,12},{12,8},{9,1... | collective-permute-start | bytes 1179656 | tf_op jit(solution)/shard_map/weight_qkv/ppermute | solution.py:52
  23.3 53.7 %collective-permute-start.13 = (bf16[1,1,1,1,1,64,2048]{6,5,4,3,2,1,0:T(8,128)(2,1)S(1)}, bf16[1,1,1,1,1,64,2048]{6,5,4,3,2,1,0:T(8,128)(2,1)S(1)}, u32[]{:S(2)}, u32[]{:S(2)}) collective-permute-start(bf16[1,1,1,1,1,64,2048]{6,5,4,3,2,1,0:T(8,128)(2,1)S(1)} %bitcast.316), channel_id=1, source_target_pairs={{0,4},{4,0},{1,5},{5,1},{2,6},{6,2},{3,7},{7,3},{8,12},{12,8},{9,1... | collective-permute-start | bytes 786440 | tf_op jit(solution)/shard_map/weight_out/ppermute | solution.py:52
  52.3 43.6 %collective-permute-start.12 = (bf16[144,2048]{1,0:T(8,128)(2,1)}, bf16[144,2048]{1,0:T(8,128)(2,1)S(1)}, u32[]{:S(2)}, u32[]{:S(2)}) collective-permute-start(bf16[144,2048]{1,0:T(8,128)(2,1)} %collective-permute-done.2), channel_id=1, source_target_pairs={{0,1},{1,0},{2,3},{3,2},{4,5},{5,4},{6,7},{7,6},{8,9},{9,8},{10,11... | collective-permute-start | bytes 1769480 | tf_op jit(solution)/shard_map/critical/ppermute | solution.py:52
  61.9 33.9 %collective-permute-start.15 = (bf16[2,1,2,64,1024]{4,3,2,1,0:T(8,128)(2,1)S(1)}, bf16[2,1,2,64,1024]{4,3,2,1,0:T(8,128)(2,1)S(1)}, u32[]{:S(2)}, u32[]{:S(2)}) collective-permute-start(bf16[2,1,2,64,1024]{4,3,2,1,0:T(8,128)(2,1)S(1)} %fusion.54), channel_id=1, source_target_pairs={{0,2},{2,0},{1,3},{3,1},{4,6},{6,4},{5,7},{7,5},{8,10},{10,8},{9,1... | collective-permute-start | bytes 1572872 | tf_op jit(solution)/shard_map/weight_up/ppermute | solution.py:52
  77.0 37.2 %collective-permute-start.16 = (bf16[144,2048]{1,0:T(8,128)(2,1)S(1)}, bf16[144,2048]{1,0:T(8,128)(2,1)S(1)}, u32[]{:S(2)}, u32[]{:S(2)}) collective-permute-start(bf16[144,2048]{1,0:T(8,128)(2,1)S(1)} %collective-permute-done.6), channel_id=1, source_target_pairs={{0,1},{1,0},{2,3},{3,2},{4,5},{5,4},{6,7},{7,6},{8,9},{9,8},{10,11... | collective-permute-start | bytes 1769480 | tf_op jit(solution)/shard_map/critical/ppermute | solution.py:52
  100.7 27.7 %collective-permute-start.22 = (bf16[256,1024]{1,0:T(8,128)(2,1)}, bf16[256,1024]{1,0:T(8,128)(2,1)}, u32[]{:S(2)}, u32[]{:S(2)}) collective-permute-start(bf16[256,1024]{1,0:T(8,128)(2,1)} %bitcast.28), channel_id=1, source_target_pairs={{0,16},{16,0},{1,17},{17,1},{2,18},{18,2},{3,19},{19,3},{4,20},{20... | collective-permute-start | bytes 1572872 | tf_op jit(solution)/shard_map/weight_up_x/ppermute | solution.py:52
  128.0 46.6 %collective-permute-start = (bf16[144,2048]{1,0:T(8,128)(2,1)S(1)}, bf16[144,2048]{1,0:T(8,128)(2,1)}, u32[]{:S(2)}, u32[]{:S(2)}) collective-permute-start(bf16[144,2048]{1,0:T(8,128)(2,1)S(1)} %cotangent_rows.1), channel_id=1, source_target_pairs={{0,1},{1,0},{2,3},{3,2},{4,5},{5,4},{6,7},{7,6},{8,9},{9,8},{10,11... | collective-permute-start | bytes 1769480 | tf_op jit(solution)/shard_map/cotangent_rows/ppermute | solution.py:52
  128.4 51.1 %collective-permute-start.1 = (bf16[144,2048]{1,0:T(8,128)(2,1)S(1)}, bf16[144,2048]{1,0:T(8,128)(2,1)}, u32[]{:S(2)}, u32[]{:S(2)}) collective-permute-start(bf16[144,2048]{1,0:T(8,128)(2,1)S(1)} %cotangent_rows.1), channel_id=1, source_target_pairs={{0,2},{2,0},{1,3},{3,1},{4,6},{6,4},{5,7},{7,5},{8,10},{10,8},{9,1... | collective-permute-start | bytes 1769480 | tf_op jit(solution)/shard_map/cotangent_rows/ppermute | solution.py:52
  158.8 29.8 %collective-permute-start.30 = (bf16[256,1024]{1,0:T(8,128)(2,1)S(1)}, bf16[256,1024]{1,0:T(8,128)(2,1)S(1)}, u32[]{:S(2)}, u32[]{:S(2)}) collective-permute-start(bf16[256,1024]{1,0:T(8,128)(2,1)S(1)} %bitcast.312), channel_id=1, source_target_pairs={{0,16},{16,0},{1,17},{17,1},{2,18},{18,2},{3,19},{19,3},{4,20},{20... | collective-permute-start | bytes 1572872 | tf_op jit(solution)/shard_map/weight_up_x/ppermute | solution.py:52
  179.5 32.7 %collective-permute-start.35 = (bf16[512,2048]{1,0:T(8,128)(2,1)}, bf16[512,2048]{1,0:T(8,128)(2,1)}, u32[]{:S(2)}, u32[]{:S(2)}) collective-permute-start(bf16[512,2048]{1,0:T(8,128)(2,1)} %bitcast.38), channel_id=1, source_target_pairs={{0,8},{8,0},{1,9},{9,1},{2,10},{10,2},{3,11},{11,3},{4,12},{12,4},... | collective-permute-start | bytes 6291464 | tf_op jit(solution)/shard_map/weight_out/ppermute | solution.py:52
  194.3 33.6 %collective-permute-start.33 = (bf16[256,1024]{1,0:T(8,128)(2,1)}, bf16[256,1024]{1,0:T(8,128)(2,1)}, u32[]{:S(2)}, u32[]{:S(2)}) collective-permute-start(bf16[256,1024]{1,0:T(8,128)(2,1)} %bitcast.37), channel_id=1, source_target_pairs={{0,4},{4,0},{1,5},{5,1},{2,6},{6,2},{3,7},{7,3},{8,12},{12,8},{9,1... | collective-permute-start | bytes 1572872 | tf_op jit(solution)/shard_map/weight_down/ppermute | solution.py:52
  194.3 33.6 %collective-permute-start.34 = (bf16[256,1024]{1,0:T(8,128)(2,1)}, bf16[256,1024]{1,0:T(8,128)(2,1)}, u32[]{:S(2)}, u32[]{:S(2)}) collective-permute-start(bf16[256,1024]{1,0:T(8,128)(2,1)} %bitcast.37), channel_id=1, source_target_pairs={{0,16},{16,0},{1,17},{17,1},{2,18},{18,2},{3,19},{19,3},{4,20},{20... | collective-permute-start | bytes 1572872 | tf_op jit(solution)/shard_map/weight_down_x/ppermute | solution.py:52
  200.0 39.7 %collective-permute-start.37 = (bf16[512,1024]{1,0:T(8,128)(2,1)}, bf16[512,1024]{1,0:T(8,128)(2,1)}, u32[]{:S(2)}, u32[]{:S(2)}) collective-permute-start(bf16[512,1024]{1,0:T(8,128)(2,1)} %pad_maximum_fusion.10), channel_id=1, source_target_pairs={{0,16},{16,0},{1,17},{17,1},{2,18},{18,2},{3,19},{19,3},{4,20},{20... | collective-permute-start | bytes 3145736 | tf_op jit(solution)/shard_map/weight_up/ppermute | solution.py:52
  200.6 39.1 %all-to-all-start = ((bf16[8,144,256]{2,1,0:T(8,128)(2,1)}), bf16[8,144,256]{2,1,0:T(8,128)(2,1)S(1)}, u32[]{:S(2)}, u32[]{:S(2)}) async-start(bf16[8,144,256]{2,1,0:T(8,128)(2,1)} %bitcast.36), calls=%async_computation | async-start | bytes 1179648 | tf_op jit(solution)/shard_map/critical/all_to_all | solution.py:584
  227.9 32.8 %collective-permute-start.41 = (bf16[128,1024]{1,0:T(8,128)(2,1)}, bf16[128,1024]{1,0:T(8,128)(2,1)}, u32[]{:S(2)}, u32[]{:S(2)}) collective-permute-start(bf16[128,1024]{1,0:T(8,128)(2,1)} %get-tuple-element.387), channel_id=1, source_target_pairs={{0,4},{4,0},{1,5},{5,1},{2,6},{6,2},{3,7},{7,3},{8,12},{12,8},{9,1... | collective-permute-start | bytes 786440 | tf_op jit(solution)/shard_map/weight_down/ppermute | solution.py:52
  378.9 28.3 %collective-permute-start.59 = (bf16[576,2048]{1,0:T(8,128)(2,1)}, bf16[576,2048]{1,0:T(8,128)(2,1)}, u32[]{:S(2)}, u32[]{:S(2)}) collective-permute-start(bf16[576,2048]{1,0:T(8,128)(2,1)} %slice.386), channel_id=1, source_target_pairs={{0,8},{8,0},{1,9},{9,1},{2,10},{10,2},{3,11},{11,3},{4,12},{12,4},... | collective-permute-start | bytes 7077896 | tf_op jit(solution)/shard_map/activations_back/ppermute | solution.py:52
  383.7 33.0 %collective-permute-start.62 = (bf16[256,1024]{1,0:T(8,128)(2,1)}, bf16[256,1024]{1,0:T(8,128)(2,1)}, u32[]{:S(2)}, u32[]{:S(2)}) collective-permute-start(bf16[256,1024]{1,0:T(8,128)(2,1)} %slice_add_fusion.11), channel_id=1, source_target_pairs={{0,4},{4,0},{1,5},{5,1},{2,6},{6,2},{3,7},{7,3},{8,12},{12,8},{9,1... | collective-permute-start | bytes 1572872 | tf_op jit(solution)/shard_map/down_back/ppermute | solution.py:52
  384.6 33.3 %collective-permute-start.65 = (bf16[256,1024]{1,0:T(8,128)(2,1)}, bf16[256,1024]{1,0:T(8,128)(2,1)}, u32[]{:S(2)}, u32[]{:S(2)}) collective-permute-start(bf16[256,1024]{1,0:T(8,128)(2,1)} %get-tuple-element.314), channel_id=1, source_target_pairs={{0,16},{16,0},{1,17},{17,1},{2,18},{18,2},{3,19},{19,3},{4,20},{20... | collective-permute-start | bytes 1572872 | tf_op jit(solution)/shard_map/up_back/ppermute | solution.py:52
  393.6 29.2 %all-to-all-start.1 = ((bf16[8,144,256]{2,1,0:T(8,128)(2,1)}), bf16[8,144,256]{2,1,0:T(8,128)(2,1)S(1)}, u32[]{:S(2)}, u32[]{:S(2)}) async-start(bf16[8,144,256]{2,1,0:T(8,128)(2,1)} %bitcast.294), calls=%async_computation.1 | async-start | bytes 1179648 | tf_op jit(solution)/shard_map/critical/all_to_all | solution.py:625
  416.7 41.5 %collective-permute-start.68 = (bf16[512,1024]{1,0:T(8,128)(2,1)}, bf16[512,1024]{1,0:T(8,128)(2,1)}, u32[]{:S(2)}, u32[]{:S(2)}) collective-permute-start(bf16[512,1024]{1,0:T(8,128)(2,1)} %slice.401), channel_id=1, source_target_pairs={{0,16},{16,0},{1,17},{17,1},{2,18},{18,2},{3,19},{19,3},{4,20},{20... | collective-permute-start | bytes 3145736 | tf_op jit(solution)/shard_map/down_back/ppermute | solution.py:52
  417.9 72.4 %collective-permute-start.73 = (bf16[256,2048]{1,0:T(8,128)(2,1)}, bf16[256,2048]{1,0:T(8,128)(2,1)}, u32[]{:S(2)}, u32[]{:S(2)}) collective-permute-start(bf16[256,2048]{1,0:T(8,128)(2,1)} %get-tuple-element.331), channel_id=1, source_target_pairs={{0,16},{16,0},{1,17},{17,1},{2,18},{18,2},{3,19},{19,3},{4,20},{20... | collective-permute-start | bytes 3145736 | tf_op jit(solution)/shard_map/out_back/ppermute | solution.py:52
  458.2 33.7 %collective-permute-start.74 = (bf16[256,1024]{1,0:T(8,128)(2,1)}, bf16[256,1024]{1,0:T(8,128)(2,1)}, u32[]{:S(2)}, u32[]{:S(2)}) collective-permute-start(bf16[256,1024]{1,0:T(8,128)(2,1)} %slice.495), channel_id=1, source_target_pairs={{0,4},{4,0},{1,5},{5,1},{2,6},{6,2},{3,7},{7,3},{8,12},{12,8},{9,1... | collective-permute-start | bytes 1572872 | tf_op jit(solution)/shard_map/up_back/ppermute | solution.py:52
  458.7 46.4 %collective-permute-start.80 = (bf16[128,1024]{1,0:T(8,128)(2,1)}, bf16[128,1024]{1,0:T(8,128)(2,1)}, u32[]{:S(2)}, u32[]{:S(2)}) collective-permute-start(bf16[128,1024]{1,0:T(8,128)(2,1)} %get-tuple-element.382), channel_id=1, source_target_pairs={{0,4},{4,0},{1,5},{5,1},{2,6},{6,2},{3,7},{7,3},{8,12},{12,8},{9,1... | collective-permute-start | bytes 786440 | tf_op jit(solution)/shard_map/up_back/ppermute | solution.py:52
  505.2 37.5 %collective-permute-start.85 = (bf16[512,1024]{1,0:T(8,128)(2,1)S(1)}, bf16[512,1024]{1,0:T(8,128)(2,1)S(1)}, u32[]{:S(2)}, u32[]{:S(2)}) collective-permute-start(bf16[512,1024]{1,0:T(8,128)(2,1)S(1)} %copy-done.77), channel_id=1, source_target_pairs={{0,16},{16,0},{1,17},{17,1},{2,18},{18,2},{3,19},{19,3},{4,20},{20... | collective-permute-start | bytes 3145736 | tf_op jit(solution)/shard_map/up_back/ppermute | solution.py:52
  506.6 36.6 %collective-permute-start.82 = (bf16[144,2048]{1,0:T(8,128)(2,1)S(1)}, bf16[144,2048]{1,0:T(8,128)(2,1)S(1)}, u32[]{:S(2)}, u32[]{:S(2)}) collective-permute-start(bf16[144,2048]{1,0:T(8,128)(2,1)S(1)} %slice.500), channel_id=1, source_target_pairs={{0,1},{1,0},{2,3},{3,2},{4,5},{5,4},{6,7},{7,6},{8,9},{9,8},{10,11... | collective-permute-start | bytes 1769480 | tf_op jit(solution)/shard_map/critical/ppermute | solution.py:52
  543.1 27.1 %collective-permute-start.88 = (bf16[2,1,1,64,2048]{4,3,2,1,0:T(8,128)(2,1)S(1)}, bf16[2,1,1,64,2048]{4,3,2,1,0:T(8,128)(2,1)S(1)}, u32[]{:S(2)}, u32[]{:S(2)}) collective-permute-start(bf16[2,1,1,64,2048]{4,3,2,1,0:T(8,128)(2,1)S(1)} %fusion.50), channel_id=1, source_target_pairs={{0,1},{1,0},{2,3},{3,2},{4,5},{5,4},{6,7},{7,6},{8,9},{9,8},{10,11... | collective-permute-start | bytes 1572872 | tf_op jit(solution)/shard_map/down_back/ppermute | solution.py:52
  545.0 29.6 %collective-permute-start.86 = (bf16[144,2048]{1,0:T(8,128)(2,1)S(1)}, bf16[144,2048]{1,0:T(8,128)(2,1)S(1)}, u32[]{:S(2)}, u32[]{:S(2)}) collective-permute-start(bf16[144,2048]{1,0:T(8,128)(2,1)S(1)} %fusion.40), channel_id=1, source_target_pairs={{0,6},{2,0},{4,2},{6,4},{1,7},{3,1},{5,3},{7,5},{8,14},{10,8},{12,... | collective-permute-start | bytes 1769480 | tf_op jit(solution)/shard_map/critical/ppermute | solution.py:188
  546.6 28.0 %collective-permute-start.89 = (bf16[3,1,1,2,1,1,64,512]{7,6,5,4,3,2,1,0:T(8,128)(2,1)S(1)}, bf16[3,1,1,2,1,1,64,512]{7,6,5,4,3,2,1,0:T(8,128)(2,1)S(1)}, u32[]{:S(2)}, u32[]{:S(2)}) collective-permute-start(bf16[3,1,1,2,1,1,64,512]{7,6,5,4,3,2,1,0:T(8,128)(2,1)S(1)} %fusion.73), channel_id=1, source_target_pairs={{0,2},{2,0},{1,3},{3,1},{4,6},{6,4},{5,7},{7,5},{8,10},{10,8},{9,1... | collective-permute-start | bytes 1179656 | tf_op jit(solution)/shard_map/qkv_back/ppermute | solution.py:52
  559.0 33.7 %collective-permute-start.91 = (bf16[1,1,2,2,1,64,2048]{6,5,4,3,2,1,0:T(8,128)(2,1)S(1)}, bf16[1,1,2,2,1,64,2048]{6,5,4,3,2,1,0:T(8,128)(2,1)S(1)}, u32[]{:S(2)}, u32[]{:S(2)}) collective-permute-start(bf16[1,1,2,2,1,64,2048]{6,5,4,3,2,1,0:T(8,128)(2,1)S(1)} %constant_dynamic-slice_fusion.1), channel_id=1, source_target_pairs={{0,1},{1,0},{2,3},{3,2},{4,5},{5,4},{6,7},{7,6},{8,9},{9,8},{10,11... | collective-permute-start | bytes 3145736 | tf_op jit(solution)/shard_map/out_back/ppermute | solution.py:52
  574.9 31.6 %collective-permute-start.100 = (bf16[1,1,1,64,4096]{4,3,2,1,0:T(8,128)(2,1)S(1)}, bf16[1,1,1,64,4096]{4,3,2,1,0:T(8,128)(2,1)S(1)}, u32[]{:S(2)}, u32[]{:S(2)}) collective-permute-start(bf16[1,1,1,64,4096]{4,3,2,1,0:T(8,128)(2,1)S(1)} %fusion.43), channel_id=1, source_target_pairs={{0,8},{8,0},{1,9},{9,1},{2,10},{10,2},{3,11},{11,3},{4,12},{12,4},... | collective-permute-start | bytes 1572872 | tf_op jit(solution)/shard_map/down_back/ppermute | solution.py:52
  (220 other events, 2156.3 us)

commit v5 on v4

--- a/solution.py
+++ b/solution.py
@@ -22,6 +22,30 @@
 FFN_DIMS = ("c", "zl", "y")
 FFN_NEAR = ("y", "zl", "c")
 FFN_REST = ("x", "zh")
+PLAN = {
+    "cot": 6,
+    "up": (0, 1),
+    "down": (1, 1),
+    "up_zh": ((0, 1), (0, 2), (0, 1)),
+    "up_x": ((0, 4),),
+    "up_far": ((0, 4),),
+    "down_zh": ((1, 1), (0, 1), (0, 1), (0, 1)),
+    "down_x": ((2, 2), (1, 2)),
+    "down_far": ((0, 2), (0, 2)),
+    "out": (2, 0, 0, 0),
+    "d_down_far": ((0, 2), (0, 2)),
+    "d_down_zh": ((0, 1), (0, 1), (0, 2)),
+    "d_down_near": ((1, 4),),
+    "d_down_out": (1, 1),
+    "d_up_far": ((0, 2), (0, 2)),
+    "d_up_zh": ((1, 1), (0, 1), (0, 2)),
+    "d_up_near": ((5, 4),),
+    "d_up_out": (0, 0),
+    "act": (0, 0, 3),
+    "d_out": (0, 2, 2, 0),
+    "sums": (0, 0, 0, 0),
+    "qkv": (0, 0, 0, 0),
+}
 BF = jnp.bfloat16
 F32 = jnp.float32
 
@@ -102,13 +126,38 @@
         yield ()
 
 
-def in_pieces(array, axis, *pieces):
-    first, landed = 0, []
-    for piece in pieces:
-        count = array.shape[0] * piece // sum(pieces)
-        landed.append((yield swap(array[first : first + count], axis)))
+class Rows:
+    def __init__(self, whole=None):
+        self.pieces = [] if whole is None else [(0, 4, whole)]
+
+    def add(self, first, count, array):
+        self.pieces.append((first, count, array))
+
+    def take(self, first, count):
+        while not set(range(first, first + count)) <= self.held():
+            yield ()
+        found = []
+        for start, held, array in sorted(self.pieces, key=lambda piece: piece[0]):
+            low, high = max(start, first), min(start + held, first + count)
+            if low < high:
+                step = array.shape[0] // held
+                found.append(array[(low - start) * step : (high - start) * step])
+        return found[0] if len(found) == 1 else jnp.concatenate(found, axis=0)
+
+    def held(self):
+        return {start + i for start, count, _ in self.pieces for i in range(count)}
+
+
+def send_rows(rows, axis, plan, landed, added=None):
+    first = 0
+    for rounds, count in plan:
+        array = yield from rows.take(first, count)
+        yield from pause(rounds)
+        theirs = yield swap(array, axis)
+        if added is not None:
+            theirs = theirs + (yield from added.take(first, count))
+        landed.add(first, count, theirs)
         first += count
-    return landed
 
 
 def one_round(array, axis):
@@ -188,38 +237,50 @@
     return lax.ppermute(array, ("zh", "zl"), [(i, (i + step) % 4) for i in range(4)])
 
 
-def gather_ring(array):
+def gather_ring(array, others):
     if not ring_size():
-        return [lax.all_gather(array, SEQ, axis=0, tiled=True)]
-    along, across = [array], []
-    for step in range(3):
-        coming = ring_shift(along[-1], 1)
-        across.append(swap(along[-1], "y"))
-        if step == 0:
-            coming = yield coming
-        else:
-            coming, across[step - 1] = yield (coming, across[step - 1])
-        along.append(coming)
-    across.append(swap(along[-1], "y"))
-    across[2], across[3] = yield (across[2], across[3])
-    return [jnp.concatenate(blocks, axis=0) for blocks in zip(along, across)]
-
-
-def scatter_ring(blocks):
+        array = lax.all_gather(array, SEQ, axis=0, tiled=True)
+        return jnp.concatenate([array, others], axis=0)
+    rows = array.shape[0]
+
+    def put(joined, block, place):
+        return lax.dynamic_update_slice_in_dim(joined, block, place * rows, 0)
+
+    joined = jnp.zeros((8 * rows + others.shape[0], array.shape[1]), array.dtype)
+    joined = put(put(joined, array, 0), others, 8)
+    across = [swap(array, "y")]
+    along, joined = yield (ring_shift(array, 1), joined)
+    for step in (1, 2):
+        joined = put(joined, along, 2 * step)
+        coming = ring_shift(along, 1)
+        across.append(swap(along, "y"))
+        if step == 2:
+            joined = put(joined, across[0], 1)
+        along, across[step - 1], joined = yield (coming, across[step - 1], joined)
+    joined = put(put(joined, along, 6), across[1], 3)
+    across.append(swap(along, "y"))
+    across[2], across[3], joined = yield (across[2], across[3], joined)
+    return put(put(joined, across[2], 5), across[3], 7)
+
+
+def scatter_ring(block):
     if not ring_size():
-        return lax.psum_scatter(blocks[0], SEQ, scatter_dimension=0, tiled=True)
-    half = blocks[0].shape[0] // 2
-    across = swap(blocks[3][half:], "y")
-    later = swap(blocks[2][half:], "y")
-    across = yield across
-    running = blocks[3][:half] + across
+        return lax.psum_scatter(block(0), SEQ, scatter_dimension=0, tiled=True)
+    last, later = block(3), block(2)
+    half = last.shape[0] // 2
+    across = yield swap(last[half:], "y")
+    running = last[:half] + across
+    across = swap(later[half:], "y")
     for step in (2, 1, 0):
-        across = later
+        here = later[:half]
         coming = ring_shift(running, -1)
         if step:
-            later = swap(blocks[step - 1][half:], "y")
+            later = block(step - 1)
+            across_next = swap(later[half:], "y")
         coming, across = yield (coming, across)
-        running = blocks[step][:half] + across + coming
+        running = here + across + coming
+        if step:
+            across = across_next
     return running
 
 
@@ -232,22 +293,64 @@
 
 
 def columns_of_qkv(weights):
-    array = weights.reshape((3,) + (1,) * len(AXES) + weights.shape[1:])
+    array = weights.reshape((1,) * len(AXES) + weights.shape)
     for axis in SEQ:
-        array = yield from exchange(array, axis, 7, AXES.index(axis) + 1)
+        array = yield from exchange(array, axis, 6, AXES.index(axis))
     for axis in ROWS:
-        array = yield from gather_dim(array, axis, AXES.index(axis) + 1)
-    return array.reshape(3, -1, array.shape[-1])
-
-
-def sums_of_qkv(sums):
+        array = yield from gather_dim(array, axis, AXES.index(axis))
+    return array.reshape(-1, array.shape[-1])
+
+
+def sums_of_cores(sums):
     sizes = tuple(lax.axis_size(axis) for axis in AXES)
-    array = sums.reshape((3,) + sizes + (-1, sums.shape[-1]))
-    for axis in reversed(ROWS):
-        array = yield from scatter_dim(array, axis, AXES.index(axis) + 1)
+    array = sums.reshape(sizes + (-1, sums.shape[-1]))
+    return (yield from scatter_dim(array, "c", AXES.index("c")))
+
+
+def sums_of_qkv(array):
+    array = yield from scatter_dim(array, "x", AXES.index("x"))
     for axis in reversed(SEQ):
-        array = yield from exchange(array, axis, AXES.index(axis) + 1, 7)
-    return array.reshape((3,) + array.shape[-2:])
+        array = yield from exchange(array, axis, AXES.index(axis), 6)
+    return array.reshape(array.shape[-2:])
+
+
+def side_by_side(weights, width):
+    rows, cols = weights[0].shape
+
+    def kernel(*refs):
+        for part, ref in enumerate(refs[:3]):
+            for place in range(cols // width):
+                first = (3 * place + part) * width
+                refs[3][:, first : first + width] = ref[:, place * width : (place + 1) * width]
+
+    vmem = pl.BlockSpec(memory_space=pltpu.VMEM)
+    return pl.pallas_call(
+        kernel,
+        in_specs=[vmem] * 3,
+        out_specs=vmem,
+        out_shape=jax.ShapeDtypeStruct((rows, 3 * cols), weights[0].dtype),
+        compiler_params=pltpu.CompilerParams(vmem_limit_bytes=8 * 2**20),
+    )(*weights)
+
+
+def apart(array, width):
+    rows, cols = array.shape[0], array.shape[1] // 3
+
+    def kernel(ref, *outs):
+        for part, out in enumerate(outs):
+            for place in range(cols // width):
+                first = (3 * place + part) * width
+                block = ref[:, first : first + width].astype(F32)
+                out[:, place * width : (place + 1) * width] = block
+
+    vmem = pl.BlockSpec(memory_space=pltpu.VMEM)
+    return pl.pallas_call(
+        kernel,
+        in_specs=[vmem],
+        out_specs=[vmem] * 3,
+        out_shape=[jax.ShapeDtypeStruct((rows, cols), F32)] * 3,
+        compiler_params=pltpu.CompilerParams(vmem_limit_bytes=12 * 2**20),
+    )(array)
 
 
 def exchange_first(weight):
@@ -343,12 +446,23 @@
     return lax.psum_scatter(sums[:half] + theirs, "zh", scatter_dimension=0, tiled=True)
 
 
-def load_ordered(order_ref, refs, scratches, first=0):
-    shards, _, here, _ = refs[0].shape
-    for place in range(shards):
-        block = order_ref[place]
-        for ref, scratch in zip(refs, scratches):
-            scratch[first + place * here : first + (place + 1) * here, :] = ref[block, 0]
+def load_ordered(segs, order_ref, tokens_ref, q_ref, k_ref, v_ref):
+    length, width = q_ref.shape
+    padded = k_ref.shape[0] - length
+    here, first_sum = length // order_ref.shape[0], segs * length
+    for part, ref in ((1, k_ref), (2, v_ref)):
+        ref[:padded, :] = tokens_ref[first_sum:, part * width : (part + 1) * width]
+    for place in range(order_ref.shape[0]):
+        rows = tokens_ref[rows_of(segs, order_ref, place, here), :]
+        q_ref[place * here : (place + 1) * here, :] = rows[:, :width] * BF(0.125)
+        for part, ref in ((1, k_ref), (2, v_ref)):
+            first = padded + place * here
+            ref[first : first + here, :] = rows[:, part * width : (part + 1) * width]
+
+
+def rows_of(segs, order_ref, place, here):
+    first = (order_ref[place] * segs + pl.program_id(0)) * here
+    return pl.ds(pl.multiple_of(first, 16), here)
 
 
 def block_mask(doc_col_ref, doc_row_ref, pos_row_ref, first, rows, keys):
@@ -376,14 +490,12 @@
 
 
 def forward_kernel(
-    rows, order_ref, doc_col_ref, doc_row_ref, pos_row_ref, q_in, k_in, v_in, sk_ref, sv_ref, out_ref,
+    rows, segs, order_ref, doc_col_ref, doc_row_ref, pos_row_ref, tokens_ref, out_ref,
     q_ref, k_ref, v_ref,
 ):
     shards, _, here, width = out_ref.shape
-    padded = sk_ref.shape[0]
-    k_ref[:padded, :], v_ref[:padded, :] = sk_ref[...], sv_ref[...]
-    load_ordered(order_ref, (q_in,), (q_ref,))
-    load_ordered(order_ref, (k_in, v_in), (k_ref, v_ref), padded)
+    padded = k_ref.shape[0] - shards * here
+    load_ordered(segs, order_ref, tokens_ref, q_ref, k_ref, v_ref)
     heads = heads_of(width)
     for first in range(0, shards * here, rows):
         keys = padded + first + rows
@@ -399,22 +511,18 @@
 
 
 def backward_kernel(
-    rows, order_ref, doc_col_ref, doc_row_ref, pos_row_ref, q_in, k_in, v_in, sk_ref, sv_ref, g_in,
-    dq_out, dk_out, dv_out, dsk_ref, dsv_ref,
-    q_ref, k_ref, v_ref, g_ref, dk_sum, dv_sum,
+    rows, segs, order_ref, doc_col_ref, doc_row_ref, pos_row_ref, tokens_ref, g_in, grads_out,
+    q_ref, k_ref, v_ref, g_ref, dk_sum, dv_sum, sums,
 ):
     shards, _, here, width = g_in.shape
-    padded = sk_ref.shape[0]
-    k_ref[:padded, :], v_ref[:padded, :] = sk_ref[...], sv_ref[...]
-    load_ordered(order_ref, (q_in,), (q_ref,))
-    load_ordered(order_ref, (k_in, v_in), (k_ref, v_ref), padded)
+    padded = sums.shape[0]
+    load_ordered(segs, order_ref, tokens_ref, q_ref, k_ref, v_ref)
     for place in range(shards):
         g_ref[place * here : (place + 1) * here, :] = g_in[place, 0]
 
-    @pl.when(pl.program_id(1) == 0)
+    @pl.when(pl.program_id(0) == 0)
     def _():
-        dsk_ref[...] = jnp.zeros_like(dsk_ref)
-        dsv_ref[...] = jnp.zeros_like(dsv_ref)
+        sums[...] = jnp.zeros_like(sums)
 
     heads = heads_of(width)
     for first in reversed(range(0, shards * here, rows)):
@@ -443,61 +551,63 @@
         d_query = of_heads(d_queries, heads).astype(BF)
         q_ref[first : first + rows, :] = (d_query.astype(F32) * 0.125).astype(BF)
     d_key, d_value = dk_sum[...].T, dv_sum[...].T
-    dsk_ref[...] += d_key[:padded]
-    dsv_ref[...] += d_value[:padded]
+    sums[:, width : 2 * width] += d_key[:padded]
+    sums[:, 2 * width :] += d_value[:padded]
     k_ref[...], v_ref[...] = d_key.astype(BF), d_value.astype(BF)
     for place in range(shards):
-        block = order_ref[place]
-        tokens = slice(place * here, (place + 1) * here)
-        dq_out[block, 0] = q_ref[tokens, :]
+        block = rows_of(segs, order_ref, place, here)
+        grads_out[block, :width] = q_ref[place * here : (place + 1) * here, :]
         tokens = slice(padded + place * here, padded + (place + 1) * here)
-        dk_out[block, 0], dv_out[block, 0] = k_ref[tokens, :], v_ref[tokens, :]
+        grads_out[block, width : 2 * width] = k_ref[tokens, :]
+        grads_out[block, 2 * width :] = v_ref[tokens, :]
+
+    @pl.when(pl.program_id(0) == segs - 1)
+    def _():
+        grads_out[segs * shards * here :, :] = sums[...].astype(BF)
 
 
 def attention_calls(segs, shards, here, width, padded):
-    lanes = min(4 * HEAD, width)
     length = shards * here
     rows = length if length <= 512 else 384
-    grid = (width // lanes, segs)
-    tok = pl.BlockSpec((shards, 1, here, lanes), lambda h, s: (0, s, 0, h))
-    summed = pl.BlockSpec((padded, lanes), lambda h, s: (0, h))
-    row = pl.BlockSpec((1, 1, padded + length), lambda h, s: (s, 0, 0))
+    block = pl.BlockSpec((shards, 1, here, width), lambda s: (0, s, 0, 0))
+    joint_shape = (segs * length + padded, 3 * width)
+    joint = pl.BlockSpec(joint_shape, lambda s: (0, 0))
+    row = pl.BlockSpec((1, 1, padded + length), lambda s: (s, 0, 0))
     docs = [
         pl.BlockSpec(memory_space=pltpu.SMEM),
-        pl.BlockSpec((1, length, 1), lambda h, s: (s, 0, 0)),
+        pl.BlockSpec((1, length, 1), lambda s: (s, 0, 0)),
         row,
         row,
     ]
     params = pltpu.CompilerParams(
-        dimension_semantics=("arbitrary", "arbitrary"), vmem_limit_bytes=24 * 2**20
-    )
-    tokens = jax.ShapeDtypeStruct((shards, segs, here, width), BF)
-    sums = jax.ShapeDtypeStruct((padded, width), F32)
-    queries, keys = pltpu.VMEM((length, lanes), BF), pltpu.VMEM((padded + length, lanes), BF)
-    key_sums = pltpu.VMEM((lanes, padded + length), F32)
+        dimension_semantics=("arbitrary",), vmem_limit_bytes=24 * 2**20
+    )
+    queries, keys = pltpu.VMEM((length, width), BF), pltpu.VMEM((padded + length, width), BF)
+    key_sums = pltpu.VMEM((width, padded + length), F32)
     work = 2 * segs * length * (length // 2 + padded) * width
     forward = pl.pallas_call(
-        functools.partial(forward_kernel, rows),
-        grid=grid,
-        in_specs=docs + [tok] * 3 + [summed] * 2,
-        out_specs=tok,
-        out_shape=tokens,
+        functools.partial(forward_kernel, rows, segs),
+        grid=(segs,),
+        in_specs=docs + [joint],
+        out_specs=block,
+        out_shape=jax.ShapeDtypeStruct((shards, segs, here, width), BF),
         scratch_shapes=[queries, keys, keys],
         compiler_params=params,
         cost_estimate=pl.CostEstimate(
-            flops=120 * work, bytes_accessed=8 * segs * length * width, transcendentals=0
+            flops=60 * work, bytes_accessed=8 * segs * length * width, transcendentals=0
         ),
     )
     backward = pl.pallas_call(
-        functools.partial(backward_kernel, rows),
-        grid=grid,
-        in_specs=docs + [tok] * 3 + [summed] * 2 + [tok],
-        out_specs=[tok] * 3 + [summed] * 2,
-        out_shape=[tokens] * 3 + [sums] * 2,
-        scratch_shapes=[queries, keys, keys, queries, key_sums, key_sums],
+        functools.partial(backward_kernel, rows, segs),
+        grid=(segs,),
+        in_specs=docs + [joint, block],
+        out_specs=joint,
+        out_shape=jax.ShapeDtypeStruct(joint_shape, BF),
+        scratch_shapes=[queries, keys, keys, queries, key_sums, key_sums]
+        + [pltpu.VMEM((padded, 3 * width), F32)],
         compiler_params=params,
         cost_estimate=pl.CostEstimate(
-            flops=160 * work, bytes_accessed=14 * segs * length * width, transcendentals=0
+            flops=90 * work, bytes_accessed=14 * segs * length * width, transcendentals=0
         ),
     )
     return forward, backward
@@ -548,7 +658,7 @@
     split = (shards, segs, here, width)
     block_rows = shards * rows // max(ring_size(), 1)
 
-    box = Box()
+    box = Box(hidden_sum=hidden_sum)
     out = {}
 
     half_sums = -(-sum_rows // 2)
@@ -564,21 +674,15 @@
             lax.dynamic_index_in_dim(in_halves(array), place_y, 0, False)
             for array in (standard_sum, inverse_sum)
         ]
-        ready = yield (doc_args, hidden_sum, sum_parts)
-        box["doc_args"], box["hidden_sum"], box["sum_parts"] = ready
+        box["doc_args"], box["sum_parts"] = yield (doc_args, sum_parts)
 
     def critical():
-        hidden_blocks = yield from gather_ring(hidden)
+        left = yield from gather_ring(hidden, box["hidden_sum"])
         w_qkv = yield from box.wait("w_qkv")
-        doc_args, hidden_sum = box["doc_args"], box["hidden_sum"]
-        def project(weight, scale=1.0):
-            blocks = [(dot(block, weight) * scale).astype(BF) for block in hidden_blocks]
-            return jnp.concatenate(blocks, axis=0).reshape(split)
-
-        operands = [project(w_qkv[0], 0.125), project(w_qkv[1]), project(w_qkv[2])]
-        operands += [dot(hidden_sum, w_qkv[1]).astype(BF), dot(hidden_sum, w_qkv[2]).astype(BF)]
+        doc_args = box["doc_args"]
+        operands = dot(left, w_qkv).astype(BF)
         operands = yield operands
-        attended = yield attend(*doc_args, *operands)
+        attended = yield attend(*doc_args, operands)
 
         attended = attended.reshape(shards, rows, width)
         attended = yield lax.all_to_all(attended, SEQ, 0, 0, tiled=True)
@@ -604,12 +708,10 @@
         near = scatter_plane(grad_normed_part, *FFN_NEAR)
         in_flight = next(near)
         d_w_up = dot(normed_all, grad_upper, 0, 0).astype(BF)
-        in_flight, d_w_up, late_active, blocks = yield (in_flight, d_w_up, active, hidden_blocks)
+        in_flight, d_w_up, late_active = yield (in_flight, d_w_up, active)
         box["d_w_up"] = d_w_up
         ffn_out_part = dot(late_active, w_down_here, 1, 1).astype(BF)
-        left = jnp.concatenate(blocks + [hidden_sum], axis=0)
-        in_flight, ffn_out_part, left = yield (near.send(in_flight), ffn_out_part, left)
-        box["ffn_out_part"] = ffn_out_part
+        in_flight, ffn_out_part = yield (near.send(in_flight), ffn_out_part)
         try:
             near.send(in_flight)
         except StopIteration as end:
@@ -621,100 +723,111 @@
         grad_branch = grad_mixed.astype(BF)
         grad_attended = near_blocks(dot(grad_branch, w_out_all, 1, 1).astype(BF), ROWS)
         grad_attended = grad_attended.reshape(rows, shards, width).swapaxes(0, 1)
+        held = (attended, grad_branch, ffn_out_part, d_w_down, d_w_up)
+        grad_attended, held = lax.optimization_barrier((grad_attended, held))
+        attended, grad_branch, box["ffn_out_part"], box["d_w_down_late"], box["d_w_up_late"] = held
         box["for_out"] = attended, grad_branch
         grad_attended = yield lax.all_to_all(grad_attended, SEQ, 0, 0, tiled=True)
-        grads = yield attend_back(*doc_args, *operands, grad_attended.reshape(split))
+        grads = yield attend_back(*doc_args, operands, grad_attended.reshape(split))
 
         box["F"] = True
-        d_qkv = [part.reshape(shards * rows, width) for part in grads[:3]]
-        d_sums = [part.astype(BF) for part in grads[3:]]
-
-        def grad_block(first):
-            parts = [dot(d[first : first + block_rows], w, 1, 1) for d, w in zip(d_qkv, w_qkv)]
-            return sum(parts).astype(BF)
-
-        grad_hidden_blocks = [grad_block(i) for i in range(0, shards * rows, block_rows)]
-        grad_sum_part = sum(dot(d, w, 1, 1) for d, w in zip(d_sums, w_qkv[1:])).astype(BF)
-        d_w_qkv = [dot(left[: shards * rows], d_qkv[0], 0, 0).astype(BF)]
-        for d, d_sum in zip(d_qkv[1:], d_sums):
-            d_w_qkv.append(dot(left, jnp.concatenate([d, d_sum], axis=0), 0, 0).astype(BF))
-        d_w_qkv = jnp.stack(d_w_qkv)
-        box["sums"] = grad_sum_part
-        scatter = scatter_ring(grad_hidden_blocks)
+        def grad_block(k):
+            rows_of_k = (late or [grads])[0][k * block_rows : (k + 1) * block_rows]
+            return dot(rows_of_k, w_qkv, 1, 1).astype(BF)
+
+        late = []
+        d_w_qkv = yield from sums_of_cores(dot(left, grads, 0, 0).astype(BF))
+        scatter = scatter_ring(grad_block)
         try:
             in_flight = next(scatter)
-            in_flight, d_w_qkv = yield (in_flight, d_w_qkv)
+            in_flight, d_w_qkv, grads = yield (in_flight, d_w_qkv, grads)
+            late.append(grads)
             box["d_w_qkv"] = d_w_qkv
+            box["sums"] = dot(grads[shards * rows :], w_qkv, 1, 1).astype(BF)
             while True:
                 in_flight = yield scatter.send(in_flight)
         except StopIteration as end:
             grad_hidden = end.value.astype(F32)
-        box["d_w_qkv"] = d_w_qkv
+        if not late:
+            box["d_w_qkv"] = d_w_qkv
+            box["sums"] = dot(grads[shards * rows :], w_qkv, 1, 1).astype(BF)
         out["d_tokens"] = grad_mixed + normalize_back(grad_hidden, gain_attn, standard, inverse)
         ffn_out = yield from box.wait("ffn_out")
         ffn_out = near_blocks_back(ffn_out, FFN_REST, ("c",))
         out["activations"] = (mixed + ffn_out.astype(F32)).astype(BF)
 
     def cotangent_rows():
-        yield from pause(5)
+        yield from pause(PLAN["cot"])
         cot_all = yield from gather_plane(near_blocks(cot, FFN_REST, ("c",)), *FFN_NEAR)
         box["cot_all"] = yield cot_all
 
-    def weight_up():
-        part = yield from exchange_first(w_up)
-        yield ()
-        part = yield from exchange_last(part)
-        box["up"] = part
-        far = []
+    def weight(name, shard):
+        part, far, part_x, far_x = Rows(), Rows(), Rows(), Rows()
+
+        def columns():
+            yield from pause(PLAN[name][0])
+            array = yield from exchange_first(shard)
+            yield from pause(PLAN[name][1])
+            array = yield from exchange_last(array)
+            part.add(0, 4, array)
+
+        def all_columns():
+            parts = [(yield from part.take(0, 4))]
+            if lax.axis_size("zh") == 2:
+                parts.append((yield from far.take(0, 4)))
+            parts.append((yield from part_x.take(0, 4)))
+            if lax.axis_size("zh") == 2:
+                parts.append((yield from far_x.take(0, 4)))
+            box["w_" + name] = all_rows(parts)
+
+        threads = {name: columns(), name + "_x": send_rows(part, "x", PLAN[name + "_x"], part_x)}
         if lax.axis_size("zh") == 2:
-            far = [jnp.concatenate((yield from in_pieces(part, "zh", 1, 2, 1)), axis=0)]
-            far.append((yield swap(far[0], "x")))
-        part_x = yield from box.wait("up_x")
-        box["w_up"] = yield all_rows([part] + far[:1] + [part_x] + far[1:])
-
-    def weight_up_x():
-        part = yield from box.wait("up")
-        half = part.shape[0] // 2
-        low = yield swap(part[:half], "x")
-        yield ()
-        high = yield swap(part[half:], "x")
-        box["up_x"] = jnp.concatenate([low, high], axis=0)
-
-    def weight_down():
-        yield ()
-        part = yield from exchange_first(w_down)
-        yield ()
-        part = yield from exchange_last(part)
-        box["down"] = part
-        yield from pause(2)
-        far = far_x = []
+            threads[name + "_zh"] = send_rows(part, "zh", PLAN[name + "_zh"], far)
+            threads[name + "_far"] = send_rows(far, "x", PLAN[name + "_far"], far_x)
+        threads[name + "_all"] = all_columns()
+        return threads
+
+    def weight_sums(name):
+        sent, own, near, far, landed, sent_near = (Rows() for _ in range(6))
+
+        def start():
+            sums = yield from box.wait("d_w_" + name)
+            sent.add(0, 4, part_of(sums, 1, 1))
+            own.add(0, 4, part_of(sums, 0, 1))
+            sums = yield from box.wait("d_w_" + name + "_late")
+            sent_near.add(0, 4, part_of(sums, 1, 0))
+
+        def all_sums():
+            sums = yield from box.wait("d_w_" + name + "_late")
+            if lax.axis_size("zh") != 2:
+                array = yield from sums_over_all_zh(sums)
+            else:
+                array = part_of(sums, 0, 0) + (yield from near.take(0, 4))
+                array = array + (yield from landed.take(0, 4))
+            waits = PLAN["d_" + name + "_out"]
+            yield from pause(waits[0])
+            array = yield from sums_of_ffn(array, waits[1])
+            out["d_w_" + name] = array.astype(F32)
+
+        threads = {"d_" + name: start()}
         if lax.axis_size("zh") == 2:
-            step = part.shape[0] // 4
-            low = yield swap(part[: 2 * step], "zh")
-            third, low_x = yield (swap(part[2 * step : 3 * step], "zh"), swap(low, "x"))
-            fourth = yield swap(part[3 * step :], "zh")
-            high = jnp.concatenate([third, fourth], axis=0)
-            high_x = yield swap(high, "x")
-            far, far_x = [low, high], [low_x, high_x]
-        part_x = yield from box.wait("down_x")
-        box["w_down"] = all_rows([part, *far, part_x, *far_x])
-
-    def weight_down_x():
-        part = yield from box.wait("down")
-        yield from pause(2)
-        half = part.shape[0] // 2
-        low = yield swap(part[:half], "x")
-        yield ()
-        high = yield swap(part[half:], "x")
-        box["down_x"] = jnp.concatenate([low, high], axis=0)
+            plans = {step: PLAN["d_" + name + "_" + step] for step in ("far", "zh", "near")}
+            threads["d_" + name + "_far"] = send_rows(sent, "x", plans["far"], far, own)
+            threads["d_" + name + "_zh"] = send_rows(far, "zh", plans["zh"], landed)
+            threads["d_" + name + "_near"] = send_rows(sent_near, "x", plans["near"], near)
+        threads["d_" + name + "_all"] = all_sums()
+        return threads
 
     def weight_out():
-        yield from pause(2)
+        waits = PLAN["out"]
         array = w_out.reshape((1,) * len(AXES) + w_out.shape)
-        for axis in ("zh", "zl"):
+        for rounds, axis in zip(waits, ("zh", "zl")):
+            yield from pause(rounds)
             array = yield from gather_dim(array, axis, AXES.index(axis))
+        yield from pause(waits[2])
         half = array.shape[-1] // 2
         by_x, by_y = yield (swap(array, "x"), swap(array, "y"))
+        yield from pause(waits[3])
         low, high = yield (swap(by_y[..., :half], "x"), swap(by_x[..., half:], "y"))
         both = jnp.concatenate([low, high], axis=-1)
         dim_y = AXES.index("y")
@@ -728,70 +841,43 @@
         half = model // 2
         far = dot(attended[:, half:], grad_branch, 0, 0).astype(BF)
         far = far[: half // 2] + swap(far[half // 2 :], "c")
+        waits = PLAN["d_out"]
+        yield from pause(waits[0])
         low = yield swap(far[: half // 4], "x")
         near = dot(attended[:, :half], grad_branch, 0, 0).astype(BF)
         near = near[: half // 2] + swap(near[half // 2 :], "c")
         near = yield near
+        yield from pause(waits[1] - 1)
         high = yield swap(far[half // 4 :], "x")
         array = near + jnp.concatenate([low, high], axis=0)
         seq_sizes = tuple(lax.axis_size(axis) for axis in SEQ)
         array = array.reshape((1, 1) + seq_sizes + (shard_rows, model))
-        yield from pause(3)
+        yield from pause(waits[2])
         array = yield from scatter_dim(array, "y", AXES.index("y"))
+        yield from pause(waits[3])
         array = yield from scatter_line(array[0, 0])
         out["d_w_out"] = array.reshape(shard_rows, model).astype(F32)
 
-    def down_back():
-        sums = yield from box.wait("d_w_down")
-        if lax.axis_size("zh") != 2:
-            array = yield from sums_over_all_zh(sums)
-        else:
-            far, sent = part_of(sums, 0, 1), part_of(sums, 1, 1)
-            near = part_of(sums, 1, 0)
-            half = far.shape[0] // 2
-            step = half // 2
-            low = (yield swap(sent[:half], "x")) + far[:half]
-            first, high = yield (swap(low[:step], "zh"), swap(sent[half:], "x"))
-            high = high + far[half:]
-            second = yield swap(low[step:], "zh")
-            third = yield swap(high, "zh")
-            near = yield swap(near, "x")
-            far = jnp.concatenate([first, second, third], axis=0)
-            array = part_of(sums, 0, 0) + near + far
-        array = yield from sums_of_ffn(array, 2)
-        out["d_w_down"] = array.astype(F32)
-
-    def up_back():
-        sums = yield from box.wait("d_w_up")
-        if lax.axis_size("zh") != 2:
-            array = yield from sums_over_all_zh(sums)
-        else:
-            far, sent = part_of(sums, 0, 1), part_of(sums, 1, 1)
-            near = part_of(sums, 1, 0)
-            far = far + jnp.concatenate((yield from in_pieces(sent, "x", 1, 1)), axis=0)
-            pieces = yield from in_pieces(far, "zh", 1, 2, 1)
-            near = yield swap(near, "x")
-            array = part_of(sums, 0, 0) + near + jnp.concatenate(pieces, axis=0)
-            yield ()
-        array = yield from sums_of_ffn(array)
-        out["d_w_up"] = array.astype(F32)
-
     def activations_back():
         part = yield from box.wait("ffn_out_part")
+        waits = PLAN["act"]
+        yield from pause(waits[0])
         part = yield from scatter_plane(part, *FFN_NEAR)
-        yield from pause(3)
+        yield from pause(waits[2])
         box["ffn_out"] = yield part
 
     def qkv_back():
         array = yield from box.wait("d_w_qkv")
         array = yield from sums_of_qkv(array)
-        out["d_w_query"], out["d_w_key"], out["d_w_value"] = array.astype(F32)
+        out["d_w_query"], out["d_w_key"], out["d_w_value"] = apart(array, width)
 
     def sums_back():
         grad_sum_part = yield from box.wait("sums")
-        yield ()
+        waits = PLAN["sums"]
+        yield from pause(waits[0])
         array = yield from scatter_dim(in_halves(grad_sum_part), "y", 0)
-        for axis in ("zl", "zh"):
+        for rounds, axis in zip(waits[1:], ("zl", "zh")):
+            yield from pause(rounds)
             if lax.axis_size(axis) == 2:
                 theirs = yield swap(array, axis)
                 array = array + theirs
@@ -800,23 +886,22 @@
         grad_sum = array[0].astype(F32)
         standard_part, inverse_part = box["sum_parts"]
         part = normalize_back(grad_sum, gain_attn, standard_part, inverse_part).astype(BF)
+        yield from pause(waits[3])
         theirs = yield swap(part, "y")
         part = pair(part[None], theirs[None], "y", 0).reshape(2 * half_sums, model)
         out["d_summary"] = part[:sum_rows].astype(F32)
 
     together(
         ready_early=ready_early(),
-        weight_qkv=box.put("w_qkv", columns_of_qkv(jnp.stack([w_query, w_key, w_value]))),
-        weight_up=weight_up(),
-        weight_up_x=weight_up_x(),
-        weight_down=weight_down(),
-        weight_down_x=weight_down_x(),
+        weight_qkv=box.put("w_qkv", columns_of_qkv(side_by_side((w_query, w_key, w_value), width))),
+        **weight("up", w_up),
+        **weight("down", w_down),
         weight_out=weight_out(),
         cotangent_rows=cotangent_rows(),
         critical=critical(),
         out_back=out_back(),
-        down_back=down_back(),
-        up_back=up_back(),
+        **weight_sums("down"),
+        **weight_sums("up"),
         activations_back=activations_back(),
         sums_back=sums_back(),
         qkv_back=qkv_back(),

time: 634 us -> 615 us (0.970)
  starting transfers between devices: 103 us -> 115 us
  matrix products: 78 us -> 68.2 us
  other arithmetic: 84.5 us -> 75.9 us
  waiting for transfers between devices: 258 us -> 251 us
    unnamed x330 -> x205, local copies, waits for them, and re-layouts: 35.4 us -> 17 us
    dynamic_update_slice x0 -> x8, local copies, waits for them, and re-layouts: none -> 11.1 us  [put(): return lax.dynamic_update_slice_in_dim(joined, block, place * rows, 0)]
    dot_general x41 -> x17, matrix products: 78 us -> 68.2 us  [dot(): lax.dot_general(left, right, (((left_dim,), (right_dim,)), ((), ())), pre...]
    all_to_all x1, waiting for transfers between devices: 7.94 us -> 0.01 us  [critical(): attended = (yield lax.all_to_all(attended, SEQ, 0, 0, tiled=True))]
    ppermute x92, waiting for transfers between devices: 222 us -> 229 us  [swap(): return lax.ppermute(array, axis, [(0, 1), (1, 0)])]
    pallas_call x2 -> x4, Pallas kernels: 19.3 us -> 19.8 us  [the longest x1 11.4 us: critical(): attend_back(*doc_args, operands, grad_attended.reshape(split))]
  transfers between devices with their start and end apart: 103 -> 103, of which waited for: 40 -> 42; matrix products, arithmetic and copies ran while one was open for 33% -> 30% of each run, Pallas kernels for 4% -> 4%
where the time goes in v5:
time: 615 us; the launch traced here: 606 us
  waiting for transfers between devices  251 us (41%)
  starting transfers between devices  115 us (19%)
  other arithmetic  75.9 us (12%)
  local copies, waits for them, and re-layouts  68.9 us (11%)
  matrix products  68.2 us (11%)
  Pallas kernels  23.4 us (4%)
    ppermute x92, waiting for transfers between devices, swap(): return lax.ppermute(array, axis, [(0, 1), (1, 0)])  229 us
    ppermute x92, starting transfers between devices, swap(): return lax.ppermute(array, axis, [(0, 1), (1, 0)])  84.9 us
    dot_general x17, matrix products, dot(): lax.dot_general(left, right, (((left_dim,), (right_dim,)), ((), ())), pre...  68.2 us
    unnamed x205, local copies, waits for them, and re-layouts  17 us
    ppermute x6, starting transfers between devices, ring_shift(): lax.ppermute(array, ('zh', 'zl'), [(i, (i + step) % 4) for i in range(4)])  15 us
  transfers between devices with their start and end apart: 103, of which 42 were waited for; matrix products, arithmetic and copies ran while one was open for 30% of the time, Pallas kernels for 4%

profile of v5, /device:TPU:0, one launch (start us, length us, event | category | flops | bytes accessed | tf_op | source)
XLA Modules:
  0.0 606.4 jit_solution(7799506775318090456)
XLA Ops:
  33.6 12.5 %collective-permute-done.5 = bf16[1,1,1,1,1,64,3072]{6,5,4,3,2,1,0:T(8,128)(2,1)} collective-permute-done((bf16[1,1,1,1,1,64,3072]{6,5,4,3,2,1,0:T(8,128)(2,1)}, bf16[1,1,1,1,1,64,3072]{6,5,4,3,2,1,0:T(8,128)(2,1)}, u32[]{:S(2)}, u32[]{:S(2)}) %collective-permute-start.5) | collective-permute-done | bytes 393248 | tf_op jit(solution)/shard_map/weight_qkv/ppermute | solution.py:76
  54.5 6.4 %collective-permute-done.9 = bf16[2,1,1,64,2048]{4,3,2,1,0:T(8,128)(2,1)S(1)} collective-permute-done((bf16[2,1,1,64,2048]{4,3,2,1,0:T(8,128)(2,1)S(1)}, bf16[2,1,1,64,2048]{4,3,2,1,0:T(8,128)(2,1)S(1)}, u32[]{:S(2)}, u32[]{:S(2)}) %collective-permute-start.9) | collective-permute-done | bytes 524320 | tf_op jit(solution)/shard_map/down/ppermute | solution.py:76
  60.9 11.6 %collective-permute-done.10 = bf16[1,1,2,1,1,64,1536]{6,5,4,3,2,1,0:T(8,128)(2,1)S(1)} collective-permute-done((bf16[1,1,2,1,1,64,1536]{6,5,4,3,2,1,0:T(8,128)(2,1)S(1)}, bf16[1,1,2,1,1,64,1536]{6,5,4,3,2,1,0:T(8,128)(2,1)S(1)}, u32[]{:S(2)}, u32[]{:S(2)}) %collective-permute-start.10) | collective-permute-done | bytes 393248 | tf_op jit(solution)/shard_map/weight_qkv/ppermute | solution.py:76
  82.8 12.2 %collective-permute-done.14 = bf16[2,1,2,64,1024]{4,3,2,1,0:T(8,128)(2,1)} collective-permute-done((bf16[2,1,2,64,1024]{4,3,2,1,0:T(8,128)(2,1)}, bf16[2,1,2,64,1024]{4,3,2,1,0:T(8,128)(2,1)}, u32[]{:S(2)}, u32[]{:S(2)}) %collective-permute-start.14) | collective-permute-done | bytes 524320 | tf_op jit(solution)/shard_map/up/ppermute | solution.py:76
  104.5 5.5 collective-permute-done.18
  114.9 27.7 %collective-permute-done.20 = bf16[128,1024]{1,0:T(8,128)(2,1)S(1)} collective-permute-done((bf16[128,1024]{1,0:T(8,128)(2,1)S(1)}, bf16[128,1024]{1,0:T(8,128)(2,1)S(1)}, u32[]{:S(2)}, u32[]{:S(2)}) %collective-permute-start.20) | collective-permute-done | bytes 262176 | tf_op jit(solution)/shard_map/up_zh/ppermute | solution.py:76
  155.5 8.6 %collective-permute-done.24 = bf16[256,1024]{1,0:T(8,128)(2,1)S(1)} collective-permute-done((bf16[256,1024]{1,0:T(8,128)(2,1)S(1)}, bf16[256,1024]{1,0:T(8,128)(2,1)S(1)}, u32[]{:S(2)}, u32[]{:S(2)}) %collective-permute-start.24) | collective-permute-done | bytes 524320 | tf_op jit(solution)/shard_map/up_zh/ppermute | solution.py:76
  164.0 7.7 %collective-permute-done.25 = bf16[1,1,2,2,1,64,2048]{6,5,4,3,2,1,0:T(8,128)(2,1)S(1)} collective-permute-done((bf16[1,1,2,2,1,64,2048]{6,5,4,3,2,1,0:T(8,128)(2,1)S(1)}, bf16[1,1,2,2,1,64,2048]{6,5,4,3,2,1,0:T(8,128)(2,1)S(1)}, u32[]{:S(2)}, u32[]{:S(2)}) %collective-permute-start.25) | collective-permute-done | bytes 1048608 | tf_op jit(solution)/shard_map/weight_out/ppermute | solution.py:76
  175.6 7.1 %critical.7 = bf16[8,3,48,256]{3,2,1,0:T(8,128)(2,1)} custom-call(s32[8]{0:T(128)S(1)} %fusion.62.order_ref, s32[3,384,1]{2,1,0:T(8,128)S(1)} %copy.42.doc_col_ref, s32[3,1,512]{2,1,0:T(1,128)S(1)} %broadcast_in_dim.20.doc_row_ref, s32[3,1,512]{2,1,0:T(1,128)S(1)} %broadcast_in_dim.24.pos_row_ref, bf16[1280,768]{1,0:T(8,128)(2,1)S(1)} %convolution_convert_fusion.7.tokens_ref), custom_call_target="tpu_custom_call" | custom-call | flops 11324620800 | bytes 2359296 | tf_op jit(solution)/shard_map/critical/pallas_call | solution.py:685
  203.7 7.0 %pad_maximum_fusion = bf16[2048,2048]{1,0:T(8,128)(2,1)} fusion(bf16[512,2048]{1,0:T(8,128)(2,1)} %collective-permute-done.35, bf16[512,2048]{1,0:T(8,128)(2,1)} %bitcast.30, bf16[512,2048]{1,0:T(8,128)(2,1)} %collective-permute-done.34, bf16[512,2048]{1,0:T(8,128)(2,1)} %bitcast.29), kind=kLoop, calls=%fused_computation | loop fusion | flops 33554432 | bytes 16777216 | tf_op jit(solution)/shard_map/weight_out/concatenate | solution.py:837
  210.7 6.7 %collective-permute-done = bf16[144,2048]{1,0:T(8,128)(2,1)} collective-permute-done((bf16[144,2048]{1,0:T(8,128)(2,1)S(1)}, bf16[144,2048]{1,0:T(8,128)(2,1)}, u32[]{:S(2)}, u32[]{:S(2)}) %collective-permute-start) | collective-permute-done | bytes 589856 | tf_op jit(solution)/shard_map/cotangent_rows/ppermute | solution.py:76
  219.8 7.9 %collective-permute-done.1 = bf16[144,2048]{1,0:T(8,128)(2,1)} collective-permute-done((bf16[144,2048]{1,0:T(8,128)(2,1)S(1)}, bf16[144,2048]{1,0:T(8,128)(2,1)}, u32[]{:S(2)}, u32[]{:S(2)}) %collective-permute-start.1) | collective-permute-done | bytes 589856 | tf_op jit(solution)/shard_map/cotangent_rows/ppermute | solution.py:76
  230.3 5.2 fusion.78
  246.7 12.6 %collective-permute-done.37 = bf16[64,2048]{1,0:T(8,128)(2,1)S(1)} collective-permute-done((bf16[64,2048]{1,0:T(8,128)(2,1)S(1)}, bf16[64,2048]{1,0:T(8,128)(2,1)S(1)}, u32[]{:S(2)}, u32[]{:S(2)}) %collective-permute-start.37) | collective-permute-done | bytes 262176 | tf_op jit(solution)/shard_map/cotangent_rows/ppermute | solution.py:76
  264.3 10.6 %collective-permute-done.46 = bf16[128,1024]{1,0:T(8,128)(2,1)S(1)} collective-permute-done((bf16[128,1024]{1,0:T(8,128)(2,1)S(1)}, bf16[128,1024]{1,0:T(8,128)(2,1)S(1)}, u32[]{:S(2)}, u32[]{:S(2)}) %collective-permute-start.46) | collective-permute-done | bytes 262176 | tf_op jit(solution)/shard_map/down_zh/ppermute | solution.py:76
  281.8 6.5 %fusion.3 = (f32[1152,1024]{1,0:T(8,128)S(1)}, bf16[1152,1024]{1,0:T(8,128)(2,1)S(1)}) fusion(bf16[1152,2048]{1,0:T(8,128)(2,1)S(1)} %constant_dynamic-update-slice_fusion.18, bf16[2048,1024]{1,0:T(8,128)(2,1)S(1)} %constant_dynamic-update-slice_fusion.24), kind=kOutput, calls=%fused_computation.7 | convolution fusion | flops 4843634688 | bytes 15990784 | tf_op jit(solution)/shard_map/critical/dot_general | solution.py:54
  288.3 6.4 %convolution_convert_fusion.5 = bf16[2048,1024]{1,0:T(8,128)(2,1)S(1)} fusion(bf16[1152,2048]{1,0:T(8,128)(2,1)S(1)} %constant_dynamic-update-slice_fusion.7, bf16[1152,1024]{1,0:T(8,128)(2,1)S(1)} %get-tuple-element.199), kind=kOutput, calls=%fused_computation.14 | convolution fusion | flops 4833935360 | bytes 11272192 | tf_op jit(solution)/shard_map/critical/dot_general | solution.py:54
  302.2 5.4 convolution_convert_fusion.1
  307.6 6.5 %collective-permute-done.49 = bf16[256,1024]{1,0:T(8,128)(2,1)S(1)} collective-permute-done((bf16[256,1024]{1,0:T(8,128)(2,1)S(1)}, bf16[256,1024]{1,0:T(8,128)(2,1)S(1)}, u32[]{:S(2)}, u32[]{:S(2)}) %collective-permute-start.49) | collective-permute-done | bytes 524320 | tf_op jit(solution)/shard_map/d_down_far/ppermute | solution.py:76
  324.0 8.4 %convolution_convert_fusion.4 = bf16[2048,1024]{1,0:T(8,128)(2,1)S(1)} fusion(bf16[1152,2048]{1,0:T(8,128)(2,1)} %copy-done.75, bf16[1152,1024]{1,0:T(8,128)(2,1)S(1)} %copy-done.39), kind=kOutput, calls=%fused_computation.13 | convolution fusion | flops 4833935360 | bytes 11272192 | tf_op jit(solution)/shard_map/critical/dot_general | solution.py:54
  341.5 5.4 convolution_convert_fusion
  347.2 6.3 %collective-permute-done.58 = bf16[256,1024]{1,0:T(8,128)(2,1)S(1)} collective-permute-done((bf16[256,1024]{1,0:T(8,128)(2,1)S(1)}, bf16[256,1024]{1,0:T(8,128)(2,1)S(1)}, u32[]{:S(2)}, u32[]{:S(2)}) %collective-permute-start.58) | collective-permute-done | bytes 524320 | tf_op jit(solution)/shard_map/d_up_far/ppermute | solution.py:76
  426.9 11.4 %critical.12 = bf16[1280,768]{1,0:T(8,128)(2,1)S(1)} custom-call(s32[8]{0:T(128)S(1)} %fusion.62.order_ref, s32[3,384,1]{2,1,0:T(8,128)S(1)} %copy.42.doc_col_ref, s32[3,1,512]{2,1,0:T(1,128)S(1)} %broadcast_in_dim.20.doc_row_ref, s32[3,1,512]{2,1,0:T(1,128)S(1)} %broadcast_in_dim.24.pos_row_ref, bf16[1280,768]{1,0:T(8,128)(2,1)S(1)} %copy-done.9, ...), custom_call_target="tpu_custom_call" | custom-call | flops 16986931200 | bytes 4128768 | tf_op jit(solution)/shard_map/critical/pallas_call | solution.py:731
  442.3 7.4 %convolution_convert_fusion.6 = bf16[2048,768]{1,0:T(8,128)(2,1)S(1)} fusion(bf16[1280,2048]{1,0:T(8,128)(2,1)} %copy-done.27, bf16[1280,768]{1,0:T(8,128)(2,1)S(1)} %critical.12), kind=kOutput, calls=%fused_computation.15 | convolution fusion | flops 4028104704 | bytes 10354688 | tf_op jit(solution)/shard_map/critical/dot_general | solution.py:54
  488.6 9.7 %collective-permute-done.76 = bf16[2,1,2,64,1024]{4,3,2,1,0:T(8,128)(2,1)S(1)} collective-permute-done((bf16[2,1,2,64,1024]{4,3,2,1,0:T(8,128)(2,1)}, bf16[2,1,2,64,1024]{4,3,2,1,0:T(8,128)(2,1)S(1)}, u32[]{:S(2)}, u32[]{:S(2)}) %collective-permute-start.76) | collective-permute-done | bytes 524320 | tf_op jit(solution)/shard_map/d_down_all/ppermute | solution.py:76
  508.2 7.9 %collective-permute-done.82 = bf16[144,2048]{1,0:T(8,128)(2,1)S(1)} collective-permute-done((bf16[144,2048]{1,0:T(8,128)(2,1)S(1)}, bf16[144,2048]{1,0:T(8,128)(2,1)S(1)}, u32[]{:S(2)}, u32[]{:S(2)}) %collective-permute-start.82) | collective-permute-done | bytes 589856 | tf_op jit(solution)/shard_map/critical/ppermute | solution.py:76
  518.1 6.4 %collective-permute-done.83 = bf16[1,1,2,2,1,64,768]{6,5,4,3,2,1,0:T(8,128)(2,1)S(1)} collective-permute-done((bf16[1,1,2,2,1,64,768]{6,5,4,3,2,1,0:T(8,128)(2,1)S(1)}, bf16[1,1,2,2,1,64,768]{6,5,4,3,2,1,0:T(8,128)(2,1)S(1)}, u32[]{:S(2)}, u32[]{:S(2)}) %collective-permute-start.83) | collective-permute-done | bytes 393248 | tf_op jit(solution)/shard_map/qkv_back/ppermute | solution.py:76
  531.4 5.8 collective-permute-done.86
  538.6 9.8 %collective-permute-done.87 = bf16[2,1,1,64,2048]{4,3,2,1,0:T(8,128)(2,1)S(1)} collective-permute-done((bf16[2,1,1,64,2048]{4,3,2,1,0:T(8,128)(2,1)S(1)}, bf16[2,1,1,64,2048]{4,3,2,1,0:T(8,128)(2,1)S(1)}, u32[]{:S(2)}, u32[]{:S(2)}) %collective-permute-start.87) | collective-permute-done | bytes 524320 | tf_op jit(solution)/shard_map/d_down_all/ppermute | solution.py:76
  563.3 7.5 %collective-permute-done.92 = bf16[1,1,2,2,1,64,2048]{6,5,4,3,2,1,0:T(8,128)(2,1)S(1)} collective-permute-done((bf16[1,1,2,2,1,64,2048]{6,5,4,3,2,1,0:T(8,128)(2,1)S(1)}, bf16[1,1,2,2,1,64,2048]{6,5,4,3,2,1,0:T(8,128)(2,1)S(1)}, u32[]{:S(2)}, u32[]{:S(2)}) %collective-permute-start.92) | collective-permute-done | bytes 1048608 | tf_op jit(solution)/shard_map/out_back/ppermute | solution.py:76
  575.0 6.3 %collective-permute-start.97 = (bf16[1,64,2048]{2,1,0:T(8,128)(2,1)S(1)}, bf16[1,64,2048]{2,1,0:T(8,128)(2,1)S(1)}, u32[]{:S(2)}, u32[]{:S(2)}) collective-permute-start(bf16[1,64,2048]{2,1,0:T(8,128)(2,1)S(1)} %get-tuple-element.357), channel_id=1, source_target_pairs={{0,4},{2,6},{4,0},{6,2},{1,5},{3,7},{5,1},{7,3},{8,12},{10,14},{12... | collective-permute-start | bytes 786440 | tf_op jit(solution)/shard_map/out_back/ppermute | solution.py:222
  587.9 11.9 %collective-permute-done.97 = bf16[1,64,2048]{2,1,0:T(8,128)(2,1)S(1)} collective-permute-done((bf16[1,64,2048]{2,1,0:T(8,128)(2,1)S(1)}, bf16[1,64,2048]{2,1,0:T(8,128)(2,1)S(1)}, u32[]{:S(2)}, u32[]{:S(2)}) %collective-permute-start.97) | collective-permute-done | bytes 262176 | tf_op jit(solution)/shard_map/out_back/ppermute | solution.py:222
  (608 shorter events, 325.0 us)
Async XLA Ops:
  5.1 42.6 %collective-permute-start.2 = (bf16[144,2048]{1,0:T(8,128)(2,1)S(1)}, bf16[144,2048]{1,0:T(8,128)(2,1)}, u32[]{:S(2)}, u32[]{:S(2)}) collective-permute-start(bf16[144,2048]{1,0:T(8,128)(2,1)S(1)} %multiply_convert_fusion.3), channel_id=1, source_target_pairs={{0,2},{2,4},{4,6},{6,0},{1,3},{3,5},{5,7},{7,1},{8,10},{10,12},{12... | collective-permute-start | bytes 1769480 | tf_op jit(solution)/shard_map/critical/ppermute | solution.py:237
  8.2 45.9 %collective-permute-start.7 = (bf16[144,2048]{1,0:T(8,128)(2,1)S(1)}, bf16[144,2048]{1,0:T(8,128)(2,1)}, u32[]{:S(2)}, u32[]{:S(2)}) collective-permute-start(bf16[144,2048]{1,0:T(8,128)(2,1)S(1)} %multiply_convert_fusion.3), channel_id=1, source_target_pairs={{0,1},{1,0},{2,3},{3,2},{4,5},{5,4},{6,7},{7,6},{8,9},{9,8},{10,11... | collective-permute-start | bytes 1769480 | tf_op jit(solution)/shard_map/critical/ppermute | solution.py:76
  11.4 34.8 %collective-permute-start.5 = (bf16[1,1,1,1,1,64,3072]{6,5,4,3,2,1,0:T(8,128)(2,1)}, bf16[1,1,1,1,1,64,3072]{6,5,4,3,2,1,0:T(8,128)(2,1)}, u32[]{:S(2)}, u32[]{:S(2)}) collective-permute-start(bf16[1,1,1,1,1,64,3072]{6,5,4,3,2,1,0:T(8,128)(2,1)} %dynamic-slice_bitcast_fusion.3), channel_id=1, source_target_pairs={{0,4},{4,0},{1,5},{5,1},{2,6},{6,2},{3,7},{7,3},{8,12},{12,8},{9,1... | collective-permute-start | bytes 1179656 | tf_op jit(solution)/shard_map/weight_qkv/ppermute | solution.py:76
  30.0 51.3 %collective-permute-start.15 = (bf16[1,1,1,1,1,64,2048]{6,5,4,3,2,1,0:T(8,128)(2,1)}, bf16[1,1,1,1,1,64,2048]{6,5,4,3,2,1,0:T(8,128)(2,1)}, u32[]{:S(2)}, u32[]{:S(2)}) collective-permute-start(bf16[1,1,1,1,1,64,2048]{6,5,4,3,2,1,0:T(8,128)(2,1)} %bitcast.23), channel_id=1, source_target_pairs={{0,4},{4,0},{1,5},{5,1},{2,6},{6,2},{3,7},{7,3},{8,12},{12,8},{9,1... | collective-permute-start | bytes 786440 | tf_op jit(solution)/shard_map/weight_out/ppermute | solution.py:76
  54.0 40.9 %collective-permute-start.13 = (bf16[144,2048]{1,0:T(8,128)(2,1)}, bf16[144,2048]{1,0:T(8,128)(2,1)}, u32[]{:S(2)}, u32[]{:S(2)}) collective-permute-start(bf16[144,2048]{1,0:T(8,128)(2,1)} %collective-permute-done.2), channel_id=1, source_target_pairs={{0,1},{1,0},{2,3},{3,2},{4,5},{5,4},{6,7},{7,6},{8,9},{9,8},{10,11... | collective-permute-start | bytes 1769480 | tf_op jit(solution)/shard_map/critical/ppermute | solution.py:76
  60.9 34.0 %collective-permute-start.14 = (bf16[2,1,2,64,1024]{4,3,2,1,0:T(8,128)(2,1)}, bf16[2,1,2,64,1024]{4,3,2,1,0:T(8,128)(2,1)}, u32[]{:S(2)}, u32[]{:S(2)}) collective-permute-start(bf16[2,1,2,64,1024]{4,3,2,1,0:T(8,128)(2,1)} %fusion.28), channel_id=1, source_target_pairs={{0,2},{2,0},{1,3},{3,1},{4,6},{6,4},{5,7},{7,5},{8,10},{10,8},{9,1... | collective-permute-start | bytes 1572872 | tf_op jit(solution)/shard_map/up/ppermute | solution.py:76
  81.3 31.3 %collective-permute-start.11 = (bf16[144,2048]{1,0:T(8,128)(2,1)}, bf16[144,2048]{1,0:T(8,128)(2,1)S(1)}, u32[]{:S(2)}, u32[]{:S(2)}) collective-permute-start(bf16[144,2048]{1,0:T(8,128)(2,1)} %collective-permute-done.6), channel_id=1, source_target_pairs={{0,1},{1,0},{2,3},{3,2},{4,5},{5,4},{6,7},{7,6},{8,9},{9,8},{10,11... | collective-permute-start | bytes 1769480 | tf_op jit(solution)/shard_map/critical/ppermute | solution.py:76
  99.8 45.8 %collective-permute-start.22 = (bf16[1,1,2,2,2,64,768]{6,5,4,3,2,1,0:T(8,128)(2,1)S(1)}, bf16[1,1,2,2,2,64,768]{6,5,4,3,2,1,0:T(8,128)(2,1)S(1)}, u32[]{:S(2)}, u32[]{:S(2)}) collective-permute-start(bf16[1,1,2,2,2,64,768]{6,5,4,3,2,1,0:T(8,128)(2,1)S(1)} %pad_maximum_fusion.9), channel_id=1, source_target_pairs={{0,16},{16,0},{1,17},{17,1},{2,18},{18,2},{3,19},{19,3},{4,20},{20... | collective-permute-start | bytes 2359304 | tf_op jit(solution)/shard_map/weight_qkv/ppermute | solution.py:76
  102.7 42.9 %collective-permute-start.19 = (bf16[512,1024]{1,0:T(8,128)(2,1)S(1)}, bf16[512,1024]{1,0:T(8,128)(2,1)}, u32[]{:S(2)}, u32[]{:S(2)}) collective-permute-start(bf16[512,1024]{1,0:T(8,128)(2,1)S(1)} %bitcast.166), channel_id=1, source_target_pairs={{0,16},{16,0},{1,17},{17,1},{2,18},{18,2},{3,19},{19,3},{4,20},{20... | collective-permute-start | bytes 3145736 | tf_op jit(solution)/shard_map/up_x/ppermute | solution.py:76
  104.4 38.2 %collective-permute-start.21 = (bf16[1,1,2,1,1,64,2048]{6,5,4,3,2,1,0:T(8,128)(2,1)S(1)}, bf16[1,1,2,1,1,64,2048]{6,5,4,3,2,1,0:T(8,128)(2,1)S(1)}, u32[]{:S(2)}, u32[]{:S(2)}) collective-permute-start(bf16[1,1,2,1,1,64,2048]{6,5,4,3,2,1,0:T(8,128)(2,1)S(1)} %pad_maximum_fusion.14), channel_id=1, source_target_pairs={{0,2},{2,0},{1,3},{3,1},{4,6},{6,4},{5,7},{7,5},{8,10},{10,8},{9,1... | collective-permute-start | bytes 1572872 | tf_op jit(solution)/shard_map/weight_out/ppermute | solution.py:76
  110.1 35.5 %collective-permute-start.17 = (bf16[144,2048]{1,0:T(8,128)(2,1)}, bf16[144,2048]{1,0:T(8,128)(2,1)S(1)}, u32[]{:S(2)}, u32[]{:S(2)}) collective-permute-start(bf16[144,2048]{1,0:T(8,128)(2,1)} %collective-permute-done.12), channel_id=1, source_target_pairs={{0,1},{1,0},{2,3},{3,2},{4,5},{5,4},{6,7},{7,6},{8,9},{9,8},{10,11... | collective-permute-start | bytes 1769480 | tf_op jit(solution)/shard_map/critical/ppermute | solution.py:76
  112.6 30.1 %collective-permute-start.20 = (bf16[128,1024]{1,0:T(8,128)(2,1)S(1)}, bf16[128,1024]{1,0:T(8,128)(2,1)S(1)}, u32[]{:S(2)}, u32[]{:S(2)}) collective-permute-start(bf16[128,1024]{1,0:T(8,128)(2,1)S(1)} %get-tuple-element.366), channel_id=1, source_target_pairs={{0,4},{4,0},{1,5},{5,1},{2,6},{6,2},{3,7},{7,3},{8,12},{12,8},{9,1... | collective-permute-start | bytes 786440 | tf_op jit(solution)/shard_map/up_zh/ppermute | solution.py:76
  142.6 40.1 %collective-permute-start.28 = (bf16[128,1024]{1,0:T(8,128)(2,1)S(1)}, bf16[128,1024]{1,0:T(8,128)(2,1)S(1)}, u32[]{:S(2)}, u32[]{:S(2)}) collective-permute-start(bf16[128,1024]{1,0:T(8,128)(2,1)S(1)} %get-tuple-element.365), channel_id=1, source_target_pairs={{0,4},{4,0},{1,5},{5,1},{2,6},{6,2},{3,7},{7,3},{8,12},{12,8},{9,1... | collective-permute-start | bytes 786440 | tf_op jit(solution)/shard_map/up_zh/ppermute | solution.py:76
  150.5 32.2 %collective-permute-start.27 = (bf16[128,1024]{1,0:T(8,128)(2,1)S(1)}, bf16[128,1024]{1,0:T(8,128)(2,1)S(1)}, u32[]{:S(2)}, u32[]{:S(2)}) collective-permute-start(bf16[128,1024]{1,0:T(8,128)(2,1)S(1)} %get-tuple-element.362), channel_id=1, source_target_pairs={{0,4},{4,0},{1,5},{5,1},{2,6},{6,2},{3,7},{7,3},{8,12},{12,8},{9,1... | collective-permute-start | bytes 786440 | tf_op jit(solution)/shard_map/down_zh/ppermute | solution.py:76
  189.7 38.1 %collective-permute-start.33 = (bf16[512,1024]{1,0:T(8,128)(2,1)}, bf16[512,1024]{1,0:T(8,128)(2,1)}, u32[]{:S(2)}, u32[]{:S(2)}) collective-permute-start(bf16[512,1024]{1,0:T(8,128)(2,1)} %pad_maximum_fusion.8), channel_id=1, source_target_pairs={{0,16},{16,0},{1,17},{17,1},{2,18},{18,2},{3,19},{19,3},{4,20},{20... | collective-permute-start | bytes 3145736 | tf_op jit(solution)/shard_map/up_far/ppermute | solution.py:76
  191.1 36.7 %all-to-all-start = ((bf16[8,144,256]{2,1,0:T(8,128)(2,1)}), bf16[8,144,256]{2,1,0:T(8,128)(2,1)}, u32[]{:S(2)}, u32[]{:S(2)}) async-start(bf16[8,144,256]{2,1,0:T(8,128)(2,1)} %bitcast.27), calls=%async_computation | async-start | bytes 1179648 | tf_op jit(solution)/shard_map/critical/all_to_all | solution.py:688
  198.3 29.5 %collective-permute-start.1 = (bf16[144,2048]{1,0:T(8,128)(2,1)S(1)}, bf16[144,2048]{1,0:T(8,128)(2,1)}, u32[]{:S(2)}, u32[]{:S(2)}) collective-permute-start(bf16[144,2048]{1,0:T(8,128)(2,1)S(1)} %cotangent_rows.1), channel_id=1, source_target_pairs={{0,2},{2,0},{1,3},{3,1},{4,6},{6,4},{5,7},{7,5},{8,10},{10,8},{9,1... | collective-permute-start | bytes 1769480 | tf_op jit(solution)/shard_map/cotangent_rows/ppermute | solution.py:76
  200.7 27.0 %collective-permute-start.31 = (bf16[256,1024]{1,0:T(8,128)(2,1)S(1)}, bf16[256,1024]{1,0:T(8,128)(2,1)S(1)}, u32[]{:S(2)}, u32[]{:S(2)}) collective-permute-start(bf16[256,1024]{1,0:T(8,128)(2,1)S(1)} %bitcast.189), channel_id=1, source_target_pairs={{0,16},{16,0},{1,17},{17,1},{2,18},{18,2},{3,19},{19,3},{4,20},{20... | collective-permute-start | bytes 1572872 | tf_op jit(solution)/shard_map/down_x/ppermute | solution.py:76
  201.3 26.4 %collective-permute-start.32 = (bf16[128,1024]{1,0:T(8,128)(2,1)}, bf16[128,1024]{1,0:T(8,128)(2,1)S(1)}, u32[]{:S(2)}, u32[]{:S(2)}) collective-permute-start(bf16[128,1024]{1,0:T(8,128)(2,1)} %get-tuple-element.361), channel_id=1, source_target_pairs={{0,4},{4,0},{1,5},{5,1},{2,6},{6,2},{3,7},{7,3},{8,12},{12,8},{9,1... | collective-permute-start | bytes 786440 | tf_op jit(solution)/shard_map/down_zh/ppermute | solution.py:76
  372.3 32.0 %collective-permute-start.62 = (bf16[256,1024]{1,0:T(8,128)(2,1)}, bf16[256,1024]{1,0:T(8,128)(2,1)}, u32[]{:S(2)}, u32[]{:S(2)}) collective-permute-start(bf16[256,1024]{1,0:T(8,128)(2,1)} %slice_add_fusion.12), channel_id=1, source_target_pairs={{0,4},{4,0},{1,5},{5,1},{2,6},{6,2},{3,7},{7,3},{8,12},{12,8},{9,1... | collective-permute-start | bytes 1572872 | tf_op jit(solution)/shard_map/d_down_zh/ppermute | solution.py:76
  372.3 32.6 %collective-permute-start.63 = (bf16[256,1024]{1,0:T(8,128)(2,1)}, bf16[256,1024]{1,0:T(8,128)(2,1)}, u32[]{:S(2)}, u32[]{:S(2)}) collective-permute-start(bf16[256,1024]{1,0:T(8,128)(2,1)} %get-tuple-element.298), channel_id=1, source_target_pairs={{0,16},{16,0},{1,17},{17,1},{2,18},{18,2},{3,19},{19,3},{4,20},{20... | collective-permute-start | bytes 1572872 | tf_op jit(solution)/shard_map/d_up_far/ppermute | solution.py:76
  377.7 32.9 %all-to-all-start.1 = ((bf16[8,144,256]{2,1,0:T(8,128)(2,1)}), bf16[8,144,256]{2,1,0:T(8,128)(2,1)S(1)}, u32[]{:S(2)}, u32[]{:S(2)}) async-start(bf16[8,144,256]{2,1,0:T(8,128)(2,1)} %bitcast.149), calls=%async_computation.1 | async-start | bytes 1179648 | tf_op jit(solution)/shard_map/critical/all_to_all | solution.py:730
  404.3 34.3 %collective-permute-start.68 = (bf16[512,1024]{1,0:T(8,128)(2,1)S(1)}, bf16[512,1024]{1,0:T(8,128)(2,1)}, u32[]{:S(2)}, u32[]{:S(2)}) collective-permute-start(bf16[512,1024]{1,0:T(8,128)(2,1)S(1)} %slice.309), channel_id=1, source_target_pairs={{0,16},{16,0},{1,17},{17,1},{2,18},{18,2},{3,19},{19,3},{4,20},{20... | collective-permute-start | bytes 3145736 | tf_op jit(solution)/shard_map/d_down_near/ppermute | solution.py:76
  404.9 77.9 %collective-permute-start.78 = (bf16[256,2048]{1,0:T(8,128)(2,1)}, bf16[256,2048]{1,0:T(8,128)(2,1)}, u32[]{:S(2)}, u32[]{:S(2)}) collective-permute-start(bf16[256,2048]{1,0:T(8,128)(2,1)} %get-tuple-element.312), channel_id=1, source_target_pairs={{0,16},{16,0},{1,17},{17,1},{2,18},{18,2},{3,19},{19,3},{4,20},{20... | collective-permute-start | bytes 3145736 | tf_op jit(solution)/shard_map/out_back/ppermute | solution.py:76
  441.6 42.3 %collective-permute-start.77 = (bf16[256,1024]{1,0:T(8,128)(2,1)}, bf16[256,1024]{1,0:T(8,128)(2,1)}, u32[]{:S(2)}, u32[]{:S(2)}) collective-permute-start(bf16[256,1024]{1,0:T(8,128)(2,1)} %get-tuple-element.296), channel_id=1, source_target_pairs={{0,4},{4,0},{1,5},{5,1},{2,6},{6,2},{3,7},{7,3},{8,12},{12,8},{9,1... | collective-permute-start | bytes 1572872 | tf_op jit(solution)/shard_map/d_up_zh/ppermute | solution.py:76
  460.0 39.8 %collective-permute-start.75 = (bf16[144,2048]{1,0:T(8,128)(2,1)}, bf16[144,2048]{1,0:T(8,128)(2,1)}, u32[]{:S(2)}, u32[]{:S(2)}) collective-permute-start(bf16[144,2048]{1,0:T(8,128)(2,1)} %slice.375), channel_id=1, source_target_pairs={{0,1},{1,0},{2,3},{3,2},{4,5},{5,4},{6,7},{7,6},{8,9},{9,8},{10,11... | collective-permute-start | bytes 1769480 | tf_op jit(solution)/shard_map/critical/ppermute | solution.py:76
  470.0 31.3 %collective-permute-start.79 = (bf16[1,1,2,2,2,64,768]{6,5,4,3,2,1,0:T(8,128)(2,1)}, bf16[1,1,2,2,2,64,768]{6,5,4,3,2,1,0:T(8,128)(2,1)}, u32[]{:S(2)}, u32[]{:S(2)}) collective-permute-start(bf16[1,1,2,2,2,64,768]{6,5,4,3,2,1,0:T(8,128)(2,1)} %constant_dynamic-slice_fusion.4), channel_id=1, source_target_pairs={{0,16},{16,0},{1,17},{17,1},{2,18},{18,2},{3,19},{19,3},{4,20},{20... | collective-permute-start | bytes 2359304 | tf_op jit(solution)/shard_map/qkv_back/ppermute | solution.py:76
  472.3 28.9 %collective-permute-start.74 = (bf16[144,2048]{1,0:T(8,128)(2,1)}, bf16[144,2048]{1,0:T(8,128)(2,1)}, u32[]{:S(2)}, u32[]{:S(2)}) collective-permute-start(bf16[144,2048]{1,0:T(8,128)(2,1)} %slice_add_fusion.5), channel_id=1, source_target_pairs={{0,6},{2,0},{4,2},{6,4},{1,7},{3,1},{5,3},{7,5},{8,14},{10,8},{12,... | collective-permute-start | bytes 1769480 | tf_op jit(solution)/shard_map/critical/ppermute | solution.py:237
  498.4 32.3 %collective-permute-start.88 = (bf16[512,1024]{1,0:T(8,128)(2,1)S(1)}, bf16[512,1024]{1,0:T(8,128)(2,1)S(1)}, u32[]{:S(2)}, u32[]{:S(2)}) collective-permute-start(bf16[512,1024]{1,0:T(8,128)(2,1)S(1)} %copy-done.46), channel_id=1, source_target_pairs={{0,16},{16,0},{1,17},{17,1},{2,18},{18,2},{3,19},{19,3},{4,20},{20... | collective-permute-start | bytes 3145736 | tf_op jit(solution)/shard_map/d_up_near/ppermute | solution.py:76
  517.5 30.9 %collective-permute-start.87 = (bf16[2,1,1,64,2048]{4,3,2,1,0:T(8,128)(2,1)S(1)}, bf16[2,1,1,64,2048]{4,3,2,1,0:T(8,128)(2,1)S(1)}, u32[]{:S(2)}, u32[]{:S(2)}) collective-permute-start(bf16[2,1,1,64,2048]{4,3,2,1,0:T(8,128)(2,1)S(1)} %fusion.24), channel_id=1, source_target_pairs={{0,1},{1,0},{2,3},{3,2},{4,5},{5,4},{6,7},{7,6},{8,9},{9,8},{10,11... | collective-permute-start | bytes 1572872 | tf_op jit(solution)/shard_map/d_down_all/ppermute | solution.py:76
  537.2 33.7 %collective-permute-start.92 = (bf16[1,1,2,2,1,64,2048]{6,5,4,3,2,1,0:T(8,128)(2,1)S(1)}, bf16[1,1,2,2,1,64,2048]{6,5,4,3,2,1,0:T(8,128)(2,1)S(1)}, u32[]{:S(2)}, u32[]{:S(2)}) collective-permute-start(bf16[1,1,2,2,1,64,2048]{6,5,4,3,2,1,0:T(8,128)(2,1)S(1)} %constant_dynamic-slice_fusion), channel_id=1, source_target_pairs={{0,1},{1,0},{2,3},{3,2},{4,5},{5,4},{6,7},{7,6},{8,9},{9,8},{10,11... | collective-permute-start | bytes 3145736 | tf_op jit(solution)/shard_map/out_back/ppermute | solution.py:76
  549.1 36.6 %collective-permute-start.100 = (bf16[1,1,1,64,4096]{4,3,2,1,0:T(8,128)(2,1)S(1)}, bf16[1,1,1,64,4096]{4,3,2,1,0:T(8,128)(2,1)S(1)}, u32[]{:S(2)}, u32[]{:S(2)}) collective-permute-start(bf16[1,1,1,64,4096]{4,3,2,1,0:T(8,128)(2,1)S(1)} %fusion.17), channel_id=1, source_target_pairs={{0,8},{8,0},{1,9},{9,1},{2,10},{10,2},{3,11},{11,3},{4,12},{12,4},... | collective-permute-start | bytes 1572872 | tf_op jit(solution)/shard_map/d_down_all/ppermute | solution.py:76
  (161 other events, 2021.2 us)

commit v6 on v5

--- a/solution.py
+++ b/solution.py
@@ -28,7 +28,7 @@
     "down": (1, 1),
     "up_zh": ((0, 1), (0, 2), (0, 1)),
     "up_x": ((0, 4),),
-    "up_far": ((0, 4),),
+    "up_far": ((1, 4),),
     "down_zh": ((1, 1), (0, 1), (0, 1), (0, 1)),
     "down_x": ((2, 2), (1, 2)),
     "down_far": ((0, 2), (0, 2)),
@@ -38,10 +38,10 @@
     "d_down_near": ((1, 4),),
     "d_down_out": (1, 1),
     "d_up_far": ((0, 2), (0, 2)),
-    "d_up_zh": ((1, 1), (0, 1), (0, 2)),
+    "d_up_zh": ((0, 1), (0, 1), (0, 2)),
     "d_up_near": ((5, 4),),
     "d_up_out": (0, 0),
-    "act": (0, 0, 3),
+    "act": (0, 0, 2),
     "d_out": (0, 2, 2, 0),
     "sums": (0, 0, 0, 0),
     "qkv": (0, 0, 0, 0),
@@ -394,6 +394,10 @@
 
 
 def reorder(array, firsts, lanes):
+    if lanes % 128:
+        parts = [lax.dynamic_slice_in_dim(array, first * lanes, lanes, 1) for first in firsts]
+        return jnp.concatenate(parts, axis=1)
+
     def kernel(firsts_ref, array_ref, out_ref):
         for place in range(len(firsts)):
             first = pl.multiple_of(firsts_ref[place] * lanes, 128)
@@ -697,7 +701,7 @@
         cot_all = yield from box.wait("cot_all")
         w_up_here = yield from box.wait("w_up")
         active, slope = gelu_both(dot(normed_all, w_up_here))
-        active = active.astype(BF)
+        active, slope = active.astype(BF), slope.astype(BF)
         d_w_down = dot(cot_all, active, 0, 0).astype(BF)
         active, slope, d_w_down = yield (active, slope, d_w_down)
         box["d_w_down"] = d_w_down

time: 615 us -> 605 us (0.984)
  starting transfers between devices: 115 us -> 103 us
  waiting for transfers between devices: 251 us -> 259 us
    ppermute x92, waiting for transfers between devices: 229 us -> 237 us  [swap(): return lax.ppermute(array, axis, [(0, 1), (1, 0)])]
    ppermute x92, starting transfers between devices: 84.9 us -> 77.7 us  [swap(): return lax.ppermute(array, axis, [(0, 1), (1, 0)])]
    unnamed x205 -> x201, local copies, waits for them, and re-layouts: 17 us -> 18.9 us
  transfers between devices with their start and end apart: 103 -> 103, of which waited for: 42 -> 45; matrix products, arithmetic and copies ran while one was open for 30% -> 30% of each run, Pallas kernels for 4% -> 4%
where the time goes in v6:
time: 605 us; the launch traced here: 597 us
  waiting for transfers between devices  259 us (43%)
  starting transfers between devices  103 us (17%)
  other arithmetic  77.6 us (13%)
  matrix products  67 us (11%)
  local copies, waits for them, and re-layouts  64.4 us (11%)
  Pallas kernels  23.3 us (4%)
    ppermute x92, waiting for transfers between devices, swap(): return lax.ppermute(array, axis, [(0, 1), (1, 0)])  237 us
    ppermute x92, starting transfers between devices, swap(): return lax.ppermute(array, axis, [(0, 1), (1, 0)])  77.7 us
    dot_general x17, matrix products, dot(): lax.dot_general(left, right, (((left_dim,), (right_dim,)), ((), ())), pre...  67 us
    unnamed x201, local copies, waits for them, and re-layouts  18.9 us
  transfers between devices with their start and end apart: 103, of which 45 were waited for; matrix products, arithmetic and copies ran while one was open for 30% of the time, Pallas kernels for 4%

profile of v6, /device:TPU:0, one launch (start us, length us, event | category | flops | bytes accessed | tf_op | source)
XLA Modules:
  0.0 597.2 jit_solution(11515185093063006359)
XLA Ops:
  30.7 16.5 %collective-permute-done.5 = bf16[1,1,1,1,1,64,3072]{6,5,4,3,2,1,0:T(8,128)(2,1)} collective-permute-done((bf16[1,1,1,1,1,64,3072]{6,5,4,3,2,1,0:T(8,128)(2,1)}, bf16[1,1,1,1,1,64,3072]{6,5,4,3,2,1,0:T(8,128)(2,1)}, u32[]{:S(2)}, u32[]{:S(2)}) %collective-permute-start.5) | collective-permute-done | bytes 393248 | tf_op jit(solution)/shard_map/weight_qkv/ppermute | solution.py:76
  55.5 6.5 %collective-permute-done.9 = bf16[2,1,1,64,2048]{4,3,2,1,0:T(8,128)(2,1)S(1)} collective-permute-done((bf16[2,1,1,64,2048]{4,3,2,1,0:T(8,128)(2,1)S(1)}, bf16[2,1,1,64,2048]{4,3,2,1,0:T(8,128)(2,1)S(1)}, u32[]{:S(2)}, u32[]{:S(2)}) %collective-permute-start.9) | collective-permute-done | bytes 524320 | tf_op jit(solution)/shard_map/down/ppermute | solution.py:76
  61.9 11.9 %collective-permute-done.10 = bf16[1,1,2,1,1,64,1536]{6,5,4,3,2,1,0:T(8,128)(2,1)S(1)} collective-permute-done((bf16[1,1,2,1,1,64,1536]{6,5,4,3,2,1,0:T(8,128)(2,1)S(1)}, bf16[1,1,2,1,1,64,1536]{6,5,4,3,2,1,0:T(8,128)(2,1)S(1)}, u32[]{:S(2)}, u32[]{:S(2)}) %collective-permute-start.10) | collective-permute-done | bytes 393248 | tf_op jit(solution)/shard_map/weight_qkv/ppermute | solution.py:76
  83.7 12.2 %collective-permute-done.14 = bf16[2,1,2,64,1024]{4,3,2,1,0:T(8,128)(2,1)} collective-permute-done((bf16[2,1,2,64,1024]{4,3,2,1,0:T(8,128)(2,1)}, bf16[2,1,2,64,1024]{4,3,2,1,0:T(8,128)(2,1)}, u32[]{:S(2)}, u32[]{:S(2)}) %collective-permute-start.14) | collective-permute-done | bytes 524320 | tf_op jit(solution)/shard_map/up/ppermute | solution.py:76
  105.4 5.6 collective-permute-done.18
  116.0 28.5 %collective-permute-done.20 = bf16[128,1024]{1,0:T(8,128)(2,1)S(1)} collective-permute-done((bf16[128,1024]{1,0:T(8,128)(2,1)S(1)}, bf16[128,1024]{1,0:T(8,128)(2,1)S(1)}, u32[]{:S(2)}, u32[]{:S(2)}) %collective-permute-start.20) | collective-permute-done | bytes 262176 | tf_op jit(solution)/shard_map/up_zh/ppermute | solution.py:76
  157.1 8.3 %collective-permute-done.24 = bf16[256,1024]{1,0:T(8,128)(2,1)S(1)} collective-permute-done((bf16[256,1024]{1,0:T(8,128)(2,1)S(1)}, bf16[256,1024]{1,0:T(8,128)(2,1)S(1)}, u32[]{:S(2)}, u32[]{:S(2)}) %collective-permute-start.24) | collective-permute-done | bytes 524320 | tf_op jit(solution)/shard_map/up_zh/ppermute | solution.py:76
  165.4 8.1 %collective-permute-done.25 = bf16[1,1,2,2,1,64,2048]{6,5,4,3,2,1,0:T(8,128)(2,1)S(1)} collective-permute-done((bf16[1,1,2,2,1,64,2048]{6,5,4,3,2,1,0:T(8,128)(2,1)S(1)}, bf16[1,1,2,2,1,64,2048]{6,5,4,3,2,1,0:T(8,128)(2,1)S(1)}, u32[]{:S(2)}, u32[]{:S(2)}) %collective-permute-start.25) | collective-permute-done | bytes 1048608 | tf_op jit(solution)/shard_map/weight_out/ppermute | solution.py:76
  177.4 7.0 %critical.7 = bf16[8,3,48,256]{3,2,1,0:T(8,128)(2,1)} custom-call(s32[8]{0:T(128)S(1)} %fusion.63.order_ref, s32[3,384,1]{2,1,0:T(8,128)S(1)} %copy.42.doc_col_ref, s32[3,1,512]{2,1,0:T(1,128)S(1)} %broadcast_in_dim.20.doc_row_ref, s32[3,1,512]{2,1,0:T(1,128)S(1)} %broadcast_in_dim.24.pos_row_ref, bf16[1280,768]{1,0:T(8,128)(2,1)S(1)} %convolution_convert_fusion.7.tokens_ref), custom_call_target="tpu_custom_call" | custom-call | flops 11324620800 | bytes 2359296 | tf_op jit(solution)/shard_map/critical/pallas_call | solution.py:689
  203.9 7.0 %pad_maximum_fusion = bf16[2048,2048]{1,0:T(8,128)(2,1)} fusion(bf16[512,2048]{1,0:T(8,128)(2,1)} %collective-permute-done.34, bf16[512,2048]{1,0:T(8,128)(2,1)} %bitcast.30, bf16[512,2048]{1,0:T(8,128)(2,1)} %collective-permute-done.33, bf16[512,2048]{1,0:T(8,128)(2,1)} %bitcast.29), kind=kLoop, calls=%fused_computation | loop fusion | flops 33554432 | bytes 16777216 | tf_op jit(solution)/shard_map/weight_out/concatenate | solution.py:841
  211.6 6.4 %collective-permute-done.1 = bf16[144,2048]{1,0:T(8,128)(2,1)} collective-permute-done((bf16[144,2048]{1,0:T(8,128)(2,1)S(1)}, bf16[144,2048]{1,0:T(8,128)(2,1)}, u32[]{:S(2)}, u32[]{:S(2)}) %collective-permute-start.1) | collective-permute-done | bytes 589856 | tf_op jit(solution)/shard_map/cotangent_rows/ppermute | solution.py:76
  218.0 12.7 %collective-permute-done.32 = bf16[128,1024]{1,0:T(8,128)(2,1)S(1)} collective-permute-done((bf16[128,1024]{1,0:T(8,128)(2,1)S(1)}, bf16[128,1024]{1,0:T(8,128)(2,1)S(1)}, u32[]{:S(2)}, u32[]{:S(2)}) %collective-permute-start.32) | collective-permute-done | bytes 262176 | tf_op jit(solution)/shard_map/down_zh/ppermute | solution.py:76
  231.4 5.0 fusion.78
  247.7 9.3 %collective-permute-done.36 = bf16[64,2048]{1,0:T(8,128)(2,1)S(1)} collective-permute-done((bf16[64,2048]{1,0:T(8,128)(2,1)S(1)}, bf16[64,2048]{1,0:T(8,128)(2,1)S(1)}, u32[]{:S(2)}, u32[]{:S(2)}) %collective-permute-start.36) | collective-permute-done | bytes 262176 | tf_op jit(solution)/shard_map/cotangent_rows/ppermute | solution.py:76
  262.2 11.2 %collective-permute-done.46 = bf16[128,1024]{1,0:T(8,128)(2,1)S(1)} collective-permute-done((bf16[128,1024]{1,0:T(8,128)(2,1)S(1)}, bf16[128,1024]{1,0:T(8,128)(2,1)S(1)}, u32[]{:S(2)}, u32[]{:S(2)}) %collective-permute-start.46) | collective-permute-done | bytes 262176 | tf_op jit(solution)/shard_map/down_zh/ppermute | solution.py:76
  280.4 6.9 %fusion.4 = (bf16[1152,1024]{1,0:T(8,128)(2,1)S(1)}, bf16[1152,1024]{1,0:T(8,128)(2,1)S(1)}) fusion(bf16[1152,2048]{1,0:T(8,128)(2,1)S(1)} %constant_dynamic-update-slice_fusion.18, bf16[2048,1024]{1,0:T(8,128)(2,1)S(1)} %constant_dynamic-update-slice_fusion.24), kind=kOutput, calls=%fused_computation.8 | convolution fusion | flops 4844814336 | bytes 13631488 | tf_op jit(solution)/shard_map/critical/dot_general | solution.py:54
  287.3 6.0 %convolution_convert_fusion.5 = bf16[2048,1024]{1,0:T(8,128)(2,1)S(1)} fusion(bf16[1152,2048]{1,0:T(8,128)(2,1)S(1)} %constant_dynamic-update-slice_fusion.7, bf16[1152,1024]{1,0:T(8,128)(2,1)S(1)} %get-tuple-element.199), kind=kOutput, calls=%fused_computation.15 | convolution fusion | flops 4833935360 | bytes 11272192 | tf_op jit(solution)/shard_map/critical/dot_general | solution.py:54
  299.0 5.5 multiply_convert_fusion
  304.5 5.4 convolution_convert_fusion.1
  321.1 6.1 %convolution_convert_fusion.4 = bf16[2048,1024]{1,0:T(8,128)(2,1)S(1)} fusion(bf16[1152,2048]{1,0:T(8,128)(2,1)S(1)} %bitcast.193, bf16[1152,1024]{1,0:T(8,128)(2,1)S(1)} %copy-done.77), kind=kOutput, calls=%fused_computation.14 | convolution fusion | flops 4833935360 | bytes 11272192 | tf_op jit(solution)/shard_map/critical/dot_general | solution.py:54
  328.7 6.5 %collective-permute-done.52 = bf16[64,2048]{1,0:T(8,128)(2,1)S(1)} collective-permute-done((bf16[64,2048]{1,0:T(8,128)(2,1)S(1)}, bf16[64,2048]{1,0:T(8,128)(2,1)S(1)}, u32[]{:S(2)}, u32[]{:S(2)}) %collective-permute-start.52) | collective-permute-done | bytes 262176 | tf_op jit(solution)/shard_map/critical/ppermute | solution.py:76
  337.5 5.4 convolution_convert_fusion
  342.9 7.0 %collective-permute-done.58 = bf16[256,1024]{1,0:T(8,128)(2,1)S(1)} collective-permute-done((bf16[256,1024]{1,0:T(8,128)(2,1)S(1)}, bf16[256,1024]{1,0:T(8,128)(2,1)S(1)}, u32[]{:S(2)}, u32[]{:S(2)}) %collective-permute-start.58) | collective-permute-done | bytes 524320 | tf_op jit(solution)/shard_map/d_up_far/ppermute | solution.py:76
  393.1 12.5 %collective-permute-done.62 = bf16[256,1024]{1,0:T(8,128)(2,1)} collective-permute-done((bf16[256,1024]{1,0:T(8,128)(2,1)}, bf16[256,1024]{1,0:T(8,128)(2,1)}, u32[]{:S(2)}, u32[]{:S(2)}) %collective-permute-start.62) | collective-permute-done | bytes 524320 | tf_op jit(solution)/shard_map/d_down_zh/ppermute | solution.py:76
  411.9 4.8 collective-permute-done.61
  418.2 4.9 all-to-all-done.1
  428.1 11.4 %critical.12 = bf16[1280,768]{1,0:T(8,128)(2,1)S(1)} custom-call(s32[8]{0:T(128)S(1)} %fusion.63.order_ref, s32[3,384,1]{2,1,0:T(8,128)S(1)} %copy.42.doc_col_ref, s32[3,1,512]{2,1,0:T(1,128)S(1)} %broadcast_in_dim.20.doc_row_ref, s32[3,1,512]{2,1,0:T(1,128)S(1)} %broadcast_in_dim.24.pos_row_ref, bf16[1280,768]{1,0:T(8,128)(2,1)S(1)} %copy-done.9, ...), custom_call_target="tpu_custom_call" | custom-call | flops 16986931200 | bytes 4128768 | tf_op jit(solution)/shard_map/critical/pallas_call | solution.py:735
  443.0 7.4 %convolution_convert_fusion.6 = bf16[2048,768]{1,0:T(8,128)(2,1)S(1)} fusion(bf16[1280,2048]{1,0:T(8,128)(2,1)} %copy-done.27, bf16[1280,768]{1,0:T(8,128)(2,1)S(1)} %critical.12), kind=kOutput, calls=%fused_computation.16 | convolution fusion | flops 4028104704 | bytes 10354688 | tf_op jit(solution)/shard_map/critical/dot_general | solution.py:54
  505.5 6.4 %collective-permute-done.83 = bf16[1,1,2,2,1,64,768]{6,5,4,3,2,1,0:T(8,128)(2,1)S(1)} collective-permute-done((bf16[1,1,2,2,1,64,768]{6,5,4,3,2,1,0:T(8,128)(2,1)S(1)}, bf16[1,1,2,2,1,64,768]{6,5,4,3,2,1,0:T(8,128)(2,1)S(1)}, u32[]{:S(2)}, u32[]{:S(2)}) %collective-permute-start.83) | collective-permute-done | bytes 393248 | tf_op jit(solution)/shard_map/qkv_back/ppermute | solution.py:76
  525.5 10.3 %collective-permute-done.87 = bf16[2,1,1,64,2048]{4,3,2,1,0:T(8,128)(2,1)S(1)} collective-permute-done((bf16[2,1,1,64,2048]{4,3,2,1,0:T(8,128)(2,1)S(1)}, bf16[2,1,1,64,2048]{4,3,2,1,0:T(8,128)(2,1)S(1)}, u32[]{:S(2)}, u32[]{:S(2)}) %collective-permute-start.87) | collective-permute-done | bytes 524320 | tf_op jit(solution)/shard_map/d_down_all/ppermute | solution.py:76
  563.0 5.1 collective-permute-done.91
  580.8 10.0 %collective-permute-done.97 = bf16[1,64,2048]{2,1,0:T(8,128)(2,1)S(1)} collective-permute-done((bf16[1,64,2048]{2,1,0:T(8,128)(2,1)S(1)}, bf16[1,64,2048]{2,1,0:T(8,128)(2,1)S(1)}, u32[]{:S(2)}, u32[]{:S(2)}) %collective-permute-start.97) | collective-permute-done | bytes 262176 | tf_op jit(solution)/shard_map/out_back/ppermute | solution.py:222
  (605 shorter events, 316.5 us)
Async XLA Ops:
  5.9 42.7 %collective-permute-start.2 = (bf16[144,2048]{1,0:T(8,128)(2,1)}, bf16[144,2048]{1,0:T(8,128)(2,1)}, u32[]{:S(2)}, u32[]{:S(2)}) collective-permute-start(bf16[144,2048]{1,0:T(8,128)(2,1)} %multiply_convert_fusion.3), channel_id=1, source_target_pairs={{0,2},{2,4},{4,6},{6,0},{1,3},{3,5},{5,7},{7,1},{8,10},{10,12},{12... | collective-permute-start | bytes 1769480 | tf_op jit(solution)/shard_map/critical/ppermute | solution.py:237
  8.9 46.0 %collective-permute-start.7 = (bf16[144,2048]{1,0:T(8,128)(2,1)}, bf16[144,2048]{1,0:T(8,128)(2,1)}, u32[]{:S(2)}, u32[]{:S(2)}) collective-permute-start(bf16[144,2048]{1,0:T(8,128)(2,1)} %multiply_convert_fusion.3), channel_id=1, source_target_pairs={{0,1},{1,0},{2,3},{3,2},{4,5},{5,4},{6,7},{7,6},{8,9},{9,8},{10,11... | collective-permute-start | bytes 1769480 | tf_op jit(solution)/shard_map/critical/ppermute | solution.py:76
  12.2 35.0 %collective-permute-start.5 = (bf16[1,1,1,1,1,64,3072]{6,5,4,3,2,1,0:T(8,128)(2,1)}, bf16[1,1,1,1,1,64,3072]{6,5,4,3,2,1,0:T(8,128)(2,1)}, u32[]{:S(2)}, u32[]{:S(2)}) collective-permute-start(bf16[1,1,1,1,1,64,3072]{6,5,4,3,2,1,0:T(8,128)(2,1)} %dynamic-slice_bitcast_fusion.3), channel_id=1, source_target_pairs={{0,4},{4,0},{1,5},{5,1},{2,6},{6,2},{3,7},{7,3},{8,12},{12,8},{9,1... | collective-permute-start | bytes 1179656 | tf_op jit(solution)/shard_map/weight_qkv/ppermute | solution.py:76
  27.0 55.2 %collective-permute-start.15 = (bf16[1,1,1,1,1,64,2048]{6,5,4,3,2,1,0:T(8,128)(2,1)}, bf16[1,1,1,1,1,64,2048]{6,5,4,3,2,1,0:T(8,128)(2,1)}, u32[]{:S(2)}, u32[]{:S(2)}) collective-permute-start(bf16[1,1,1,1,1,64,2048]{6,5,4,3,2,1,0:T(8,128)(2,1)} %bitcast.23), channel_id=1, source_target_pairs={{0,4},{4,0},{1,5},{5,1},{2,6},{6,2},{3,7},{7,3},{8,12},{12,8},{9,1... | collective-permute-start | bytes 786440 | tf_op jit(solution)/shard_map/weight_out/ppermute | solution.py:76
  54.9 41.0 %collective-permute-start.13 = (bf16[144,2048]{1,0:T(8,128)(2,1)}, bf16[144,2048]{1,0:T(8,128)(2,1)}, u32[]{:S(2)}, u32[]{:S(2)}) collective-permute-start(bf16[144,2048]{1,0:T(8,128)(2,1)} %collective-permute-done.2), channel_id=1, source_target_pairs={{0,1},{1,0},{2,3},{3,2},{4,5},{5,4},{6,7},{7,6},{8,9},{9,8},{10,11... | collective-permute-start | bytes 1769480 | tf_op jit(solution)/shard_map/critical/ppermute | solution.py:76
  61.9 34.1 %collective-permute-start.14 = (bf16[2,1,2,64,1024]{4,3,2,1,0:T(8,128)(2,1)}, bf16[2,1,2,64,1024]{4,3,2,1,0:T(8,128)(2,1)}, u32[]{:S(2)}, u32[]{:S(2)}) collective-permute-start(bf16[2,1,2,64,1024]{4,3,2,1,0:T(8,128)(2,1)} %fusion.29), channel_id=1, source_target_pairs={{0,2},{2,0},{1,3},{3,1},{4,6},{6,4},{5,7},{7,5},{8,10},{10,8},{9,1... | collective-permute-start | bytes 1572872 | tf_op jit(solution)/shard_map/up/ppermute | solution.py:76
  82.2 31.3 %collective-permute-start.11 = (bf16[144,2048]{1,0:T(8,128)(2,1)}, bf16[144,2048]{1,0:T(8,128)(2,1)S(1)}, u32[]{:S(2)}, u32[]{:S(2)}) collective-permute-start(bf16[144,2048]{1,0:T(8,128)(2,1)} %collective-permute-done.6), channel_id=1, source_target_pairs={{0,1},{1,0},{2,3},{3,2},{4,5},{5,4},{6,7},{7,6},{8,9},{9,8},{10,11... | collective-permute-start | bytes 1769480 | tf_op jit(solution)/shard_map/critical/ppermute | solution.py:76
  100.7 46.7 %collective-permute-start.22 = (bf16[1,1,2,2,2,64,768]{6,5,4,3,2,1,0:T(8,128)(2,1)S(1)}, bf16[1,1,2,2,2,64,768]{6,5,4,3,2,1,0:T(8,128)(2,1)S(1)}, u32[]{:S(2)}, u32[]{:S(2)}) collective-permute-start(bf16[1,1,2,2,2,64,768]{6,5,4,3,2,1,0:T(8,128)(2,1)S(1)} %pad_maximum_fusion.9), channel_id=1, source_target_pairs={{0,16},{16,0},{1,17},{17,1},{2,18},{18,2},{3,19},{19,3},{4,20},{20... | collective-permute-start | bytes 2359304 | tf_op jit(solution)/shard_map/weight_qkv/ppermute | solution.py:76
  103.6 43.7 %collective-permute-start.19 = (bf16[512,1024]{1,0:T(8,128)(2,1)S(1)}, bf16[512,1024]{1,0:T(8,128)(2,1)}, u32[]{:S(2)}, u32[]{:S(2)}) collective-permute-start(bf16[512,1024]{1,0:T(8,128)(2,1)S(1)} %bitcast.166), channel_id=1, source_target_pairs={{0,16},{16,0},{1,17},{17,1},{2,18},{18,2},{3,19},{19,3},{4,20},{20... | collective-permute-start | bytes 3145736 | tf_op jit(solution)/shard_map/up_x/ppermute | solution.py:76
  105.3 39.1 %collective-permute-start.21 = (bf16[1,1,2,1,1,64,2048]{6,5,4,3,2,1,0:T(8,128)(2,1)S(1)}, bf16[1,1,2,1,1,64,2048]{6,5,4,3,2,1,0:T(8,128)(2,1)S(1)}, u32[]{:S(2)}, u32[]{:S(2)}) collective-permute-start(bf16[1,1,2,1,1,64,2048]{6,5,4,3,2,1,0:T(8,128)(2,1)S(1)} %pad_maximum_fusion.14), channel_id=1, source_target_pairs={{0,2},{2,0},{1,3},{3,1},{4,6},{6,4},{5,7},{7,5},{8,10},{10,8},{9,1... | collective-permute-start | bytes 1572872 | tf_op jit(solution)/shard_map/weight_out/ppermute | solution.py:76
  111.1 36.3 %collective-permute-start.17 = (bf16[144,2048]{1,0:T(8,128)(2,1)}, bf16[144,2048]{1,0:T(8,128)(2,1)S(1)}, u32[]{:S(2)}, u32[]{:S(2)}) collective-permute-start(bf16[144,2048]{1,0:T(8,128)(2,1)} %collective-permute-done.12), channel_id=1, source_target_pairs={{0,1},{1,0},{2,3},{3,2},{4,5},{5,4},{6,7},{7,6},{8,9},{9,8},{10,11... | collective-permute-start | bytes 1769480 | tf_op jit(solution)/shard_map/critical/ppermute | solution.py:76
  113.6 30.8 %collective-permute-start.20 = (bf16[128,1024]{1,0:T(8,128)(2,1)S(1)}, bf16[128,1024]{1,0:T(8,128)(2,1)S(1)}, u32[]{:S(2)}, u32[]{:S(2)}) collective-permute-start(bf16[128,1024]{1,0:T(8,128)(2,1)S(1)} %get-tuple-element.364), channel_id=1, source_target_pairs={{0,4},{4,0},{1,5},{5,1},{2,6},{6,2},{3,7},{7,3},{8,12},{12,8},{9,1... | collective-permute-start | bytes 786440 | tf_op jit(solution)/shard_map/up_zh/ppermute | solution.py:76
  144.4 40.0 %collective-permute-start.28 = (bf16[128,1024]{1,0:T(8,128)(2,1)S(1)}, bf16[128,1024]{1,0:T(8,128)(2,1)S(1)}, u32[]{:S(2)}, u32[]{:S(2)}) collective-permute-start(bf16[128,1024]{1,0:T(8,128)(2,1)S(1)} %get-tuple-element.363), channel_id=1, source_target_pairs={{0,4},{4,0},{1,5},{5,1},{2,6},{6,2},{3,7},{7,3},{8,12},{12,8},{9,1... | collective-permute-start | bytes 786440 | tf_op jit(solution)/shard_map/up_zh/ppermute | solution.py:76
  152.2 32.2 %collective-permute-start.27 = (bf16[128,1024]{1,0:T(8,128)(2,1)S(1)}, bf16[128,1024]{1,0:T(8,128)(2,1)S(1)}, u32[]{:S(2)}, u32[]{:S(2)}) collective-permute-start(bf16[128,1024]{1,0:T(8,128)(2,1)S(1)} %get-tuple-element.360), channel_id=1, source_target_pairs={{0,4},{4,0},{1,5},{5,1},{2,6},{6,2},{3,7},{7,3},{8,12},{12,8},{9,1... | collective-permute-start | bytes 786440 | tf_op jit(solution)/shard_map/down_zh/ppermute | solution.py:76
  191.8 38.9 %all-to-all-start = ((bf16[8,144,256]{2,1,0:T(8,128)(2,1)}), bf16[8,144,256]{2,1,0:T(8,128)(2,1)S(1)}, u32[]{:S(2)}, u32[]{:S(2)}) async-start(bf16[8,144,256]{2,1,0:T(8,128)(2,1)} %bitcast.27), calls=%async_computation | async-start | bytes 1179648 | tf_op jit(solution)/shard_map/critical/all_to_all | solution.py:692
  197.4 33.3 %collective-permute-start.31 = (bf16[256,1024]{1,0:T(8,128)(2,1)S(1)}, bf16[256,1024]{1,0:T(8,128)(2,1)}, u32[]{:S(2)}, u32[]{:S(2)}) collective-permute-start(bf16[256,1024]{1,0:T(8,128)(2,1)S(1)} %bitcast.191), channel_id=1, source_target_pairs={{0,16},{16,0},{1,17},{17,1},{2,18},{18,2},{3,19},{19,3},{4,20},{20... | collective-permute-start | bytes 1572872 | tf_op jit(solution)/shard_map/down_x/ppermute | solution.py:76
  200.9 29.8 %collective-permute-start.32 = (bf16[128,1024]{1,0:T(8,128)(2,1)S(1)}, bf16[128,1024]{1,0:T(8,128)(2,1)S(1)}, u32[]{:S(2)}, u32[]{:S(2)}) collective-permute-start(bf16[128,1024]{1,0:T(8,128)(2,1)S(1)} %copy-done.67), channel_id=1, source_target_pairs={{0,4},{4,0},{1,5},{5,1},{2,6},{6,2},{3,7},{7,3},{8,12},{12,8},{9,1... | collective-permute-start | bytes 786440 | tf_op jit(solution)/shard_map/down_zh/ppermute | solution.py:76
  203.8 38.7 %collective-permute-start.40 = (bf16[128,1024]{1,0:T(8,128)(2,1)}, bf16[128,1024]{1,0:T(8,128)(2,1)S(1)}, u32[]{:S(2)}, u32[]{:S(2)}) collective-permute-start(bf16[128,1024]{1,0:T(8,128)(2,1)} %get-tuple-element.358), channel_id=1, source_target_pairs={{0,4},{4,0},{1,5},{5,1},{2,6},{6,2},{3,7},{7,3},{8,12},{12,8},{9,1... | collective-permute-start | bytes 786440 | tf_op jit(solution)/shard_map/down_zh/ppermute | solution.py:76
  210.9 32.3 %collective-permute-start.41 = (bf16[512,1024]{1,0:T(8,128)(2,1)}, bf16[512,1024]{1,0:T(8,128)(2,1)}, u32[]{:S(2)}, u32[]{:S(2)}) collective-permute-start(bf16[512,1024]{1,0:T(8,128)(2,1)} %pad_maximum_fusion.8), channel_id=1, source_target_pairs={{0,16},{16,0},{1,17},{17,1},{2,18},{18,2},{3,19},{19,3},{4,20},{20... | collective-permute-start | bytes 3145736 | tf_op jit(solution)/shard_map/up_far/ppermute | solution.py:76
  368.2 37.4 %collective-permute-start.62 = (bf16[256,1024]{1,0:T(8,128)(2,1)}, bf16[256,1024]{1,0:T(8,128)(2,1)}, u32[]{:S(2)}, u32[]{:S(2)}) collective-permute-start(bf16[256,1024]{1,0:T(8,128)(2,1)} %slice_add_fusion.12), channel_id=1, source_target_pairs={{0,4},{4,0},{1,5},{5,1},{2,6},{6,2},{3,7},{7,3},{8,12},{12,8},{9,1... | collective-permute-start | bytes 1572872 | tf_op jit(solution)/shard_map/d_down_zh/ppermute | solution.py:76
  371.2 40.0 %collective-permute-start.64 = (bf16[128,1024]{1,0:T(8,128)(2,1)}, bf16[128,1024]{1,0:T(8,128)(2,1)}, u32[]{:S(2)}, u32[]{:S(2)}) collective-permute-start(bf16[128,1024]{1,0:T(8,128)(2,1)} %get-tuple-element.380), channel_id=1, source_target_pairs={{0,4},{4,0},{1,5},{5,1},{2,6},{6,2},{3,7},{7,3},{8,12},{12,8},{9,1... | collective-permute-start | bytes 786440 | tf_op jit(solution)/shard_map/d_up_zh/ppermute | solution.py:76
  374.1 37.1 %collective-permute-start.63 = (bf16[256,1024]{1,0:T(8,128)(2,1)}, bf16[256,1024]{1,0:T(8,128)(2,1)S(1)}, u32[]{:S(2)}, u32[]{:S(2)}) collective-permute-start(bf16[256,1024]{1,0:T(8,128)(2,1)} %get-tuple-element.297), channel_id=1, source_target_pairs={{0,16},{16,0},{1,17},{17,1},{2,18},{18,2},{3,19},{19,3},{4,20},{20... | collective-permute-start | bytes 1572872 | tf_op jit(solution)/shard_map/d_up_far/ppermute | solution.py:76
  374.8 48.4 %all-to-all-start.1 = ((bf16[8,144,256]{2,1,0:T(8,128)(2,1)}), bf16[8,144,256]{2,1,0:T(8,128)(2,1)S(1)}, u32[]{:S(2)}, u32[]{:S(2)}) async-start(bf16[8,144,256]{2,1,0:T(8,128)(2,1)} %bitcast.186), calls=%async_computation.1 | async-start | bytes 1179648 | tf_op jit(solution)/shard_map/critical/all_to_all | solution.py:734
  389.7 33.4 %collective-permute-start.66 = (bf16[256,2048]{1,0:T(8,128)(2,1)}, bf16[256,2048]{1,0:T(8,128)(2,1)}, u32[]{:S(2)}, u32[]{:S(2)}) collective-permute-start(bf16[256,2048]{1,0:T(8,128)(2,1)} %get-tuple-element.311), channel_id=1, source_target_pairs={{0,16},{16,0},{1,17},{17,1},{2,18},{18,2},{3,19},{19,3},{4,20},{20... | collective-permute-start | bytes 3145736 | tf_op jit(solution)/shard_map/out_back/ppermute | solution.py:76
  411.2 29.8 %collective-permute-start.70 = (bf16[128,1024]{1,0:T(8,128)(2,1)}, bf16[128,1024]{1,0:T(8,128)(2,1)}, u32[]{:S(2)}, u32[]{:S(2)}) collective-permute-start(bf16[128,1024]{1,0:T(8,128)(2,1)} %get-tuple-element.379), channel_id=1, source_target_pairs={{0,4},{4,0},{1,5},{5,1},{2,6},{6,2},{3,7},{7,3},{8,12},{12,8},{9,1... | collective-permute-start | bytes 786440 | tf_op jit(solution)/shard_map/d_up_zh/ppermute | solution.py:76
  411.3 31.7 %collective-permute-start.69 = (bf16[512,1024]{1,0:T(8,128)(2,1)}, bf16[512,1024]{1,0:T(8,128)(2,1)}, u32[]{:S(2)}, u32[]{:S(2)}) collective-permute-start(bf16[512,1024]{1,0:T(8,128)(2,1)} %slice.311), channel_id=1, source_target_pairs={{0,16},{16,0},{1,17},{17,1},{2,18},{18,2},{3,19},{19,3},{4,20},{20... | collective-permute-start | bytes 3145736 | tf_op jit(solution)/shard_map/d_down_near/ppermute | solution.py:76
  417.4 64.0 %collective-permute-start.78 = (bf16[256,2048]{1,0:T(8,128)(2,1)}, bf16[256,2048]{1,0:T(8,128)(2,1)}, u32[]{:S(2)}, u32[]{:S(2)}) collective-permute-start(bf16[256,2048]{1,0:T(8,128)(2,1)} %get-tuple-element.310), channel_id=1, source_target_pairs={{0,16},{16,0},{1,17},{17,1},{2,18},{18,2},{3,19},{19,3},{4,20},{20... | collective-permute-start | bytes 3145736 | tf_op jit(solution)/shard_map/out_back/ppermute | solution.py:76
  458.7 27.0 %collective-permute-start.77 = (bf16[2,1,2,64,1024]{4,3,2,1,0:T(8,128)(2,1)}, bf16[2,1,2,64,1024]{4,3,2,1,0:T(8,128)(2,1)}, u32[]{:S(2)}, u32[]{:S(2)}) collective-permute-start(bf16[2,1,2,64,1024]{4,3,2,1,0:T(8,128)(2,1)} %constant_dynamic-slice_fusion.5), channel_id=1, source_target_pairs={{0,2},{2,0},{1,3},{3,1},{4,6},{6,4},{5,7},{7,5},{8,10},{10,8},{9,1... | collective-permute-start | bytes 1572872 | tf_op jit(solution)/shard_map/d_down_all/ppermute | solution.py:76
  485.7 32.9 %collective-permute-start.88 = (bf16[512,1024]{1,0:T(8,128)(2,1)S(1)}, bf16[512,1024]{1,0:T(8,128)(2,1)S(1)}, u32[]{:S(2)}, u32[]{:S(2)}) collective-permute-start(bf16[512,1024]{1,0:T(8,128)(2,1)S(1)} %copy-done.42), channel_id=1, source_target_pairs={{0,16},{16,0},{1,17},{17,1},{2,18},{18,2},{3,19},{19,3},{4,20},{20... | collective-permute-start | bytes 3145736 | tf_op jit(solution)/shard_map/d_up_near/ppermute | solution.py:76
  504.4 31.4 %collective-permute-start.87 = (bf16[2,1,1,64,2048]{4,3,2,1,0:T(8,128)(2,1)S(1)}, bf16[2,1,1,64,2048]{4,3,2,1,0:T(8,128)(2,1)S(1)}, u32[]{:S(2)}, u32[]{:S(2)}) collective-permute-start(bf16[2,1,1,64,2048]{4,3,2,1,0:T(8,128)(2,1)S(1)} %fusion.25), channel_id=1, source_target_pairs={{0,1},{1,0},{2,3},{3,2},{4,5},{5,4},{6,7},{7,6},{8,9},{9,8},{10,11... | collective-permute-start | bytes 1572872 | tf_op jit(solution)/shard_map/d_down_all/ppermute | solution.py:76
  524.5 32.8 %collective-permute-start.92 = (bf16[1,1,2,2,1,64,2048]{6,5,4,3,2,1,0:T(8,128)(2,1)S(1)}, bf16[1,1,2,2,1,64,2048]{6,5,4,3,2,1,0:T(8,128)(2,1)S(1)}, u32[]{:S(2)}, u32[]{:S(2)}) collective-permute-start(bf16[1,1,2,2,1,64,2048]{6,5,4,3,2,1,0:T(8,128)(2,1)S(1)} %constant_dynamic-slice_fusion), channel_id=1, source_target_pairs={{0,1},{1,0},{2,3},{3,2},{4,5},{5,4},{6,7},{7,6},{8,9},{9,8},{10,11... | collective-permute-start | bytes 3145736 | tf_op jit(solution)/shard_map/out_back/ppermute | solution.py:76
  540.8 36.6 %collective-permute-start.100 = (bf16[1,1,1,64,4096]{4,3,2,1,0:T(8,128)(2,1)S(1)}, bf16[1,1,1,64,4096]{4,3,2,1,0:T(8,128)(2,1)S(1)}, u32[]{:S(2)}, u32[]{:S(2)}) collective-permute-start(bf16[1,1,1,64,4096]{4,3,2,1,0:T(8,128)(2,1)S(1)} %fusion.18), channel_id=1, source_target_pairs={{0,8},{8,0},{1,9},{9,1},{2,10},{10,2},{3,11},{11,3},{4,12},{12,4},... | collective-permute-start | bytes 1572872 | tf_op jit(solution)/shard_map/d_down_all/ppermute | solution.py:76
  (159 other events, 1875.8 us)

commit v7 on v6

--- a/solution.py
+++ b/solution.py
@@ -782,7 +782,10 @@
             parts.append((yield from part_x.take(0, 4)))
             if lax.axis_size("zh") == 2:
                 parts.append((yield from far_x.take(0, 4)))
-            box["w_" + name] = all_rows(parts)
+            columns_here = all_rows(parts)
+            if name == "up":
+                columns_here = yield columns_here
+            box["w_" + name] = columns_here
 
         threads = {name: columns(), name + "_x": send_rows(part, "x", PLAN[name + "_x"], part_x)}
         if lax.axis_size("zh") == 2:

time: 605 us -> 604 us (level)
  waiting for transfers between devices: 259 us -> 252 us
    ppermute x92, waiting for transfers between devices: 237 us -> 227 us  [swap(): return lax.ppermute(array, axis, [(0, 1), (1, 0)])]
    unnamed x201 -> x205, local copies, waits for them, and re-layouts: 18.9 us -> 19.8 us
  transfers between devices with their start and end apart: 103 -> 103, of which waited for: 45 -> 44; matrix products, arithmetic and copies ran while one was open for 30% -> 30% of each run, Pallas kernels for 4% -> 4%
where the time goes in v7:
time: 604 us; the launch traced here: 595 us
  waiting for transfers between devices  252 us (42%)
  starting transfers between devices  108 us (18%)
  other arithmetic  77.1 us (13%)
  matrix products  66.9 us (11%)
  local copies, waits for them, and re-layouts  65.1 us (11%)
  Pallas kernels  23.4 us (4%)
    ppermute x92, waiting for transfers between devices, swap(): return lax.ppermute(array, axis, [(0, 1), (1, 0)])  227 us
    ppermute x92, starting transfers between devices, swap(): return lax.ppermute(array, axis, [(0, 1), (1, 0)])  83.2 us
    dot_general x17, matrix products, dot(): lax.dot_general(left, right, (((left_dim,), (right_dim,)), ((), ())), pre...  66.9 us
    unnamed x205, local copies, waits for them, and re-layouts  19.8 us
  transfers between devices with their start and end apart: 103, of which 44 were waited for; matrix products, arithmetic and copies ran while one was open for 30% of the time, Pallas kernels for 4%

profile of v7, /device:TPU:0, one launch (start us, length us, event | category | flops | bytes accessed | tf_op | source)
XLA Modules:
  0.0 595.4 jit_solution(3777925366111819997)
XLA Ops:
  33.7 12.5 %collective-permute-done.5 = bf16[1,1,1,1,1,64,3072]{6,5,4,3,2,1,0:T(8,128)(2,1)} collective-permute-done((bf16[1,1,1,1,1,64,3072]{6,5,4,3,2,1,0:T(8,128)(2,1)}, bf16[1,1,1,1,1,64,3072]{6,5,4,3,2,1,0:T(8,128)(2,1)}, u32[]{:S(2)}, u32[]{:S(2)}) %collective-permute-start.5) | collective-permute-done | bytes 393248 | tf_op jit(solution)/shard_map/weight_qkv/ppermute | solution.py:76
  54.5 6.4 %collective-permute-done.9 = bf16[2,1,1,64,2048]{4,3,2,1,0:T(8,128)(2,1)S(1)} collective-permute-done((bf16[2,1,1,64,2048]{4,3,2,1,0:T(8,128)(2,1)S(1)}, bf16[2,1,1,64,2048]{4,3,2,1,0:T(8,128)(2,1)S(1)}, u32[]{:S(2)}, u32[]{:S(2)}) %collective-permute-start.9) | collective-permute-done | bytes 524320 | tf_op jit(solution)/shard_map/down/ppermute | solution.py:76
  60.9 11.5 %collective-permute-done.10 = bf16[1,1,2,1,1,64,1536]{6,5,4,3,2,1,0:T(8,128)(2,1)S(1)} collective-permute-done((bf16[1,1,2,1,1,64,1536]{6,5,4,3,2,1,0:T(8,128)(2,1)S(1)}, bf16[1,1,2,1,1,64,1536]{6,5,4,3,2,1,0:T(8,128)(2,1)S(1)}, u32[]{:S(2)}, u32[]{:S(2)}) %collective-permute-start.10) | collective-permute-done | bytes 393248 | tf_op jit(solution)/shard_map/weight_qkv/ppermute | solution.py:76
  82.8 12.2 %collective-permute-done.14 = bf16[2,1,2,64,1024]{4,3,2,1,0:T(8,128)(2,1)} collective-permute-done((bf16[2,1,2,64,1024]{4,3,2,1,0:T(8,128)(2,1)}, bf16[2,1,2,64,1024]{4,3,2,1,0:T(8,128)(2,1)}, u32[]{:S(2)}, u32[]{:S(2)}) %collective-permute-start.14) | collective-permute-done | bytes 524320 | tf_op jit(solution)/shard_map/up/ppermute | solution.py:76
  104.5 5.5 collective-permute-done.18
  115.0 27.5 %collective-permute-done.20 = bf16[128,1024]{1,0:T(8,128)(2,1)S(1)} collective-permute-done((bf16[128,1024]{1,0:T(8,128)(2,1)S(1)}, bf16[128,1024]{1,0:T(8,128)(2,1)S(1)}, u32[]{:S(2)}, u32[]{:S(2)}) %collective-permute-start.20) | collective-permute-done | bytes 262176 | tf_op jit(solution)/shard_map/up_zh/ppermute | solution.py:76
  155.2 8.6 %collective-permute-done.24 = bf16[256,1024]{1,0:T(8,128)(2,1)S(1)} collective-permute-done((bf16[256,1024]{1,0:T(8,128)(2,1)S(1)}, bf16[256,1024]{1,0:T(8,128)(2,1)S(1)}, u32[]{:S(2)}, u32[]{:S(2)}) %collective-permute-start.24) | collective-permute-done | bytes 524320 | tf_op jit(solution)/shard_map/up_zh/ppermute | solution.py:76
  163.8 7.7 %collective-permute-done.25 = bf16[1,1,2,2,1,64,2048]{6,5,4,3,2,1,0:T(8,128)(2,1)S(1)} collective-permute-done((bf16[1,1,2,2,1,64,2048]{6,5,4,3,2,1,0:T(8,128)(2,1)S(1)}, bf16[1,1,2,2,1,64,2048]{6,5,4,3,2,1,0:T(8,128)(2,1)S(1)}, u32[]{:S(2)}, u32[]{:S(2)}) %collective-permute-start.25) | collective-permute-done | bytes 1048608 | tf_op jit(solution)/shard_map/weight_out/ppermute | solution.py:76
  175.5 7.1 %critical.7 = bf16[8,3,48,256]{3,2,1,0:T(8,128)(2,1)} custom-call(s32[8]{0:T(128)S(1)} %fusion.63.order_ref, s32[3,384,1]{2,1,0:T(8,128)S(1)} %copy.42.doc_col_ref, s32[3,1,512]{2,1,0:T(1,128)S(1)} %broadcast_in_dim.20.doc_row_ref, s32[3,1,512]{2,1,0:T(1,128)S(1)} %broadcast_in_dim.24.pos_row_ref, bf16[1280,768]{1,0:T(8,128)(2,1)S(1)} %convolution_convert_fusion.7.tokens_ref), custom_call_target="tpu_custom_call" | custom-call | flops 11324620800 | bytes 2359296 | tf_op jit(solution)/shard_map/critical/pallas_call | solution.py:689
  202.1 7.0 %pad_maximum_fusion = bf16[2048,2048]{1,0:T(8,128)(2,1)} fusion(bf16[512,2048]{1,0:T(8,128)(2,1)} %collective-permute-done.34, bf16[512,2048]{1,0:T(8,128)(2,1)} %bitcast.30, bf16[512,2048]{1,0:T(8,128)(2,1)} %collective-permute-done.33, bf16[512,2048]{1,0:T(8,128)(2,1)} %bitcast.29), kind=kLoop, calls=%fused_computation | loop fusion | flops 33554432 | bytes 16777216 | tf_op jit(solution)/shard_map/weight_out/concatenate | solution.py:844
  209.7 6.3 %collective-permute-done.1 = bf16[144,2048]{1,0:T(8,128)(2,1)} collective-permute-done((bf16[144,2048]{1,0:T(8,128)(2,1)S(1)}, bf16[144,2048]{1,0:T(8,128)(2,1)}, u32[]{:S(2)}, u32[]{:S(2)}) %collective-permute-start.1) | collective-permute-done | bytes 589856 | tf_op jit(solution)/shard_map/cotangent_rows/ppermute | solution.py:76
  216.1 12.7 %collective-permute-done.32 = bf16[128,1024]{1,0:T(8,128)(2,1)S(1)} collective-permute-done((bf16[128,1024]{1,0:T(8,128)(2,1)S(1)}, bf16[128,1024]{1,0:T(8,128)(2,1)S(1)}, u32[]{:S(2)}, u32[]{:S(2)}) %collective-permute-start.32) | collective-permute-done | bytes 262176 | tf_op jit(solution)/shard_map/down_zh/ppermute | solution.py:76
  229.4 4.9 fusion.78
  245.8 9.2 %collective-permute-done.36 = bf16[64,2048]{1,0:T(8,128)(2,1)S(1)} collective-permute-done((bf16[64,2048]{1,0:T(8,128)(2,1)S(1)}, bf16[64,2048]{1,0:T(8,128)(2,1)S(1)}, u32[]{:S(2)}, u32[]{:S(2)}) %collective-permute-start.36) | collective-permute-done | bytes 262176 | tf_op jit(solution)/shard_map/cotangent_rows/ppermute | solution.py:76
  262.1 9.5 %collective-permute-done.46 = bf16[128,1024]{1,0:T(8,128)(2,1)S(1)} collective-permute-done((bf16[128,1024]{1,0:T(8,128)(2,1)S(1)}, bf16[128,1024]{1,0:T(8,128)(2,1)S(1)}, u32[]{:S(2)}, u32[]{:S(2)}) %collective-permute-start.46) | collective-permute-done | bytes 262176 | tf_op jit(solution)/shard_map/down_zh/ppermute | solution.py:76
  278.8 6.9 %fusion.4 = (bf16[1152,1024]{1,0:T(8,128)(2,1)S(1)}, bf16[1152,1024]{1,0:T(8,128)(2,1)S(1)}) fusion(bf16[1152,2048]{1,0:T(8,128)(2,1)S(1)} %constant_dynamic-update-slice_fusion.24, bf16[2048,1024]{1,0:T(8,128)(2,1)S(1)} %constant_dynamic-update-slice_fusion.13), kind=kOutput, calls=%fused_computation.8 | convolution fusion | flops 4844814336 | bytes 13631488 | tf_op jit(solution)/shard_map/critical/dot_general | solution.py:54
  285.7 5.9 convolution_convert_fusion.5
  296.4 5.5 multiply_convert_fusion
  301.9 5.3 convolution_convert_fusion.1
  318.5 6.0 %convolution_convert_fusion.4 = bf16[2048,1024]{1,0:T(8,128)(2,1)S(1)} fusion(bf16[1152,2048]{1,0:T(8,128)(2,1)S(1)} %bitcast.193, bf16[1152,1024]{1,0:T(8,128)(2,1)S(1)} %copy-done.79), kind=kOutput, calls=%fused_computation.14 | convolution fusion | flops 4833935360 | bytes 11272192 | tf_op jit(solution)/shard_map/critical/dot_general | solution.py:54
  326.2 6.4 %collective-permute-done.52 = bf16[64,2048]{1,0:T(8,128)(2,1)S(1)} collective-permute-done((bf16[64,2048]{1,0:T(8,128)(2,1)S(1)}, bf16[64,2048]{1,0:T(8,128)(2,1)S(1)}, u32[]{:S(2)}, u32[]{:S(2)}) %collective-permute-start.52) | collective-permute-done | bytes 262176 | tf_op jit(solution)/shard_map/critical/ppermute | solution.py:76
  335.2 5.4 convolution_convert_fusion
  340.6 6.8 %collective-permute-done.58 = bf16[256,1024]{1,0:T(8,128)(2,1)S(1)} collective-permute-done((bf16[256,1024]{1,0:T(8,128)(2,1)S(1)}, bf16[256,1024]{1,0:T(8,128)(2,1)S(1)}, u32[]{:S(2)}, u32[]{:S(2)}) %collective-permute-start.58) | collective-permute-done | bytes 524320 | tf_op jit(solution)/shard_map/d_up_far/ppermute | solution.py:76
  390.7 12.3 %collective-permute-done.62 = bf16[256,1024]{1,0:T(8,128)(2,1)} collective-permute-done((bf16[256,1024]{1,0:T(8,128)(2,1)}, bf16[256,1024]{1,0:T(8,128)(2,1)}, u32[]{:S(2)}, u32[]{:S(2)}) %collective-permute-start.62) | collective-permute-done | bytes 524320 | tf_op jit(solution)/shard_map/d_down_zh/ppermute | solution.py:76
  425.6 11.4 %critical.12 = bf16[1280,768]{1,0:T(8,128)(2,1)S(1)} custom-call(s32[8]{0:T(128)S(1)} %fusion.63.order_ref, s32[3,384,1]{2,1,0:T(8,128)S(1)} %copy.42.doc_col_ref, s32[3,1,512]{2,1,0:T(1,128)S(1)} %broadcast_in_dim.20.doc_row_ref, s32[3,1,512]{2,1,0:T(1,128)S(1)} %broadcast_in_dim.24.pos_row_ref, bf16[1280,768]{1,0:T(8,128)(2,1)S(1)} %copy-done.9, ...), custom_call_target="tpu_custom_call" | custom-call | flops 16986931200 | bytes 4128768 | tf_op jit(solution)/shard_map/critical/pallas_call | solution.py:735
  440.8 7.4 %convolution_convert_fusion.6 = bf16[2048,768]{1,0:T(8,128)(2,1)S(1)} fusion(bf16[1280,2048]{1,0:T(8,128)(2,1)} %copy-done.27, bf16[1280,768]{1,0:T(8,128)(2,1)S(1)} %critical.12), kind=kOutput, calls=%fused_computation.16 | convolution fusion | flops 4028104704 | bytes 10354688 | tf_op jit(solution)/shard_map/critical/dot_general | solution.py:54
  508.6 5.3 collective-permute-start.90
  521.1 9.5 %collective-permute-done.87 = bf16[2,1,1,64,2048]{4,3,2,1,0:T(8,128)(2,1)S(1)} collective-permute-done((bf16[2,1,1,64,2048]{4,3,2,1,0:T(8,128)(2,1)S(1)}, bf16[2,1,1,64,2048]{4,3,2,1,0:T(8,128)(2,1)S(1)}, u32[]{:S(2)}, u32[]{:S(2)}) %collective-permute-start.87) | collective-permute-done | bytes 524320 | tf_op jit(solution)/shard_map/d_down_all/ppermute | solution.py:76
  530.6 8.0 %collective-permute-done.89 = bf16[1,1,2,1,1,64,1536]{6,5,4,3,2,1,0:T(8,128)(2,1)S(1)} collective-permute-done((bf16[1,1,2,1,1,64,1536]{6,5,4,3,2,1,0:T(8,128)(2,1)S(1)}, bf16[1,1,2,1,1,64,1536]{6,5,4,3,2,1,0:T(8,128)(2,1)S(1)}, u32[]{:S(2)}, u32[]{:S(2)}) %collective-permute-start.89) | collective-permute-done | bytes 393248 | tf_op jit(solution)/shard_map/qkv_back/ppermute | solution.py:76
  555.5 5.7 collective-permute-done.93
  561.2 5.1 collective-permute-done.91
  579.0 10.0 %collective-permute-done.97 = bf16[1,64,2048]{2,1,0:T(8,128)(2,1)S(1)} collective-permute-done((bf16[1,64,2048]{2,1,0:T(8,128)(2,1)S(1)}, bf16[1,64,2048]{2,1,0:T(8,128)(2,1)S(1)}, u32[]{:S(2)}, u32[]{:S(2)}) %collective-permute-start.97) | collective-permute-done | bytes 262176 | tf_op jit(solution)/shard_map/out_back/ppermute | solution.py:222
  (609 shorter events, 320.7 us)
Async XLA Ops:
  5.1 42.6 %collective-permute-start.2 = (bf16[144,2048]{1,0:T(8,128)(2,1)S(1)}, bf16[144,2048]{1,0:T(8,128)(2,1)}, u32[]{:S(2)}, u32[]{:S(2)}) collective-permute-start(bf16[144,2048]{1,0:T(8,128)(2,1)S(1)} %multiply_convert_fusion.3), channel_id=1, source_target_pairs={{0,2},{2,4},{4,6},{6,0},{1,3},{3,5},{5,7},{7,1},{8,10},{10,12},{12... | collective-permute-start | bytes 1769480 | tf_op jit(solution)/shard_map/critical/ppermute | solution.py:237
  8.2 45.8 %collective-permute-start.7 = (bf16[144,2048]{1,0:T(8,128)(2,1)S(1)}, bf16[144,2048]{1,0:T(8,128)(2,1)}, u32[]{:S(2)}, u32[]{:S(2)}) collective-permute-start(bf16[144,2048]{1,0:T(8,128)(2,1)S(1)} %multiply_convert_fusion.3), channel_id=1, source_target_pairs={{0,1},{1,0},{2,3},{3,2},{4,5},{5,4},{6,7},{7,6},{8,9},{9,8},{10,11... | collective-permute-start | bytes 1769480 | tf_op jit(solution)/shard_map/critical/ppermute | solution.py:76
  11.4 34.8 %collective-permute-start.5 = (bf16[1,1,1,1,1,64,3072]{6,5,4,3,2,1,0:T(8,128)(2,1)}, bf16[1,1,1,1,1,64,3072]{6,5,4,3,2,1,0:T(8,128)(2,1)}, u32[]{:S(2)}, u32[]{:S(2)}) collective-permute-start(bf16[1,1,1,1,1,64,3072]{6,5,4,3,2,1,0:T(8,128)(2,1)} %dynamic-slice_bitcast_fusion.3), channel_id=1, source_target_pairs={{0,4},{4,0},{1,5},{5,1},{2,6},{6,2},{3,7},{7,3},{8,12},{12,8},{9,1... | collective-permute-start | bytes 1179656 | tf_op jit(solution)/shard_map/weight_qkv/ppermute | solution.py:76
  30.1 51.2 %collective-permute-start.15 = (bf16[1,1,1,1,1,64,2048]{6,5,4,3,2,1,0:T(8,128)(2,1)}, bf16[1,1,1,1,1,64,2048]{6,5,4,3,2,1,0:T(8,128)(2,1)}, u32[]{:S(2)}, u32[]{:S(2)}) collective-permute-start(bf16[1,1,1,1,1,64,2048]{6,5,4,3,2,1,0:T(8,128)(2,1)} %bitcast.23), channel_id=1, source_target_pairs={{0,4},{4,0},{1,5},{5,1},{2,6},{6,2},{3,7},{7,3},{8,12},{12,8},{9,1... | collective-permute-start | bytes 786440 | tf_op jit(solution)/shard_map/weight_out/ppermute | solution.py:76
  54.0 41.0 %collective-permute-start.13 = (bf16[144,2048]{1,0:T(8,128)(2,1)}, bf16[144,2048]{1,0:T(8,128)(2,1)}, u32[]{:S(2)}, u32[]{:S(2)}) collective-permute-start(bf16[144,2048]{1,0:T(8,128)(2,1)} %collective-permute-done.2), channel_id=1, source_target_pairs={{0,1},{1,0},{2,3},{3,2},{4,5},{5,4},{6,7},{7,6},{8,9},{9,8},{10,11... | collective-permute-start | bytes 1769480 | tf_op jit(solution)/shard_map/critical/ppermute | solution.py:76
  60.9 34.0 %collective-permute-start.14 = (bf16[2,1,2,64,1024]{4,3,2,1,0:T(8,128)(2,1)}, bf16[2,1,2,64,1024]{4,3,2,1,0:T(8,128)(2,1)}, u32[]{:S(2)}, u32[]{:S(2)}) collective-permute-start(bf16[2,1,2,64,1024]{4,3,2,1,0:T(8,128)(2,1)} %fusion.29), channel_id=1, source_target_pairs={{0,2},{2,0},{1,3},{3,1},{4,6},{6,4},{5,7},{7,5},{8,10},{10,8},{9,1... | collective-permute-start | bytes 1572872 | tf_op jit(solution)/shard_map/up/ppermute | solution.py:76
  81.3 31.3 %collective-permute-start.11 = (bf16[144,2048]{1,0:T(8,128)(2,1)}, bf16[144,2048]{1,0:T(8,128)(2,1)S(1)}, u32[]{:S(2)}, u32[]{:S(2)}) collective-permute-start(bf16[144,2048]{1,0:T(8,128)(2,1)} %collective-permute-done.6), channel_id=1, source_target_pairs={{0,1},{1,0},{2,3},{3,2},{4,5},{5,4},{6,7},{7,6},{8,9},{9,8},{10,11... | collective-permute-start | bytes 1769480 | tf_op jit(solution)/shard_map/critical/ppermute | solution.py:76
  99.8 45.6 %collective-permute-start.22 = (bf16[1,1,2,2,2,64,768]{6,5,4,3,2,1,0:T(8,128)(2,1)S(1)}, bf16[1,1,2,2,2,64,768]{6,5,4,3,2,1,0:T(8,128)(2,1)S(1)}, u32[]{:S(2)}, u32[]{:S(2)}) collective-permute-start(bf16[1,1,2,2,2,64,768]{6,5,4,3,2,1,0:T(8,128)(2,1)S(1)} %pad_maximum_fusion.9), channel_id=1, source_target_pairs={{0,16},{16,0},{1,17},{17,1},{2,18},{18,2},{3,19},{19,3},{4,20},{20... | collective-permute-start | bytes 2359304 | tf_op jit(solution)/shard_map/weight_qkv/ppermute | solution.py:76
  102.7 42.7 %collective-permute-start.19 = (bf16[512,1024]{1,0:T(8,128)(2,1)S(1)}, bf16[512,1024]{1,0:T(8,128)(2,1)}, u32[]{:S(2)}, u32[]{:S(2)}) collective-permute-start(bf16[512,1024]{1,0:T(8,128)(2,1)S(1)} %bitcast.166), channel_id=1, source_target_pairs={{0,16},{16,0},{1,17},{17,1},{2,18},{18,2},{3,19},{19,3},{4,20},{20... | collective-permute-start | bytes 3145736 | tf_op jit(solution)/shard_map/up_x/ppermute | solution.py:76
  104.4 38.0 %collective-permute-start.21 = (bf16[1,1,2,1,1,64,2048]{6,5,4,3,2,1,0:T(8,128)(2,1)S(1)}, bf16[1,1,2,1,1,64,2048]{6,5,4,3,2,1,0:T(8,128)(2,1)S(1)}, u32[]{:S(2)}, u32[]{:S(2)}) collective-permute-start(bf16[1,1,2,1,1,64,2048]{6,5,4,3,2,1,0:T(8,128)(2,1)S(1)} %pad_maximum_fusion.14), channel_id=1, source_target_pairs={{0,2},{2,0},{1,3},{3,1},{4,6},{6,4},{5,7},{7,5},{8,10},{10,8},{9,1... | collective-permute-start | bytes 1572872 | tf_op jit(solution)/shard_map/weight_out/ppermute | solution.py:76
  110.1 35.3 %collective-permute-start.17 = (bf16[144,2048]{1,0:T(8,128)(2,1)}, bf16[144,2048]{1,0:T(8,128)(2,1)S(1)}, u32[]{:S(2)}, u32[]{:S(2)}) collective-permute-start(bf16[144,2048]{1,0:T(8,128)(2,1)} %collective-permute-done.12), channel_id=1, source_target_pairs={{0,1},{1,0},{2,3},{3,2},{4,5},{5,4},{6,7},{7,6},{8,9},{9,8},{10,11... | collective-permute-start | bytes 1769480 | tf_op jit(solution)/shard_map/critical/ppermute | solution.py:76
  112.6 29.9 %collective-permute-start.20 = (bf16[128,1024]{1,0:T(8,128)(2,1)S(1)}, bf16[128,1024]{1,0:T(8,128)(2,1)S(1)}, u32[]{:S(2)}, u32[]{:S(2)}) collective-permute-start(bf16[128,1024]{1,0:T(8,128)(2,1)S(1)} %get-tuple-element.366), channel_id=1, source_target_pairs={{0,4},{4,0},{1,5},{5,1},{2,6},{6,2},{3,7},{7,3},{8,12},{12,8},{9,1... | collective-permute-start | bytes 786440 | tf_op jit(solution)/shard_map/up_zh/ppermute | solution.py:76
  142.4 40.1 %collective-permute-start.28 = (bf16[128,1024]{1,0:T(8,128)(2,1)S(1)}, bf16[128,1024]{1,0:T(8,128)(2,1)S(1)}, u32[]{:S(2)}, u32[]{:S(2)}) collective-permute-start(bf16[128,1024]{1,0:T(8,128)(2,1)S(1)} %get-tuple-element.365), channel_id=1, source_target_pairs={{0,4},{4,0},{1,5},{5,1},{2,6},{6,2},{3,7},{7,3},{8,12},{12,8},{9,1... | collective-permute-start | bytes 786440 | tf_op jit(solution)/shard_map/up_zh/ppermute | solution.py:76
  150.3 32.3 %collective-permute-start.27 = (bf16[128,1024]{1,0:T(8,128)(2,1)S(1)}, bf16[128,1024]{1,0:T(8,128)(2,1)S(1)}, u32[]{:S(2)}, u32[]{:S(2)}) collective-permute-start(bf16[128,1024]{1,0:T(8,128)(2,1)S(1)} %get-tuple-element.362), channel_id=1, source_target_pairs={{0,4},{4,0},{1,5},{5,1},{2,6},{6,2},{3,7},{7,3},{8,12},{12,8},{9,1... | collective-permute-start | bytes 786440 | tf_op jit(solution)/shard_map/down_zh/ppermute | solution.py:76
  189.8 26.3 %collective-permute-start.1 = (bf16[144,2048]{1,0:T(8,128)(2,1)S(1)}, bf16[144,2048]{1,0:T(8,128)(2,1)}, u32[]{:S(2)}, u32[]{:S(2)}) collective-permute-start(bf16[144,2048]{1,0:T(8,128)(2,1)S(1)} %cotangent_rows.1), channel_id=1, source_target_pairs={{0,2},{2,0},{1,3},{3,1},{4,6},{6,4},{5,7},{7,5},{8,10},{10,8},{9,1... | collective-permute-start | bytes 1769480 | tf_op jit(solution)/shard_map/cotangent_rows/ppermute | solution.py:76
  189.9 38.9 %all-to-all-start = ((bf16[8,144,256]{2,1,0:T(8,128)(2,1)}), bf16[8,144,256]{2,1,0:T(8,128)(2,1)S(1)}, u32[]{:S(2)}, u32[]{:S(2)}) async-start(bf16[8,144,256]{2,1,0:T(8,128)(2,1)} %bitcast.27), calls=%async_computation | async-start | bytes 1179648 | tf_op jit(solution)/shard_map/critical/all_to_all | solution.py:692
  195.4 33.3 %collective-permute-start.31 = (bf16[256,1024]{1,0:T(8,128)(2,1)S(1)}, bf16[256,1024]{1,0:T(8,128)(2,1)}, u32[]{:S(2)}, u32[]{:S(2)}) collective-permute-start(bf16[256,1024]{1,0:T(8,128)(2,1)S(1)} %bitcast.191), channel_id=1, source_target_pairs={{0,16},{16,0},{1,17},{17,1},{2,18},{18,2},{3,19},{19,3},{4,20},{20... | collective-permute-start | bytes 1572872 | tf_op jit(solution)/shard_map/down_x/ppermute | solution.py:76
  199.0 29.7 %collective-permute-start.32 = (bf16[128,1024]{1,0:T(8,128)(2,1)S(1)}, bf16[128,1024]{1,0:T(8,128)(2,1)S(1)}, u32[]{:S(2)}, u32[]{:S(2)}) collective-permute-start(bf16[128,1024]{1,0:T(8,128)(2,1)S(1)} %copy-done.69), channel_id=1, source_target_pairs={{0,4},{4,0},{1,5},{5,1},{2,6},{6,2},{3,7},{7,3},{8,12},{12,8},{9,1... | collective-permute-start | bytes 786440 | tf_op jit(solution)/shard_map/down_zh/ppermute | solution.py:76
  202.0 38.6 %collective-permute-start.40 = (bf16[128,1024]{1,0:T(8,128)(2,1)}, bf16[128,1024]{1,0:T(8,128)(2,1)S(1)}, u32[]{:S(2)}, u32[]{:S(2)}) collective-permute-start(bf16[128,1024]{1,0:T(8,128)(2,1)} %get-tuple-element.360), channel_id=1, source_target_pairs={{0,4},{4,0},{1,5},{5,1},{2,6},{6,2},{3,7},{7,3},{8,12},{12,8},{9,1... | collective-permute-start | bytes 786440 | tf_op jit(solution)/shard_map/down_zh/ppermute | solution.py:76
  209.1 32.2 %collective-permute-start.41 = (bf16[512,1024]{1,0:T(8,128)(2,1)}, bf16[512,1024]{1,0:T(8,128)(2,1)}, u32[]{:S(2)}, u32[]{:S(2)}) collective-permute-start(bf16[512,1024]{1,0:T(8,128)(2,1)} %pad_maximum_fusion.8), channel_id=1, source_target_pairs={{0,16},{16,0},{1,17},{17,1},{2,18},{18,2},{3,19},{19,3},{4,20},{20... | collective-permute-start | bytes 3145736 | tf_op jit(solution)/shard_map/up_far/ppermute | solution.py:76
  365.6 37.4 %collective-permute-start.62 = (bf16[256,1024]{1,0:T(8,128)(2,1)}, bf16[256,1024]{1,0:T(8,128)(2,1)}, u32[]{:S(2)}, u32[]{:S(2)}) collective-permute-start(bf16[256,1024]{1,0:T(8,128)(2,1)} %slice_add_fusion.12), channel_id=1, source_target_pairs={{0,4},{4,0},{1,5},{5,1},{2,6},{6,2},{3,7},{7,3},{8,12},{12,8},{9,1... | collective-permute-start | bytes 1572872 | tf_op jit(solution)/shard_map/d_down_zh/ppermute | solution.py:76
  368.6 40.0 %collective-permute-start.64 = (bf16[128,1024]{1,0:T(8,128)(2,1)}, bf16[128,1024]{1,0:T(8,128)(2,1)}, u32[]{:S(2)}, u32[]{:S(2)}) collective-permute-start(bf16[128,1024]{1,0:T(8,128)(2,1)} %get-tuple-element.382), channel_id=1, source_target_pairs={{0,4},{4,0},{1,5},{5,1},{2,6},{6,2},{3,7},{7,3},{8,12},{12,8},{9,1... | collective-permute-start | bytes 786440 | tf_op jit(solution)/shard_map/d_up_zh/ppermute | solution.py:76
  371.6 37.1 %collective-permute-start.63 = (bf16[256,1024]{1,0:T(8,128)(2,1)}, bf16[256,1024]{1,0:T(8,128)(2,1)S(1)}, u32[]{:S(2)}, u32[]{:S(2)}) collective-permute-start(bf16[256,1024]{1,0:T(8,128)(2,1)} %get-tuple-element.299), channel_id=1, source_target_pairs={{0,16},{16,0},{1,17},{17,1},{2,18},{18,2},{3,19},{19,3},{4,20},{20... | collective-permute-start | bytes 1572872 | tf_op jit(solution)/shard_map/d_up_far/ppermute | solution.py:76
  373.0 47.5 %all-to-all-start.1 = ((bf16[8,144,256]{2,1,0:T(8,128)(2,1)}), bf16[8,144,256]{2,1,0:T(8,128)(2,1)S(1)}, u32[]{:S(2)}, u32[]{:S(2)}) async-start(bf16[8,144,256]{2,1,0:T(8,128)(2,1)} %bitcast.186), calls=%async_computation.1 | async-start | bytes 1179648 | tf_op jit(solution)/shard_map/critical/all_to_all | solution.py:734
  388.0 32.6 %collective-permute-start.66 = (bf16[256,2048]{1,0:T(8,128)(2,1)}, bf16[256,2048]{1,0:T(8,128)(2,1)}, u32[]{:S(2)}, u32[]{:S(2)}) collective-permute-start(bf16[256,2048]{1,0:T(8,128)(2,1)} %get-tuple-element.313), channel_id=1, source_target_pairs={{0,16},{16,0},{1,17},{17,1},{2,18},{18,2},{3,19},{19,3},{4,20},{20... | collective-permute-start | bytes 3145736 | tf_op jit(solution)/shard_map/out_back/ppermute | solution.py:76
  408.7 29.9 %collective-permute-start.70 = (bf16[128,1024]{1,0:T(8,128)(2,1)}, bf16[128,1024]{1,0:T(8,128)(2,1)}, u32[]{:S(2)}, u32[]{:S(2)}) collective-permute-start(bf16[128,1024]{1,0:T(8,128)(2,1)} %get-tuple-element.381), channel_id=1, source_target_pairs={{0,4},{4,0},{1,5},{5,1},{2,6},{6,2},{3,7},{7,3},{8,12},{12,8},{9,1... | collective-permute-start | bytes 786440 | tf_op jit(solution)/shard_map/d_up_zh/ppermute | solution.py:76
  408.7 32.1 %collective-permute-start.69 = (bf16[512,1024]{1,0:T(8,128)(2,1)}, bf16[512,1024]{1,0:T(8,128)(2,1)}, u32[]{:S(2)}, u32[]{:S(2)}) collective-permute-start(bf16[512,1024]{1,0:T(8,128)(2,1)} %slice.311), channel_id=1, source_target_pairs={{0,16},{16,0},{1,17},{17,1},{2,18},{18,2},{3,19},{19,3},{4,20},{20... | collective-permute-start | bytes 3145736 | tf_op jit(solution)/shard_map/d_down_near/ppermute | solution.py:76
  415.1 62.7 %collective-permute-start.78 = (bf16[256,2048]{1,0:T(8,128)(2,1)}, bf16[256,2048]{1,0:T(8,128)(2,1)}, u32[]{:S(2)}, u32[]{:S(2)}) collective-permute-start(bf16[256,2048]{1,0:T(8,128)(2,1)} %get-tuple-element.312), channel_id=1, source_target_pairs={{0,16},{16,0},{1,17},{17,1},{2,18},{18,2},{3,19},{19,3},{4,20},{20... | collective-permute-start | bytes 3145736 | tf_op jit(solution)/shard_map/out_back/ppermute | solution.py:76
  482.2 34.6 %collective-permute-start.88 = (bf16[512,1024]{1,0:T(8,128)(2,1)S(1)}, bf16[512,1024]{1,0:T(8,128)(2,1)S(1)}, u32[]{:S(2)}, u32[]{:S(2)}) collective-permute-start(bf16[512,1024]{1,0:T(8,128)(2,1)S(1)} %copy-done.44), channel_id=1, source_target_pairs={{0,16},{16,0},{1,17},{17,1},{2,18},{18,2},{3,19},{19,3},{4,20},{20... | collective-permute-start | bytes 3145736 | tf_op jit(solution)/shard_map/d_up_near/ppermute | solution.py:76
  501.8 28.8 %collective-permute-start.87 = (bf16[2,1,1,64,2048]{4,3,2,1,0:T(8,128)(2,1)S(1)}, bf16[2,1,1,64,2048]{4,3,2,1,0:T(8,128)(2,1)S(1)}, u32[]{:S(2)}, u32[]{:S(2)}) collective-permute-start(bf16[2,1,1,64,2048]{4,3,2,1,0:T(8,128)(2,1)S(1)} %fusion.25), channel_id=1, source_target_pairs={{0,1},{1,0},{2,3},{3,2},{4,5},{5,4},{6,7},{7,6},{8,9},{9,8},{10,11... | collective-permute-start | bytes 1572872 | tf_op jit(solution)/shard_map/d_down_all/ppermute | solution.py:76
  519.4 32.5 %collective-permute-start.92 = (bf16[1,1,2,2,1,64,2048]{6,5,4,3,2,1,0:T(8,128)(2,1)S(1)}, bf16[1,1,2,2,1,64,2048]{6,5,4,3,2,1,0:T(8,128)(2,1)S(1)}, u32[]{:S(2)}, u32[]{:S(2)}) collective-permute-start(bf16[1,1,2,2,1,64,2048]{6,5,4,3,2,1,0:T(8,128)(2,1)S(1)} %constant_dynamic-slice_fusion), channel_id=1, source_target_pairs={{0,1},{1,0},{2,3},{3,2},{4,5},{5,4},{6,7},{7,6},{8,9},{9,8},{10,11... | collective-permute-start | bytes 3145736 | tf_op jit(solution)/shard_map/out_back/ppermute | solution.py:76
  538.9 36.6 %collective-permute-start.100 = (bf16[1,1,1,64,4096]{4,3,2,1,0:T(8,128)(2,1)S(1)}, bf16[1,1,1,64,4096]{4,3,2,1,0:T(8,128)(2,1)S(1)}, u32[]{:S(2)}, u32[]{:S(2)}) collective-permute-start(bf16[1,1,1,64,4096]{4,3,2,1,0:T(8,128)(2,1)S(1)} %fusion.18), channel_id=1, source_target_pairs={{0,8},{8,0},{1,9},{9,1},{2,10},{10,2},{3,11},{11,3},{4,12},{12,4},... | collective-permute-start | bytes 1572872 | tf_op jit(solution)/shard_map/d_down_all/ppermute | solution.py:76
  (161 other events, 1875.5 us)
